TPU v7x, 512 devices: a whole 4x8x8 slice. The times are simulated.
512 devices in a mesh: fsdp: 32 (over y, x), ctx: 8 (over z), tp: 2 (over core).
Axes of the slice: x: 4, y: 8, z: 8, core: 2. Of those that a mesh axis runs over, the one named last changes fastest.
Arguments:
- tokens: bfloat16 [1, 4096, 8192], P(None, 'ctx', ('fsdp', 'tp')), may hold values from -6 to 6
- w_in: bfloat16 [8192, 3, 8192], P('ctx', None, ('fsdp', 'tp')), may hold values from -0.0625 to 0.0625
- short_taps: float32 [7, 3, 8192], P(None, None, ('fsdp', 'tp')), may hold values from -2 to 2
- mr_taps: float32 [128, 8192], P(None, ('fsdp', 'tp')), may hold values from -1 to 1
- skip: float32 [8192], P(('fsdp', 'tp')), may hold values from 0.5 to 1.5
- genome_ids: int32 [1, 4096], replicated, may hold values from 0 to 3, never falling along the last dimension, each value on 1 to 2048 neighbouring positions
Outputs:
- gated: bfloat16 [1, 4096, 8192], P(None, 'ctx', ('fsdp', 'tp'))
Inputs may be any that keep to these rules, and one draw needn't show every extreme that they name: `genome_ids`: ids never fall along a sequence; each genome holds 1 to 2048 positions, and one holds exactly 2048.
All inputs are finite; a program needn't handle non-finite values.
Results may differ from a plain program's by a relative error of at most 0.007.
Values may be sent and summed in bfloat16 or wider, within the bound.
No kernel may reach another device: no remote copies, remote signals or barrier semaphores. Data moves between devices by JAX's collectives and lax.ppermute only.
A program may use at most 64 MiB of HBM per device.

v0:
```python
import jax
import jax.numpy as jnp
from jax import lax
from jax.sharding import PartitionSpec as P


def passed_along(value, axis, steps):
    count = lax.axis_size(axis)
    leading, last = (max(0, -steps), min(count, count - steps))
    return lax.ppermute(value, axis, [(source, source + steps) for source in range(leading, last)])


def causal_mix(padded, segment_pad, taps, count):
    reach = taps.shape[0] - 1
    target = segment_pad[:, reach : reach + count]

    def add_lag(offset, total):
        piece = lax.dynamic_slice_in_dim(padded, reach - offset, count, 1).astype(jnp.float32)
        source = lax.dynamic_slice_in_dim(segment_pad, reach - offset, count, 1)
        same = (source == target).astype(jnp.float32)[..., None]
        weight = lax.dynamic_index_in_dim(taps, offset, 0, keepdims=False)
        return total + weight * piece * same

    start = jnp.zeros(padded.shape[:1] + (count,) + padded.shape[2:], jnp.float32)
    return lax.fori_loop(0, reach + 1, add_lag, start)


def body(tokens, w_in, short_taps, mr_taps, skip, genome_ids):
    length = tokens.shape[1]
    channels = short_taps.shape[2]
    short_reach = short_taps.shape[0] - 1
    long_reach = mr_taps.shape[0] - 1
    block = lax.all_gather(tokens, "tp", axis=2, tiled=True)
    panel_all = lax.all_gather(w_in, "ctx", axis=0, tiled=True).reshape(-1, 3 * channels)
    summed = jnp.einsum(
        "bld,dk->blk",
        lax.all_gather(block, "fsdp", axis=2, tiled=True),
        panel_all,
        preferred_element_type=jnp.float32,
    )
    raw = summed.astype(jnp.bfloat16)
    position = lax.axis_index("ctx") * length
    both_reach = long_reach + short_reach
    ids_padded = jnp.pad(genome_ids, ((0, 0), (both_reach, 0)), constant_values=-1)
    segment_long = lax.dynamic_slice_in_dim(
        ids_padded, position + short_reach, length + long_reach, 1
    )
    taps_short = short_taps.reshape(short_taps.shape[0], -1)
    rim_rows = passed_along(raw[:, length - short_reach :, :], "ctx", 1)
    segment_short = lax.dynamic_slice_in_dim(
        ids_padded, position + long_reach, length + short_reach, 1
    )
    featured = causal_mix(jnp.concatenate([rim_rows, raw], 1), segment_short, taps_short, length)
    queries = featured[..., :channels]
    mixed = (featured[..., channels : 2 * channels] * featured[..., 2 * channels :]).astype(
        jnp.bfloat16
    )
    earlier = passed_along(mixed[:, length - long_reach :, :], "ctx", 1)
    mixed_pad = jnp.concatenate([earlier, mixed], 1)
    filtered = causal_mix(mixed_pad, segment_long, mr_taps, length)
    return (queries * (filtered + skip * mixed.astype(jnp.float32))).astype(jnp.bfloat16)


def solution(mesh):
    in_specs = (
        P(None, "ctx", ("fsdp", "tp")),
        P("ctx", None, ("fsdp", "tp")),
        P(None, None, ("fsdp", "tp")),
        P(None, ("fsdp", "tp")),
        P(("fsdp", "tp")),
        P(),
    )
    out_specs = P(None, "ctx", ("fsdp", "tp"))
    return jax.shard_map(body, mesh=mesh, in_specs=in_specs, out_specs=out_specs, check_vma=False)
```

profile of v0, /device:TPU:192, one launch (start us, length us, event | category | flops | bytes accessed | tf_op | source)
XLA Modules:
  0.0 362.7 jit_solution(16559129843898876737)
XLA Ops:
  6.5 2.3 copy.7
  8.9 3.5 all_gather.9
  12.5 0.8 constant_dynamic-slice_fusion.1
  13.3 75.4 %all-gather.5.cloned.1.call-done = bf16[8192,3,128]{0,2,1:T(8,128)(2,1)} async-done(((bf16[1024,3,128]{0,2,1:T(8,128)(2,1)}), bf16[8192,3,128]{0,2,1:T(8,128)(2,1)}) %all-gather.5.cloned.1.call-update) | async-done | bytes 6291472 | tf_op jit(solution)/shard_map/all_gather | solution.py:34
  88.7 111.1 %all-gather.3.cloned.1.call-done = bf16[1,512,8192]{2,1,0:T(8,128)(2,1)} async-done(((bf16[1,512,256]{2,1,0:T(8,128)(2,1)}), bf16[1,512,8192]{2,1,0:T(8,128)(2,1)}) %all-gather.3.cloned.1.call-update) | async-done | bytes 8388624 | tf_op jit(solution)/shard_map/all_gather | solution.py:37
  199.9 9.7 %fusion.6 = bf16[1,512,384]{2,1,0:T(8,128)(2,1)S(1)} fusion(bf16[8192,384]{0,1:T(8,128)(2,1)} %bitcast.25, bf16[1,512,8192]{2,1,0:T(8,128)(2,1)} %all-gather.3.cloned.1.call-done), kind=kOutput, calls=%fused_computation.10 | convolution fusion | flops 3221422080 | bytes 15073280 | tf_op jit(solution)/shard_map/bld,dk->blk/dot_general | solution.py:35
  209.6 4.8 %collective-permute-start = (bf16[1,6,384]{2,1,0:T(8,128)(2,1)S(1)}, bf16[1,6,384]{2,1,0:T(8,128)(2,1)S(1)}, u32[]{:S(2)}, u32[]{:S(2)}) collective-permute-start(bf16[1,6,384]{2,1,0:T(8,128)(2,1)S(1)} %slice.28), channel_id=1, source_target_pairs={{0,2},{2,4},{4,6},{6,8},{8,10},{10,12},{12,14},{1,3},{3,5},{5,7},{... | collective-permute-start | bytes 13832 | tf_op jit(solution)/shard_map/ppermute | solution.py:10
  214.5 1.2 collective-permute-done
  215.8 7.9 %while.32 = (s32[]{:T(128)}, f32[1,512,384]{2,1,0:T(8,128)S(1)}, f32[7,384]{1,0:T(8,128)}, bf16[1,518,384]{2,1,0:T(8,128)(2,1)S(1)}, s32[1,518]{1,0:T(1,128)S(1)...) while((s32[]{:T(128)}, f32[1,512,384]{2,1,0:T(8,128)S(1)}, ...), condition=%wide.region_1.2_spmd.clone, body=%wide.region_0.1_spmd.clone.sunk | while | flops 984071 | bytes 1979049 | solution.py:25
  215.9 0.7 dynamic-slice_reduce_fusion.2
  217.0 0.7 dynamic-slice_reduce_fusion.2
  218.2 0.7 dynamic-slice_reduce_fusion.2
  219.3 0.7 dynamic-slice_reduce_fusion.2
  220.4 0.7 dynamic-slice_reduce_fusion.2
  221.6 0.7 dynamic-slice_reduce_fusion.2
  222.7 0.7 dynamic-slice_reduce_fusion.2
  223.8 5.4 %collective-permute-start.1 = (bf16[1,127,128]{2,1,0:T(8,128)(2,1)S(1)}, bf16[1,127,128]{2,1,0:T(8,128)(2,1)S(1)}, u32[]{:S(2)}, u32[]{:S(2)}) collective-permute-start(bf16[1,127,128]{2,1,0:T(8,128)(2,1)S(1)} %slice.29), channel_id=1, source_target_pairs={{0,2},{2,4},{4,6},{6,8},{8,10},{10,12},{12,14},{1,3},{3,5},{5,7},{... | collective-permute-start | bytes 97544 | tf_op jit(solution)/shard_map/ppermute | solution.py:10
  229.3 1.5 collective-permute-done.1
  230.8 124.3 %while.33 = (s32[]{:T(128)}, f32[1,512,128]{2,1,0:T(8,128)S(1)}, f32[128,128]{1,0:T(8,128)}, bf16[1,639,128]{2,1,0:T(8,128)(2,1)S(1)}, s32[1,639]{1,0:T(1,128)S(...) while((s32[]{:T(128)}, f32[1,512,128]{2,1,0:T(8,128)S(1)}, ...), condition=%wide.region_3.4_spmd.clone, body=%wide.region_2.3_spmd.clone.sunk | while | flops 328711 | bytes 665257 | solution.py:25
  230.9 0.7 fusion.11
  231.9 0.7 fusion.11
  232.8 0.7 fusion.11
  233.8 0.7 fusion.11
  234.8 0.7 fusion.11
  235.8 0.7 fusion.11
  236.7 0.7 fusion.11
  237.7 0.7 fusion.11
  239.6 0.7 fusion.11
  240.6 0.7 fusion.11
  241.6 0.7 fusion.11
  242.6 0.7 fusion.11
  355.1 0.7 multiply_convert_fusion
  (403 shorter events, 115.4 us)
Async XLA Ops:
  6.5 82.2 %all-gather.5.cloned.1.call-start = ((), (), s32[]{:S(2)}) async-start(), calls=%async_computation.1 | async-start | bytes 7077888 | tf_op jit(solution)/shard_map/all_gather | solution.py:34
  8.9 191.0 %all-gather.3.cloned.1.call-start = ((), (), s32[]{:S(2)}) async-start(), calls=%async_computation | async-start | bytes 8650752 | tf_op jit(solution)/shard_map/all_gather | solution.py:37
  199.9 14.5 %copy-start = (s32[1,4096]{1,0:T(1,128)S(1)}, s32[1,4096]{1,0:T(1,128)}, u32[]{:S(2)}) copy-start(s32[1,4096]{1,0:T(1,128)} %param.15) | copy-start | bytes 49156
  209.6 145.5 %copy-start.1 = (f32[128]{0:T(128)S(1)}, f32[128]{0:T(128)}, u32[]{:S(2)}) copy-start(f32[128]{0:T(128)} %param.14) | copy-start | bytes 1540
  209.6 6.1 %collective-permute-start = (bf16[1,6,384]{2,1,0:T(8,128)(2,1)S(1)}, bf16[1,6,384]{2,1,0:T(8,128)(2,1)S(1)}, u32[]{:S(2)}, u32[]{:S(2)}) collective-permute-start(bf16[1,6,384]{2,1,0:T(8,128)(2,1)S(1)} %slice.28), channel_id=1, source_target_pairs={{0,2},{2,4},{4,6},{6,8},{8,10},{10,12},{12,14},{1,3},{3,5},{5,7},{... | collective-permute-start | bytes 13832 | tf_op jit(solution)/shard_map/ppermute | solution.py:10
  223.8 7.0 %collective-permute-start.1 = (bf16[1,127,128]{2,1,0:T(8,128)(2,1)S(1)}, bf16[1,127,128]{2,1,0:T(8,128)(2,1)S(1)}, u32[]{:S(2)}, u32[]{:S(2)}) collective-permute-start(bf16[1,127,128]{2,1,0:T(8,128)(2,1)S(1)} %slice.29), channel_id=1, source_target_pairs={{0,2},{2,4},{4,6},{6,8},{8,10},{10,12},{12,14},{1,3},{3,5},{5,7},{... | collective-permute-start | bytes 97544 | tf_op jit(solution)/shard_map/ppermute | solution.py:10
Sparse Core Ops, SparseCore 0:
  9.4 79.2 all-gather.4
  91.8 108.0 all-gather.2
where the time goes:
time: 367 us; the launch traced here: 363 us
  waiting for transfers between devices  189 us (51%)
  local copies, waits for them, and re-layouts  97 us (26%)
  other arithmetic  35.6 us (10%)
  between operations  13.5 us (4%)
  starting transfers between devices  10.2 us (3%)
  matrix products  9.68 us (3%)
  loops' own time  3.83 us (1%)
    all_gather x1, waiting for transfers between devices, body(): lax.all_gather(block, 'fsdp', axis=2, tiled=True)  111 us
    mul x128, local copies, waits for them, and re-layouts, add_lag(): return total + weight * piece * same  88.5 us
    all_gather x1, waiting for transfers between devices, body(): lax.all_gather(w_in, 'ctx', axis=0, tiled=True).reshape(-1, 3 * channels)  75.4 us
    add x135, other arithmetic, add_lag(): return total + weight * piece * same  24 us
    mul x135, other arithmetic, add_lag(): return total + weight * piece * same  10.7 us
    ppermute x2, starting transfers between devices, passed_along(): lax.ppermute(value, axis, [(source, source + steps) for source in range(l...  10.2 us
    dot_general x1, matrix products, body(): jnp.einsum('bld,dk->blk', lax.all_gather(block, 'fsdp', axis=2, tiled=Tru...  9.68 us
  transfers between devices with their start and end apart: 4, of which 4 were waited for; matrix products, arithmetic and copies ran while one was open for 0% of the time, Pallas kernels for 0%

commit v1 on v0

v1 whole, which is shorter than its diff:
```python
import functools

import jax
import jax.numpy as jnp
from jax import lax
from jax.experimental import pallas as pl
from jax.experimental.pallas import tpu as pltpu
from jax.sharding import PartitionSpec as P

HALO = 16
GROUP = 64
BF16, F32 = jnp.bfloat16, jnp.float32
VMEM = pl.BlockSpec(memory_space=pltpu.VMEM)
SMEM = pl.BlockSpec(memory_space=pltpu.SMEM)
ANY = pl.BlockSpec(memory_space=pl.ANY)
MIB = 1 << 20


def call(kernel, out_shape, in_specs, out_specs, scratch=(), flops=0, nbytes=0, vmem=8):
    return pl.pallas_call(
        kernel,
        out_shape=out_shape,
        in_specs=in_specs,
        out_specs=out_specs,
        scratch_shapes=list(scratch),
        compiler_params=pltpu.CompilerParams(vmem_limit_bytes=vmem * MIB),
        cost_estimate=pl.CostEstimate(flops=flops, bytes_accessed=nbytes, transcendentals=0),
    )


def product(token_block, weights):
    left = jnp.concatenate([token_block[j] for j in range(token_block.shape[0])], 1)
    right = jnp.concatenate([weights[g] for g in range(3)], 1)
    return jnp.dot(left, right, preferred_element_type=F32)


def first_sums(count, done, offsets, place, ids, ends, *refs):
    blocks, refs = refs[:count], refs[count:]
    theirs, mine, refs = refs[:done], refs[done : 2 * done], refs[2 * done :]
    theirs_ref, mine_ref, last_ref, held, sem = refs
    y, z, step = place[0], place[1], place[2]
    copies = []
    for k, offset in enumerate(offsets):
        slot = lax.rem(y + offset + count, count)
        copies.append(pltpu.make_async_copy(blocks[k], held.at[slot], sem.at[k]))
    for copy in copies:
        copy.start()
    for copy in copies:
        copy.wait()
    for weights, out in ((theirs, theirs_ref), (mine, mine_ref)):
        for s in range(done):
            slot = lax.rem(z + s * step + s * count, count)
            term = product(held[slot], weights[s])
            if s == 0:
                out[...] = term
            else:
                out[...] += term
    last_ref[...] = held[lax.rem(z + done * step + done * count, count)]


def last_theirs(block, weights, total, out):
    out[...] = (total[...] + product(block, weights)).astype(out.dtype)


def feature(block, weights, total, received, ids, taps, mixed_ref, queries_ref, raw):
    rows = mixed_ref.shape[0]
    summed = total[...] + product(block, weights) + received[...].astype(F32)
    raw[...] = summed.astype(BF16).astype(F32)
    reach = taps.shape[0] - 1
    step = 64

    def part(i, _):
        base = pl.multiple_of(i * step, step)
        near = ids[pl.ds(base + ids.shape[0] - rows - HALO, step + HALO), :]
        held = [raw[pl.ds(base, step + HALO), 128 * g : 128 * g + 128] for g in range(3)]
        sums = [jnp.zeros((step, 128), F32) for _ in range(3)]
        for lag in range(reach + 1):
            spot = slice(HALO - lag, HALO - lag + step)
            same = near[spot] == near[HALO:]
            for g in range(3):
                piece = held[g][spot]
                weight = taps[lag : lag + 1, 128 * g : 128 * g + 128]
                sums[g] = sums[g] + jnp.where(same, piece * weight, 0.0)
        queries_ref[pl.ds(base, step), :] = sums[0]
        mixed_ref[pl.ds(base, step), :] = (sums[1] * sums[2]).astype(BF16)
        return 0

    lax.fori_loop(0, rows // step, part, 0)


def long_filter(first, last, reach, ends, mixed, ids, queries, taps, skip, out, source, window):
    def group(i, _):
        base = pl.multiple_of(first + i * GROUP, GROUP)
        here = ids[pl.ds(base + reach, GROUP), :]

        def genome(g, total):
            for k in range((reach + GROUP) // GROUP):
                spot = pl.ds(base + k * GROUP, GROUP)
                window[k * GROUP : k * GROUP + GROUP, :] = jnp.where(
                    ids[spot, :] == g, source[spot, :], 0.0
                )

            sums = jnp.zeros((GROUP, 128), F32)
            for s in range(8):
                held = window[8 - s : GROUP + reach - s, :]
                for a in range(reach // 8):
                    weight = taps[8 * a + s : 8 * a + s + 1, :]
                    start = reach - 8 - 8 * a
                    sums = sums + held[start : start + GROUP] * weight
            return jnp.where(here == g, sums, total)

        low, high = ends[2 * (base // GROUP)], ends[2 * (base // GROUP) + 1]
        total = lax.fori_loop(low, high + 1, genome, jnp.zeros((GROUP, 128), F32))
        bias = skip[...] * source[pl.ds(base + reach, GROUP), :]
        gated = queries[pl.ds(base, GROUP), :] * (total + bias)
        out[pl.ds(base, GROUP), :] = gated.astype(out.dtype)
        return 0

    lax.fori_loop(0, (last - first) // GROUP, group, 0)


def filter_main(reach, ends, mixed, ids, queries, taps, skip, out, source, window):
    rows = mixed.shape[0]
    source[reach:, :] = mixed[...].astype(F32)
    long_filter(reach, rows, reach, ends, mixed, ids, queries, taps, skip, out, source, window)


def filter_head(reach, ends, earlier, mixed, ids, queries, taps, skip, given, out, source, window):
    source[:reach, :] = earlier[...].astype(F32)
    source[reach:, :] = mixed[:reach, :].astype(F32)
    out[reach:, :] = given[reach:, :]
    long_filter(0, reach, reach, ends, mixed, ids, queries, taps, skip, out, source, window)


def body(tokens, w_in, short_taps, mr_taps, skip, genome_ids):
    length, width = tokens.shape[1], tokens.shape[2]
    ctx, tp = lax.axis_size("ctx"), lax.axis_size("tp")
    xs, ys = lax.axis_size("fsdp") // ctx, ctx
    reach = mr_taps.shape[0]
    f, z, c = lax.axis_index("fsdp"), lax.axis_index("ctx"), lax.axis_index("tp")
    x, y = f % xs, f // xs

    along_x = lambda d: [(j * xs + i, j * xs + (i + d) % xs) for j in range(ys) for i in range(xs)]
    along_y = lambda d: [(j * xs + i, (j + d) % ys * xs + i) for j in range(ys) for i in range(xs)]
    ring = [(k * tp + t, (k + 1 - 2 * t) % ctx * tp + t) for k in range(ctx) for t in range(tp)]
    swap = [(0, 1), (1, 0)]

    planes = jnp.transpose(w_in, (1, 0, 2)).reshape(3, xs, tp, width, width)
    mine = lax.dynamic_index_in_dim(planes, c, 2, False).reshape(3, xs * width, width)
    theirs = lax.dynamic_index_in_dim(planes, 1 - c, 2, False).reshape(3, xs * width, width)
    mine, theirs = [mine], [lax.ppermute(theirs, "tp", swap)]
    for _ in range(ctx - 1):
        theirs.append(lax.ppermute(theirs[-1], ("ctx", "tp"), ring))
        mine.append(lax.ppermute(mine[-1], ("ctx", "tp"), ring))

    own = tokens[0]
    before = lax.ppermute(own[length - HALO :], "ctx", [(k, (k + 1) % ctx) for k in range(ctx)])
    own = jnp.concatenate([before, own], 0)
    block = jnp.zeros((xs,) + own.shape, BF16)
    block = lax.dynamic_update_index_in_dim(block, own, x, 0)
    for d in range(1, xs):
        hop = d if d <= xs // 2 else d - xs
        piece = lax.ppermute(own, "fsdp", along_x(hop))
        block = lax.dynamic_update_index_in_dim(block, piece, (x - hop) % xs, 0)
    blocks, offsets = [block], [0]
    up = down = block
    for s in range(1, ys // 2 + 1):
        up = lax.ppermute(up, "fsdp", along_y(1))
        blocks.append(up)
        offsets.append(-s)
        if s <= (ys - 1) // 2:
            down = lax.ppermute(down, "fsdp", along_y(-1))
            blocks.append(down)
            offsets.append(s)

    start = z * length
    padded = jnp.pad(genome_ids[0], (reach, 0), constant_values=-1)
    seen = lax.dynamic_slice_in_dim(padded, start, length + reach, 0)
    ids = jnp.broadcast_to(seen[:, None], (length + reach, 128))
    ends = jnp.stack([seen[reach::GROUP], seen[reach + GROUP - 1 :: GROUP]], 1).reshape(-1)
    place = jnp.stack([y, z, 2 * c - 1]).astype(jnp.int32)

    rows, done = length + HALO, ctx - 1
    wide = jax.ShapeDtypeStruct((rows, 3 * width), F32)
    taken = jax.ShapeDtypeStruct((xs, rows, width), BF16)
    one = 2 * rows * xs * width * 3 * width
    sum_theirs, sum_mine, last = call(
        functools.partial(first_sums, ys, done, tuple(offsets)),
        (wide, wide, taken),
        [SMEM, ANY, ANY] + [ANY] * ys + [VMEM] * (2 * done),
        (VMEM, VMEM, VMEM),
        [pltpu.VMEM((ys, xs, rows, width), BF16), pltpu.SemaphoreType.DMA((ys,))],
        flops=2 * done * one,
        nbytes=12 << 20,
        vmem=16,
    )(place, ids, ends, *blocks, *theirs[:done], *mine[:done])
    give = call(
        last_theirs,
        jax.ShapeDtypeStruct((rows, 3 * width), BF16),
        [VMEM] * 3,
        VMEM,
        flops=one,
        nbytes=2 << 20,
    )(last, theirs[done], sum_theirs)
    received = lax.ppermute(give, "tp", swap)
    mixed, queries = call(
        feature,
        (jax.ShapeDtypeStruct((length, width), BF16), jax.ShapeDtypeStruct((length, width), F32)),
        [VMEM] * 6,
        (VMEM, VMEM),
        [pltpu.VMEM((rows, 3 * width), F32)],
        flops=one,
        nbytes=4 << 20,
    )(
        last,
        mine[done],
        sum_mine,
        received,
        ids,
        short_taps.reshape(short_taps.shape[0], -1),
    )
    earlier = lax.ppermute(mixed[length - reach :], "ctx", [(k, (k + 1) % ctx) for k in range(ctx)])
    bias = skip[None, :]
    outline = jax.ShapeDtypeStruct((length, width), BF16)
    part = call(
        functools.partial(filter_main, reach),
        outline,
        [SMEM] + [VMEM] * 5,
        VMEM,
        [pltpu.VMEM((reach + length, width), F32), pltpu.VMEM((reach + GROUP, width), F32)],
        flops=2 * (length - reach) * width * reach,
        nbytes=1 << 20,
    )(ends, mixed, ids, queries, mr_taps, bias)
    gated = call(
        functools.partial(filter_head, reach),
        outline,
        [SMEM] + [VMEM] * 7,
        VMEM,
        [pltpu.VMEM((2 * reach, width), F32), pltpu.VMEM((reach + GROUP, width), F32)],
        flops=2 * reach * width * reach,
        nbytes=1 << 20,
    )(ends, earlier, mixed, ids, queries, mr_taps, bias, part)
    return gated[None]


def solution(mesh):
    in_specs = (
        P(None, "ctx", ("fsdp", "tp")),
        P("ctx", None, ("fsdp", "tp")),
        P(None, None, ("fsdp", "tp")),
        P(None, ("fsdp", "tp")),
        P(("fsdp", "tp")),
        P(),
    )
    out_specs = P(None, "ctx", ("fsdp", "tp"))
    return jax.shard_map(body, mesh=mesh, in_specs=in_specs, out_specs=out_specs, check_vma=False)
```

time: 367 us -> 158 us (0.43)
  the two profiles are of different devices: /device:TPU:192 before, /device:TPU:24 now
where the time goes in v1:
time: 158 us; the launch traced here: 156 us
  starting transfers between devices  83.4 us (53%)
  waiting for transfers between devices  40.9 us (26%)
  local copies, waits for them, and re-layouts  17.6 us (11%)
  Pallas kernels  13.8 us (9%)
    ppermute x4, starting transfers between devices, body(): up = lax.ppermute(up, 'fsdp', along_y(1))  20.6 us
    ppermute x7, starting transfers between devices, body(): theirs.append(lax.ppermute(theirs[-1], ('ctx', 'tp'), ring))  18.5 us
    ppermute x7, waiting for transfers between devices, body(): mine.append(lax.ppermute(mine[-1], ('ctx', 'tp'), ring))  17.5 us
    ppermute x7, starting transfers between devices, body(): mine.append(lax.ppermute(mine[-1], ('ctx', 'tp'), ring))  17.1 us
    unnamed x46, local copies, waits for them, and re-layouts  15.6 us
    ppermute x7, waiting for transfers between devices, body(): theirs.append(lax.ppermute(theirs[-1], ('ctx', 'tp'), ring))  13.1 us
    ppermute x3, starting transfers between devices, body(): piece = lax.ppermute(own, 'fsdp', along_x(hop))  11.4 us
    ppermute x1, waiting for transfers between devices, body(): lax.ppermute(own[length - HALO:], 'ctx', [(k, (k + 1) % ctx) for k in ran...  8.24 us
  transfers between devices with their start and end apart: 28, of which 9 were waited for; matrix products, arithmetic and copies ran while one was open for 1% of the time, Pallas kernels for 6%

profile of v1, /device:TPU:24, one launch (start us, length us, event | category | flops | bytes accessed | tf_op | source)
XLA Modules:
  0.0 156.4 jit_solution(13070946569179756835)
XLA Ops:
  1.2 1.9 %collective-permute-start.11 = (bf16[3,512,128]{2,1,0:T(8,128)(2,1)S(1)}, bf16[3,512,128]{2,1,0:T(8,128)(2,1)S(1)}, u32[]{:S(2)}, u32[]{:S(2)}) collective-permute-start(bf16[3,512,128]{2,1,0:T(8,128)(2,1)S(1)} %bitcast.37), channel_id=1, source_target_pairs={{0,1},{1,0},{2,3},{3,2},{4,5},{5,4},{6,7},{7,6},{8,9},{9,8},{10,11... | collective-permute-start | bytes 1179656 | tf_op jit(solution)/shard_map/ppermute | solution.py:151
  3.2 4.3 %collective-permute-start = (bf16[16,128]{1,0:T(8,128)(2,1)S(1)}, bf16[16,128]{1,0:T(8,128)(2,1)S(1)}, u32[]{:S(2)}, u32[]{:S(2)}) collective-permute-start(bf16[16,128]{1,0:T(8,128)(2,1)S(1)} %slice_bitcast_fusion), channel_id=1, source_target_pairs={{0,2},{2,4},{4,6},{6,8},{8,10},{10,12},{12,14},{14,0},{1,3},{3,5},... | collective-permute-start | bytes 12296 | tf_op jit(solution)/shard_map/ppermute | solution.py:157
  7.5 8.2 %collective-permute-done = bf16[16,128]{1,0:T(8,128)(2,1)S(1)} collective-permute-done((bf16[16,128]{1,0:T(8,128)(2,1)S(1)}, bf16[16,128]{1,0:T(8,128)(2,1)S(1)}, u32[]{:S(2)}, u32[]{:S(2)}) %collective-permute-start) | collective-permute-done | bytes 4128 | tf_op jit(solution)/shard_map/ppermute | solution.py:157
  15.7 3.4 %collective-permute-start.1 = (bf16[528,128]{1,0:T(8,128)(2,1)S(1)}, bf16[528,128]{1,0:T(8,128)(2,1)S(1)}, u32[]{:S(2)}, u32[]{:S(2)}) collective-permute-start(bf16[528,128]{1,0:T(8,128)(2,1)S(1)} %pad_maximum_fusion), channel_id=1, source_target_pairs={{0,16},{16,32},{32,48},{48,0},{64,80},{80,96},{96,112},{112,64},{1... | collective-permute-start | bytes 405512 | tf_op jit(solution)/shard_map/ppermute | solution.py:163
  19.1 1.9 %collective-permute-start.18 = (bf16[3,512,128]{2,1,0:T(8,128)(2,1)S(1)}, bf16[3,512,128]{2,1,0:T(8,128)(2,1)S(1)}, u32[]{:S(2)}, u32[]{:S(2)}) collective-permute-start(bf16[3,512,128]{2,1,0:T(8,128)(2,1)S(1)} %bitcast.29), channel_id=1, source_target_pairs={{0,2},{1,15},{2,4},{3,1},{4,6},{5,3},{6,8},{7,5},{8,10},{9,7},{10,... | collective-permute-start | bytes 1179656 | tf_op jit(solution)/shard_map/ppermute | solution.py:154
  21.1 4.6 %collective-permute-start.2 = (bf16[528,128]{1,0:T(8,128)(2,1)S(1)}, bf16[528,128]{1,0:T(8,128)(2,1)S(1)}, u32[]{:S(2)}, u32[]{:S(2)}) collective-permute-start(bf16[528,128]{1,0:T(8,128)(2,1)S(1)} %pad_maximum_fusion), channel_id=1, source_target_pairs={{0,32},{16,48},{32,0},{48,16},{64,96},{80,112},{96,64},{112,80},{1... | collective-permute-start | bytes 405512 | tf_op jit(solution)/shard_map/ppermute | solution.py:163
  25.8 3.3 %collective-permute-start.3 = (bf16[528,128]{1,0:T(8,128)(2,1)S(1)}, bf16[528,128]{1,0:T(8,128)(2,1)S(1)}, u32[]{:S(2)}, u32[]{:S(2)}) collective-permute-start(bf16[528,128]{1,0:T(8,128)(2,1)S(1)} %pad_maximum_fusion), channel_id=1, source_target_pairs={{0,48},{16,0},{32,16},{48,32},{64,112},{80,64},{96,80},{112,96},{1... | collective-permute-start | bytes 405512 | tf_op jit(solution)/shard_map/ppermute | solution.py:163
  29.3 1.9 %collective-permute-start.12 = (bf16[3,512,128]{2,1,0:T(8,128)(2,1)S(1)}, bf16[3,512,128]{2,1,0:T(8,128)(2,1)S(1)}, u32[]{:S(2)}, u32[]{:S(2)}) collective-permute-start(bf16[3,512,128]{2,1,0:T(8,128)(2,1)S(1)} %collective-permute-done.11.refs_8_), channel_id=1, source_target_pairs={{0,2},{1,15},{2,4},{3,1},{4,6},{5,3},{6,8},{7,5},{8,10},{9,7},{10,... | collective-permute-start | bytes 1179656 | tf_op jit(solution)/shard_map/ppermute | solution.py:153
  31.3 8.9 %collective-permute-done.12.refs_9_ = bf16[3,512,128]{2,1,0:T(8,128)(2,1)S(1)} collective-permute-done((bf16[3,512,128]{2,1,0:T(8,128)(2,1)S(1)}, bf16[3,512,128]{2,1,0:T(8,128)(2,1)S(1)}, u32[]{:S(2)}, u32[]{:S(2)}) %collective-permute-start.12) | collective-permute-done | bytes 393248 | tf_op jit(solution)/shard_map/ppermute | solution.py:153
  42.8 4.7 %collective-permute-start.4 = (bf16[4,528,128]{2,1,0:T(8,128)(2,1)S(1)}, bf16[4,528,128]{2,1,0:T(8,128)(2,1)S(1)}, u32[]{:S(2)}, u32[]{:S(2)}) collective-permute-start(bf16[4,528,128]{2,1,0:T(8,128)(2,1)S(1)} %bitcast_dynamic-update-slice_fusion.refs_0_), channel_id=1, source_target_pairs={{0,64},{16,80},{32,96},{48,112},{64,128},{80,144},{96,160},{112,17... | collective-permute-start | bytes 1622024 | tf_op jit(solution)/shard_map/ppermute | solution.py:168
  47.6 3.1 %collective-permute-start.19 = (bf16[3,512,128]{2,1,0:T(8,128)(2,1)S(1)}, bf16[3,512,128]{2,1,0:T(8,128)(2,1)S(1)}, u32[]{:S(2)}, u32[]{:S(2)}) collective-permute-start(bf16[3,512,128]{2,1,0:T(8,128)(2,1)S(1)} %collective-permute-done.18.refs_16_), channel_id=1, source_target_pairs={{0,2},{1,15},{2,4},{3,1},{4,6},{5,3},{6,8},{7,5},{8,10},{9,7},{10,... | collective-permute-start | bytes 1179656 | tf_op jit(solution)/shard_map/ppermute | solution.py:154
  51.4 4.4 %collective-permute-start.14 = (bf16[3,512,128]{2,1,0:T(8,128)(2,1)S(1)}, bf16[3,512,128]{2,1,0:T(8,128)(2,1)S(1)}, u32[]{:S(2)}, u32[]{:S(2)}) collective-permute-start(bf16[3,512,128]{2,1,0:T(8,128)(2,1)S(1)} %collective-permute-done.13.refs_10_), channel_id=1, source_target_pairs={{0,2},{1,15},{2,4},{3,1},{4,6},{5,3},{6,8},{7,5},{8,10},{9,7},{10,... | collective-permute-start | bytes 1179656 | tf_op jit(solution)/shard_map/ppermute | solution.py:153
  58.6 5.6 %collective-permute-start.6 = (bf16[4,528,128]{2,1,0:T(8,128)(2,1)S(1)}, bf16[4,528,128]{2,1,0:T(8,128)(2,1)S(1)}, u32[]{:S(2)}, u32[]{:S(2)}) collective-permute-start(bf16[4,528,128]{2,1,0:T(8,128)(2,1)S(1)} %collective-permute-done.4.refs_1_), channel_id=1, source_target_pairs={{0,64},{16,80},{32,96},{48,112},{64,128},{80,144},{96,160},{112,17... | collective-permute-start | bytes 1622024 | tf_op jit(solution)/shard_map/ppermute | solution.py:168
  64.2 2.8 %collective-permute-start.20 = (bf16[3,512,128]{2,1,0:T(8,128)(2,1)S(1)}, bf16[3,512,128]{2,1,0:T(8,128)(2,1)S(1)}, u32[]{:S(2)}, u32[]{:S(2)}) collective-permute-start(bf16[3,512,128]{2,1,0:T(8,128)(2,1)S(1)} %collective-permute-done.19.refs_17_), channel_id=1, source_target_pairs={{0,2},{1,15},{2,4},{3,1},{4,6},{5,3},{6,8},{7,5},{8,10},{9,7},{10,... | collective-permute-start | bytes 1179656 | tf_op jit(solution)/shard_map/ppermute | solution.py:154
  67.8 2.2 %collective-permute-start.15 = (bf16[3,512,128]{2,1,0:T(8,128)(2,1)S(1)}, bf16[3,512,128]{2,1,0:T(8,128)(2,1)S(1)}, u32[]{:S(2)}, u32[]{:S(2)}) collective-permute-start(bf16[3,512,128]{2,1,0:T(8,128)(2,1)S(1)} %collective-permute-done.14.refs_11_), channel_id=1, source_target_pairs={{0,2},{1,15},{2,4},{3,1},{4,6},{5,3},{6,8},{7,5},{8,10},{9,7},{10,... | collective-permute-start | bytes 1179656 | tf_op jit(solution)/shard_map/ppermute | solution.py:153
  70.7 4.3 %collective-permute-done.20.refs_18_ = bf16[3,512,128]{2,1,0:T(8,128)(2,1)S(1)} collective-permute-done((bf16[3,512,128]{2,1,0:T(8,128)(2,1)S(1)}, bf16[3,512,128]{2,1,0:T(8,128)(2,1)S(1)}, u32[]{:S(2)}, u32[]{:S(2)}) %collective-permute-start.20) | collective-permute-done | bytes 393248 | tf_op jit(solution)/shard_map/ppermute | solution.py:154
  79.7 5.1 %collective-permute-start.8 = (bf16[4,528,128]{2,1,0:T(8,128)(2,1)S(1)}, bf16[4,528,128]{2,1,0:T(8,128)(2,1)}, u32[]{:S(2)}, u32[]{:S(2)}) collective-permute-start(bf16[4,528,128]{2,1,0:T(8,128)(2,1)S(1)} %collective-permute-done.6.refs_3_), channel_id=1, source_target_pairs={{0,64},{16,80},{32,96},{48,112},{64,128},{80,144},{96,160},{112,17... | collective-permute-start | bytes 1622024 | tf_op jit(solution)/shard_map/ppermute | solution.py:168
  84.8 1.9 %collective-permute-start.16 = (bf16[3,512,128]{2,1,0:T(8,128)(2,1)S(1)}, bf16[3,512,128]{2,1,0:T(8,128)(2,1)}, u32[]{:S(2)}, u32[]{:S(2)}) collective-permute-start(bf16[3,512,128]{2,1,0:T(8,128)(2,1)S(1)} %collective-permute-done.15.refs_12_), channel_id=1, source_target_pairs={{0,2},{1,15},{2,4},{3,1},{4,6},{5,3},{6,8},{7,5},{8,10},{9,7},{10,... | collective-permute-start | bytes 1179656 | tf_op jit(solution)/shard_map/ppermute | solution.py:153
  87.5 3.3 %collective-permute-start.22 = (bf16[3,512,128]{2,1,0:T(8,128)(2,1)S(1)}, bf16[3,512,128]{2,1,0:T(8,128)(2,1)}, u32[]{:S(2)}, u32[]{:S(2)}) collective-permute-start(bf16[3,512,128]{2,1,0:T(8,128)(2,1)S(1)} %collective-permute-done.21.refs_19_), channel_id=1, source_target_pairs={{0,2},{1,15},{2,4},{3,1},{4,6},{5,3},{6,8},{7,5},{8,10},{9,7},{10,... | collective-permute-start | bytes 1179656 | tf_op jit(solution)/shard_map/ppermute | solution.py:154
  91.6 4.2 %collective-permute-done.16.refs_13_ = bf16[3,512,128]{2,1,0:T(8,128)(2,1)} collective-permute-done((bf16[3,512,128]{2,1,0:T(8,128)(2,1)S(1)}, bf16[3,512,128]{2,1,0:T(8,128)(2,1)}, u32[]{:S(2)}, u32[]{:S(2)}) %collective-permute-start.16) | collective-permute-done | bytes 393248 | tf_op jit(solution)/shard_map/ppermute | solution.py:153
  95.8 1.9 %collective-permute-start.17 = (bf16[3,512,128]{2,1,0:T(8,128)(2,1)}, bf16[3,512,128]{2,1,0:T(8,128)(2,1)}, u32[]{:S(2)}, u32[]{:S(2)}) collective-permute-start(bf16[3,512,128]{2,1,0:T(8,128)(2,1)} %collective-permute-done.16.refs_13_), channel_id=1, source_target_pairs={{0,2},{1,15},{2,4},{3,1},{4,6},{5,3},{6,8},{7,5},{8,10},{9,7},{10,... | collective-permute-start | bytes 1179656 | tf_op jit(solution)/shard_map/ppermute | solution.py:153
  97.7 1.9 %collective-permute-start.9 = (bf16[4,528,128]{2,1,0:T(8,128)(2,1)S(1)}, bf16[4,528,128]{2,1,0:T(8,128)(2,1)}, u32[]{:S(2)}, u32[]{:S(2)}) collective-permute-start(bf16[4,528,128]{2,1,0:T(8,128)(2,1)S(1)} %collective-permute-done.7.refs_4_), channel_id=1, source_target_pairs={{0,448},{16,464},{32,480},{48,496},{64,0},{80,16},{96,32},{112,48}... | collective-permute-start | bytes 1622024 | tf_op jit(solution)/shard_map/ppermute | solution.py:172
  99.7 5.1 %collective-permute-start.10 = (bf16[4,528,128]{2,1,0:T(8,128)(2,1)}, bf16[4,528,128]{2,1,0:T(8,128)(2,1)}, u32[]{:S(2)}, u32[]{:S(2)}) collective-permute-start(bf16[4,528,128]{2,1,0:T(8,128)(2,1)} %collective-permute-done.8.refs_5_), channel_id=1, source_target_pairs={{0,64},{16,80},{32,96},{48,112},{64,128},{80,144},{96,160},{112,17... | collective-permute-start | bytes 1622024 | tf_op jit(solution)/shard_map/ppermute | solution.py:168
  104.8 2.1 %collective-permute-start.23 = (bf16[3,512,128]{2,1,0:T(8,128)(2,1)}, bf16[3,512,128]{2,1,0:T(8,128)(2,1)}, u32[]{:S(2)}, u32[]{:S(2)}) collective-permute-start(bf16[3,512,128]{2,1,0:T(8,128)(2,1)} %collective-permute-done.22.refs_20_), channel_id=1, source_target_pairs={{0,2},{1,15},{2,4},{3,1},{4,6},{5,3},{6,8},{7,5},{8,10},{9,7},{10,... | collective-permute-start | bytes 1179656 | tf_op jit(solution)/shard_map/ppermute | solution.py:154
  107.2 4.3 %collective-permute-start.25 = (bf16[3,512,128]{2,1,0:T(8,128)(2,1)}, bf16[3,512,128]{2,1,0:T(8,128)(2,1)S(1)}, u32[]{:S(2)}, u32[]{:S(2)}) collective-permute-start(bf16[3,512,128]{2,1,0:T(8,128)(2,1)} %collective-permute-done.17.refs_14_), channel_id=1, source_target_pairs={{0,2},{1,15},{2,4},{3,1},{4,6},{5,3},{6,8},{7,5},{8,10},{9,7},{10,... | collective-permute-start | bytes 1179656 | tf_op jit(solution)/shard_map/ppermute | solution.py:153
  112.0 4.0 %collective-permute-done.23.refs_21_ = bf16[3,512,128]{2,1,0:T(8,128)(2,1)} collective-permute-done((bf16[3,512,128]{2,1,0:T(8,128)(2,1)}, bf16[3,512,128]{2,1,0:T(8,128)(2,1)}, u32[]{:S(2)}, u32[]{:S(2)}) %collective-permute-start.23) | collective-permute-done | bytes 393248 | tf_op jit(solution)/shard_map/ppermute | solution.py:154
  125.1 7.2 %shard_map.64 = (f32[528,384]{1,0:T(8,128)S(1)}, f32[528,384]{1,0:T(8,128)S(1)}, bf16[4,528,128]{2,1,0:T(8,128)(2,1)S(1)}) custom-call(s32[3]{0:T(128)S(1)} %pad_add_fusion.1.place, s32[640,128]{1,0:T(8,128)S(1)} %broadcast_in_dim.28.ids, s32[16]{0:T(128)S(1)} %reshape.19.ends, bf16[4,528,128]{2,1,0:T(8,128)(2,1)S(1)} %bitcast_dynamic-update-slice_fusion.refs_0_, ...), custom_call_target="tpu_custom_call" | custom-call | flops 2906652672 | bytes 12582912 | tf_op jit(solution)/shard_map/pallas_call | solution.py:187
  132.9 1.9 %collective-permute-start.26 = (bf16[528,384]{1,0:T(8,128)(2,1)S(1)}, bf16[528,384]{1,0:T(8,128)(2,1)S(1)}, u32[]{:S(2)}, u32[]{:S(2)}) collective-permute-start(bf16[528,384]{1,0:T(8,128)(2,1)S(1)} %shard_map.65), channel_id=1, source_target_pairs={{0,1},{1,0},{2,3},{3,2},{4,5},{5,4},{6,7},{7,6},{8,9},{9,8},{10,11... | collective-permute-start | bytes 1216520 | tf_op jit(solution)/shard_map/ppermute | solution.py:205
  134.8 1.9 %collective-permute-start.24 = (bf16[3,512,128]{2,1,0:T(8,128)(2,1)}, bf16[3,512,128]{2,1,0:T(8,128)(2,1)S(1)}, u32[]{:S(2)}, u32[]{:S(2)}) collective-permute-start(bf16[3,512,128]{2,1,0:T(8,128)(2,1)} %collective-permute-done.23.refs_21_), channel_id=1, source_target_pairs={{0,2},{1,15},{2,4},{3,1},{4,6},{5,3},{6,8},{7,5},{8,10},{9,7},{10,... | collective-permute-start | bytes 1179656 | tf_op jit(solution)/shard_map/ppermute | solution.py:154
  136.7 9.2 %collective-permute-done.24.weights = bf16[3,512,128]{2,1,0:T(8,128)(2,1)S(1)} collective-permute-done((bf16[3,512,128]{2,1,0:T(8,128)(2,1)}, bf16[3,512,128]{2,1,0:T(8,128)(2,1)S(1)}, u32[]{:S(2)}, u32[]{:S(2)}) %collective-permute-start.24) | collective-permute-done | bytes 393248 | tf_op jit(solution)/shard_map/ppermute | solution.py:154
  147.5 1.9 %collective-permute-start.27 = (bf16[128,128]{1,0:T(8,128)(2,1)S(1)}, bf16[128,128]{1,0:T(8,128)(2,1)S(1)}, u32[]{:S(2)}, u32[]{:S(2)}) collective-permute-start(bf16[128,128]{1,0:T(8,128)(2,1)S(1)} %slice.19), channel_id=1, source_target_pairs={{0,2},{2,4},{4,6},{6,8},{8,10},{10,12},{12,14},{14,0},{1,3},{3,5},... | collective-permute-start | bytes 98312 | tf_op jit(solution)/shard_map/ppermute | solution.py:222
  150.1 2.7 %shard_map.67.given = bf16[512,128]{1,0:T(8,128)(2,1)S(1)} custom-call(s32[16]{0:T(128)S(1)} %reshape.19.ends, bf16[512,128]{1,0:T(8,128)(2,1)S(1)} %get-tuple-element.13.mixed, s32[640,128]{1,0:T(8,128)S(1)} %broadcast_in_dim.28.ids, f32[512,128]{1,0:T(8,128)S(1)} %get-tuple-element.14.queries, f32[128,128]{1,0:T(8,128)S(1)} %copy-done, f32[1,128]{1,0:T(1,128)S(1)} %bitcast.32), custom_call_target="tpu_custom_call" | custom-call | flops 12582912 | bytes 1048576 | tf_op jit(solution)/shard_map/pallas_call | solution.py:225
  (92 shorter events, 31.2 us)
Async XLA Ops:
  0.0 3.2 %copy-start.21 = (bf16[1,512,128]{2,1,0:T(8,128)(2,1)S(1)}, bf16[1,512,128]{2,1,0:T(8,128)(2,1)}, u32[]{:S(2)}) copy-start(bf16[1,512,128]{2,1,0:T(8,128)(2,1)} %param.6) | copy-start | bytes 393220
  1.2 28.0 %collective-permute-start.11 = (bf16[3,512,128]{2,1,0:T(8,128)(2,1)S(1)}, bf16[3,512,128]{2,1,0:T(8,128)(2,1)S(1)}, u32[]{:S(2)}, u32[]{:S(2)}) collective-permute-start(bf16[3,512,128]{2,1,0:T(8,128)(2,1)S(1)} %bitcast.37), channel_id=1, source_target_pairs={{0,1},{1,0},{2,3},{3,2},{4,5},{5,4},{6,7},{7,6},{8,9},{9,8},{10,11... | collective-permute-start | bytes 1179656 | tf_op jit(solution)/shard_map/ppermute | solution.py:151
  3.2 12.5 %collective-permute-start = (bf16[16,128]{1,0:T(8,128)(2,1)S(1)}, bf16[16,128]{1,0:T(8,128)(2,1)S(1)}, u32[]{:S(2)}, u32[]{:S(2)}) collective-permute-start(bf16[16,128]{1,0:T(8,128)(2,1)S(1)} %slice_bitcast_fusion), channel_id=1, source_target_pairs={{0,2},{2,4},{4,6},{6,8},{8,10},{10,12},{12,14},{14,0},{1,3},{3,5},... | collective-permute-start | bytes 12296 | tf_op jit(solution)/shard_map/ppermute | solution.py:157
  15.7 15.5 %collective-permute-start.1 = (bf16[528,128]{1,0:T(8,128)(2,1)S(1)}, bf16[528,128]{1,0:T(8,128)(2,1)S(1)}, u32[]{:S(2)}, u32[]{:S(2)}) collective-permute-start(bf16[528,128]{1,0:T(8,128)(2,1)S(1)} %pad_maximum_fusion), channel_id=1, source_target_pairs={{0,16},{16,32},{32,48},{48,0},{64,80},{80,96},{96,112},{112,64},{1... | collective-permute-start | bytes 405512 | tf_op jit(solution)/shard_map/ppermute | solution.py:163
  19.1 28.4 %collective-permute-start.18 = (bf16[3,512,128]{2,1,0:T(8,128)(2,1)S(1)}, bf16[3,512,128]{2,1,0:T(8,128)(2,1)S(1)}, u32[]{:S(2)}, u32[]{:S(2)}) collective-permute-start(bf16[3,512,128]{2,1,0:T(8,128)(2,1)S(1)} %bitcast.29), channel_id=1, source_target_pairs={{0,2},{1,15},{2,4},{3,1},{4,6},{5,3},{6,8},{7,5},{8,10},{9,7},{10,... | collective-permute-start | bytes 1179656 | tf_op jit(solution)/shard_map/ppermute | solution.py:154
  21.1 10.1 %collective-permute-start.2 = (bf16[528,128]{1,0:T(8,128)(2,1)S(1)}, bf16[528,128]{1,0:T(8,128)(2,1)S(1)}, u32[]{:S(2)}, u32[]{:S(2)}) collective-permute-start(bf16[528,128]{1,0:T(8,128)(2,1)S(1)} %pad_maximum_fusion), channel_id=1, source_target_pairs={{0,32},{16,48},{32,0},{48,16},{64,96},{80,112},{96,64},{112,80},{1... | collective-permute-start | bytes 405512 | tf_op jit(solution)/shard_map/ppermute | solution.py:163
  25.8 17.0 %collective-permute-start.3 = (bf16[528,128]{1,0:T(8,128)(2,1)S(1)}, bf16[528,128]{1,0:T(8,128)(2,1)S(1)}, u32[]{:S(2)}, u32[]{:S(2)}) collective-permute-start(bf16[528,128]{1,0:T(8,128)(2,1)S(1)} %pad_maximum_fusion), channel_id=1, source_target_pairs={{0,48},{16,0},{32,16},{48,32},{64,112},{80,64},{96,80},{112,96},{1... | collective-permute-start | bytes 405512 | tf_op jit(solution)/shard_map/ppermute | solution.py:163
  29.3 13.6 %copy-start.3 = (bf16[3,512,128]{2,1,0:T(8,128)(2,1)}, bf16[3,512,128]{2,1,0:T(8,128)(2,1)S(1)}, u32[]{:S(2)}) copy-start(bf16[3,512,128]{2,1,0:T(8,128)(2,1)S(1)} %collective-permute-done.11.refs_8_) | copy-start | bytes 1179652
  29.3 10.9 %collective-permute-start.12 = (bf16[3,512,128]{2,1,0:T(8,128)(2,1)S(1)}, bf16[3,512,128]{2,1,0:T(8,128)(2,1)S(1)}, u32[]{:S(2)}, u32[]{:S(2)}) collective-permute-start(bf16[3,512,128]{2,1,0:T(8,128)(2,1)S(1)} %collective-permute-done.11.refs_8_), channel_id=1, source_target_pairs={{0,2},{1,15},{2,4},{3,1},{4,6},{5,3},{6,8},{7,5},{8,10},{9,7},{10,... | collective-permute-start | bytes 1179656 | tf_op jit(solution)/shard_map/ppermute | solution.py:153
  40.1 11.2 %collective-permute-start.13 = (bf16[3,512,128]{2,1,0:T(8,128)(2,1)S(1)}, bf16[3,512,128]{2,1,0:T(8,128)(2,1)S(1)}, u32[]{:S(2)}, u32[]{:S(2)}) collective-permute-start(bf16[3,512,128]{2,1,0:T(8,128)(2,1)S(1)} %collective-permute-done.12.refs_9_), channel_id=1, source_target_pairs={{0,2},{1,15},{2,4},{3,1},{4,6},{5,3},{6,8},{7,5},{8,10},{9,7},{10,... | collective-permute-start | bytes 1179656 | tf_op jit(solution)/shard_map/ppermute | solution.py:153
  42.8 64.2 %copy-start.22 = (s32[1,4096]{1,0:T(1,128)S(1)}, s32[1,4096]{1,0:T(1,128)}, u32[]{:S(2)}) copy-start(s32[1,4096]{1,0:T(1,128)} %param.11) | copy-start | bytes 49156
  42.8 15.7 %collective-permute-start.4 = (bf16[4,528,128]{2,1,0:T(8,128)(2,1)S(1)}, bf16[4,528,128]{2,1,0:T(8,128)(2,1)S(1)}, u32[]{:S(2)}, u32[]{:S(2)}) collective-permute-start(bf16[4,528,128]{2,1,0:T(8,128)(2,1)S(1)} %bitcast_dynamic-update-slice_fusion.refs_0_), channel_id=1, source_target_pairs={{0,64},{16,80},{32,96},{48,112},{64,128},{80,144},{96,160},{112,17... | collective-permute-start | bytes 1622024 | tf_op jit(solution)/shard_map/ppermute | solution.py:168
  47.6 16.6 %collective-permute-start.19 = (bf16[3,512,128]{2,1,0:T(8,128)(2,1)S(1)}, bf16[3,512,128]{2,1,0:T(8,128)(2,1)S(1)}, u32[]{:S(2)}, u32[]{:S(2)}) collective-permute-start(bf16[3,512,128]{2,1,0:T(8,128)(2,1)S(1)} %collective-permute-done.18.refs_16_), channel_id=1, source_target_pairs={{0,2},{1,15},{2,4},{3,1},{4,6},{5,3},{6,8},{7,5},{8,10},{9,7},{10,... | collective-permute-start | bytes 1179656 | tf_op jit(solution)/shard_map/ppermute | solution.py:154
  51.4 16.4 %collective-permute-start.14 = (bf16[3,512,128]{2,1,0:T(8,128)(2,1)S(1)}, bf16[3,512,128]{2,1,0:T(8,128)(2,1)S(1)}, u32[]{:S(2)}, u32[]{:S(2)}) collective-permute-start(bf16[3,512,128]{2,1,0:T(8,128)(2,1)S(1)} %collective-permute-done.13.refs_10_), channel_id=1, source_target_pairs={{0,2},{1,15},{2,4},{3,1},{4,6},{5,3},{6,8},{7,5},{8,10},{9,7},{10,... | collective-permute-start | bytes 1179656 | tf_op jit(solution)/shard_map/ppermute | solution.py:153
  56.5 21.2 %collective-permute-start.5 = (bf16[4,528,128]{2,1,0:T(8,128)(2,1)S(1)}, bf16[4,528,128]{2,1,0:T(8,128)(2,1)S(1)}, u32[]{:S(2)}, u32[]{:S(2)}) collective-permute-start(bf16[4,528,128]{2,1,0:T(8,128)(2,1)S(1)} %bitcast_dynamic-update-slice_fusion.refs_0_), channel_id=1, source_target_pairs={{0,448},{16,464},{32,480},{48,496},{64,0},{80,16},{96,32},{112,48}... | collective-permute-start | bytes 1622024 | tf_op jit(solution)/shard_map/ppermute | solution.py:172
  58.6 21.1 %collective-permute-start.6 = (bf16[4,528,128]{2,1,0:T(8,128)(2,1)S(1)}, bf16[4,528,128]{2,1,0:T(8,128)(2,1)S(1)}, u32[]{:S(2)}, u32[]{:S(2)}) collective-permute-start(bf16[4,528,128]{2,1,0:T(8,128)(2,1)S(1)} %collective-permute-done.4.refs_1_), channel_id=1, source_target_pairs={{0,64},{16,80},{32,96},{48,112},{64,128},{80,144},{96,160},{112,17... | collective-permute-start | bytes 1622024 | tf_op jit(solution)/shard_map/ppermute | solution.py:168
  64.2 10.9 %collective-permute-start.20 = (bf16[3,512,128]{2,1,0:T(8,128)(2,1)S(1)}, bf16[3,512,128]{2,1,0:T(8,128)(2,1)S(1)}, u32[]{:S(2)}, u32[]{:S(2)}) collective-permute-start(bf16[3,512,128]{2,1,0:T(8,128)(2,1)S(1)} %collective-permute-done.19.refs_17_), channel_id=1, source_target_pairs={{0,2},{1,15},{2,4},{3,1},{4,6},{5,3},{6,8},{7,5},{8,10},{9,7},{10,... | collective-permute-start | bytes 1179656 | tf_op jit(solution)/shard_map/ppermute | solution.py:154
  67.8 17.0 %collective-permute-start.15 = (bf16[3,512,128]{2,1,0:T(8,128)(2,1)S(1)}, bf16[3,512,128]{2,1,0:T(8,128)(2,1)S(1)}, u32[]{:S(2)}, u32[]{:S(2)}) collective-permute-start(bf16[3,512,128]{2,1,0:T(8,128)(2,1)S(1)} %collective-permute-done.14.refs_11_), channel_id=1, source_target_pairs={{0,2},{1,15},{2,4},{3,1},{4,6},{5,3},{6,8},{7,5},{8,10},{9,7},{10,... | collective-permute-start | bytes 1179656 | tf_op jit(solution)/shard_map/ppermute | solution.py:153
  75.1 12.5 %collective-permute-start.21 = (bf16[3,512,128]{2,1,0:T(8,128)(2,1)S(1)}, bf16[3,512,128]{2,1,0:T(8,128)(2,1)S(1)}, u32[]{:S(2)}, u32[]{:S(2)}) collective-permute-start(bf16[3,512,128]{2,1,0:T(8,128)(2,1)S(1)} %collective-permute-done.20.refs_18_), channel_id=1, source_target_pairs={{0,2},{1,15},{2,4},{3,1},{4,6},{5,3},{6,8},{7,5},{8,10},{9,7},{10,... | collective-permute-start | bytes 1179656 | tf_op jit(solution)/shard_map/ppermute | solution.py:154
  77.7 20.0 %collective-permute-start.7 = (bf16[4,528,128]{2,1,0:T(8,128)(2,1)S(1)}, bf16[4,528,128]{2,1,0:T(8,128)(2,1)S(1)}, u32[]{:S(2)}, u32[]{:S(2)}) collective-permute-start(bf16[4,528,128]{2,1,0:T(8,128)(2,1)S(1)} %collective-permute-done.5.refs_2_), channel_id=1, source_target_pairs={{0,448},{16,464},{32,480},{48,496},{64,0},{80,16},{96,32},{112,48}... | collective-permute-start | bytes 1622024 | tf_op jit(solution)/shard_map/ppermute | solution.py:172
  79.7 20.0 %collective-permute-start.8 = (bf16[4,528,128]{2,1,0:T(8,128)(2,1)S(1)}, bf16[4,528,128]{2,1,0:T(8,128)(2,1)}, u32[]{:S(2)}, u32[]{:S(2)}) collective-permute-start(bf16[4,528,128]{2,1,0:T(8,128)(2,1)S(1)} %collective-permute-done.6.refs_3_), channel_id=1, source_target_pairs={{0,64},{16,80},{32,96},{48,112},{64,128},{80,144},{96,160},{112,17... | collective-permute-start | bytes 1622024 | tf_op jit(solution)/shard_map/ppermute | solution.py:168
  84.8 11.0 %collective-permute-start.16 = (bf16[3,512,128]{2,1,0:T(8,128)(2,1)S(1)}, bf16[3,512,128]{2,1,0:T(8,128)(2,1)}, u32[]{:S(2)}, u32[]{:S(2)}) collective-permute-start(bf16[3,512,128]{2,1,0:T(8,128)(2,1)S(1)} %collective-permute-done.15.refs_12_), channel_id=1, source_target_pairs={{0,2},{1,15},{2,4},{3,1},{4,6},{5,3},{6,8},{7,5},{8,10},{9,7},{10,... | collective-permute-start | bytes 1179656 | tf_op jit(solution)/shard_map/ppermute | solution.py:153
  87.5 17.3 %collective-permute-start.22 = (bf16[3,512,128]{2,1,0:T(8,128)(2,1)S(1)}, bf16[3,512,128]{2,1,0:T(8,128)(2,1)}, u32[]{:S(2)}, u32[]{:S(2)}) collective-permute-start(bf16[3,512,128]{2,1,0:T(8,128)(2,1)S(1)} %collective-permute-done.21.refs_19_), channel_id=1, source_target_pairs={{0,2},{1,15},{2,4},{3,1},{4,6},{5,3},{6,8},{7,5},{8,10},{9,7},{10,... | collective-permute-start | bytes 1179656 | tf_op jit(solution)/shard_map/ppermute | solution.py:154
  95.8 11.4 %collective-permute-start.17 = (bf16[3,512,128]{2,1,0:T(8,128)(2,1)}, bf16[3,512,128]{2,1,0:T(8,128)(2,1)}, u32[]{:S(2)}, u32[]{:S(2)}) collective-permute-start(bf16[3,512,128]{2,1,0:T(8,128)(2,1)} %collective-permute-done.16.refs_13_), channel_id=1, source_target_pairs={{0,2},{1,15},{2,4},{3,1},{4,6},{5,3},{6,8},{7,5},{8,10},{9,7},{10,... | collective-permute-start | bytes 1179656 | tf_op jit(solution)/shard_map/ppermute | solution.py:153
  97.7 14.1 %collective-permute-start.9 = (bf16[4,528,128]{2,1,0:T(8,128)(2,1)S(1)}, bf16[4,528,128]{2,1,0:T(8,128)(2,1)}, u32[]{:S(2)}, u32[]{:S(2)}) collective-permute-start(bf16[4,528,128]{2,1,0:T(8,128)(2,1)S(1)} %collective-permute-done.7.refs_4_), channel_id=1, source_target_pairs={{0,448},{16,464},{32,480},{48,496},{64,0},{80,16},{96,32},{112,48}... | collective-permute-start | bytes 1622024 | tf_op jit(solution)/shard_map/ppermute | solution.py:172
  99.7 12.3 %collective-permute-start.10 = (bf16[4,528,128]{2,1,0:T(8,128)(2,1)}, bf16[4,528,128]{2,1,0:T(8,128)(2,1)}, u32[]{:S(2)}, u32[]{:S(2)}) collective-permute-start(bf16[4,528,128]{2,1,0:T(8,128)(2,1)} %collective-permute-done.8.refs_5_), channel_id=1, source_target_pairs={{0,64},{16,80},{32,96},{48,112},{64,128},{80,144},{96,160},{112,17... | collective-permute-start | bytes 1622024 | tf_op jit(solution)/shard_map/ppermute | solution.py:168
  104.8 11.2 %collective-permute-start.23 = (bf16[3,512,128]{2,1,0:T(8,128)(2,1)}, bf16[3,512,128]{2,1,0:T(8,128)(2,1)}, u32[]{:S(2)}, u32[]{:S(2)}) collective-permute-start(bf16[3,512,128]{2,1,0:T(8,128)(2,1)} %collective-permute-done.22.refs_20_), channel_id=1, source_target_pairs={{0,2},{1,15},{2,4},{3,1},{4,6},{5,3},{6,8},{7,5},{8,10},{9,7},{10,... | collective-permute-start | bytes 1179656 | tf_op jit(solution)/shard_map/ppermute | solution.py:154
  107.2 25.2 %collective-permute-start.25 = (bf16[3,512,128]{2,1,0:T(8,128)(2,1)}, bf16[3,512,128]{2,1,0:T(8,128)(2,1)S(1)}, u32[]{:S(2)}, u32[]{:S(2)}) collective-permute-start(bf16[3,512,128]{2,1,0:T(8,128)(2,1)} %collective-permute-done.17.refs_14_), channel_id=1, source_target_pairs={{0,2},{1,15},{2,4},{3,1},{4,6},{5,3},{6,8},{7,5},{8,10},{9,7},{10,... | collective-permute-start | bytes 1179656 | tf_op jit(solution)/shard_map/ppermute | solution.py:153
  132.4 13.5 %copy-start.1 = (f32[7,3,128]{2,0,1:T(8,128)S(1)}, f32[7,3,128]{2,0,1:T(8,128)}, u32[]{:S(2)}) copy-start(f32[7,3,128]{2,0,1:T(8,128)} %param.8) | copy-start | bytes 32260
  132.9 13.0 %collective-permute-start.26 = (bf16[528,384]{1,0:T(8,128)(2,1)S(1)}, bf16[528,384]{1,0:T(8,128)(2,1)S(1)}, u32[]{:S(2)}, u32[]{:S(2)}) collective-permute-start(bf16[528,384]{1,0:T(8,128)(2,1)S(1)} %shard_map.65), channel_id=1, source_target_pairs={{0,1},{1,0},{2,3},{3,2},{4,5},{5,4},{6,7},{7,6},{8,9},{9,8},{10,11... | collective-permute-start | bytes 1216520 | tf_op jit(solution)/shard_map/ppermute | solution.py:205
  134.8 11.1 %collective-permute-start.24 = (bf16[3,512,128]{2,1,0:T(8,128)(2,1)}, bf16[3,512,128]{2,1,0:T(8,128)(2,1)S(1)}, u32[]{:S(2)}, u32[]{:S(2)}) collective-permute-start(bf16[3,512,128]{2,1,0:T(8,128)(2,1)} %collective-permute-done.23.refs_21_), channel_id=1, source_target_pairs={{0,2},{1,15},{2,4},{3,1},{4,6},{5,3},{6,8},{7,5},{8,10},{9,7},{10,... | collective-permute-start | bytes 1179656 | tf_op jit(solution)/shard_map/ppermute | solution.py:154
  147.5 7.0 %collective-permute-start.27 = (bf16[128,128]{1,0:T(8,128)(2,1)S(1)}, bf16[128,128]{1,0:T(8,128)(2,1)S(1)}, u32[]{:S(2)}, u32[]{:S(2)}) collective-permute-start(bf16[128,128]{1,0:T(8,128)(2,1)S(1)} %slice.19), channel_id=1, source_target_pairs={{0,2},{2,4},{4,6},{6,8},{8,10},{10,12},{12,14},{14,0},{1,3},{3,5},... | collective-permute-start | bytes 98312 | tf_op jit(solution)/shard_map/ppermute | solution.py:222
  (19 other events, 17.7 us)

commit v2 on v0

v2 whole, which is shorter than its diff:
```python
import functools

import jax
import jax.numpy as jnp
from jax import lax
from jax.experimental import pallas as pl
from jax.experimental.pallas import tpu as pltpu
from jax.sharding import PartitionSpec as P

PAD = 16
LEAD = 128 + PAD
HEAD = 192
STEP = 64
CHUNK = 2
GROUP = 64
BF16, F32 = jnp.bfloat16, jnp.float32
VMEM = pl.BlockSpec(memory_space=pltpu.VMEM)
SMEM = pl.BlockSpec(memory_space=pltpu.SMEM)
ANY = pl.BlockSpec(memory_space=pl.ANY)
HBM = pl.BlockSpec(memory_space=pltpu.HBM)
MIB = 1 << 20


def call(kernel, out_shape, in_specs, out_specs, scratch=(), flops=0, nbytes=0, vmem=8):
    return pl.pallas_call(
        kernel,
        out_shape=out_shape,
        in_specs=in_specs,
        out_specs=out_specs,
        scratch_shapes=list(scratch),
        compiler_params=pltpu.CompilerParams(vmem_limit_bytes=vmem * MIB),
        cost_estimate=pl.CostEstimate(flops=flops, bytes_accessed=nbytes, transcendentals=0),
    )


def wide(planes, groups=None):
    return jnp.concatenate([planes[j] for j in range(planes.shape[0])], 1)


def fetch(pairs, sem):
    copies = [pltpu.make_async_copy(src, dst, sem.at[k]) for k, (src, dst) in enumerate(pairs)]
    for copy in copies:
        copy.start()
    return copies


def product(blocks, weights, ready):
    total = None
    for s in range(0, blocks.shape[0], CHUNK):
        these = range(s, s + CHUNK)
        for t in these:
            ready(t)
        left = [blocks[t, j] for t in these for j in range(blocks.shape[1])]
        right = [wide(weights[t]) for t in these]
        term = jnp.dot(
            jnp.concatenate(left, 1), jnp.concatenate(right, 0), preferred_element_type=F32
        )
        total = term if total is None else total + term
    return total


def theirs_sum(count, tokens_from, weights_from, place, ids, ends, *refs):
    token_refs, weight_refs = refs[:count], refs[count : 2 * count]
    out, held_out, held, weights, sem, out_sem = refs[2 * count :]
    pairs, kept = [], []
    for k in range(count):
        slot = lax.rem(place[0] + tokens_from[k] + count, count)
        pairs.append((token_refs[k], held.at[slot]))
        kept.append((token_refs[k], held_out.at[slot]))
        slot = lax.rem(place[1] + weights_from[k] + count, count)
        pairs.append((weight_refs[k], weights.at[slot]))
    copies = fetch(pairs, sem)
    kept = fetch(kept, out_sem)
    for copy in copies:
        copy.wait()
    out[...] = product(held, weights, lambda t: None).astype(out.dtype)
    for copy in kept:
        copy.wait()


def mine_sum(held_in, weights_in, held, weights, sem):
    count, rows = held.shape[0], held.shape[2]
    first = held_in.shape[2] - rows
    pairs = []
    for t in range(count):
        pairs.append((held_in.at[t, :, first:, :], held.at[t]))
        pairs.append((weights_in.at[t], weights.at[t]))
    copies = fetch(pairs, sem)

    def ready(t):
        copies[2 * t].wait()
        copies[2 * t + 1].wait()

    return product(held, weights, ready)


def rim_sum(held_in, weights_in, received, out, held, weights, sem):
    first = received.shape[0] - out.shape[0]
    total = mine_sum(held_in, weights_in, held, weights, sem)
    out[...] = (total + received[first:, :].astype(F32)).astype(BF16)


def features(first, last, shift, raw, ids, taps, mixed, queries):
    reach = taps.shape[0] - 1
    for base in range(first, last, STEP):
        step = min(STEP, last - base)
        near = ids[base + LEAD - PAD : base + LEAD + step, :]
        begin = base + shift - PAD
        sums = [jnp.zeros((step, 128), F32) for _ in range(3)]
        for g in range(3):
            if g == 0 and base < 0:
                continue
            held = raw[begin : begin + PAD + step, 128 * g : 128 * g + 128]
            for lag in range(reach + 1):
                spot = slice(PAD - lag, PAD - lag + step)
                weight = taps[lag : lag + 1, 128 * g : 128 * g + 128]
                same = near[spot] == near[PAD:]
                sums[g] = sums[g] + jnp.where(same, held[spot] * weight, 0.0)
        if base >= 0:
            queries[base : base + step, :] = sums[0]
        mixed[base + shift : base + shift + step, :] = (sums[1] * sums[2]).astype(BF16).astype(F32)


def long_filter(first, last, shift, ends, ids, mixed, queries, taps, skip, out, window):
    reach = taps.shape[0]

    def group(i, _):
        base = pl.multiple_of(first + i * GROUP, GROUP)
        here = ids[pl.ds(base + LEAD, GROUP), :]

        def genome(g, total):
            for k in range((reach + GROUP) // GROUP):
                spot = pl.ds(base + k * GROUP + LEAD - reach, GROUP)
                source = pl.ds(pl.multiple_of(base + k * GROUP + shift - reach, PAD), GROUP)
                window[k * GROUP : k * GROUP + GROUP, :] = jnp.where(
                    ids[spot, :] == g, mixed[source, :], 0.0
                )
            sums = jnp.zeros((GROUP, 128), F32)
            for s in range(8):
                held = window[8 - s : GROUP + reach - s, :]
                for a in range(reach // 8):
                    weight = taps[8 * a + s : 8 * a + s + 1, :]
                    start = reach - 8 - 8 * a
                    sums = sums + held[start : start + GROUP] * weight
            return jnp.where(here == g, sums, total)

        low, high = ends[2 * (base // GROUP)], ends[2 * (base // GROUP) + 1]
        total = lax.fori_loop(low, high + 1, genome, jnp.zeros((GROUP, 128), F32))
        bias = skip[...] * mixed[pl.ds(pl.multiple_of(base + shift, PAD), GROUP), :]
        gated = queries[pl.ds(base, GROUP), :] * (total + bias)
        out[pl.ds(base, GROUP), :] = gated.astype(out.dtype)
        return 0

    lax.fori_loop(0, (last - first) // GROUP, group, 0)


def main_part(
    ends, held_in, weights_in, received, ids, short, taps, skip, out, top,
    raw, mixed, queries, window, held, weights, sem,
):
    rows = held.shape[2]
    summed = mine_sum(held_in, weights_in, held, weights, sem) + received[...].astype(F32)
    rounded = summed.astype(BF16)
    top[...] = rounded[: top.shape[0]]
    raw[...] = rounded.astype(F32)
    features(PAD, rows, 0, raw, ids, short, mixed, queries)
    long_filter(HEAD, rows, 0, ends, ids, mixed, queries, taps, skip, out, window)


def head_part(ends, before, top, ids, short, taps, skip, given, out, raw, mixed, queries, window):
    rim = before.shape[0]
    raw[:rim, :] = before[...].astype(F32)
    raw[rim:, :] = top[...].astype(F32)
    features(PAD - rim, 0, rim, raw, ids, short, mixed, queries)
    features(0, HEAD, rim, raw, ids, short, mixed, queries)
    out[HEAD:, :] = given[HEAD:, :]
    long_filter(0, HEAD, rim, ends, ids, mixed, queries, taps, skip, out, window)


def two_way(block, axis, count, hop):
    blocks, offsets, up, down = [block], [0], block, block
    for s in range(1, count // 2 + 1):
        up = lax.ppermute(up, axis, hop(1))
        blocks.append(up)
        offsets.append(-s)
        if s <= (count - 1) // 2:
            down = lax.ppermute(down, axis, hop(-1))
            blocks.append(down)
            offsets.append(s)
    return blocks, tuple(offsets)


def body(tokens, w_in, short_taps, mr_taps, skip, genome_ids):
    length, width = tokens.shape[1], tokens.shape[2]
    ctx, tp = lax.axis_size("ctx"), lax.axis_size("tp")
    xs, ys = lax.axis_size("fsdp") // ctx, ctx
    reach = mr_taps.shape[0]
    f, z, c = lax.axis_index("fsdp"), lax.axis_index("ctx"), lax.axis_index("tp")
    x, y = f % xs, f // xs

    along_x = lambda d: [(j * xs + i, j * xs + (i + d) % xs) for j in range(ys) for i in range(xs)]
    along_y = lambda d: [(j * xs + i, (j + d) % ys * xs + i) for j in range(ys) for i in range(xs)]
    along_z = lambda d: [(k, (k + d) % ctx) for k in range(ctx)]
    swap = [(0, 1), (1, 0)]

    planes = jnp.transpose(w_in, (1, 0, 2)).reshape(3, xs, tp, width, width)
    mine = lax.dynamic_index_in_dim(planes, c, 2, False).reshape(3, xs * width, width)
    theirs = lax.dynamic_index_in_dim(planes, 1 - c, 2, False).reshape(3, xs * width, width)
    mine_all = lax.all_gather(mine, "ctx", axis=0)
    theirs = lax.ppermute(theirs, "tp", swap)
    weights, weights_from = two_way(theirs, "ctx", ctx, along_z)

    own = tokens[0]
    block = jnp.zeros((xs,) + own.shape, BF16)
    block = lax.dynamic_update_index_in_dim(block, own, x, 0)
    for d in range(1, xs):
        hop = d if d <= xs // 2 else d - xs
        piece = lax.ppermute(own, "fsdp", along_x(hop))
        block = lax.dynamic_update_index_in_dim(block, piece, (x - hop) % xs, 0)
    blocks, tokens_from = two_way(block, "fsdp", ys, along_y)

    padded = jnp.pad(genome_ids[0], (LEAD, 0), constant_values=-1)
    seen = lax.dynamic_slice_in_dim(padded, z * length, length + LEAD, 0)
    ids = jnp.broadcast_to(seen[:, None], (length + LEAD, 128))
    ends = jnp.stack([seen[LEAD::GROUP], seen[LEAD + GROUP - 1 :: GROUP]], 1).reshape(-1)
    place = jnp.stack([y, z]).astype(jnp.int32)
    short = short_taps.reshape(short_taps.shape[0], -1)
    bias = skip[None, :]

    every = 2 * length * ctx * xs * width * 3 * width
    block_shape = (ys, xs, length, width)
    buffers = lambda rows: [
        pltpu.VMEM((ys, xs, rows, width), BF16),
        pltpu.VMEM((ctx,) + theirs.shape, BF16),
        pltpu.SemaphoreType.DMA((2 * ctx,)),
    ]
    give, held = call(
        functools.partial(theirs_sum, ctx, tokens_from, weights_from),
        (
            jax.ShapeDtypeStruct((length, 3 * width), BF16),
            jax.ShapeDtypeStruct(block_shape, BF16),
        ),
        [SMEM, ANY, ANY] + [HBM] * (2 * ctx),
        (VMEM, HBM),
        buffers(length) + [pltpu.SemaphoreType.DMA((ctx,))],
        flops=every,
        nbytes=8 * MIB,
        vmem=60,
    )(place, ids, ends, *blocks, *weights)
    received = lax.ppermute(give, "tp", swap)
    rim = call(
        rim_sum,
        jax.ShapeDtypeStruct((LEAD, 3 * width), BF16),
        [HBM, HBM, VMEM],
        VMEM,
        buffers(LEAD),
        flops=every * LEAD // length,
        nbytes=8 * MIB,
        vmem=60,
    )(held, mine_all, received)
    before = lax.ppermute(rim, "ctx", along_z(1))
    work = lambda rows: [
        pltpu.VMEM((rows, 3 * width), F32),
        pltpu.VMEM((rows, width), F32),
        pltpu.VMEM((length, width), F32),
        pltpu.VMEM((reach + GROUP, width), F32),
    ]
    outline = jax.ShapeDtypeStruct((length, width), BF16)
    part, top = call(
        main_part,
        (outline, jax.ShapeDtypeStruct((HEAD, 3 * width), BF16)),
        [SMEM, HBM, HBM] + [VMEM] * 5,
        (VMEM, VMEM),
        work(length) + buffers(length),
        flops=2 * every,
        nbytes=8 * MIB,
        vmem=60,
    )(ends, held, mine_all, received, ids, short, mr_taps, bias)
    gated = call(
        head_part,
        outline,
        [SMEM] + [VMEM] * 7,
        VMEM,
        work(LEAD + HEAD),
        flops=every // 4,
        nbytes=1 * MIB,
    )(ends, before, top, ids, short, mr_taps, bias, part)
    return gated[None]


def solution(mesh):
    in_specs = (
        P(None, "ctx", ("fsdp", "tp")),
        P("ctx", None, ("fsdp", "tp")),
        P(None, None, ("fsdp", "tp")),
        P(None, ("fsdp", "tp")),
        P(("fsdp", "tp")),
        P(),
    )
    out_specs = P(None, "ctx", ("fsdp", "tp"))
    return jax.shard_map(body, mesh=mesh, in_specs=in_specs, out_specs=out_specs, check_vma=False)
```

time: 367 us -> 271 us (0.74)
  the two profiles are of different devices: /device:TPU:192 before, /device:TPU:1 now
where the time goes in v2:
time: 271 us; the launch traced here: 270 us
  Pallas kernels  146 us (54%)
  starting transfers between devices  72 us (27%)
  waiting for transfers between devices  28.4 us (10%)
  between operations  14 us (5%)
  local copies, waits for them, and re-layouts  8.21 us (3%)
    pallas_call x1, Pallas kernels, body(): call(functools.partial(theirs_sum, ctx, tokens_from, weights_from), (jax....  130 us
    ppermute x6, starting transfers between devices, two_way(): down = lax.ppermute(down, axis, hop(-1))  31.2 us
    ppermute x8, waiting for transfers between devices, two_way(): up = lax.ppermute(up, axis, hop(1))  21.8 us
    ppermute x8, starting transfers between devices, two_way(): up = lax.ppermute(up, axis, hop(1))  16.8 us
    ppermute x3, starting transfers between devices, body(): piece = lax.ppermute(own, 'fsdp', along_x(hop))  11.4 us
    pallas_call x1, Pallas kernels, body(): call(main_part, (outline, jax.ShapeDtypeStruct((HEAD, 3 * width), BF16)),...  9.32 us
    ppermute x1, starting transfers between devices, body(): theirs = lax.ppermute(theirs, 'tp', swap)  6.24 us
  transfers between devices with their start and end apart: 21, of which 6 were waited for; matrix products, arithmetic and copies ran while one was open for 2% of the time, Pallas kernels for 52%

profile of v2, /device:TPU:1, one launch (start us, length us, event | category | flops | bytes accessed | tf_op | source)
XLA Modules:
  0.0 269.7 jit_solution(12276971255145976312)
XLA Ops:
  6.5 1.9 constant_dynamic-slice_fusion
  8.5 4.0 %collective-permute-start = (bf16[512,128]{1,0:T(8,128)(2,1)}, bf16[512,128]{1,0:T(8,128)(2,1)S(1)}, u32[]{:S(2)}, u32[]{:S(2)}) collective-permute-start(bf16[512,128]{1,0:T(8,128)(2,1)} %bitcast.31), channel_id=1, source_target_pairs={{0,16},{16,32},{32,48},{48,0},{64,80},{80,96},{96,112},{112,64},{1... | collective-permute-start | bytes 393224 | tf_op jit(solution)/shard_map/ppermute | solution.py:218
  12.5 4.4 %collective-permute-start.1 = (bf16[512,128]{1,0:T(8,128)(2,1)}, bf16[512,128]{1,0:T(8,128)(2,1)S(1)}, u32[]{:S(2)}, u32[]{:S(2)}) collective-permute-start(bf16[512,128]{1,0:T(8,128)(2,1)} %bitcast.32), channel_id=1, source_target_pairs={{0,32},{16,48},{32,0},{48,16},{64,96},{80,112},{96,64},{112,80},{1... | collective-permute-start | bytes 393224 | tf_op jit(solution)/shard_map/ppermute | solution.py:218
  16.8 3.1 %collective-permute-start.2 = (bf16[512,128]{1,0:T(8,128)(2,1)}, bf16[512,128]{1,0:T(8,128)(2,1)S(1)}, u32[]{:S(2)}, u32[]{:S(2)}) collective-permute-start(bf16[512,128]{1,0:T(8,128)(2,1)} %bitcast.33), channel_id=1, source_target_pairs={{0,48},{16,0},{32,16},{48,32},{64,112},{80,64},{96,80},{112,96},{1... | collective-permute-start | bytes 393224 | tf_op jit(solution)/shard_map/ppermute | solution.py:218
  20.0 0.9 constant_dynamic-update-slice_fusion
  21.1 2.0 collective-permute-done.2
  23.1 2.9 %collective-permute-start.3 = (bf16[4,512,128]{2,1,0:T(8,128)(2,1)S(1)}, bf16[4,512,128]{2,1,0:T(8,128)(2,1)S(1)}, u32[]{:S(2)}, u32[]{:S(2)}) collective-permute-start(bf16[4,512,128]{2,1,0:T(8,128)(2,1)S(1)} %bitcast_dynamic-update-slice_fusion.refs_0_), channel_id=1, source_target_pairs={{0,64},{16,80},{32,96},{48,112},{64,128},{80,144},{96,160},{112,17... | collective-permute-start | bytes 1572872 | tf_op jit(solution)/shard_map/ppermute | solution.py:183
  26.0 6.2 %collective-permute-start.10 = (bf16[3,512,128]{2,1,0:T(8,128)(2,1)S(1)}, bf16[3,512,128]{2,1,0:T(8,128)(2,1)S(1)}, u32[]{:S(2)}, u32[]{:S(2)}) collective-permute-start(bf16[3,512,128]{2,1,0:T(8,128)(2,1)S(1)} %bitcast.30), channel_id=1, source_target_pairs={{0,1},{1,0},{2,3},{3,2},{4,5},{5,4},{6,7},{7,6},{8,9},{9,8},{10,11... | collective-permute-start | bytes 1179656 | tf_op jit(solution)/shard_map/ppermute | solution.py:210
  32.2 4.9 %collective-permute-start.4 = (bf16[4,512,128]{2,1,0:T(8,128)(2,1)S(1)}, bf16[4,512,128]{2,1,0:T(8,128)(2,1)S(1)}, u32[]{:S(2)}, u32[]{:S(2)}) collective-permute-start(bf16[4,512,128]{2,1,0:T(8,128)(2,1)S(1)} %bitcast_dynamic-update-slice_fusion.refs_0_), channel_id=1, source_target_pairs={{0,448},{16,464},{32,480},{48,496},{64,0},{80,16},{96,32},{112,48}... | collective-permute-start | bytes 1572872 | tf_op jit(solution)/shard_map/ppermute | solution.py:187
  37.1 1.9 collective-permute-start.11
  39.1 1.9 collective-permute-start.5
  41.0 9.4 %collective-permute-start.12 = (bf16[3,512,128]{2,1,0:T(8,128)(2,1)S(1)}, bf16[3,512,128]{2,1,0:T(8,128)(2,1)S(1)}, u32[]{:S(2)}, u32[]{:S(2)}) collective-permute-start(bf16[3,512,128]{2,1,0:T(8,128)(2,1)S(1)} %collective-permute-done.10.refs_8_), channel_id=1, source_target_pairs={{0,14},{2,0},{4,2},{6,4},{8,6},{10,8},{12,10},{14,12},{1,15},{3,1}... | collective-permute-start | bytes 1179656 | tf_op jit(solution)/shard_map/ppermute | solution.py:187
  50.4 12.1 %collective-permute-done.11.refs_9_ = bf16[3,512,128]{2,1,0:T(8,128)(2,1)S(1)} collective-permute-done((bf16[3,512,128]{2,1,0:T(8,128)(2,1)S(1)}, bf16[3,512,128]{2,1,0:T(8,128)(2,1)S(1)}, u32[]{:S(2)}, u32[]{:S(2)}) %collective-permute-start.11) | collective-permute-done | bytes 393248 | tf_op jit(solution)/shard_map/ppermute | solution.py:183
  62.5 1.9 collective-permute-start.13
  64.5 3.7 %collective-permute-start.6 = (bf16[4,512,128]{2,1,0:T(8,128)(2,1)S(1)}, bf16[4,512,128]{2,1,0:T(8,128)(2,1)S(1)}, u32[]{:S(2)}, u32[]{:S(2)}) collective-permute-start(bf16[4,512,128]{2,1,0:T(8,128)(2,1)S(1)} %collective-permute-done.4.refs_2_), channel_id=1, source_target_pairs={{0,448},{16,464},{32,480},{48,496},{64,0},{80,16},{96,32},{112,48}... | collective-permute-start | bytes 1572872 | tf_op jit(solution)/shard_map/ppermute | solution.py:187
  68.2 1.9 collective-permute-start.7
  70.1 4.6 %collective-permute-start.14 = (bf16[3,512,128]{2,1,0:T(8,128)(2,1)S(1)}, bf16[3,512,128]{2,1,0:T(8,128)(2,1)}, u32[]{:S(2)}, u32[]{:S(2)}) collective-permute-start(bf16[3,512,128]{2,1,0:T(8,128)(2,1)S(1)} %collective-permute-done.12.refs_10_), channel_id=1, source_target_pairs={{0,14},{2,0},{4,2},{6,4},{8,6},{10,8},{12,10},{14,12},{1,15},{3,1}... | collective-permute-start | bytes 1179656 | tf_op jit(solution)/shard_map/ppermute | solution.py:187
  74.7 4.7 %collective-permute-done.13.refs_11_ = bf16[3,512,128]{2,1,0:T(8,128)(2,1)S(1)} collective-permute-done((bf16[3,512,128]{2,1,0:T(8,128)(2,1)S(1)}, bf16[3,512,128]{2,1,0:T(8,128)(2,1)S(1)}, u32[]{:S(2)}, u32[]{:S(2)}) %collective-permute-start.13) | collective-permute-done | bytes 393248 | tf_op jit(solution)/shard_map/ppermute | solution.py:183
  79.4 2.3 collective-permute-start.15
  81.8 4.3 %collective-permute-start.8 = (bf16[4,512,128]{2,1,0:T(8,128)(2,1)S(1)}, bf16[4,512,128]{2,1,0:T(8,128)(2,1)}, u32[]{:S(2)}, u32[]{:S(2)}) collective-permute-start(bf16[4,512,128]{2,1,0:T(8,128)(2,1)S(1)} %collective-permute-done.6.refs_4_), channel_id=1, source_target_pairs={{0,448},{16,464},{32,480},{48,496},{64,0},{80,16},{96,32},{112,48}... | collective-permute-start | bytes 1572872 | tf_op jit(solution)/shard_map/ppermute | solution.py:187
  86.1 1.9 collective-permute-start.9
  88.1 4.3 %collective-permute-start.16 = (bf16[3,512,128]{2,1,0:T(8,128)(2,1)}, bf16[3,512,128]{2,1,0:T(8,128)(2,1)}, u32[]{:S(2)}, u32[]{:S(2)}) collective-permute-start(bf16[3,512,128]{2,1,0:T(8,128)(2,1)} %collective-permute-done.14.refs_12_), channel_id=1, source_target_pairs={{0,14},{2,0},{4,2},{6,4},{8,6},{10,8},{12,10},{14,12},{1,15},{3,1}... | collective-permute-start | bytes 1179656 | tf_op jit(solution)/shard_map/ppermute | solution.py:187
  92.4 1.9 collective-permute-start.17
  96.7 3.0 %collective-permute-done.16.refs_14_ = bf16[3,512,128]{2,1,0:T(8,128)(2,1)} collective-permute-done((bf16[3,512,128]{2,1,0:T(8,128)(2,1)}, bf16[3,512,128]{2,1,0:T(8,128)(2,1)}, u32[]{:S(2)}, u32[]{:S(2)}) %collective-permute-start.16) | collective-permute-done | bytes 393248 | tf_op jit(solution)/shard_map/ppermute | solution.py:187
  99.7 5.1 %collective-permute-done.17.refs_15_ = bf16[3,512,128]{2,1,0:T(8,128)(2,1)} collective-permute-done((bf16[3,512,128]{2,1,0:T(8,128)(2,1)}, bf16[3,512,128]{2,1,0:T(8,128)(2,1)}, u32[]{:S(2)}, u32[]{:S(2)}) %collective-permute-start.17) | collective-permute-done | bytes 393248 | tf_op jit(solution)/shard_map/ppermute | solution.py:183
  105.7 129.9 %shard_map.64 = (bf16[512,384]{1,0:T(8,128)(2,1)}, bf16[8,4,512,128]{3,2,1,0:T(8,128)(2,1)}) custom-call(s32[2]{0:T(128)} %pad_add_fusion.1.place, s32[656,128]{1,0:T(8,128)} %broadcast_in_dim.26.ids, s32[16]{0:T(128)} %reshape.15.ends, bf16[4,512,128]{2,1,0:T(8,128)(2,1)} %copy-done.7, bf16[4,512,128]{2,1,0:T(8,128)(2,1)} %copy-done.8, ...), custom_call_target="tpu_custom_call" | custom-call | flops 1610612736 | bytes 8388608 | tf_op jit(solution)/shard_map/pallas_call | solution.py:237
  235.6 4.5 %collective-permute-start.18 = (bf16[512,384]{1,0:T(8,128)(2,1)}, bf16[512,384]{1,0:T(8,128)(2,1)S(1)}, u32[]{:S(2)}, u32[]{:S(2)}) collective-permute-start(bf16[512,384]{1,0:T(8,128)(2,1)} %get-tuple-element.10), channel_id=1, source_target_pairs={{0,1},{1,0},{2,3},{3,2},{4,5},{5,4},{6,7},{7,6},{8,9},{9,8},{10,11... | collective-permute-start | bytes 1179656 | tf_op jit(solution)/shard_map/ppermute | solution.py:250
  240.1 1.5 collective-permute-done.18.received
  242.4 4.4 %shard_map.65 = bf16[144,384]{1,0:T(8,128)(2,1)} custom-call(bf16[8,4,512,128]{3,2,1,0:T(8,128)(2,1)} %get-tuple-element.9.held_in, bf16[8,3,512,128]{3,2,1,0:T(8,128)(2,1)} %all-gather.2.cloned.1.call-done.weights_in, bf16[512,384]{1,0:T(8,128)(2,1)} %copy-done.17), custom_call_target="tpu_custom_call" | custom-call | flops 452984832 | bytes 8388608 | tf_op jit(solution)/shard_map/pallas_call | solution.py:251
  246.8 1.9 collective-permute-start.19
  248.8 9.3 %shard_map.66 = (bf16[512,128]{1,0:T(8,128)(2,1)}, bf16[192,384]{1,0:T(8,128)(2,1)}) custom-call(s32[16]{0:T(128)} %reshape.15.ends, bf16[8,4,512,128]{3,2,1,0:T(8,128)(2,1)} %get-tuple-element.9.held_in, bf16[8,3,512,128]{3,2,1,0:T(8,128)(2,1)} %all-gather.2.cloned.1.call-done.weights_in, bf16[512,384]{1,0:T(8,128)(2,1)} %copy-done.17, ...), custom_call_target="tpu_custom_call" | custom-call | flops 3221225472 | bytes 8388608 | tf_op jit(solution)/shard_map/pallas_call | solution.py:269
  260.0 2.8 %shard_map.67 = bf16[512,128]{1,0:T(8,128)(2,1)} custom-call(s32[16]{0:T(128)S(1)} %copy-done.1, bf16[144,384]{1,0:T(8,128)(2,1)S(1)} %collective-permute-done.19.before, bf16[192,384]{1,0:T(8,128)(2,1)S(1)} %copy-done.5, s32[656,128]{1,0:T(8,128)S(1)} %copy-done, f32[7,384]{1,0:T(8,128)S(1)} %bitcast.25, f32[128,128]{1,0:T(8,128)S(1)} %copy-done.2, ...), custom_call_target="tpu_custom_call" | custom-call | flops 402653184 | bytes 1048576 | tf_op jit(solution)/shard_map/pallas_call | solution.py:279
  (65 shorter events, 6.1 us)
Async XLA Ops:
  6.5 235.1 %all-gather.2.cloned.1.call-start = ((), (), s32[]{:S(2)}) async-start(), calls=%async_computation | async-start | bytes 3538944 | tf_op jit(solution)/shard_map/all_gather | solution.py:209
  8.5 12.5 %collective-permute-start = (bf16[512,128]{1,0:T(8,128)(2,1)}, bf16[512,128]{1,0:T(8,128)(2,1)S(1)}, u32[]{:S(2)}, u32[]{:S(2)}) collective-permute-start(bf16[512,128]{1,0:T(8,128)(2,1)} %bitcast.31), channel_id=1, source_target_pairs={{0,16},{16,32},{32,48},{48,0},{64,80},{80,96},{96,112},{112,64},{1... | collective-permute-start | bytes 393224 | tf_op jit(solution)/shard_map/ppermute | solution.py:218
  12.5 8.6 %collective-permute-start.1 = (bf16[512,128]{1,0:T(8,128)(2,1)}, bf16[512,128]{1,0:T(8,128)(2,1)S(1)}, u32[]{:S(2)}, u32[]{:S(2)}) collective-permute-start(bf16[512,128]{1,0:T(8,128)(2,1)} %bitcast.32), channel_id=1, source_target_pairs={{0,32},{16,48},{32,0},{48,16},{64,96},{80,112},{96,64},{112,80},{1... | collective-permute-start | bytes 393224 | tf_op jit(solution)/shard_map/ppermute | solution.py:218
  16.8 6.2 %collective-permute-start.2 = (bf16[512,128]{1,0:T(8,128)(2,1)}, bf16[512,128]{1,0:T(8,128)(2,1)S(1)}, u32[]{:S(2)}, u32[]{:S(2)}) collective-permute-start(bf16[512,128]{1,0:T(8,128)(2,1)} %bitcast.33), channel_id=1, source_target_pairs={{0,48},{16,0},{32,16},{48,32},{64,112},{80,64},{96,80},{112,96},{1... | collective-permute-start | bytes 393224 | tf_op jit(solution)/shard_map/ppermute | solution.py:218
  23.1 82.6 %copy-start.7 = (bf16[4,512,128]{2,1,0:T(8,128)(2,1)}, bf16[4,512,128]{2,1,0:T(8,128)(2,1)S(1)}, u32[]{:S(2)}) copy-start(bf16[4,512,128]{2,1,0:T(8,128)(2,1)S(1)} %bitcast_dynamic-update-slice_fusion.refs_0_) | copy-start | bytes 1572868
  23.1 16.0 %collective-permute-start.3 = (bf16[4,512,128]{2,1,0:T(8,128)(2,1)S(1)}, bf16[4,512,128]{2,1,0:T(8,128)(2,1)S(1)}, u32[]{:S(2)}, u32[]{:S(2)}) collective-permute-start(bf16[4,512,128]{2,1,0:T(8,128)(2,1)S(1)} %bitcast_dynamic-update-slice_fusion.refs_0_), channel_id=1, source_target_pairs={{0,64},{16,80},{32,96},{48,112},{64,128},{80,144},{96,160},{112,17... | collective-permute-start | bytes 1572872 | tf_op jit(solution)/shard_map/ppermute | solution.py:183
  26.0 11.1 %collective-permute-start.10 = (bf16[3,512,128]{2,1,0:T(8,128)(2,1)S(1)}, bf16[3,512,128]{2,1,0:T(8,128)(2,1)S(1)}, u32[]{:S(2)}, u32[]{:S(2)}) collective-permute-start(bf16[3,512,128]{2,1,0:T(8,128)(2,1)S(1)} %bitcast.30), channel_id=1, source_target_pairs={{0,1},{1,0},{2,3},{3,2},{4,5},{5,4},{6,7},{7,6},{8,9},{9,8},{10,11... | collective-permute-start | bytes 1179656 | tf_op jit(solution)/shard_map/ppermute | solution.py:210
  32.2 32.2 %collective-permute-start.4 = (bf16[4,512,128]{2,1,0:T(8,128)(2,1)S(1)}, bf16[4,512,128]{2,1,0:T(8,128)(2,1)S(1)}, u32[]{:S(2)}, u32[]{:S(2)}) collective-permute-start(bf16[4,512,128]{2,1,0:T(8,128)(2,1)S(1)} %bitcast_dynamic-update-slice_fusion.refs_0_), channel_id=1, source_target_pairs={{0,448},{16,464},{32,480},{48,496},{64,0},{80,16},{96,32},{112,48}... | collective-permute-start | bytes 1572872 | tf_op jit(solution)/shard_map/ppermute | solution.py:187
  37.1 68.6 %copy-start.13 = (bf16[3,512,128]{2,1,0:T(8,128)(2,1)}, bf16[3,512,128]{2,1,0:T(8,128)(2,1)S(1)}, u32[]{:S(2)}) copy-start(bf16[3,512,128]{2,1,0:T(8,128)(2,1)S(1)} %collective-permute-done.10.refs_8_) | copy-start | bytes 1179652
  37.1 25.4 %collective-permute-start.11 = (bf16[3,512,128]{2,1,0:T(8,128)(2,1)S(1)}, bf16[3,512,128]{2,1,0:T(8,128)(2,1)S(1)}, u32[]{:S(2)}, u32[]{:S(2)}) collective-permute-start(bf16[3,512,128]{2,1,0:T(8,128)(2,1)S(1)} %collective-permute-done.10.refs_8_), channel_id=1, source_target_pairs={{0,2},{2,4},{4,6},{6,8},{8,10},{10,12},{12,14},{14,0},{1,3},{3,5},... | collective-permute-start | bytes 1179656 | tf_op jit(solution)/shard_map/ppermute | solution.py:183
  39.1 66.6 %copy-start.8 = (bf16[4,512,128]{2,1,0:T(8,128)(2,1)}, bf16[4,512,128]{2,1,0:T(8,128)(2,1)S(1)}, u32[]{:S(2)}) copy-start(bf16[4,512,128]{2,1,0:T(8,128)(2,1)S(1)} %collective-permute-done.3.refs_1_) | copy-start | bytes 1572868
  39.1 29.1 %collective-permute-start.5 = (bf16[4,512,128]{2,1,0:T(8,128)(2,1)S(1)}, bf16[4,512,128]{2,1,0:T(8,128)(2,1)S(1)}, u32[]{:S(2)}, u32[]{:S(2)}) collective-permute-start(bf16[4,512,128]{2,1,0:T(8,128)(2,1)S(1)} %collective-permute-done.3.refs_1_), channel_id=1, source_target_pairs={{0,64},{16,80},{32,96},{48,112},{64,128},{80,144},{96,160},{112,17... | collective-permute-start | bytes 1572872 | tf_op jit(solution)/shard_map/ppermute | solution.py:183
  41.0 29.1 %collective-permute-start.12 = (bf16[3,512,128]{2,1,0:T(8,128)(2,1)S(1)}, bf16[3,512,128]{2,1,0:T(8,128)(2,1)S(1)}, u32[]{:S(2)}, u32[]{:S(2)}) collective-permute-start(bf16[3,512,128]{2,1,0:T(8,128)(2,1)S(1)} %collective-permute-done.10.refs_8_), channel_id=1, source_target_pairs={{0,14},{2,0},{4,2},{6,4},{8,6},{10,8},{12,10},{14,12},{1,15},{3,1}... | collective-permute-start | bytes 1179656 | tf_op jit(solution)/shard_map/ppermute | solution.py:187
  62.5 23.6 %copy-start.14 = (bf16[3,512,128]{2,1,0:T(8,128)(2,1)}, bf16[3,512,128]{2,1,0:T(8,128)(2,1)S(1)}, u32[]{:S(2)}) copy-start(bf16[3,512,128]{2,1,0:T(8,128)(2,1)S(1)} %collective-permute-done.11.refs_9_) | copy-start | bytes 1179652
  62.5 16.8 %collective-permute-start.13 = (bf16[3,512,128]{2,1,0:T(8,128)(2,1)S(1)}, bf16[3,512,128]{2,1,0:T(8,128)(2,1)S(1)}, u32[]{:S(2)}, u32[]{:S(2)}) collective-permute-start(bf16[3,512,128]{2,1,0:T(8,128)(2,1)S(1)} %collective-permute-done.11.refs_9_), channel_id=1, source_target_pairs={{0,2},{2,4},{4,6},{6,8},{8,10},{10,12},{12,14},{14,0},{1,3},{3,5},... | collective-permute-start | bytes 1179656 | tf_op jit(solution)/shard_map/ppermute | solution.py:183
  64.5 41.2 %copy-start.9 = (bf16[4,512,128]{2,1,0:T(8,128)(2,1)}, bf16[4,512,128]{2,1,0:T(8,128)(2,1)S(1)}, u32[]{:S(2)}) copy-start(bf16[4,512,128]{2,1,0:T(8,128)(2,1)S(1)} %collective-permute-done.4.refs_2_) | copy-start | bytes 1572868
  64.5 17.3 %collective-permute-start.6 = (bf16[4,512,128]{2,1,0:T(8,128)(2,1)S(1)}, bf16[4,512,128]{2,1,0:T(8,128)(2,1)S(1)}, u32[]{:S(2)}, u32[]{:S(2)}) collective-permute-start(bf16[4,512,128]{2,1,0:T(8,128)(2,1)S(1)} %collective-permute-done.4.refs_2_), channel_id=1, source_target_pairs={{0,448},{16,464},{32,480},{48,496},{64,0},{80,16},{96,32},{112,48}... | collective-permute-start | bytes 1572872 | tf_op jit(solution)/shard_map/ppermute | solution.py:187
  68.2 37.5 %copy-start.10 = (bf16[4,512,128]{2,1,0:T(8,128)(2,1)}, bf16[4,512,128]{2,1,0:T(8,128)(2,1)S(1)}, u32[]{:S(2)}) copy-start(bf16[4,512,128]{2,1,0:T(8,128)(2,1)S(1)} %collective-permute-done.5.refs_3_) | copy-start | bytes 1572868
  68.2 17.9 %collective-permute-start.7 = (bf16[4,512,128]{2,1,0:T(8,128)(2,1)S(1)}, bf16[4,512,128]{2,1,0:T(8,128)(2,1)S(1)}, u32[]{:S(2)}, u32[]{:S(2)}) collective-permute-start(bf16[4,512,128]{2,1,0:T(8,128)(2,1)S(1)} %collective-permute-done.5.refs_3_), channel_id=1, source_target_pairs={{0,64},{16,80},{32,96},{48,112},{64,128},{80,144},{96,160},{112,17... | collective-permute-start | bytes 1572872 | tf_op jit(solution)/shard_map/ppermute | solution.py:183
  70.1 17.9 %copy-start.15 = (bf16[3,512,128]{2,1,0:T(8,128)(2,1)}, bf16[3,512,128]{2,1,0:T(8,128)(2,1)S(1)}, u32[]{:S(2)}) copy-start(bf16[3,512,128]{2,1,0:T(8,128)(2,1)S(1)} %collective-permute-done.12.refs_10_) | copy-start | bytes 1179652
  70.1 17.9 %collective-permute-start.14 = (bf16[3,512,128]{2,1,0:T(8,128)(2,1)S(1)}, bf16[3,512,128]{2,1,0:T(8,128)(2,1)}, u32[]{:S(2)}, u32[]{:S(2)}) collective-permute-start(bf16[3,512,128]{2,1,0:T(8,128)(2,1)S(1)} %collective-permute-done.12.refs_10_), channel_id=1, source_target_pairs={{0,14},{2,0},{4,2},{6,4},{8,6},{10,8},{12,10},{14,12},{1,15},{3,1}... | collective-permute-start | bytes 1179656 | tf_op jit(solution)/shard_map/ppermute | solution.py:187
  79.4 13.0 %collective-permute-start.15 = (bf16[3,512,128]{2,1,0:T(8,128)(2,1)S(1)}, bf16[3,512,128]{2,1,0:T(8,128)(2,1)}, u32[]{:S(2)}, u32[]{:S(2)}) collective-permute-start(bf16[3,512,128]{2,1,0:T(8,128)(2,1)S(1)} %collective-permute-done.13.refs_11_), channel_id=1, source_target_pairs={{0,2},{2,4},{4,6},{6,8},{8,10},{10,12},{12,14},{14,0},{1,3},{3,5},... | collective-permute-start | bytes 1179656 | tf_op jit(solution)/shard_map/ppermute | solution.py:183
  81.7 23.9 %copy-start.11 = (bf16[4,512,128]{2,1,0:T(8,128)(2,1)}, bf16[4,512,128]{2,1,0:T(8,128)(2,1)S(1)}, u32[]{:S(2)}) copy-start(bf16[4,512,128]{2,1,0:T(8,128)(2,1)S(1)} %collective-permute-done.6.refs_4_) | copy-start | bytes 1572868
  81.8 18.0 %collective-permute-start.8 = (bf16[4,512,128]{2,1,0:T(8,128)(2,1)S(1)}, bf16[4,512,128]{2,1,0:T(8,128)(2,1)}, u32[]{:S(2)}, u32[]{:S(2)}) collective-permute-start(bf16[4,512,128]{2,1,0:T(8,128)(2,1)S(1)} %collective-permute-done.6.refs_4_), channel_id=1, source_target_pairs={{0,448},{16,464},{32,480},{48,496},{64,0},{80,16},{96,32},{112,48}... | collective-permute-start | bytes 1572872 | tf_op jit(solution)/shard_map/ppermute | solution.py:187
  86.1 19.6 %copy-start.12 = (bf16[4,512,128]{2,1,0:T(8,128)(2,1)}, bf16[4,512,128]{2,1,0:T(8,128)(2,1)S(1)}, u32[]{:S(2)}) copy-start(bf16[4,512,128]{2,1,0:T(8,128)(2,1)S(1)} %collective-permute-done.7.refs_5_) | copy-start | bytes 1572868
  86.1 18.6 %collective-permute-start.9 = (bf16[4,512,128]{2,1,0:T(8,128)(2,1)S(1)}, bf16[4,512,128]{2,1,0:T(8,128)(2,1)}, u32[]{:S(2)}, u32[]{:S(2)}) collective-permute-start(bf16[4,512,128]{2,1,0:T(8,128)(2,1)S(1)} %collective-permute-done.7.refs_5_), channel_id=1, source_target_pairs={{0,64},{16,80},{32,96},{48,112},{64,128},{80,144},{96,160},{112,17... | collective-permute-start | bytes 1572872 | tf_op jit(solution)/shard_map/ppermute | solution.py:183
  88.1 11.6 %collective-permute-start.16 = (bf16[3,512,128]{2,1,0:T(8,128)(2,1)}, bf16[3,512,128]{2,1,0:T(8,128)(2,1)}, u32[]{:S(2)}, u32[]{:S(2)}) collective-permute-start(bf16[3,512,128]{2,1,0:T(8,128)(2,1)} %collective-permute-done.14.refs_12_), channel_id=1, source_target_pairs={{0,14},{2,0},{4,2},{6,4},{8,6},{10,8},{12,10},{14,12},{1,15},{3,1}... | collective-permute-start | bytes 1179656 | tf_op jit(solution)/shard_map/ppermute | solution.py:187
  92.4 12.3 %collective-permute-start.17 = (bf16[3,512,128]{2,1,0:T(8,128)(2,1)}, bf16[3,512,128]{2,1,0:T(8,128)(2,1)}, u32[]{:S(2)}, u32[]{:S(2)}) collective-permute-start(bf16[3,512,128]{2,1,0:T(8,128)(2,1)} %collective-permute-done.15.refs_13_), channel_id=1, source_target_pairs={{0,2},{2,4},{4,6},{6,8},{8,10},{10,12},{12,14},{14,0},{1,3},{3,5},... | collective-permute-start | bytes 1179656 | tf_op jit(solution)/shard_map/ppermute | solution.py:183
  235.6 6.1 %collective-permute-start.18 = (bf16[512,384]{1,0:T(8,128)(2,1)}, bf16[512,384]{1,0:T(8,128)(2,1)S(1)}, u32[]{:S(2)}, u32[]{:S(2)}) collective-permute-start(bf16[512,384]{1,0:T(8,128)(2,1)} %get-tuple-element.10), channel_id=1, source_target_pairs={{0,1},{1,0},{2,3},{3,2},{4,5},{5,4},{6,7},{7,6},{8,9},{9,8},{10,11... | collective-permute-start | bytes 1179656 | tf_op jit(solution)/shard_map/ppermute | solution.py:250
  246.8 11.3 %collective-permute-start.19 = (bf16[144,384]{1,0:T(8,128)(2,1)}, bf16[144,384]{1,0:T(8,128)(2,1)S(1)}, u32[]{:S(2)}, u32[]{:S(2)}) collective-permute-start(bf16[144,384]{1,0:T(8,128)(2,1)} %shard_map.65), channel_id=1, source_target_pairs={{0,2},{2,4},{4,6},{6,8},{8,10},{10,12},{12,14},{14,0},{1,3},{3,5},... | collective-permute-start | bytes 331784 | tf_op jit(solution)/shard_map/ppermute | solution.py:261
  248.8 9.4 %copy-start = (s32[656,128]{1,0:T(8,128)S(1)}, s32[656,128]{1,0:T(8,128)}, u32[]{:S(2)}) copy-start(s32[656,128]{1,0:T(8,128)} %broadcast_in_dim.26.ids) | copy-start | bytes 1007620
  248.8 9.4 %copy-start.1 = (s32[16]{0:T(128)S(1)}, s32[16]{0:T(128)}, u32[]{:S(2)}) copy-start(s32[16]{0:T(128)} %reshape.15.ends) | copy-start | bytes 196
  (7 other events, 39.5 us)
Sparse Core Ops, SparseCore 0:
  9.4 65.0 all-gather.1

commit v3 on v2

--- a/solution.py
+++ b/solution.py
@@ -44,60 +44,45 @@
     return copies
 
 
-def product(blocks, weights, ready):
-    total = None
-    for s in range(0, blocks.shape[0], CHUNK):
-        these = range(s, s + CHUNK)
-        for t in these:
-            ready(t)
-        left = [blocks[t, j] for t in these for j in range(blocks.shape[1])]
-        right = [wide(weights[t]) for t in these]
-        term = jnp.dot(
-            jnp.concatenate(left, 1), jnp.concatenate(right, 0), preferred_element_type=F32
-        )
-        total = term if total is None else total + term
-    return total
-
-
-def theirs_sum(count, tokens_from, weights_from, place, ids, ends, *refs):
-    token_refs, weight_refs = refs[:count], refs[count : 2 * count]
-    out, held_out, held, weights, sem, out_sem = refs[2 * count :]
-    pairs, kept = [], []
+def fetch(pairs, sem):
+    copies = [pltpu.make_async_copy(src, dst, sem.at[k]) for k, (src, dst) in enumerate(pairs)]
+    for copy in copies:
+        copy.start()
+    return copies
+
+
+def pack(count, offsets, place, ids, ends, *refs):
+    mine, other = refs[:count], refs[count : 2 * count]
+    held, sem = refs[2 * count :]
+    pairs = []
     for k in range(count):
-        slot = lax.rem(place[0] + tokens_from[k] + count, count)
-        pairs.append((token_refs[k], held.at[slot]))
-        kept.append((token_refs[k], held_out.at[slot]))
-        slot = lax.rem(place[1] + weights_from[k] + count, count)
-        pairs.append((weight_refs[k], weights.at[slot]))
-    copies = fetch(pairs, sem)
-    kept = fetch(kept, out_sem)
-    for copy in copies:
+        slot = lax.rem(place[0] + offsets[k] + count, count)
+        pairs.append((mine[k], held.at[slot, :, place[1]]))
+        pairs.append((other[k], held.at[slot, :, 1 - place[1]]))
+    for copy in fetch(pairs, sem):
         copy.wait()
-    out[...] = product(held, weights, lambda t: None).astype(out.dtype)
-    for copy in kept:
-        copy.wait()
-
-
-def mine_sum(held_in, weights_in, held, weights, sem):
-    count, rows = held.shape[0], held.shape[2]
-    first = held_in.shape[2] - rows
+
+
+def project(held_in, weights_in, raw, rim, total, held, weights, sem):
+    count = weights.shape[0]
     pairs = []
     for t in range(count):
-        pairs.append((held_in.at[t, :, first:, :], held.at[t]))
+        pairs.append((held_in.at[t], held.at[t]))
         pairs.append((weights_in.at[t], weights.at[t]))
     copies = fetch(pairs, sem)
-
-    def ready(t):
+    for t in range(count):
         copies[2 * t].wait()
         copies[2 * t + 1].wait()
-
-    return product(held, weights, ready)
-
-
-def rim_sum(held_in, weights_in, received, out, held, weights, sem):
-    first = received.shape[0] - out.shape[0]
-    total = mine_sum(held_in, weights_in, held, weights, sem)
-    out[...] = (total + received[first:, :].astype(F32)).astype(BF16)
+        left = [held[t, j, c] for j in range(held.shape[1]) for c in range(held.shape[2])]
+        term = jnp.dot(jnp.concatenate(left, 1), wide(weights[t]), preferred_element_type=F32)
+        if t == 0:
+            total[...] = term
+        elif t < count - 1:
+            total[...] += term
+        else:
+            rounded = (total[...] + term).astype(BF16)
+            raw[...] = rounded
+            rim[...] = rounded[rounded.shape[0] - rim.shape[0] :]
 
 
 def features(first, last, shift, raw, ids, taps, mixed, queries):
@@ -154,25 +139,19 @@
     lax.fori_loop(0, (last - first) // GROUP, group, 0)
 
 
-def main_part(
-    ends, held_in, weights_in, received, ids, short, taps, skip, out, top,
-    raw, mixed, queries, window, held, weights, sem,
-):
-    rows = held.shape[2]
-    summed = mine_sum(held_in, weights_in, held, weights, sem) + received[...].astype(F32)
-    rounded = summed.astype(BF16)
-    top[...] = rounded[: top.shape[0]]
-    raw[...] = rounded.astype(F32)
-    features(PAD, rows, 0, raw, ids, short, mixed, queries)
+def main_part(ends, raw, ids, short, taps, skip, out, wider, mixed, queries, window):
+    rows = raw.shape[0]
+    wider[...] = raw[...].astype(F32)
+    features(PAD, rows, 0, wider, ids, short, mixed, queries)
     long_filter(HEAD, rows, 0, ends, ids, mixed, queries, taps, skip, out, window)
 
 
-def head_part(ends, before, top, ids, short, taps, skip, given, out, raw, mixed, queries, window):
+def head_part(ends, before, raw, ids, short, taps, skip, given, out, wider, mixed, queries, window):
     rim = before.shape[0]
-    raw[:rim, :] = before[...].astype(F32)
-    raw[rim:, :] = top[...].astype(F32)
-    features(PAD - rim, 0, rim, raw, ids, short, mixed, queries)
-    features(0, HEAD, rim, raw, ids, short, mixed, queries)
+    wider[:rim, :] = before[...].astype(F32)
+    wider[rim:, :] = raw[:HEAD, :].astype(F32)
+    features(PAD - rim, 0, rim, wider, ids, short, mixed, queries)
+    features(0, HEAD, rim, wider, ids, short, mixed, queries)
     out[HEAD:, :] = given[HEAD:, :]
     long_filter(0, HEAD, rim, ends, ids, mixed, queries, taps, skip, out, window)
 
@@ -203,12 +182,7 @@
     along_z = lambda d: [(k, (k + d) % ctx) for k in range(ctx)]
     swap = [(0, 1), (1, 0)]
 
-    planes = jnp.transpose(w_in, (1, 0, 2)).reshape(3, xs, tp, width, width)
-    mine = lax.dynamic_index_in_dim(planes, c, 2, False).reshape(3, xs * width, width)
-    theirs = lax.dynamic_index_in_dim(planes, 1 - c, 2, False).reshape(3, xs * width, width)
-    mine_all = lax.all_gather(mine, "ctx", axis=0)
-    theirs = lax.ppermute(theirs, "tp", swap)
-    weights, weights_from = two_way(theirs, "ctx", ctx, along_z)
+    weights = lax.all_gather(jnp.transpose(w_in, (1, 0, 2)), "ctx", axis=0)
 
     own = tokens[0]
     block = jnp.zeros((xs,) + own.shape, BF16)
@@ -217,47 +191,45 @@
         hop = d if d <= xs // 2 else d - xs
         piece = lax.ppermute(own, "fsdp", along_x(hop))
         block = lax.dynamic_update_index_in_dim(block, piece, (x - hop) % xs, 0)
-    blocks, tokens_from = two_way(block, "fsdp", ys, along_y)
+    blocks, offsets = two_way(block, "fsdp", ys, along_y)
+    others = [lax.ppermute(b, "tp", swap) for b in blocks]
 
     padded = jnp.pad(genome_ids[0], (LEAD, 0), constant_values=-1)
     seen = lax.dynamic_slice_in_dim(padded, z * length, length + LEAD, 0)
     ids = jnp.broadcast_to(seen[:, None], (length + LEAD, 128))
     ends = jnp.stack([seen[LEAD::GROUP], seen[LEAD + GROUP - 1 :: GROUP]], 1).reshape(-1)
-    place = jnp.stack([y, z]).astype(jnp.int32)
+    place = jnp.stack([y, c]).astype(jnp.int32)
     short = short_taps.reshape(short_taps.shape[0], -1)
     bias = skip[None, :]
 
-    every = 2 * length * ctx * xs * width * 3 * width
-    block_shape = (ys, xs, length, width)
-    buffers = lambda rows: [
-        pltpu.VMEM((ys, xs, rows, width), BF16),
-        pltpu.VMEM((ctx,) + theirs.shape, BF16),
-        pltpu.SemaphoreType.DMA((2 * ctx,)),
-    ]
-    give, held = call(
-        functools.partial(theirs_sum, ctx, tokens_from, weights_from),
+    every = 2 * length * ctx * xs * tp * width * 3 * width
+    held = call(
+        functools.partial(pack, ys, offsets),
+        jax.ShapeDtypeStruct((ys, xs, tp, length, width), BF16),
+        [SMEM, ANY, ANY] + [ANY] * (2 * ys),
+        VMEM,
+        [pltpu.SemaphoreType.DMA((2 * ys,))],
+        nbytes=8 * MIB,
+        vmem=60,
+    )(place, ids, ends, *blocks, *others)
+    raw, rim = call(
+        project,
         (
             jax.ShapeDtypeStruct((length, 3 * width), BF16),
-            jax.ShapeDtypeStruct(block_shape, BF16),
+            jax.ShapeDtypeStruct((LEAD, 3 * width), BF16),
         ),
-        [SMEM, ANY, ANY] + [HBM] * (2 * ctx),
-        (VMEM, HBM),
-        buffers(length) + [pltpu.SemaphoreType.DMA((ctx,))],
+        [HBM, HBM],
+        (VMEM, VMEM),
+        [
+            pltpu.VMEM((length, 3 * width), F32),
+            pltpu.VMEM(held.shape, BF16),
+            pltpu.VMEM(weights.shape, BF16),
+            pltpu.SemaphoreType.DMA((2 * ctx,)),
+        ],
         flops=every,
-        nbytes=8 * MIB,
+        nbytes=16 * MIB,
         vmem=60,
-    )(place, ids, ends, *blocks, *weights)
-    received = lax.ppermute(give, "tp", swap)
-    rim = call(
-        rim_sum,
-        jax.ShapeDtypeStruct((LEAD, 3 * width), BF16),
-        [HBM, HBM, VMEM],
-        VMEM,
-        buffers(LEAD),
-        flops=every * LEAD // length,
-        nbytes=8 * MIB,
-        vmem=60,
-    )(held, mine_all, received)
+    )(held, weights)
     before = lax.ppermute(rim, "ctx", along_z(1))
     work = lambda rows: [
         pltpu.VMEM((rows, 3 * width), F32),
@@ -266,16 +238,15 @@
         pltpu.VMEM((reach + GROUP, width), F32),
     ]
     outline = jax.ShapeDtypeStruct((length, width), BF16)
-    part, top = call(
+    part = call(
         main_part,
-        (outline, jax.ShapeDtypeStruct((HEAD, 3 * width), BF16)),
-        [SMEM, HBM, HBM] + [VMEM] * 5,
-        (VMEM, VMEM),
-        work(length) + buffers(length),
-        flops=2 * every,
-        nbytes=8 * MIB,
-        vmem=60,
-    )(ends, held, mine_all, received, ids, short, mr_taps, bias)
+        outline,
+        [SMEM] + [VMEM] * 5,
+        VMEM,
+        work(length),
+        flops=every // 2,
+        nbytes=2 * MIB,
+    )(ends, raw, ids, short, mr_taps, bias)
     gated = call(
         head_part,
         outline,
@@ -284,7 +255,7 @@
         work(LEAD + HEAD),
         flops=every // 4,
         nbytes=1 * MIB,
-    )(ends, before, top, ids, short, mr_taps, bias, part)
+    )(ends, before, raw, ids, short, mr_taps, bias, part)
     return gated[None]
 
 

time: 271 us -> 131 us (0.48)
  Pallas kernels: 146 us -> 21.1 us
  starting transfers between devices: 72 us -> 64.3 us
  waiting for transfers between devices: 28.4 us -> 24 us
  local copies, waits for them, and re-layouts: 8.21 us -> 4.68 us
    pallas_call x3, Pallas kernels: 144 us -> 18.3 us  [the longest x1 7.48 us: body(): call(functools.partial(pack, ys, offsets), jax.ShapeDtypeStruct((ys, xs,...]
    ppermute x6 -> x3, starting transfers between devices: 31.2 us -> 13.5 us  [two_way(): down = lax.ppermute(down, axis, hop(-1))]
    ppermute x2 -> x8, starting transfers between devices: 10.8 us -> 23.7 us  [body(): others = [lax.ppermute(b, 'tp', swap) for b in blocks]]
    ppermute x8 -> x4, waiting for transfers between devices: 21.8 us -> 12.7 us  [two_way(): up = lax.ppermute(up, axis, hop(1))]
    ppermute x8 -> x4, starting transfers between devices: 16.8 us -> 10.3 us  [two_way(): up = lax.ppermute(up, axis, hop(1))]
    ppermute x1, waiting for transfers between devices: 0.01 us -> 5.77 us  [body(): before = lax.ppermute(rim, 'ctx', along_z(1))]
    ppermute x1, starting transfers between devices: 1.92 us -> 5.39 us  [body(): before = lax.ppermute(rim, 'ctx', along_z(1))]
  transfers between devices with their start and end apart: 21 -> 20, of which waited for: 6 -> 6; matrix products, arithmetic and copies ran while one was open for 2% -> 3% of each run, Pallas kernels for 52% -> 9%
where the time goes in v3:
time: 131 us; the launch traced here: 129 us
  starting transfers between devices  64.3 us (49%)
  waiting for transfers between devices  24 us (18%)
  Pallas kernels  21.1 us (16%)
  between operations  14 us (11%)
  local copies, waits for them, and re-layouts  4.68 us (4%)
    ppermute x8, starting transfers between devices, body(): others = [lax.ppermute(b, 'tp', swap) for b in blocks]  23.7 us
    ppermute x3, starting transfers between devices, two_way(): down = lax.ppermute(down, axis, hop(-1))  13.5 us
    ppermute x4, waiting for transfers between devices, two_way(): up = lax.ppermute(up, axis, hop(1))  12.7 us
    ppermute x3, starting transfers between devices, body(): piece = lax.ppermute(own, 'fsdp', along_x(hop))  11.4 us
    ppermute x4, starting transfers between devices, two_way(): up = lax.ppermute(up, axis, hop(1))  10.3 us
    pallas_call x1, Pallas kernels, body(): call(functools.partial(pack, ys, offsets), jax.ShapeDtypeStruct((ys, xs,...  7.48 us
    pallas_call x1, Pallas kernels, body(): call(project, (jax.ShapeDtypeStruct((length, 3 * width), BF16), jax.Shape...  7.32 us
    ppermute x1, waiting for transfers between devices, body(): before = lax.ppermute(rim, 'ctx', along_z(1))  5.77 us
  transfers between devices with their start and end apart: 20, of which 6 were waited for; matrix products, arithmetic and copies ran while one was open for 3% of the time, Pallas kernels for 9%

profile of v3, /device:TPU:1, one launch (start us, length us, event | category | flops | bytes accessed | tf_op | source)
XLA Modules:
  0.0 128.6 jit_solution(972728362771417385)
XLA Ops:
  7.3 4.0 %collective-permute-start = (bf16[512,128]{1,0:T(8,128)(2,1)}, bf16[512,128]{1,0:T(8,128)(2,1)S(1)}, u32[]{:S(2)}, u32[]{:S(2)}) collective-permute-start(bf16[512,128]{1,0:T(8,128)(2,1)} %bitcast.23), channel_id=1, source_target_pairs={{0,16},{16,32},{32,48},{48,0},{64,80},{80,96},{96,112},{112,64},{1... | collective-permute-start | bytes 393224 | tf_op jit(solution)/shard_map/ppermute | solution.py:192
  11.2 4.4 %collective-permute-start.1 = (bf16[512,128]{1,0:T(8,128)(2,1)}, bf16[512,128]{1,0:T(8,128)(2,1)S(1)}, u32[]{:S(2)}, u32[]{:S(2)}) collective-permute-start(bf16[512,128]{1,0:T(8,128)(2,1)} %bitcast.24), channel_id=1, source_target_pairs={{0,32},{16,48},{32,0},{48,16},{64,96},{80,112},{96,64},{112,80},{1... | collective-permute-start | bytes 393224 | tf_op jit(solution)/shard_map/ppermute | solution.py:192
  15.6 3.1 %collective-permute-start.2 = (bf16[512,128]{1,0:T(8,128)(2,1)}, bf16[512,128]{1,0:T(8,128)(2,1)S(1)}, u32[]{:S(2)}, u32[]{:S(2)}) collective-permute-start(bf16[512,128]{1,0:T(8,128)(2,1)} %bitcast.25), channel_id=1, source_target_pairs={{0,48},{16,0},{32,16},{48,32},{64,112},{80,64},{96,80},{112,96},{1... | collective-permute-start | bytes 393224 | tf_op jit(solution)/shard_map/ppermute | solution.py:192
  18.8 0.9 constant_dynamic-update-slice_fusion
  19.8 2.0 %collective-permute-done.2 = bf16[512,128]{1,0:T(8,128)(2,1)S(1)} collective-permute-done((bf16[512,128]{1,0:T(8,128)(2,1)}, bf16[512,128]{1,0:T(8,128)(2,1)S(1)}, u32[]{:S(2)}, u32[]{:S(2)}) %collective-permute-start.2) | collective-permute-done | bytes 131104 | tf_op jit(solution)/shard_map/ppermute | solution.py:192
  21.8 2.9 %collective-permute-start.3 = (bf16[4,512,128]{2,1,0:T(8,128)(2,1)S(1)}, bf16[4,512,128]{2,1,0:T(8,128)(2,1)S(1)}, u32[]{:S(2)}, u32[]{:S(2)}) collective-permute-start(bf16[4,512,128]{2,1,0:T(8,128)(2,1)S(1)} %bitcast_dynamic-update-slice_fusion.refs_0_), channel_id=1, source_target_pairs={{0,64},{16,80},{32,96},{48,112},{64,128},{80,144},{96,160},{112,17... | collective-permute-start | bytes 1572872 | tf_op jit(solution)/shard_map/ppermute | solution.py:162
  24.8 3.8 %collective-permute-start.4 = (bf16[4,512,128]{2,1,0:T(8,128)(2,1)S(1)}, bf16[4,512,128]{2,1,0:T(8,128)(2,1)S(1)}, u32[]{:S(2)}, u32[]{:S(2)}) collective-permute-start(bf16[4,512,128]{2,1,0:T(8,128)(2,1)S(1)} %bitcast_dynamic-update-slice_fusion.refs_0_), channel_id=1, source_target_pairs={{0,448},{16,464},{32,480},{48,496},{64,0},{80,16},{96,32},{112,48}... | collective-permute-start | bytes 1572872 | tf_op jit(solution)/shard_map/ppermute | solution.py:166
  28.6 4.6 %collective-permute-done.3.refs_1_ = bf16[4,512,128]{2,1,0:T(8,128)(2,1)S(1)} collective-permute-done((bf16[4,512,128]{2,1,0:T(8,128)(2,1)S(1)}, bf16[4,512,128]{2,1,0:T(8,128)(2,1)S(1)}, u32[]{:S(2)}, u32[]{:S(2)}) %collective-permute-start.3) | collective-permute-done | bytes 524320 | tf_op jit(solution)/shard_map/ppermute | solution.py:162
  33.2 3.6 %collective-permute-start.5 = (bf16[4,512,128]{2,1,0:T(8,128)(2,1)S(1)}, bf16[4,512,128]{2,1,0:T(8,128)(2,1)S(1)}, u32[]{:S(2)}, u32[]{:S(2)}) collective-permute-start(bf16[4,512,128]{2,1,0:T(8,128)(2,1)S(1)} %collective-permute-done.3.refs_1_), channel_id=1, source_target_pairs={{0,64},{16,80},{32,96},{48,112},{64,128},{80,144},{96,160},{112,17... | collective-permute-start | bytes 1572872 | tf_op jit(solution)/shard_map/ppermute | solution.py:162
  36.8 4.8 %collective-permute-start.6 = (bf16[4,512,128]{2,1,0:T(8,128)(2,1)S(1)}, bf16[4,512,128]{2,1,0:T(8,128)(2,1)S(1)}, u32[]{:S(2)}, u32[]{:S(2)}) collective-permute-start(bf16[4,512,128]{2,1,0:T(8,128)(2,1)S(1)} %collective-permute-done.4.refs_2_), channel_id=1, source_target_pairs={{0,448},{16,464},{32,480},{48,496},{64,0},{80,16},{96,32},{112,48}... | collective-permute-start | bytes 1572872 | tf_op jit(solution)/shard_map/ppermute | solution.py:166
  41.6 5.7 %collective-permute-done.5.refs_3_ = bf16[4,512,128]{2,1,0:T(8,128)(2,1)S(1)} collective-permute-done((bf16[4,512,128]{2,1,0:T(8,128)(2,1)S(1)}, bf16[4,512,128]{2,1,0:T(8,128)(2,1)S(1)}, u32[]{:S(2)}, u32[]{:S(2)}) %collective-permute-start.5) | collective-permute-done | bytes 524320 | tf_op jit(solution)/shard_map/ppermute | solution.py:162
  47.3 1.9 %collective-permute-start.7 = (bf16[4,512,128]{2,1,0:T(8,128)(2,1)S(1)}, bf16[4,512,128]{2,1,0:T(8,128)(2,1)S(1)}, u32[]{:S(2)}, u32[]{:S(2)}) collective-permute-start(bf16[4,512,128]{2,1,0:T(8,128)(2,1)S(1)} %collective-permute-done.5.refs_3_), channel_id=1, source_target_pairs={{0,64},{16,80},{32,96},{48,112},{64,128},{80,144},{96,160},{112,17... | collective-permute-start | bytes 1572872 | tf_op jit(solution)/shard_map/ppermute | solution.py:162
  49.2 7.1 %collective-permute-start.10 = (bf16[4,512,128]{2,1,0:T(8,128)(2,1)S(1)}, bf16[4,512,128]{2,1,0:T(8,128)(2,1)S(1)}, u32[]{:S(2)}, u32[]{:S(2)}) collective-permute-start(bf16[4,512,128]{2,1,0:T(8,128)(2,1)S(1)} %bitcast_dynamic-update-slice_fusion.refs_0_), channel_id=1, source_target_pairs={{0,1},{1,0},{2,3},{3,2},{4,5},{5,4},{6,7},{7,6},{8,9},{9,8},{10,11... | collective-permute-start | bytes 1572872 | tf_op jit(solution)/shard_map/ppermute | solution.py:195
  56.4 1.9 %collective-permute-start.11 = (bf16[4,512,128]{2,1,0:T(8,128)(2,1)S(1)}, bf16[4,512,128]{2,1,0:T(8,128)(2,1)S(1)}, u32[]{:S(2)}, u32[]{:S(2)}) collective-permute-start(bf16[4,512,128]{2,1,0:T(8,128)(2,1)S(1)} %collective-permute-done.3.refs_1_), channel_id=1, source_target_pairs={{0,1},{1,0},{2,3},{3,2},{4,5},{5,4},{6,7},{7,6},{8,9},{9,8},{10,11... | collective-permute-start | bytes 1572872 | tf_op jit(solution)/shard_map/ppermute | solution.py:195
  58.3 2.4 %collective-permute-start.12 = (bf16[4,512,128]{2,1,0:T(8,128)(2,1)S(1)}, bf16[4,512,128]{2,1,0:T(8,128)(2,1)S(1)}, u32[]{:S(2)}, u32[]{:S(2)}) collective-permute-start(bf16[4,512,128]{2,1,0:T(8,128)(2,1)S(1)} %collective-permute-done.4.refs_2_), channel_id=1, source_target_pairs={{0,1},{1,0},{2,3},{3,2},{4,5},{5,4},{6,7},{7,6},{8,9},{9,8},{10,11... | collective-permute-start | bytes 1572872 | tf_op jit(solution)/shard_map/ppermute | solution.py:195
  60.7 4.9 %collective-permute-start.8 = (bf16[4,512,128]{2,1,0:T(8,128)(2,1)S(1)}, bf16[4,512,128]{2,1,0:T(8,128)(2,1)}, u32[]{:S(2)}, u32[]{:S(2)}) collective-permute-start(bf16[4,512,128]{2,1,0:T(8,128)(2,1)S(1)} %collective-permute-done.6.refs_4_), channel_id=1, source_target_pairs={{0,448},{16,464},{32,480},{48,496},{64,0},{80,16},{96,32},{112,48}... | collective-permute-start | bytes 1572872 | tf_op jit(solution)/shard_map/ppermute | solution.py:166
  65.6 1.9 %collective-permute-start.9 = (bf16[4,512,128]{2,1,0:T(8,128)(2,1)S(1)}, bf16[4,512,128]{2,1,0:T(8,128)(2,1)}, u32[]{:S(2)}, u32[]{:S(2)}) collective-permute-start(bf16[4,512,128]{2,1,0:T(8,128)(2,1)S(1)} %collective-permute-done.7.refs_5_), channel_id=1, source_target_pairs={{0,64},{16,80},{32,96},{48,112},{64,128},{80,144},{96,160},{112,17... | collective-permute-start | bytes 1572872 | tf_op jit(solution)/shard_map/ppermute | solution.py:162
  67.6 2.2 %collective-permute-start.13 = (bf16[4,512,128]{2,1,0:T(8,128)(2,1)S(1)}, bf16[4,512,128]{2,1,0:T(8,128)(2,1)}, u32[]{:S(2)}, u32[]{:S(2)}) collective-permute-start(bf16[4,512,128]{2,1,0:T(8,128)(2,1)S(1)} %collective-permute-done.5.refs_3_), channel_id=1, source_target_pairs={{0,1},{1,0},{2,3},{3,2},{4,5},{5,4},{6,7},{7,6},{8,9},{9,8},{10,11... | collective-permute-start | bytes 1572872 | tf_op jit(solution)/shard_map/ppermute | solution.py:195
  69.8 2.1 %collective-permute-start.14 = (bf16[4,512,128]{2,1,0:T(8,128)(2,1)S(1)}, bf16[4,512,128]{2,1,0:T(8,128)(2,1)}, u32[]{:S(2)}, u32[]{:S(2)}) collective-permute-start(bf16[4,512,128]{2,1,0:T(8,128)(2,1)S(1)} %collective-permute-done.6.refs_4_), channel_id=1, source_target_pairs={{0,1},{1,0},{2,3},{3,2},{4,5},{5,4},{6,7},{7,6},{8,9},{9,8},{10,11... | collective-permute-start | bytes 1572872 | tf_op jit(solution)/shard_map/ppermute | solution.py:195
  71.9 2.2 %collective-permute-start.15 = (bf16[4,512,128]{2,1,0:T(8,128)(2,1)S(1)}, bf16[4,512,128]{2,1,0:T(8,128)(2,1)}, u32[]{:S(2)}, u32[]{:S(2)}) collective-permute-start(bf16[4,512,128]{2,1,0:T(8,128)(2,1)S(1)} %collective-permute-done.7.refs_5_), channel_id=1, source_target_pairs={{0,1},{1,0},{2,3},{3,2},{4,5},{5,4},{6,7},{7,6},{8,9},{9,8},{10,11... | collective-permute-start | bytes 1572872 | tf_op jit(solution)/shard_map/ppermute | solution.py:195
  74.2 2.8 %collective-permute-done.8.refs_6_ = bf16[4,512,128]{2,1,0:T(8,128)(2,1)} collective-permute-done((bf16[4,512,128]{2,1,0:T(8,128)(2,1)S(1)}, bf16[4,512,128]{2,1,0:T(8,128)(2,1)}, u32[]{:S(2)}, u32[]{:S(2)}) %collective-permute-start.8) | collective-permute-done | bytes 524320 | tf_op jit(solution)/shard_map/ppermute | solution.py:166
  76.9 2.7 %collective-permute-start.16 = (bf16[4,512,128]{2,1,0:T(8,128)(2,1)}, bf16[4,512,128]{2,1,0:T(8,128)(2,1)}, u32[]{:S(2)}, u32[]{:S(2)}) collective-permute-start(bf16[4,512,128]{2,1,0:T(8,128)(2,1)} %collective-permute-done.8.refs_6_), channel_id=1, source_target_pairs={{0,1},{1,0},{2,3},{3,2},{4,5},{5,4},{6,7},{7,6},{8,9},{9,8},{10,11... | collective-permute-start | bytes 1572872 | tf_op jit(solution)/shard_map/ppermute | solution.py:195
  79.6 2.4 %collective-permute-done.9.refs_7_ = bf16[4,512,128]{2,1,0:T(8,128)(2,1)} collective-permute-done((bf16[4,512,128]{2,1,0:T(8,128)(2,1)S(1)}, bf16[4,512,128]{2,1,0:T(8,128)(2,1)}, u32[]{:S(2)}, u32[]{:S(2)}) %collective-permute-start.9) | collective-permute-done | bytes 524320 | tf_op jit(solution)/shard_map/ppermute | solution.py:162
  82.1 3.0 %collective-permute-start.17 = (bf16[4,512,128]{2,1,0:T(8,128)(2,1)}, bf16[4,512,128]{2,1,0:T(8,128)(2,1)}, u32[]{:S(2)}, u32[]{:S(2)}) collective-permute-start(bf16[4,512,128]{2,1,0:T(8,128)(2,1)} %collective-permute-done.9.refs_7_), channel_id=1, source_target_pairs={{0,1},{1,0},{2,3},{3,2},{4,5},{5,4},{6,7},{7,6},{8,9},{9,8},{10,11... | collective-permute-start | bytes 1572872 | tf_op jit(solution)/shard_map/ppermute | solution.py:195
  87.4 0.9 broadcast_in_dim.26.ids
  88.3 7.5 %shard_map.64.held_in = bf16[8,4,2,512,128]{4,3,2,1,0:T(8,128)(2,1)} custom-call(s32[2]{0:T(128)} %pad_add_fusion.1.place, s32[656,128]{1,0:T(8,128)} %broadcast_in_dim.26.ids, s32[16]{0:T(128)} %reshape.7.ends, bf16[4,512,128]{2,1,0:T(8,128)(2,1)} %copy-done.6, bf16[4,512,128]{2,1,0:T(8,128)(2,1)} %copy-done.7, bf16[4,512,128]{2,1,0:T(8,128)(2,1)} %copy-done.8, ...), custom_call_target="tpu_custom_call" | custom-call | bytes 8388608 | tf_op jit(solution)/shard_map/pallas_call | solution.py:206
  95.9 7.3 %shard_map.65 = (bf16[512,384]{1,0:T(8,128)(2,1)}, bf16[144,384]{1,0:T(8,128)(2,1)}) custom-call(bf16[8,4,2,512,128]{4,3,2,1,0:T(8,128)(2,1)} %shard_map.64.held_in, bf16[8,3,1024,128]{3,2,1,0:T(8,128)(2,1)} %bitcast.21), custom_call_target="tpu_custom_call" | custom-call | flops 3221225472 | bytes 16777216 | tf_op jit(solution)/shard_map/pallas_call | solution.py:215
  103.2 5.4 %collective-permute-start.18 = (bf16[144,384]{1,0:T(8,128)(2,1)}, bf16[144,384]{1,0:T(8,128)(2,1)S(1)}, u32[]{:S(2)}, u32[]{:S(2)}) collective-permute-start(bf16[144,384]{1,0:T(8,128)(2,1)} %get-tuple-element.7), channel_id=1, source_target_pairs={{0,2},{2,4},{4,6},{6,8},{8,10},{10,12},{12,14},{14,0},{1,3},{3,5},... | collective-permute-start | bytes 331784 | tf_op jit(solution)/shard_map/ppermute | solution.py:233
  108.7 1.0 copy-done.2
  109.6 3.5 %shard_map.66.given = bf16[512,128]{1,0:T(8,128)(2,1)S(1)} custom-call(s32[16]{0:T(128)S(1)} %copy-done.1, bf16[512,384]{1,0:T(8,128)(2,1)S(1)} %copy-done.2, s32[656,128]{1,0:T(8,128)S(1)} %copy-done, f32[7,384]{1,0:T(8,128)S(1)} %bitcast.17, f32[128,128]{1,0:T(8,128)S(1)} %copy-done.3, f32[1,128]{1,0:T(1,128)S(1)} %bitcast.19), custom_call_target="tpu_custom_call" | custom-call | flops 1610612736 | bytes 2097152 | tf_op jit(solution)/shard_map/pallas_call | solution.py:241
  113.2 5.8 %collective-permute-done.18.before = bf16[144,384]{1,0:T(8,128)(2,1)S(1)} collective-permute-done((bf16[144,384]{1,0:T(8,128)(2,1)}, bf16[144,384]{1,0:T(8,128)(2,1)S(1)}, u32[]{:S(2)}, u32[]{:S(2)}) %collective-permute-start.18) | collective-permute-done | bytes 110624 | tf_op jit(solution)/shard_map/ppermute | solution.py:233
  119.0 2.8 %shard_map.67 = bf16[512,128]{1,0:T(8,128)(2,1)} custom-call(s32[16]{0:T(128)S(1)} %copy-done.1, bf16[144,384]{1,0:T(8,128)(2,1)S(1)} %collective-permute-done.18.before, bf16[512,384]{1,0:T(8,128)(2,1)S(1)} %copy-done.2, s32[656,128]{1,0:T(8,128)S(1)} %copy-done, f32[7,384]{1,0:T(8,128)S(1)} %bitcast.18, f32[128,128]{1,0:T(8,128)S(1)} %copy-done.3, ...), custom_call_target="tpu_custom_call" | custom-call | flops 805306368 | bytes 1048576 | tf_op jit(solution)/shard_map/pallas_call | solution.py:250
  (56 shorter events, 3.2 us)
Async XLA Ops:
  6.5 89.3 %all-gather.3.cloned.1.call-start = ((), (), s32[]{:S(2)}) async-start(), calls=%async_computation | async-start | bytes 7077888 | tf_op jit(solution)/shard_map/all_gather | solution.py:185
  7.3 12.5 %collective-permute-start = (bf16[512,128]{1,0:T(8,128)(2,1)}, bf16[512,128]{1,0:T(8,128)(2,1)S(1)}, u32[]{:S(2)}, u32[]{:S(2)}) collective-permute-start(bf16[512,128]{1,0:T(8,128)(2,1)} %bitcast.23), channel_id=1, source_target_pairs={{0,16},{16,32},{32,48},{48,0},{64,80},{80,96},{96,112},{112,64},{1... | collective-permute-start | bytes 393224 | tf_op jit(solution)/shard_map/ppermute | solution.py:192
  11.2 8.6 %collective-permute-start.1 = (bf16[512,128]{1,0:T(8,128)(2,1)}, bf16[512,128]{1,0:T(8,128)(2,1)S(1)}, u32[]{:S(2)}, u32[]{:S(2)}) collective-permute-start(bf16[512,128]{1,0:T(8,128)(2,1)} %bitcast.24), channel_id=1, source_target_pairs={{0,32},{16,48},{32,0},{48,16},{64,96},{80,112},{96,64},{112,80},{1... | collective-permute-start | bytes 393224 | tf_op jit(solution)/shard_map/ppermute | solution.py:192
  15.6 6.2 %collective-permute-start.2 = (bf16[512,128]{1,0:T(8,128)(2,1)}, bf16[512,128]{1,0:T(8,128)(2,1)S(1)}, u32[]{:S(2)}, u32[]{:S(2)}) collective-permute-start(bf16[512,128]{1,0:T(8,128)(2,1)} %bitcast.25), channel_id=1, source_target_pairs={{0,48},{16,0},{32,16},{48,32},{64,112},{80,64},{96,80},{112,96},{1... | collective-permute-start | bytes 393224 | tf_op jit(solution)/shard_map/ppermute | solution.py:192
  21.8 66.4 %copy-start.6 = (bf16[4,512,128]{2,1,0:T(8,128)(2,1)}, bf16[4,512,128]{2,1,0:T(8,128)(2,1)S(1)}, u32[]{:S(2)}) copy-start(bf16[4,512,128]{2,1,0:T(8,128)(2,1)S(1)} %bitcast_dynamic-update-slice_fusion.refs_0_) | copy-start | bytes 1572868
  21.8 11.4 %collective-permute-start.3 = (bf16[4,512,128]{2,1,0:T(8,128)(2,1)S(1)}, bf16[4,512,128]{2,1,0:T(8,128)(2,1)S(1)}, u32[]{:S(2)}, u32[]{:S(2)}) collective-permute-start(bf16[4,512,128]{2,1,0:T(8,128)(2,1)S(1)} %bitcast_dynamic-update-slice_fusion.refs_0_), channel_id=1, source_target_pairs={{0,64},{16,80},{32,96},{48,112},{64,128},{80,144},{96,160},{112,17... | collective-permute-start | bytes 1572872 | tf_op jit(solution)/shard_map/ppermute | solution.py:162
  24.8 12.0 %collective-permute-start.4 = (bf16[4,512,128]{2,1,0:T(8,128)(2,1)S(1)}, bf16[4,512,128]{2,1,0:T(8,128)(2,1)S(1)}, u32[]{:S(2)}, u32[]{:S(2)}) collective-permute-start(bf16[4,512,128]{2,1,0:T(8,128)(2,1)S(1)} %bitcast_dynamic-update-slice_fusion.refs_0_), channel_id=1, source_target_pairs={{0,448},{16,464},{32,480},{48,496},{64,0},{80,16},{96,32},{112,48}... | collective-permute-start | bytes 1572872 | tf_op jit(solution)/shard_map/ppermute | solution.py:166
  33.2 55.1 %copy-start.7 = (bf16[4,512,128]{2,1,0:T(8,128)(2,1)}, bf16[4,512,128]{2,1,0:T(8,128)(2,1)S(1)}, u32[]{:S(2)}) copy-start(bf16[4,512,128]{2,1,0:T(8,128)(2,1)S(1)} %collective-permute-done.3.refs_1_) | copy-start | bytes 1572868
  33.2 14.1 %collective-permute-start.5 = (bf16[4,512,128]{2,1,0:T(8,128)(2,1)S(1)}, bf16[4,512,128]{2,1,0:T(8,128)(2,1)S(1)}, u32[]{:S(2)}, u32[]{:S(2)}) collective-permute-start(bf16[4,512,128]{2,1,0:T(8,128)(2,1)S(1)} %collective-permute-done.3.refs_1_), channel_id=1, source_target_pairs={{0,64},{16,80},{32,96},{48,112},{64,128},{80,144},{96,160},{112,17... | collective-permute-start | bytes 1572872 | tf_op jit(solution)/shard_map/ppermute | solution.py:162
  36.8 51.5 %copy-start.8 = (bf16[4,512,128]{2,1,0:T(8,128)(2,1)}, bf16[4,512,128]{2,1,0:T(8,128)(2,1)S(1)}, u32[]{:S(2)}) copy-start(bf16[4,512,128]{2,1,0:T(8,128)(2,1)S(1)} %collective-permute-done.4.refs_2_) | copy-start | bytes 1572868
  36.8 23.9 %collective-permute-start.6 = (bf16[4,512,128]{2,1,0:T(8,128)(2,1)S(1)}, bf16[4,512,128]{2,1,0:T(8,128)(2,1)S(1)}, u32[]{:S(2)}, u32[]{:S(2)}) collective-permute-start(bf16[4,512,128]{2,1,0:T(8,128)(2,1)S(1)} %collective-permute-done.4.refs_2_), channel_id=1, source_target_pairs={{0,448},{16,464},{32,480},{48,496},{64,0},{80,16},{96,32},{112,48}... | collective-permute-start | bytes 1572872 | tf_op jit(solution)/shard_map/ppermute | solution.py:166
  47.3 41.0 %copy-start.9 = (bf16[4,512,128]{2,1,0:T(8,128)(2,1)}, bf16[4,512,128]{2,1,0:T(8,128)(2,1)S(1)}, u32[]{:S(2)}) copy-start(bf16[4,512,128]{2,1,0:T(8,128)(2,1)S(1)} %collective-permute-done.5.refs_3_) | copy-start | bytes 1572868
  47.3 18.3 %collective-permute-start.7 = (bf16[4,512,128]{2,1,0:T(8,128)(2,1)S(1)}, bf16[4,512,128]{2,1,0:T(8,128)(2,1)S(1)}, u32[]{:S(2)}, u32[]{:S(2)}) collective-permute-start(bf16[4,512,128]{2,1,0:T(8,128)(2,1)S(1)} %collective-permute-done.5.refs_3_), channel_id=1, source_target_pairs={{0,64},{16,80},{32,96},{48,112},{64,128},{80,144},{96,160},{112,17... | collective-permute-start | bytes 1572872 | tf_op jit(solution)/shard_map/ppermute | solution.py:162
  49.2 18.3 %collective-permute-start.10 = (bf16[4,512,128]{2,1,0:T(8,128)(2,1)S(1)}, bf16[4,512,128]{2,1,0:T(8,128)(2,1)S(1)}, u32[]{:S(2)}, u32[]{:S(2)}) collective-permute-start(bf16[4,512,128]{2,1,0:T(8,128)(2,1)S(1)} %bitcast_dynamic-update-slice_fusion.refs_0_), channel_id=1, source_target_pairs={{0,1},{1,0},{2,3},{3,2},{4,5},{5,4},{6,7},{7,6},{8,9},{9,8},{10,11... | collective-permute-start | bytes 1572872 | tf_op jit(solution)/shard_map/ppermute | solution.py:195
  56.4 13.4 %collective-permute-start.11 = (bf16[4,512,128]{2,1,0:T(8,128)(2,1)S(1)}, bf16[4,512,128]{2,1,0:T(8,128)(2,1)S(1)}, u32[]{:S(2)}, u32[]{:S(2)}) collective-permute-start(bf16[4,512,128]{2,1,0:T(8,128)(2,1)S(1)} %collective-permute-done.3.refs_1_), channel_id=1, source_target_pairs={{0,1},{1,0},{2,3},{3,2},{4,5},{5,4},{6,7},{7,6},{8,9},{9,8},{10,11... | collective-permute-start | bytes 1572872 | tf_op jit(solution)/shard_map/ppermute | solution.py:195
  58.3 13.6 %collective-permute-start.12 = (bf16[4,512,128]{2,1,0:T(8,128)(2,1)S(1)}, bf16[4,512,128]{2,1,0:T(8,128)(2,1)S(1)}, u32[]{:S(2)}, u32[]{:S(2)}) collective-permute-start(bf16[4,512,128]{2,1,0:T(8,128)(2,1)S(1)} %collective-permute-done.4.refs_2_), channel_id=1, source_target_pairs={{0,1},{1,0},{2,3},{3,2},{4,5},{5,4},{6,7},{7,6},{8,9},{9,8},{10,11... | collective-permute-start | bytes 1572872 | tf_op jit(solution)/shard_map/ppermute | solution.py:195
  60.7 27.6 %copy-start.10 = (bf16[4,512,128]{2,1,0:T(8,128)(2,1)}, bf16[4,512,128]{2,1,0:T(8,128)(2,1)S(1)}, u32[]{:S(2)}) copy-start(bf16[4,512,128]{2,1,0:T(8,128)(2,1)S(1)} %collective-permute-done.6.refs_4_) | copy-start | bytes 1572868
  60.7 16.2 %collective-permute-start.8 = (bf16[4,512,128]{2,1,0:T(8,128)(2,1)S(1)}, bf16[4,512,128]{2,1,0:T(8,128)(2,1)}, u32[]{:S(2)}, u32[]{:S(2)}) collective-permute-start(bf16[4,512,128]{2,1,0:T(8,128)(2,1)S(1)} %collective-permute-done.6.refs_4_), channel_id=1, source_target_pairs={{0,448},{16,464},{32,480},{48,496},{64,0},{80,16},{96,32},{112,48}... | collective-permute-start | bytes 1572872 | tf_op jit(solution)/shard_map/ppermute | solution.py:166
  65.6 22.7 %copy-start.11 = (bf16[4,512,128]{2,1,0:T(8,128)(2,1)}, bf16[4,512,128]{2,1,0:T(8,128)(2,1)S(1)}, u32[]{:S(2)}) copy-start(bf16[4,512,128]{2,1,0:T(8,128)(2,1)S(1)} %collective-permute-done.7.refs_5_) | copy-start | bytes 1572868
  65.6 16.4 %collective-permute-start.9 = (bf16[4,512,128]{2,1,0:T(8,128)(2,1)S(1)}, bf16[4,512,128]{2,1,0:T(8,128)(2,1)}, u32[]{:S(2)}, u32[]{:S(2)}) collective-permute-start(bf16[4,512,128]{2,1,0:T(8,128)(2,1)S(1)} %collective-permute-done.7.refs_5_), channel_id=1, source_target_pairs={{0,64},{16,80},{32,96},{48,112},{64,128},{80,144},{96,160},{112,17... | collective-permute-start | bytes 1572872 | tf_op jit(solution)/shard_map/ppermute | solution.py:162
  67.5 14.5 %copy-start.12 = (bf16[4,512,128]{2,1,0:T(8,128)(2,1)}, bf16[4,512,128]{2,1,0:T(8,128)(2,1)S(1)}, u32[]{:S(2)}) copy-start(bf16[4,512,128]{2,1,0:T(8,128)(2,1)S(1)} %collective-permute-done.10.refs_8_) | copy-start | bytes 1572868
  67.6 19.8 %collective-permute-start.13 = (bf16[4,512,128]{2,1,0:T(8,128)(2,1)S(1)}, bf16[4,512,128]{2,1,0:T(8,128)(2,1)}, u32[]{:S(2)}, u32[]{:S(2)}) collective-permute-start(bf16[4,512,128]{2,1,0:T(8,128)(2,1)S(1)} %collective-permute-done.5.refs_3_), channel_id=1, source_target_pairs={{0,1},{1,0},{2,3},{3,2},{4,5},{5,4},{6,7},{7,6},{8,9},{9,8},{10,11... | collective-permute-start | bytes 1572872 | tf_op jit(solution)/shard_map/ppermute | solution.py:195
  69.8 17.6 %collective-permute-start.14 = (bf16[4,512,128]{2,1,0:T(8,128)(2,1)S(1)}, bf16[4,512,128]{2,1,0:T(8,128)(2,1)}, u32[]{:S(2)}, u32[]{:S(2)}) collective-permute-start(bf16[4,512,128]{2,1,0:T(8,128)(2,1)S(1)} %collective-permute-done.6.refs_4_), channel_id=1, source_target_pairs={{0,1},{1,0},{2,3},{3,2},{4,5},{5,4},{6,7},{7,6},{8,9},{9,8},{10,11... | collective-permute-start | bytes 1572872 | tf_op jit(solution)/shard_map/ppermute | solution.py:195
  71.9 15.4 %collective-permute-start.15 = (bf16[4,512,128]{2,1,0:T(8,128)(2,1)S(1)}, bf16[4,512,128]{2,1,0:T(8,128)(2,1)}, u32[]{:S(2)}, u32[]{:S(2)}) collective-permute-start(bf16[4,512,128]{2,1,0:T(8,128)(2,1)S(1)} %collective-permute-done.7.refs_5_), channel_id=1, source_target_pairs={{0,1},{1,0},{2,3},{3,2},{4,5},{5,4},{6,7},{7,6},{8,9},{9,8},{10,11... | collective-permute-start | bytes 1572872 | tf_op jit(solution)/shard_map/ppermute | solution.py:195
  76.9 10.5 %collective-permute-start.16 = (bf16[4,512,128]{2,1,0:T(8,128)(2,1)}, bf16[4,512,128]{2,1,0:T(8,128)(2,1)}, u32[]{:S(2)}, u32[]{:S(2)}) collective-permute-start(bf16[4,512,128]{2,1,0:T(8,128)(2,1)} %collective-permute-done.8.refs_6_), channel_id=1, source_target_pairs={{0,1},{1,0},{2,3},{3,2},{4,5},{5,4},{6,7},{7,6},{8,9},{9,8},{10,11... | collective-permute-start | bytes 1572872 | tf_op jit(solution)/shard_map/ppermute | solution.py:195
  82.1 5.3 %collective-permute-start.17 = (bf16[4,512,128]{2,1,0:T(8,128)(2,1)}, bf16[4,512,128]{2,1,0:T(8,128)(2,1)}, u32[]{:S(2)}, u32[]{:S(2)}) collective-permute-start(bf16[4,512,128]{2,1,0:T(8,128)(2,1)} %collective-permute-done.9.refs_7_), channel_id=1, source_target_pairs={{0,1},{1,0},{2,3},{3,2},{4,5},{5,4},{6,7},{7,6},{8,9},{9,8},{10,11... | collective-permute-start | bytes 1572872 | tf_op jit(solution)/shard_map/ppermute | solution.py:195
  95.8 12.8 %copy-start = (s32[656,128]{1,0:T(8,128)S(1)}, s32[656,128]{1,0:T(8,128)}, u32[]{:S(2)}) copy-start(s32[656,128]{1,0:T(8,128)} %broadcast_in_dim.26.ids) | copy-start | bytes 1007620
  95.8 12.8 %copy-start.1 = (s32[16]{0:T(128)S(1)}, s32[16]{0:T(128)}, u32[]{:S(2)}) copy-start(s32[16]{0:T(128)} %reshape.7.ends) | copy-start | bytes 196
  95.8 12.8 %copy-start.3 = (f32[128,128]{1,0:T(8,128)S(1)}, f32[128,128]{1,0:T(8,128)}, u32[]{:S(2)}) copy-start(f32[128,128]{1,0:T(8,128)} %taps.3) | copy-start | bytes 196612
  95.8 12.8 %copy-start.4 = (f32[7,3,128]{2,0,1:T(8,128)S(1)}, f32[7,3,128]{2,0,1:T(8,128)}, u32[]{:S(2)}) copy-start(f32[7,3,128]{2,0,1:T(8,128)} %param.8) | copy-start | bytes 32260
  95.8 12.8 %copy-start.5 = (f32[128]{0:T(128)S(1)}, f32[128]{0:T(128)}, u32[]{:S(2)}) copy-start(f32[128]{0:T(128)} %param.10) | copy-start | bytes 1540
  103.2 15.8 %collective-permute-start.18 = (bf16[144,384]{1,0:T(8,128)(2,1)}, bf16[144,384]{1,0:T(8,128)(2,1)S(1)}, u32[]{:S(2)}, u32[]{:S(2)}) collective-permute-start(bf16[144,384]{1,0:T(8,128)(2,1)} %get-tuple-element.7), channel_id=1, source_target_pairs={{0,2},{2,4},{4,6},{6,8},{8,10},{10,12},{12,14},{14,0},{1,3},{3,5},... | collective-permute-start | bytes 331784 | tf_op jit(solution)/shard_map/ppermute | solution.py:233
  (3 other events, 23.4 us)
Sparse Core Ops, SparseCore 0:
  9.4 83.3 all-gather.2

commit v4 on v3

--- a/solution.py
+++ b/solution.py
@@ -11,7 +11,8 @@
 LEAD = 128 + PAD
 HEAD = 192
 STEP = 64
-CHUNK = 2
+AHEAD = 3
+VMEM_DOT = 52
 GROUP = 64
 BF16, F32 = jnp.bfloat16, jnp.float32
 VMEM = pl.BlockSpec(memory_space=pltpu.VMEM)
@@ -37,52 +38,50 @@
     return jnp.concatenate([planes[j] for j in range(planes.shape[0])], 1)
 
 
-def fetch(pairs, sem):
-    copies = [pltpu.make_async_copy(src, dst, sem.at[k]) for k, (src, dst) in enumerate(pairs)]
-    for copy in copies:
-        copy.start()
-    return copies
-
-
-def fetch(pairs, sem):
-    copies = [pltpu.make_async_copy(src, dst, sem.at[k]) for k, (src, dst) in enumerate(pairs)]
-    for copy in copies:
-        copy.start()
-    return copies
-
-
-def pack(count, offsets, place, ids, ends, *refs):
+def project(count, offsets, place, *refs):
     mine, other = refs[:count], refs[count : 2 * count]
-    held, sem = refs[2 * count :]
-    pairs = []
+    weights_in, raw, rim, total, held, weights, sem = refs[2 * count :]
+    core = place[1]
+
+    def copies(k):
+        slot = lax.rem(place[0] + offsets[k] + count, count)
+        return [
+            pltpu.make_async_copy(mine[k], held.at[k, :, core], sem.at[3 * k]),
+            pltpu.make_async_copy(other[k], held.at[k, :, 1 - core], sem.at[3 * k + 1]),
+            pltpu.make_async_copy(weights_in.at[slot], weights.at[k], sem.at[3 * k + 2]),
+        ]
+
+    for k in range(min(AHEAD, count)):
+        for copy in copies(k):
+            copy.start()
     for k in range(count):
-        slot = lax.rem(place[0] + offsets[k] + count, count)
-        pairs.append((mine[k], held.at[slot, :, place[1]]))
-        pairs.append((other[k], held.at[slot, :, 1 - place[1]]))
-    for copy in fetch(pairs, sem):
-        copy.wait()
-
-
-def project(held_in, weights_in, raw, rim, total, held, weights, sem):
-    count = weights.shape[0]
-    pairs = []
-    for t in range(count):
-        pairs.append((held_in.at[t], held.at[t]))
-        pairs.append((weights_in.at[t], weights.at[t]))
-    copies = fetch(pairs, sem)
-    for t in range(count):
-        copies[2 * t].wait()
-        copies[2 * t + 1].wait()
-        left = [held[t, j, c] for j in range(held.shape[1]) for c in range(held.shape[2])]
-        term = jnp.dot(jnp.concatenate(left, 1), wide(weights[t]), preferred_element_type=F32)
-        if t == 0:
+        if k + AHEAD < count:
+            for copy in copies(k + AHEAD):
+                copy.start()
+        for copy in copies(k):
+            copy.wait()
+        left = [held[k, j, c] for j in range(held.shape[1]) for c in range(held.shape[2])]
+        term = jnp.dot(jnp.concatenate(left, 1), wide(weights[k]), preferred_element_type=F32)
+        if k == 0:
             total[...] = term
-        elif t < count - 1:
+        elif k < count - 1:
             total[...] += term
         else:
             rounded = (total[...] + term).astype(BF16)
             raw[...] = rounded
             rim[...] = rounded[rounded.shape[0] - rim.shape[0] :]
+
+
+def genome(place, row):
+    total = (row >= place[3]).astype(jnp.int32)
+    for g in (4, 5):
+        total = total + (row >= place[g]).astype(jnp.int32)
+    return jnp.where(row < 0, -1, total)
+
+
+def fill(place, length, ids):
+    row = lax.broadcasted_iota(jnp.int32, ids.shape, 0) + (place[2] * length - LEAD)
+    ids[...] = genome(place, row)
 
 
 def features(first, last, shift, raw, ids, taps, mixed, queries):
@@ -106,14 +105,14 @@
         mixed[base + shift : base + shift + step, :] = (sums[1] * sums[2]).astype(BF16).astype(F32)
 
 
-def long_filter(first, last, shift, ends, ids, mixed, queries, taps, skip, out, window):
+def long_filter(first, last, shift, place, ids, mixed, queries, taps, skip, out, window):
     reach = taps.shape[0]
 
     def group(i, _):
         base = pl.multiple_of(first + i * GROUP, GROUP)
         here = ids[pl.ds(base + LEAD, GROUP), :]
 
-        def genome(g, total):
+        def one(g, total):
             for k in range((reach + GROUP) // GROUP):
                 spot = pl.ds(base + k * GROUP + LEAD - reach, GROUP)
                 source = pl.ds(pl.multiple_of(base + k * GROUP + shift - reach, PAD), GROUP)
@@ -129,8 +128,9 @@
                     sums = sums + held[start : start + GROUP] * weight
             return jnp.where(here == g, sums, total)
 
-        low, high = ends[2 * (base // GROUP)], ends[2 * (base // GROUP) + 1]
-        total = lax.fori_loop(low, high + 1, genome, jnp.zeros((GROUP, 128), F32))
+        row = place[2] * out.shape[0] + base
+        low, high = genome(place, row), genome(place, row + GROUP - 1)
+        total = lax.fori_loop(low, high + 1, one, jnp.zeros((GROUP, 128), F32))
         bias = skip[...] * mixed[pl.ds(pl.multiple_of(base + shift, PAD), GROUP), :]
         gated = queries[pl.ds(base, GROUP), :] * (total + bias)
         out[pl.ds(base, GROUP), :] = gated.astype(out.dtype)
@@ -139,21 +139,25 @@
     lax.fori_loop(0, (last - first) // GROUP, group, 0)
 
 
-def main_part(ends, raw, ids, short, taps, skip, out, wider, mixed, queries, window):
+def main_part(place, raw, short, taps, skip, out, wider, mixed, queries, window, ids):
     rows = raw.shape[0]
+    fill(place, rows, ids)
     wider[...] = raw[...].astype(F32)
     features(PAD, rows, 0, wider, ids, short, mixed, queries)
-    long_filter(HEAD, rows, 0, ends, ids, mixed, queries, taps, skip, out, window)
-
-
-def head_part(ends, before, raw, ids, short, taps, skip, given, out, wider, mixed, queries, window):
+    long_filter(HEAD, rows, 0, place, ids, mixed, queries, taps, skip, out, window)
+
+
+def head_part(
+    place, before, raw, short, taps, skip, given, out, wider, mixed, queries, window, ids
+):
     rim = before.shape[0]
+    fill(place, out.shape[0], ids)
     wider[:rim, :] = before[...].astype(F32)
     wider[rim:, :] = raw[:HEAD, :].astype(F32)
     features(PAD - rim, 0, rim, wider, ids, short, mixed, queries)
     features(0, HEAD, rim, wider, ids, short, mixed, queries)
     out[HEAD:, :] = given[HEAD:, :]
-    long_filter(0, HEAD, rim, ends, ids, mixed, queries, taps, skip, out, window)
+    long_filter(0, HEAD, rim, place, ids, mixed, queries, taps, skip, out, window)
 
 
 def two_way(block, axis, count, hop):
@@ -179,7 +183,6 @@
 
     along_x = lambda d: [(j * xs + i, j * xs + (i + d) % xs) for j in range(ys) for i in range(xs)]
     along_y = lambda d: [(j * xs + i, (j + d) % ys * xs + i) for j in range(ys) for i in range(xs)]
-    along_z = lambda d: [(k, (k + d) % ctx) for k in range(ctx)]
     swap = [(0, 1), (1, 0)]
 
     weights = lax.all_gather(jnp.transpose(w_in, (1, 0, 2)), "ctx", axis=0)
@@ -194,68 +197,57 @@
     blocks, offsets = two_way(block, "fsdp", ys, along_y)
     others = [lax.ppermute(b, "tp", swap) for b in blocks]
 
-    padded = jnp.pad(genome_ids[0], (LEAD, 0), constant_values=-1)
-    seen = lax.dynamic_slice_in_dim(padded, z * length, length + LEAD, 0)
-    ids = jnp.broadcast_to(seen[:, None], (length + LEAD, 128))
-    ends = jnp.stack([seen[LEAD::GROUP], seen[LEAD + GROUP - 1 :: GROUP]], 1).reshape(-1)
-    place = jnp.stack([y, c]).astype(jnp.int32)
+    starts = jnp.sum(genome_ids[0][None, :] < jnp.arange(1, 4)[:, None], axis=1, dtype=jnp.int32)
+    place = jnp.concatenate([jnp.stack([y, c, z]).astype(jnp.int32), starts])
     short = short_taps.reshape(short_taps.shape[0], -1)
     bias = skip[None, :]
 
     every = 2 * length * ctx * xs * tp * width * 3 * width
-    held = call(
-        functools.partial(pack, ys, offsets),
-        jax.ShapeDtypeStruct((ys, xs, tp, length, width), BF16),
-        [SMEM, ANY, ANY] + [ANY] * (2 * ys),
-        VMEM,
-        [pltpu.SemaphoreType.DMA((2 * ys,))],
-        nbytes=8 * MIB,
-        vmem=60,
-    )(place, ids, ends, *blocks, *others)
     raw, rim = call(
-        project,
+        functools.partial(project, ys, offsets),
         (
             jax.ShapeDtypeStruct((length, 3 * width), BF16),
             jax.ShapeDtypeStruct((LEAD, 3 * width), BF16),
         ),
-        [HBM, HBM],
+        [SMEM] + [HBM] * (2 * ys + 1),
         (VMEM, VMEM),
         [
             pltpu.VMEM((length, 3 * width), F32),
-            pltpu.VMEM(held.shape, BF16),
+            pltpu.VMEM((ys, xs, tp, length, width), BF16),
             pltpu.VMEM(weights.shape, BF16),
-            pltpu.SemaphoreType.DMA((2 * ctx,)),
+            pltpu.SemaphoreType.DMA((3 * ctx,)),
         ],
         flops=every,
         nbytes=16 * MIB,
-        vmem=60,
-    )(held, weights)
-    before = lax.ppermute(rim, "ctx", along_z(1))
+        vmem=VMEM_DOT,
+    )(place, *blocks, *others, weights)
+    before = lax.ppermute(rim, "ctx", [(k, k + 1) for k in range(ctx - 1)])
     work = lambda rows: [
         pltpu.VMEM((rows, 3 * width), F32),
         pltpu.VMEM((rows, width), F32),
         pltpu.VMEM((length, width), F32),
         pltpu.VMEM((reach + GROUP, width), F32),
+        pltpu.VMEM((LEAD + length, width), jnp.int32),
     ]
     outline = jax.ShapeDtypeStruct((length, width), BF16)
     part = call(
         main_part,
         outline,
-        [SMEM] + [VMEM] * 5,
+        [SMEM] + [VMEM] * 4,
         VMEM,
         work(length),
         flops=every // 2,
         nbytes=2 * MIB,
-    )(ends, raw, ids, short, mr_taps, bias)
+    )(place, raw, short, mr_taps, bias)
     gated = call(
         head_part,
         outline,
-        [SMEM] + [VMEM] * 7,
+        [SMEM] + [VMEM] * 6,
         VMEM,
         work(LEAD + HEAD),
         flops=every // 4,
         nbytes=1 * MIB,
-    )(ends, before, raw, ids, short, mr_taps, bias, part)
+    )(place, before, raw, short, mr_taps, bias, part)
     return gated[None]
 
 

time: 131 us -> 116 us (0.89); the launches traced: 129 us -> 115 us
  Pallas kernels: 21.1 us -> 13.9 us
  local copies, waits for them, and re-layouts: 4.68 us -> 1.11 us
  starting transfers between devices: 64.3 us -> 62.1 us
    pallas_call x4 -> x3, Pallas kernels: 21.1 us -> 13.9 us  [the longest x1 6.99 us: body(): call(functools.partial(project, ys, offsets), (jax.ShapeDtypeStruct((leng...]
    ppermute x1, waiting for transfers between devices: 5.77 us -> 0.01 us  [body(): before = lax.ppermute(rim, 'ctx', [(k, k + 1) for k in range(ctx - 1)])]
    ppermute x1, starting transfers between devices: 5.39 us -> 1.3 us  [body(): before = lax.ppermute(rim, 'ctx', [(k, k + 1) for k in range(ctx - 1)])]
    all_gather x1, waiting for transfers between devices: 0.02 us -> 3.19 us  [body(): weights = lax.all_gather(jnp.transpose(w_in, (1, 0, 2)), 'ctx', axis=0)]
    ppermute x8, starting transfers between devices: 23.7 us -> 26.1 us  [body(): others = [lax.ppermute(b, 'tp', swap) for b in blocks]]
  transfers between devices with their start and end apart: 20 -> 20, of which waited for: 6 -> 7; matrix products, arithmetic and copies ran while one was open for 3% -> 2% of each run, Pallas kernels for 9% -> 3%
where the time goes in v4:
time: 116 us; the launch traced here: 115 us
  starting transfers between devices  62.1 us (54%)
  waiting for transfers between devices  23 us (20%)
  Pallas kernels  13.9 us (12%)
  between operations  13.9 us (12%)
    ppermute x8, starting transfers between devices, body(): others = [lax.ppermute(b, 'tp', swap) for b in blocks]  26.1 us
    ppermute x3, starting transfers between devices, two_way(): down = lax.ppermute(down, axis, hop(-1))  13.5 us
    ppermute x4, waiting for transfers between devices, two_way(): up = lax.ppermute(up, axis, hop(1))  12.8 us
    ppermute x3, starting transfers between devices, body(): piece = lax.ppermute(own, 'fsdp', along_x(hop))  10.8 us
    ppermute x4, starting transfers between devices, two_way(): up = lax.ppermute(up, axis, hop(1))  10.4 us
    pallas_call x1, Pallas kernels, body(): call(functools.partial(project, ys, offsets), (jax.ShapeDtypeStruct((leng...  6.99 us
    pallas_call x1, Pallas kernels, body(): call(main_part, outline, [SMEM] + [VMEM] * 4, VMEM, work(length), flops=e...  3.87 us
    all_gather x1, waiting for transfers between devices, body(): weights = lax.all_gather(jnp.transpose(w_in, (1, 0, 2)), 'ctx', axis=0)  3.19 us
  transfers between devices with their start and end apart: 20, of which 7 were waited for; matrix products, arithmetic and copies ran while one was open for 2% of the time, Pallas kernels for 3%

profile of v4, /device:TPU:1, one launch (start us, length us, event | category | flops | bytes accessed | tf_op | source)
XLA Modules:
  0.0 115.0 jit_solution(3433257330836901055)
XLA Ops:
  6.5 0.7 all-gather.3.cloned.1.call-update
  7.3 4.0 %collective-permute-start = (bf16[512,128]{1,0:T(8,128)(2,1)}, bf16[512,128]{1,0:T(8,128)(2,1)S(1)}, u32[]{:S(2)}, u32[]{:S(2)}) collective-permute-start(bf16[512,128]{1,0:T(8,128)(2,1)} %bitcast.22), channel_id=1, source_target_pairs={{0,16},{16,32},{32,48},{48,0},{64,80},{80,96},{96,112},{112,64},{1... | collective-permute-start | bytes 393224 | tf_op jit(solution)/shard_map/ppermute | solution.py:195
  11.2 3.2 %collective-permute-start.2 = (bf16[512,128]{1,0:T(8,128)(2,1)}, bf16[512,128]{1,0:T(8,128)(2,1)S(1)}, u32[]{:S(2)}, u32[]{:S(2)}) collective-permute-start(bf16[512,128]{1,0:T(8,128)(2,1)} %bitcast.23), channel_id=1, source_target_pairs={{0,48},{16,0},{32,16},{48,32},{64,112},{80,64},{96,80},{112,96},{1... | collective-permute-start | bytes 393224 | tf_op jit(solution)/shard_map/ppermute | solution.py:195
  14.4 3.6 %collective-permute-start.1 = (bf16[512,128]{1,0:T(8,128)(2,1)}, bf16[512,128]{1,0:T(8,128)(2,1)S(1)}, u32[]{:S(2)}, u32[]{:S(2)}) collective-permute-start(bf16[512,128]{1,0:T(8,128)(2,1)} %bitcast.24), channel_id=1, source_target_pairs={{0,32},{16,48},{32,0},{48,16},{64,96},{80,112},{96,64},{112,80},{1... | collective-permute-start | bytes 393224 | tf_op jit(solution)/shard_map/ppermute | solution.py:195
  18.2 0.9 constant_dynamic-update-slice_fusion
  19.2 2.8 %collective-permute-done.1 = bf16[512,128]{1,0:T(8,128)(2,1)S(1)} collective-permute-done((bf16[512,128]{1,0:T(8,128)(2,1)}, bf16[512,128]{1,0:T(8,128)(2,1)S(1)}, u32[]{:S(2)}, u32[]{:S(2)}) %collective-permute-start.1) | collective-permute-done | bytes 131104 | tf_op jit(solution)/shard_map/ppermute | solution.py:195
  22.0 3.3 %collective-permute-start.3 = (bf16[4,512,128]{2,1,0:T(8,128)(2,1)S(1)}, bf16[4,512,128]{2,1,0:T(8,128)(2,1)S(1)}, u32[]{:S(2)}, u32[]{:S(2)}) collective-permute-start(bf16[4,512,128]{2,1,0:T(8,128)(2,1)S(1)} %bitcast_dynamic-update-slice_fusion.refs_0_), channel_id=1, source_target_pairs={{0,64},{16,80},{32,96},{48,112},{64,128},{80,144},{96,160},{112,17... | collective-permute-start | bytes 1572872 | tf_op jit(solution)/shard_map/ppermute | solution.py:166
  25.3 3.8 %collective-permute-start.4 = (bf16[4,512,128]{2,1,0:T(8,128)(2,1)S(1)}, bf16[4,512,128]{2,1,0:T(8,128)(2,1)S(1)}, u32[]{:S(2)}, u32[]{:S(2)}) collective-permute-start(bf16[4,512,128]{2,1,0:T(8,128)(2,1)S(1)} %bitcast_dynamic-update-slice_fusion.refs_0_), channel_id=1, source_target_pairs={{0,448},{16,464},{32,480},{48,496},{64,0},{80,16},{96,32},{112,48}... | collective-permute-start | bytes 1572872 | tf_op jit(solution)/shard_map/ppermute | solution.py:170
  29.1 5.0 %collective-permute-done.3.refs_1_ = bf16[4,512,128]{2,1,0:T(8,128)(2,1)S(1)} collective-permute-done((bf16[4,512,128]{2,1,0:T(8,128)(2,1)S(1)}, bf16[4,512,128]{2,1,0:T(8,128)(2,1)S(1)}, u32[]{:S(2)}, u32[]{:S(2)}) %collective-permute-start.3) | collective-permute-done | bytes 524320 | tf_op jit(solution)/shard_map/ppermute | solution.py:166
  34.2 3.2 %collective-permute-start.5 = (bf16[4,512,128]{2,1,0:T(8,128)(2,1)S(1)}, bf16[4,512,128]{2,1,0:T(8,128)(2,1)S(1)}, u32[]{:S(2)}, u32[]{:S(2)}) collective-permute-start(bf16[4,512,128]{2,1,0:T(8,128)(2,1)S(1)} %collective-permute-done.3.refs_1_), channel_id=1, source_target_pairs={{0,64},{16,80},{32,96},{48,112},{64,128},{80,144},{96,160},{112,17... | collective-permute-start | bytes 1572872 | tf_op jit(solution)/shard_map/ppermute | solution.py:166
  37.3 4.8 %collective-permute-start.6 = (bf16[4,512,128]{2,1,0:T(8,128)(2,1)S(1)}, bf16[4,512,128]{2,1,0:T(8,128)(2,1)S(1)}, u32[]{:S(2)}, u32[]{:S(2)}) collective-permute-start(bf16[4,512,128]{2,1,0:T(8,128)(2,1)S(1)} %collective-permute-done.4.refs_2_), channel_id=1, source_target_pairs={{0,448},{16,464},{32,480},{48,496},{64,0},{80,16},{96,32},{112,48}... | collective-permute-start | bytes 1572872 | tf_op jit(solution)/shard_map/ppermute | solution.py:170
  42.2 5.3 %collective-permute-done.5.refs_3_ = bf16[4,512,128]{2,1,0:T(8,128)(2,1)S(1)} collective-permute-done((bf16[4,512,128]{2,1,0:T(8,128)(2,1)S(1)}, bf16[4,512,128]{2,1,0:T(8,128)(2,1)S(1)}, u32[]{:S(2)}, u32[]{:S(2)}) %collective-permute-start.5) | collective-permute-done | bytes 524320 | tf_op jit(solution)/shard_map/ppermute | solution.py:166
  47.5 2.0 %collective-permute-start.7 = (bf16[4,512,128]{2,1,0:T(8,128)(2,1)S(1)}, bf16[4,512,128]{2,1,0:T(8,128)(2,1)S(1)}, u32[]{:S(2)}, u32[]{:S(2)}) collective-permute-start(bf16[4,512,128]{2,1,0:T(8,128)(2,1)S(1)} %collective-permute-done.5.refs_3_), channel_id=1, source_target_pairs={{0,64},{16,80},{32,96},{48,112},{64,128},{80,144},{96,160},{112,17... | collective-permute-start | bytes 1572872 | tf_op jit(solution)/shard_map/ppermute | solution.py:166
  49.5 9.6 %collective-permute-start.10 = (bf16[4,512,128]{2,1,0:T(8,128)(2,1)S(1)}, bf16[4,512,128]{2,1,0:T(8,128)(2,1)S(1)}, u32[]{:S(2)}, u32[]{:S(2)}) collective-permute-start(bf16[4,512,128]{2,1,0:T(8,128)(2,1)S(1)} %bitcast_dynamic-update-slice_fusion.refs_0_), channel_id=1, source_target_pairs={{0,1},{1,0},{2,3},{3,2},{4,5},{5,4},{6,7},{7,6},{8,9},{9,8},{10,11... | collective-permute-start | bytes 1572872 | tf_op jit(solution)/shard_map/ppermute | solution.py:198
  59.1 1.9 %collective-permute-start.12 = (bf16[4,512,128]{2,1,0:T(8,128)(2,1)S(1)}, bf16[4,512,128]{2,1,0:T(8,128)(2,1)S(1)}, u32[]{:S(2)}, u32[]{:S(2)}) collective-permute-start(bf16[4,512,128]{2,1,0:T(8,128)(2,1)S(1)} %collective-permute-done.4.refs_2_), channel_id=1, source_target_pairs={{0,1},{1,0},{2,3},{3,2},{4,5},{5,4},{6,7},{7,6},{8,9},{9,8},{10,11... | collective-permute-start | bytes 1572872 | tf_op jit(solution)/shard_map/ppermute | solution.py:198
  61.0 2.4 %collective-permute-start.11 = (bf16[4,512,128]{2,1,0:T(8,128)(2,1)S(1)}, bf16[4,512,128]{2,1,0:T(8,128)(2,1)S(1)}, u32[]{:S(2)}, u32[]{:S(2)}) collective-permute-start(bf16[4,512,128]{2,1,0:T(8,128)(2,1)S(1)} %collective-permute-done.3.refs_1_), channel_id=1, source_target_pairs={{0,1},{1,0},{2,3},{3,2},{4,5},{5,4},{6,7},{7,6},{8,9},{9,8},{10,11... | collective-permute-start | bytes 1572872 | tf_op jit(solution)/shard_map/ppermute | solution.py:198
  63.5 4.9 %collective-permute-start.8 = (bf16[4,512,128]{2,1,0:T(8,128)(2,1)S(1)}, bf16[4,512,128]{2,1,0:T(8,128)(2,1)}, u32[]{:S(2)}, u32[]{:S(2)}) collective-permute-start(bf16[4,512,128]{2,1,0:T(8,128)(2,1)S(1)} %collective-permute-done.6.refs_4_), channel_id=1, source_target_pairs={{0,448},{16,464},{32,480},{48,496},{64,0},{80,16},{96,32},{112,48}... | collective-permute-start | bytes 1572872 | tf_op jit(solution)/shard_map/ppermute | solution.py:170
  68.3 1.9 %collective-permute-start.9 = (bf16[4,512,128]{2,1,0:T(8,128)(2,1)S(1)}, bf16[4,512,128]{2,1,0:T(8,128)(2,1)}, u32[]{:S(2)}, u32[]{:S(2)}) collective-permute-start(bf16[4,512,128]{2,1,0:T(8,128)(2,1)S(1)} %collective-permute-done.7.refs_5_), channel_id=1, source_target_pairs={{0,64},{16,80},{32,96},{48,112},{64,128},{80,144},{96,160},{112,17... | collective-permute-start | bytes 1572872 | tf_op jit(solution)/shard_map/ppermute | solution.py:166
  70.3 2.2 %collective-permute-start.14 = (bf16[4,512,128]{2,1,0:T(8,128)(2,1)S(1)}, bf16[4,512,128]{2,1,0:T(8,128)(2,1)}, u32[]{:S(2)}, u32[]{:S(2)}) collective-permute-start(bf16[4,512,128]{2,1,0:T(8,128)(2,1)S(1)} %collective-permute-done.6.refs_4_), channel_id=1, source_target_pairs={{0,1},{1,0},{2,3},{3,2},{4,5},{5,4},{6,7},{7,6},{8,9},{9,8},{10,11... | collective-permute-start | bytes 1572872 | tf_op jit(solution)/shard_map/ppermute | solution.py:198
  72.5 2.1 %collective-permute-start.13 = (bf16[4,512,128]{2,1,0:T(8,128)(2,1)S(1)}, bf16[4,512,128]{2,1,0:T(8,128)(2,1)}, u32[]{:S(2)}, u32[]{:S(2)}) collective-permute-start(bf16[4,512,128]{2,1,0:T(8,128)(2,1)S(1)} %collective-permute-done.5.refs_3_), channel_id=1, source_target_pairs={{0,1},{1,0},{2,3},{3,2},{4,5},{5,4},{6,7},{7,6},{8,9},{9,8},{10,11... | collective-permute-start | bytes 1572872 | tf_op jit(solution)/shard_map/ppermute | solution.py:198
  74.7 2.2 %collective-permute-start.15 = (bf16[4,512,128]{2,1,0:T(8,128)(2,1)S(1)}, bf16[4,512,128]{2,1,0:T(8,128)(2,1)}, u32[]{:S(2)}, u32[]{:S(2)}) collective-permute-start(bf16[4,512,128]{2,1,0:T(8,128)(2,1)S(1)} %collective-permute-done.7.refs_5_), channel_id=1, source_target_pairs={{0,1},{1,0},{2,3},{3,2},{4,5},{5,4},{6,7},{7,6},{8,9},{9,8},{10,11... | collective-permute-start | bytes 1572872 | tf_op jit(solution)/shard_map/ppermute | solution.py:198
  76.9 2.8 %collective-permute-done.8.refs_6_ = bf16[4,512,128]{2,1,0:T(8,128)(2,1)} collective-permute-done((bf16[4,512,128]{2,1,0:T(8,128)(2,1)S(1)}, bf16[4,512,128]{2,1,0:T(8,128)(2,1)}, u32[]{:S(2)}, u32[]{:S(2)}) %collective-permute-start.8) | collective-permute-done | bytes 524320 | tf_op jit(solution)/shard_map/ppermute | solution.py:170
  79.6 2.7 %collective-permute-start.16 = (bf16[4,512,128]{2,1,0:T(8,128)(2,1)}, bf16[4,512,128]{2,1,0:T(8,128)(2,1)}, u32[]{:S(2)}, u32[]{:S(2)}) collective-permute-start(bf16[4,512,128]{2,1,0:T(8,128)(2,1)} %collective-permute-done.8.refs_6_), channel_id=1, source_target_pairs={{0,1},{1,0},{2,3},{3,2},{4,5},{5,4},{6,7},{7,6},{8,9},{9,8},{10,11... | collective-permute-start | bytes 1572872 | tf_op jit(solution)/shard_map/ppermute | solution.py:198
  82.3 2.4 %collective-permute-done.9.refs_7_ = bf16[4,512,128]{2,1,0:T(8,128)(2,1)} collective-permute-done((bf16[4,512,128]{2,1,0:T(8,128)(2,1)S(1)}, bf16[4,512,128]{2,1,0:T(8,128)(2,1)}, u32[]{:S(2)}, u32[]{:S(2)}) %collective-permute-start.9) | collective-permute-done | bytes 524320 | tf_op jit(solution)/shard_map/ppermute | solution.py:166
  84.8 3.0 %collective-permute-start.17 = (bf16[4,512,128]{2,1,0:T(8,128)(2,1)}, bf16[4,512,128]{2,1,0:T(8,128)(2,1)}, u32[]{:S(2)}, u32[]{:S(2)}) collective-permute-start(bf16[4,512,128]{2,1,0:T(8,128)(2,1)} %collective-permute-done.9.refs_7_), channel_id=1, source_target_pairs={{0,1},{1,0},{2,3},{3,2},{4,5},{5,4},{6,7},{7,6},{8,9},{9,8},{10,11... | collective-permute-start | bytes 1572872 | tf_op jit(solution)/shard_map/ppermute | solution.py:198
  87.9 0.9 convert_reduce_fusion
  88.9 0.8 collective-permute-done.17.refs_15_
  89.7 3.2 %all-gather.3.cloned.1.call-done = bf16[24,1024,128]{2,1,0:T(8,128)(2,1)} async-done(((bf16[3,1024,128]{2,1,0:T(8,128)(2,1)}), bf16[24,1024,128]{2,1,0:T(8,128)(2,1)}) %all-gather.3.cloned.1.call-update) | async-done | bytes 6291472 | tf_op jit(solution)/shard_map/all_gather | solution.py:188
  92.9 7.0 %shard_map.64 = (bf16[512,384]{1,0:T(8,128)(2,1)S(1)}, bf16[144,384]{1,0:T(8,128)(2,1)S(1)}) custom-call(s32[6]{0:T(128)S(1)} %pad_add_fusion.place, bf16[4,512,128]{2,1,0:T(8,128)(2,1)S(1)} %bitcast_dynamic-update-slice_fusion.refs_0_, bf16[4,512,128]{2,1,0:T(8,128)(2,1)S(1)} %collective-permute-done.3.refs_1_, bf16[4,512,128]{2,1,0:T(8,128)(2,1)} %copy-done.3, ...), custom_call_target="tpu_custom_call" | custom-call | flops 3221225472 | bytes 16777216 | tf_op jit(solution)/shard_map/pallas_call | solution.py:206
  99.9 1.3 %collective-permute-start.18 = (bf16[144,384]{1,0:T(8,128)(2,1)S(1)}, bf16[144,384]{1,0:T(8,128)(2,1)S(1)}, u32[]{:S(2)}, u32[]{:S(2)}) collective-permute-start(bf16[144,384]{1,0:T(8,128)(2,1)S(1)} %get-tuple-element.7), channel_id=1, source_target_pairs={{0,2},{2,4},{4,6},{6,8},{8,10},{10,12},{12,14},{1,3},{3,5},{5,7},{... | collective-permute-start | bytes 331784 | tf_op jit(solution)/shard_map/ppermute | solution.py:224
  101.3 3.9 %shard_map.65.given = bf16[512,128]{1,0:T(8,128)(2,1)S(1)} custom-call(s32[6]{0:T(128)S(1)} %pad_add_fusion.place, bf16[512,384]{1,0:T(8,128)(2,1)S(1)} %get-tuple-element.8.raw, f32[7,384]{1,0:T(8,128)S(1)} %bitcast.16, f32[128,128]{1,0:T(8,128)S(1)} %copy-done, f32[1,128]{1,0:T(1,128)S(1)} %bitcast.18), custom_call_target="tpu_custom_call" | custom-call | flops 1610612736 | bytes 2097152 | tf_op jit(solution)/shard_map/pallas_call | solution.py:233
  105.1 3.1 %shard_map.66 = bf16[512,128]{1,0:T(8,128)(2,1)} custom-call(s32[6]{0:T(128)S(1)} %pad_add_fusion.place, bf16[144,384]{1,0:T(8,128)(2,1)S(1)} %collective-permute-done.18.before, bf16[512,384]{1,0:T(8,128)(2,1)S(1)} %get-tuple-element.8.raw, f32[7,384]{1,0:T(8,128)S(1)} %bitcast.17, f32[128,128]{1,0:T(8,128)S(1)} %copy-done, f32[1,128]{1,0:T(1,128)S(1)} %bitcast.19, ...), custom_call_target="tpu_custom_call" | custom-call | flops 805306368 | bytes 1048576 | tf_op jit(solution)/shard_map/pallas_call | solution.py:242
  (40 shorter events, 0.3 us)
Async XLA Ops:
  6.5 86.3 %all-gather.3.cloned.1.call-start = ((), (), s32[]{:S(2)}) async-start(), calls=%async_computation | async-start | bytes 7077888 | tf_op jit(solution)/shard_map/all_gather | solution.py:188
  7.3 11.9 %collective-permute-start = (bf16[512,128]{1,0:T(8,128)(2,1)}, bf16[512,128]{1,0:T(8,128)(2,1)S(1)}, u32[]{:S(2)}, u32[]{:S(2)}) collective-permute-start(bf16[512,128]{1,0:T(8,128)(2,1)} %bitcast.22), channel_id=1, source_target_pairs={{0,16},{16,32},{32,48},{48,0},{64,80},{80,96},{96,112},{112,64},{1... | collective-permute-start | bytes 393224 | tf_op jit(solution)/shard_map/ppermute | solution.py:195
  11.2 10.8 %collective-permute-start.2 = (bf16[512,128]{1,0:T(8,128)(2,1)}, bf16[512,128]{1,0:T(8,128)(2,1)S(1)}, u32[]{:S(2)}, u32[]{:S(2)}) collective-permute-start(bf16[512,128]{1,0:T(8,128)(2,1)} %bitcast.23), channel_id=1, source_target_pairs={{0,48},{16,0},{32,16},{48,32},{64,112},{80,64},{96,80},{112,96},{1... | collective-permute-start | bytes 393224 | tf_op jit(solution)/shard_map/ppermute | solution.py:195
  14.4 7.5 %collective-permute-start.1 = (bf16[512,128]{1,0:T(8,128)(2,1)}, bf16[512,128]{1,0:T(8,128)(2,1)S(1)}, u32[]{:S(2)}, u32[]{:S(2)}) collective-permute-start(bf16[512,128]{1,0:T(8,128)(2,1)} %bitcast.24), channel_id=1, source_target_pairs={{0,32},{16,48},{32,0},{48,16},{64,96},{80,112},{96,64},{112,80},{1... | collective-permute-start | bytes 393224 | tf_op jit(solution)/shard_map/ppermute | solution.py:195
  22.0 12.1 %collective-permute-start.3 = (bf16[4,512,128]{2,1,0:T(8,128)(2,1)S(1)}, bf16[4,512,128]{2,1,0:T(8,128)(2,1)S(1)}, u32[]{:S(2)}, u32[]{:S(2)}) collective-permute-start(bf16[4,512,128]{2,1,0:T(8,128)(2,1)S(1)} %bitcast_dynamic-update-slice_fusion.refs_0_), channel_id=1, source_target_pairs={{0,64},{16,80},{32,96},{48,112},{64,128},{80,144},{96,160},{112,17... | collective-permute-start | bytes 1572872 | tf_op jit(solution)/shard_map/ppermute | solution.py:166
  25.3 12.0 %collective-permute-start.4 = (bf16[4,512,128]{2,1,0:T(8,128)(2,1)S(1)}, bf16[4,512,128]{2,1,0:T(8,128)(2,1)S(1)}, u32[]{:S(2)}, u32[]{:S(2)}) collective-permute-start(bf16[4,512,128]{2,1,0:T(8,128)(2,1)S(1)} %bitcast_dynamic-update-slice_fusion.refs_0_), channel_id=1, source_target_pairs={{0,448},{16,464},{32,480},{48,496},{64,0},{80,16},{96,32},{112,48}... | collective-permute-start | bytes 1572872 | tf_op jit(solution)/shard_map/ppermute | solution.py:170
  34.2 13.3 %collective-permute-start.5 = (bf16[4,512,128]{2,1,0:T(8,128)(2,1)S(1)}, bf16[4,512,128]{2,1,0:T(8,128)(2,1)S(1)}, u32[]{:S(2)}, u32[]{:S(2)}) collective-permute-start(bf16[4,512,128]{2,1,0:T(8,128)(2,1)S(1)} %collective-permute-done.3.refs_1_), channel_id=1, source_target_pairs={{0,64},{16,80},{32,96},{48,112},{64,128},{80,144},{96,160},{112,17... | collective-permute-start | bytes 1572872 | tf_op jit(solution)/shard_map/ppermute | solution.py:166
  37.3 55.6 %copy-start.3 = (bf16[4,512,128]{2,1,0:T(8,128)(2,1)}, bf16[4,512,128]{2,1,0:T(8,128)(2,1)S(1)}, u32[]{:S(2)}) copy-start(bf16[4,512,128]{2,1,0:T(8,128)(2,1)S(1)} %collective-permute-done.4.refs_2_) | copy-start | bytes 1572868
  37.3 26.1 %collective-permute-start.6 = (bf16[4,512,128]{2,1,0:T(8,128)(2,1)S(1)}, bf16[4,512,128]{2,1,0:T(8,128)(2,1)S(1)}, u32[]{:S(2)}, u32[]{:S(2)}) collective-permute-start(bf16[4,512,128]{2,1,0:T(8,128)(2,1)S(1)} %collective-permute-done.4.refs_2_), channel_id=1, source_target_pairs={{0,448},{16,464},{32,480},{48,496},{64,0},{80,16},{96,32},{112,48}... | collective-permute-start | bytes 1572872 | tf_op jit(solution)/shard_map/ppermute | solution.py:170
  47.5 45.4 %copy-start.4 = (bf16[4,512,128]{2,1,0:T(8,128)(2,1)}, bf16[4,512,128]{2,1,0:T(8,128)(2,1)S(1)}, u32[]{:S(2)}) copy-start(bf16[4,512,128]{2,1,0:T(8,128)(2,1)S(1)} %collective-permute-done.5.refs_3_) | copy-start | bytes 1572868
  47.5 20.9 %collective-permute-start.7 = (bf16[4,512,128]{2,1,0:T(8,128)(2,1)S(1)}, bf16[4,512,128]{2,1,0:T(8,128)(2,1)S(1)}, u32[]{:S(2)}, u32[]{:S(2)}) collective-permute-start(bf16[4,512,128]{2,1,0:T(8,128)(2,1)S(1)} %collective-permute-done.5.refs_3_), channel_id=1, source_target_pairs={{0,64},{16,80},{32,96},{48,112},{64,128},{80,144},{96,160},{112,17... | collective-permute-start | bytes 1572872 | tf_op jit(solution)/shard_map/ppermute | solution.py:166
  49.5 20.8 %collective-permute-start.10 = (bf16[4,512,128]{2,1,0:T(8,128)(2,1)S(1)}, bf16[4,512,128]{2,1,0:T(8,128)(2,1)S(1)}, u32[]{:S(2)}, u32[]{:S(2)}) collective-permute-start(bf16[4,512,128]{2,1,0:T(8,128)(2,1)S(1)} %bitcast_dynamic-update-slice_fusion.refs_0_), channel_id=1, source_target_pairs={{0,1},{1,0},{2,3},{3,2},{4,5},{5,4},{6,7},{7,6},{8,9},{9,8},{10,11... | collective-permute-start | bytes 1572872 | tf_op jit(solution)/shard_map/ppermute | solution.py:198
  59.1 13.4 %collective-permute-start.12 = (bf16[4,512,128]{2,1,0:T(8,128)(2,1)S(1)}, bf16[4,512,128]{2,1,0:T(8,128)(2,1)S(1)}, u32[]{:S(2)}, u32[]{:S(2)}) collective-permute-start(bf16[4,512,128]{2,1,0:T(8,128)(2,1)S(1)} %collective-permute-done.4.refs_2_), channel_id=1, source_target_pairs={{0,1},{1,0},{2,3},{3,2},{4,5},{5,4},{6,7},{7,6},{8,9},{9,8},{10,11... | collective-permute-start | bytes 1572872 | tf_op jit(solution)/shard_map/ppermute | solution.py:198
  61.0 13.6 %collective-permute-start.11 = (bf16[4,512,128]{2,1,0:T(8,128)(2,1)S(1)}, bf16[4,512,128]{2,1,0:T(8,128)(2,1)S(1)}, u32[]{:S(2)}, u32[]{:S(2)}) collective-permute-start(bf16[4,512,128]{2,1,0:T(8,128)(2,1)S(1)} %collective-permute-done.3.refs_1_), channel_id=1, source_target_pairs={{0,1},{1,0},{2,3},{3,2},{4,5},{5,4},{6,7},{7,6},{8,9},{9,8},{10,11... | collective-permute-start | bytes 1572872 | tf_op jit(solution)/shard_map/ppermute | solution.py:198
  63.5 29.4 %copy-start.5 = (bf16[4,512,128]{2,1,0:T(8,128)(2,1)}, bf16[4,512,128]{2,1,0:T(8,128)(2,1)S(1)}, u32[]{:S(2)}) copy-start(bf16[4,512,128]{2,1,0:T(8,128)(2,1)S(1)} %collective-permute-done.6.refs_4_) | copy-start | bytes 1572868
  63.5 16.2 %collective-permute-start.8 = (bf16[4,512,128]{2,1,0:T(8,128)(2,1)S(1)}, bf16[4,512,128]{2,1,0:T(8,128)(2,1)}, u32[]{:S(2)}, u32[]{:S(2)}) collective-permute-start(bf16[4,512,128]{2,1,0:T(8,128)(2,1)S(1)} %collective-permute-done.6.refs_4_), channel_id=1, source_target_pairs={{0,448},{16,464},{32,480},{48,496},{64,0},{80,16},{96,32},{112,48}... | collective-permute-start | bytes 1572872 | tf_op jit(solution)/shard_map/ppermute | solution.py:170
  68.3 24.5 %copy-start.6 = (bf16[4,512,128]{2,1,0:T(8,128)(2,1)}, bf16[4,512,128]{2,1,0:T(8,128)(2,1)S(1)}, u32[]{:S(2)}) copy-start(bf16[4,512,128]{2,1,0:T(8,128)(2,1)S(1)} %collective-permute-done.7.refs_5_) | copy-start | bytes 1572868
  68.3 16.4 %collective-permute-start.9 = (bf16[4,512,128]{2,1,0:T(8,128)(2,1)S(1)}, bf16[4,512,128]{2,1,0:T(8,128)(2,1)}, u32[]{:S(2)}, u32[]{:S(2)}) collective-permute-start(bf16[4,512,128]{2,1,0:T(8,128)(2,1)S(1)} %collective-permute-done.7.refs_5_), channel_id=1, source_target_pairs={{0,64},{16,80},{32,96},{48,112},{64,128},{80,144},{96,160},{112,17... | collective-permute-start | bytes 1572872 | tf_op jit(solution)/shard_map/ppermute | solution.py:166
  70.3 14.5 %copy-start.7 = (bf16[4,512,128]{2,1,0:T(8,128)(2,1)}, bf16[4,512,128]{2,1,0:T(8,128)(2,1)S(1)}, u32[]{:S(2)}) copy-start(bf16[4,512,128]{2,1,0:T(8,128)(2,1)S(1)} %collective-permute-done.10.refs_8_) | copy-start | bytes 1572868
  70.3 18.6 %collective-permute-start.14 = (bf16[4,512,128]{2,1,0:T(8,128)(2,1)S(1)}, bf16[4,512,128]{2,1,0:T(8,128)(2,1)}, u32[]{:S(2)}, u32[]{:S(2)}) collective-permute-start(bf16[4,512,128]{2,1,0:T(8,128)(2,1)S(1)} %collective-permute-done.6.refs_4_), channel_id=1, source_target_pairs={{0,1},{1,0},{2,3},{3,2},{4,5},{5,4},{6,7},{7,6},{8,9},{9,8},{10,11... | collective-permute-start | bytes 1572872 | tf_op jit(solution)/shard_map/ppermute | solution.py:198
  72.5 12.3 %copy-start.8 = (bf16[4,512,128]{2,1,0:T(8,128)(2,1)}, bf16[4,512,128]{2,1,0:T(8,128)(2,1)S(1)}, u32[]{:S(2)}) copy-start(bf16[4,512,128]{2,1,0:T(8,128)(2,1)S(1)} %collective-permute-done.12.refs_10_) | copy-start | bytes 1572868
  72.5 16.3 %collective-permute-start.13 = (bf16[4,512,128]{2,1,0:T(8,128)(2,1)S(1)}, bf16[4,512,128]{2,1,0:T(8,128)(2,1)}, u32[]{:S(2)}, u32[]{:S(2)}) collective-permute-start(bf16[4,512,128]{2,1,0:T(8,128)(2,1)S(1)} %collective-permute-done.5.refs_3_), channel_id=1, source_target_pairs={{0,1},{1,0},{2,3},{3,2},{4,5},{5,4},{6,7},{7,6},{8,9},{9,8},{10,11... | collective-permute-start | bytes 1572872 | tf_op jit(solution)/shard_map/ppermute | solution.py:198
  74.7 10.1 %copy-start.9 = (bf16[4,512,128]{2,1,0:T(8,128)(2,1)}, bf16[4,512,128]{2,1,0:T(8,128)(2,1)S(1)}, u32[]{:S(2)}) copy-start(bf16[4,512,128]{2,1,0:T(8,128)(2,1)S(1)} %collective-permute-done.11.refs_9_) | copy-start | bytes 1572868
  74.7 14.2 %collective-permute-start.15 = (bf16[4,512,128]{2,1,0:T(8,128)(2,1)S(1)}, bf16[4,512,128]{2,1,0:T(8,128)(2,1)}, u32[]{:S(2)}, u32[]{:S(2)}) collective-permute-start(bf16[4,512,128]{2,1,0:T(8,128)(2,1)S(1)} %collective-permute-done.7.refs_5_), channel_id=1, source_target_pairs={{0,1},{1,0},{2,3},{3,2},{4,5},{5,4},{6,7},{7,6},{8,9},{9,8},{10,11... | collective-permute-start | bytes 1572872 | tf_op jit(solution)/shard_map/ppermute | solution.py:198
  79.6 9.2 %collective-permute-start.16 = (bf16[4,512,128]{2,1,0:T(8,128)(2,1)}, bf16[4,512,128]{2,1,0:T(8,128)(2,1)}, u32[]{:S(2)}, u32[]{:S(2)}) collective-permute-start(bf16[4,512,128]{2,1,0:T(8,128)(2,1)} %collective-permute-done.8.refs_6_), channel_id=1, source_target_pairs={{0,1},{1,0},{2,3},{3,2},{4,5},{5,4},{6,7},{7,6},{8,9},{9,8},{10,11... | collective-permute-start | bytes 1572872 | tf_op jit(solution)/shard_map/ppermute | solution.py:198
  84.8 4.9 %collective-permute-start.17 = (bf16[4,512,128]{2,1,0:T(8,128)(2,1)}, bf16[4,512,128]{2,1,0:T(8,128)(2,1)}, u32[]{:S(2)}, u32[]{:S(2)}) collective-permute-start(bf16[4,512,128]{2,1,0:T(8,128)(2,1)} %collective-permute-done.9.refs_7_), channel_id=1, source_target_pairs={{0,1},{1,0},{2,3},{3,2},{4,5},{5,4},{6,7},{7,6},{8,9},{9,8},{10,11... | collective-permute-start | bytes 1572872 | tf_op jit(solution)/shard_map/ppermute | solution.py:198
  92.9 8.3 %copy-start = (f32[128,128]{1,0:T(8,128)S(1)}, f32[128,128]{1,0:T(8,128)}, u32[]{:S(2)}) copy-start(f32[128,128]{1,0:T(8,128)} %taps.3) | copy-start | bytes 196612
  92.9 8.3 %copy-start.1 = (f32[7,3,128]{2,0,1:T(8,128)S(1)}, f32[7,3,128]{2,0,1:T(8,128)}, u32[]{:S(2)}) copy-start(f32[7,3,128]{2,0,1:T(8,128)} %param.8) | copy-start | bytes 32260
  92.9 8.3 %copy-start.2 = (f32[128]{0:T(128)S(1)}, f32[128]{0:T(128)}, u32[]{:S(2)}) copy-start(f32[128]{0:T(128)} %param.10) | copy-start | bytes 1540
  99.9 5.2 %collective-permute-start.18 = (bf16[144,384]{1,0:T(8,128)(2,1)S(1)}, bf16[144,384]{1,0:T(8,128)(2,1)S(1)}, u32[]{:S(2)}, u32[]{:S(2)}) collective-permute-start(bf16[144,384]{1,0:T(8,128)(2,1)S(1)} %get-tuple-element.7), channel_id=1, source_target_pairs={{0,2},{2,4},{4,6},{6,8},{8,10},{10,12},{12,14},{1,3},{3,5},{5,7},{... | collective-permute-start | bytes 331784 | tf_op jit(solution)/shard_map/ppermute | solution.py:224
Sparse Core Ops, SparseCore 0:
  9.4 83.3 all-gather.2

commit v5 on v4

--- a/solution.py
+++ b/solution.py
@@ -20,6 +20,8 @@
 ANY = pl.BlockSpec(memory_space=pl.ANY)
 HBM = pl.BlockSpec(memory_space=pltpu.HBM)
 MIB = 1 << 20
+COST = 20 << 30
+PACE = 2
 
 
 def call(kernel, out_shape, in_specs, out_specs, scratch=(), flops=0, nbytes=0, vmem=8):
@@ -38,30 +40,55 @@
     return jnp.concatenate([planes[j] for j in range(planes.shape[0])], 1)
 
 
-def project(count, offsets, place, *refs):
-    mine, other = refs[:count], refs[count : 2 * count]
-    weights_in, raw, rim, total, held, weights, sem = refs[2 * count :]
+def project(count, offsets, sets, place, *refs):
+    mine, other, refs = refs[: len(sets)], refs[len(sets) : 2 * len(sets)], refs[2 * len(sets) :]
+    whole, halves, refs = refs[: count - 1], refs[count - 1 : count + 1], refs[count + 1 :]
+    raw, rim, total, held, weights, sem = refs
     core = place[1]
-
-    def copies(k):
-        slot = lax.rem(place[0] + offsets[k] + count, count)
+    where = [(a, i) for a, size in enumerate(sets) for i in range(size)]
+    half = halves[0].shape[0]
+
+    def landing(k):
+        a, i = where[k]
         return [
-            pltpu.make_async_copy(mine[k], held.at[k, :, core], sem.at[3 * k]),
-            pltpu.make_async_copy(other[k], held.at[k, :, 1 - core], sem.at[3 * k + 1]),
-            pltpu.make_async_copy(weights_in.at[slot], weights.at[k], sem.at[3 * k + 2]),
+            pltpu.make_async_copy(mine[a].at[i], held.at[k, :, core], sem.at[4 * k]),
+            pltpu.make_async_copy(other[a].at[i], held.at[k, :, 1 - core], sem.at[4 * k + 1]),
         ]
 
+    def weight_halves(k, j):
+        first, second = weights.at[k, :half], weights.at[k, half:]
+        sources = halves if j == count - 1 else (whole[j].at[:half], whole[j].at[half:])
+        return [
+            pltpu.make_async_copy(sources[0], first, sem.at[4 * k + 2]),
+            pltpu.make_async_copy(sources[1], second, sem.at[4 * k + 3]),
+        ]
+
+    def start(k):
+        for copy in landing(k):
+            copy.start()
+        for j in range(count):
+            gap = place[0] + offsets[k] - place[2] - offsets[j]
+
+            @pl.when(lax.rem(gap + 2 * count, count) == 0)
+            def _():
+                for copy in weight_halves(k, j):
+                    copy.start()
+
     for k in range(min(AHEAD, count)):
-        for copy in copies(k):
-            copy.start()
+        start(k)
     for k in range(count):
         if k + AHEAD < count:
-            for copy in copies(k + AHEAD):
-                copy.start()
-        for copy in copies(k):
+            start(k + AHEAD)
+        for copy in landing(k) + weight_halves(k, count - 1):
             copy.wait()
         left = [held[k, j, c] for j in range(held.shape[1]) for c in range(held.shape[2])]
-        term = jnp.dot(jnp.concatenate(left, 1), wide(weights[k]), preferred_element_type=F32)
+        per = weights.shape[1] // 3
+        columns = [
+            jnp.concatenate([weights[k, g * per + h] for h in range(per)], 0) for g in range(3)
+        ]
+        term = jnp.dot(
+            jnp.concatenate(left, 1), jnp.concatenate(columns, 1), preferred_element_type=F32
+        )
         if k == 0:
             total[...] = term
         elif k < count - 1:
@@ -160,17 +187,22 @@
     long_filter(0, HEAD, rim, place, ids, mixed, queries, taps, skip, out, window)
 
 
-def two_way(block, axis, count, hop):
-    blocks, offsets, up, down = [block], [0], block, block
-    for s in range(1, count // 2 + 1):
-        up = lax.ppermute(up, axis, hop(1))
-        blocks.append(up)
-        offsets.append(-s)
-        if s <= (count - 1) // 2:
-            down = lax.ppermute(down, axis, hop(-1))
-            blocks.append(down)
-            offsets.append(s)
-    return blocks, tuple(offsets)
+def after(value, others, flops):
+    def kernel(*refs):
+        pass
+
+    return pl.pallas_call(
+        kernel,
+        out_shape=jax.ShapeDtypeStruct(value.shape, value.dtype),
+        in_specs=[ANY] * (1 + len(others)),
+        out_specs=ANY,
+        input_output_aliases={0: 0},
+        cost_estimate=pl.CostEstimate(flops=flops, bytes_accessed=0, transcendentals=0),
+    )(value, *others)
+
+
+def both_ways(pair, axis, hop):
+    return [lax.ppermute(pair[0], axis, hop(1)), lax.ppermute(pair[1], axis, hop(-1))]
 
 
 def body(tokens, w_in, short_taps, mr_taps, skip, genome_ids):
@@ -185,7 +217,13 @@
     along_y = lambda d: [(j * xs + i, (j + d) % ys * xs + i) for j in range(ys) for i in range(xs)]
     swap = [(0, 1), (1, 0)]
 
-    weights = lax.all_gather(jnp.transpose(w_in, (1, 0, 2)), "ctx", axis=0)
+    along_z = lambda d: [(k, (k + d) % ctx) for k in range(ctx)]
+    columns = jnp.transpose(w_in, (1, 0, 2)).reshape(6, -1, width)
+    weights, pair, half = [], [columns, columns], columns.shape[0] // 2
+    for _ in range(1, ctx // 2):
+        pair = both_ways(pair, "ctx", along_z)
+        weights.append(pair)
+    weights.append(both_ways([pair[0][:half], pair[1][half:]], "ctx", along_z))
 
     own = tokens[0]
     block = jnp.zeros((xs,) + own.shape, BF16)
@@ -194,8 +232,23 @@
         hop = d if d <= xs // 2 else d - xs
         piece = lax.ppermute(own, "fsdp", along_x(hop))
         block = lax.dynamic_update_index_in_dim(block, piece, (x - hop) % xs, 0)
-    blocks, offsets = two_way(block, "fsdp", ys, along_y)
-    others = [lax.ppermute(b, "tp", swap) for b in blocks]
+    offsets, pair, fresh, mine, other = [0], [block, block], [block], [], []
+    for r in range(1, ys // 2):
+        pair = both_ways(pair, "fsdp", along_y)
+        early = weights[r - 1] + other[:1] if r == 3 else weights[r - 1]
+        k = 0 if r <= PACE else 1
+        pair[k] = after(pair[k], early, COST)
+        fresh, offsets = fresh + pair, offsets + [-r, r]
+        if r in (1, ys // 2 - 1):
+            mine.append(jnp.stack(fresh))
+            other.append(lax.ppermute(mine[-1], "tp", swap))
+            fresh = []
+    final = lax.ppermute(pair[0], "fsdp", along_y(1))
+    final = after(final, weights[-1], COST)
+    mine.append(jnp.stack(fresh + [final]))
+    other.append(lax.ppermute(mine[-1], "tp", swap))
+    offsets = tuple(offsets + [-(ys // 2)])
+    sets = tuple(m.shape[0] for m in mine)
 
     starts = jnp.sum(genome_ids[0][None, :] < jnp.arange(1, 4)[:, None], axis=1, dtype=jnp.int32)
     place = jnp.concatenate([jnp.stack([y, c, z]).astype(jnp.int32), starts])
@@ -204,23 +257,23 @@
 
     every = 2 * length * ctx * xs * tp * width * 3 * width
     raw, rim = call(
-        functools.partial(project, ys, offsets),
+        functools.partial(project, ys, offsets, sets),
         (
             jax.ShapeDtypeStruct((length, 3 * width), BF16),
             jax.ShapeDtypeStruct((LEAD, 3 * width), BF16),
         ),
-        [SMEM] + [HBM] * (2 * ys + 1),
+        [SMEM] + [HBM] * (2 * len(sets) + ys + 1),
         (VMEM, VMEM),
         [
             pltpu.VMEM((length, 3 * width), F32),
             pltpu.VMEM((ys, xs, tp, length, width), BF16),
-            pltpu.VMEM(weights.shape, BF16),
-            pltpu.SemaphoreType.DMA((3 * ctx,)),
+            pltpu.VMEM((ctx,) + columns.shape, BF16),
+            pltpu.SemaphoreType.DMA((4 * ctx,)),
         ],
         flops=every,
         nbytes=16 * MIB,
         vmem=VMEM_DOT,
-    )(place, *blocks, *others, weights)
+    )(place, *mine, *other, columns, *[w for pair in weights for w in pair])
     before = lax.ppermute(rim, "ctx", [(k, k + 1) for k in range(ctx - 1)])
     work = lambda rows: [
         pltpu.VMEM((rows, 3 * width), F32),

time: 116 us -> 130 us (1.12); the launches traced: 115 us -> 128 us
  starting transfers between devices: 62.1 us -> 85.5 us
  between operations: 13.9 us -> 0.62 us
  waiting for transfers between devices: 23 us -> 13.8 us
  local copies, waits for them, and re-layouts: 1.11 us -> 10 us
  other arithmetic: 1.02 us -> 3.29 us
    ppermute x15 -> x18, starting transfers between devices: 50 us -> 73.4 us  [the longest x7 36.6 us: both_ways(): lax.ppermute(pair[1], axis, hop(-1))]
    unnamed x20 -> x30, local copies, waits for them, and re-layouts: 0.05 us -> 6.42 us
    all_gather x1 -> x0, waiting for transfers between devices: 3.19 us -> none  [body(): weights = lax.all_gather(jnp.transpose(w_in, (1, 0, 2)), 'ctx', axis=0)]
    another operation x0 -> x2, other arithmetic: none -> 2.99 us  [body(): mine.append(jnp.stack(fresh))]
    ppermute x3, waiting for transfers between devices: 2.77 us -> 0.01 us  [body(): piece = lax.ppermute(own, 'fsdp', along_x(hop))]
    slice x0 -> x2, local copies, waits for them, and re-layouts: none -> 2.56 us  [body(): weights.append(both_ways([pair[0][:half], pair[1][half:]], 'ctx', along_z))]
    ppermute x15 -> x18, waiting for transfers between devices: 16.3 us -> 13.8 us  [the longest x7 6.97 us: both_ways(): lax.ppermute(pair[0], axis, hop(1))]
    pallas_call x1 -> x5, Pallas kernels: 6.99 us -> 7.63 us  [the longest x1 7.62 us: body(): call(functools.partial(project, ys, offsets, sets), (jax.ShapeDtypeStruct...]
  transfers between devices with their start and end apart: 20 -> 22, of which waited for: 7 -> 3; matrix products, arithmetic and copies ran while one was open for 2% -> 5% of each run, Pallas kernels for 3% -> 3%
where the time goes in v5:
time: 130 us; the launch traced here: 128 us
  starting transfers between devices  85.5 us (66%)
  Pallas kernels  14.3 us (11%)
  waiting for transfers between devices  13.8 us (11%)
  local copies, waits for them, and re-layouts  10 us (8%)
  other arithmetic  3.29 us (3%)
    ppermute x7, starting transfers between devices, both_ways(): lax.ppermute(pair[1], axis, hop(-1))  36.6 us
    ppermute x3, starting transfers between devices, body(): other.append(lax.ppermute(mine[-1], 'tp', swap))  18 us
    ppermute x7, starting transfers between devices, both_ways(): lax.ppermute(pair[0], axis, hop(1))  16.9 us
    ppermute x3, starting transfers between devices, body(): piece = lax.ppermute(own, 'fsdp', along_x(hop))  10.8 us
    pallas_call x1, Pallas kernels, body(): call(functools.partial(project, ys, offsets, sets), (jax.ShapeDtypeStruct...  7.62 us
    ppermute x7, waiting for transfers between devices, both_ways(): lax.ppermute(pair[0], axis, hop(1))  6.97 us
    unnamed x30, local copies, waits for them, and re-layouts  6.42 us
    ppermute x7, waiting for transfers between devices, both_ways(): lax.ppermute(pair[1], axis, hop(-1))  5.44 us
  transfers between devices with their start and end apart: 22, of which 3 were waited for; matrix products, arithmetic and copies ran while one was open for 5% of the time, Pallas kernels for 3%

profile of v5, /device:TPU:1, one launch (start us, length us, event | category | flops | bytes accessed | tf_op | source)
XLA Modules:
  0.0 127.5 jit_solution(8344512166923358308)
XLA Ops:
  0.0 3.9 %collective-permute-start = (bf16[512,128]{1,0:T(8,128)(2,1)}, bf16[512,128]{1,0:T(8,128)(2,1)S(1)}, u32[]{:S(2)}, u32[]{:S(2)}) collective-permute-start(bf16[512,128]{1,0:T(8,128)(2,1)} %bitcast.36), channel_id=1, source_target_pairs={{0,16},{16,32},{32,48},{48,0},{64,80},{80,96},{96,112},{112,64},{1... | collective-permute-start | bytes 393224 | tf_op jit(solution)/shard_map/ppermute | solution.py:233
  3.9 3.2 %collective-permute-start.2 = (bf16[512,128]{1,0:T(8,128)(2,1)}, bf16[512,128]{1,0:T(8,128)(2,1)S(1)}, u32[]{:S(2)}, u32[]{:S(2)}) collective-permute-start(bf16[512,128]{1,0:T(8,128)(2,1)} %bitcast.37), channel_id=1, source_target_pairs={{0,48},{16,0},{32,16},{48,32},{64,112},{80,64},{96,80},{112,96},{1... | collective-permute-start | bytes 393224 | tf_op jit(solution)/shard_map/ppermute | solution.py:233
  7.1 3.6 %collective-permute-start.1 = (bf16[512,128]{1,0:T(8,128)(2,1)}, bf16[512,128]{1,0:T(8,128)(2,1)S(1)}, u32[]{:S(2)}, u32[]{:S(2)}) collective-permute-start(bf16[512,128]{1,0:T(8,128)(2,1)} %bitcast.38), channel_id=1, source_target_pairs={{0,32},{16,48},{32,0},{48,16},{64,96},{80,112},{96,64},{112,80},{1... | collective-permute-start | bytes 393224 | tf_op jit(solution)/shard_map/ppermute | solution.py:233
  10.8 10.7 %collective-permute-start.5 = (bf16[6,512,128]{2,1,0:T(8,128)(2,1)}, bf16[6,512,128]{2,1,0:T(8,128)(2,1)S(1)}, u32[]{:S(2)}, u32[]{:S(2)}) collective-permute-start(bf16[6,512,128]{2,1,0:T(8,128)(2,1)} %bitcast.32), channel_id=1, source_target_pairs={{0,14},{2,0},{4,2},{6,4},{8,6},{10,8},{12,10},{14,12},{1,15},{3,1}... | collective-permute-start | bytes 2359304 | tf_op jit(solution)/shard_map/ppermute | solution.py:205
  21.5 1.9 %collective-permute-start.4 = (bf16[6,512,128]{2,1,0:T(8,128)(2,1)}, bf16[6,512,128]{2,1,0:T(8,128)(2,1)}, u32[]{:S(2)}, u32[]{:S(2)}) collective-permute-start(bf16[6,512,128]{2,1,0:T(8,128)(2,1)} %bitcast.33), channel_id=1, source_target_pairs={{0,2},{2,4},{4,6},{6,8},{8,10},{10,12},{12,14},{14,0},{1,3},{3,5},... | collective-permute-start | bytes 2359304 | tf_op jit(solution)/shard_map/ppermute | solution.py:205
  24.6 3.2 %collective-permute-start.3 = (bf16[4,512,128]{2,1,0:T(8,128)(2,1)S(1)}, bf16[4,512,128]{2,1,0:T(8,128)(2,1)}, u32[]{:S(2)}, u32[]{:S(2)}) collective-permute-start(bf16[4,512,128]{2,1,0:T(8,128)(2,1)S(1)} %bitcast_dynamic-update-slice_fusion), channel_id=1, source_target_pairs={{0,64},{16,80},{32,96},{48,112},{64,128},{80,144},{96,160},{112,17... | collective-permute-start | bytes 1572872 | tf_op jit(solution)/shard_map/ppermute | solution.py:205
  27.8 3.8 %collective-permute-start.6 = (bf16[4,512,128]{2,1,0:T(8,128)(2,1)S(1)}, bf16[4,512,128]{2,1,0:T(8,128)(2,1)S(1)}, u32[]{:S(2)}, u32[]{:S(2)}) collective-permute-start(bf16[4,512,128]{2,1,0:T(8,128)(2,1)S(1)} %bitcast_dynamic-update-slice_fusion), channel_id=1, source_target_pairs={{0,448},{16,464},{32,480},{48,496},{64,0},{80,16},{96,32},{112,48}... | collective-permute-start | bytes 1572872 | tf_op jit(solution)/shard_map/ppermute | solution.py:205
  31.6 5.4 %collective-permute-done.5.refs_2_.refs_8_ = bf16[6,512,128]{2,1,0:T(8,128)(2,1)S(1)} collective-permute-done((bf16[6,512,128]{2,1,0:T(8,128)(2,1)}, bf16[6,512,128]{2,1,0:T(8,128)(2,1)S(1)}, u32[]{:S(2)}, u32[]{:S(2)}) %collective-permute-start.5) | collective-permute-done | bytes 786464 | tf_op jit(solution)/shard_map/ppermute | solution.py:205
  37.1 5.3 %collective-permute-start.9 = (bf16[6,512,128]{2,1,0:T(8,128)(2,1)S(1)}, bf16[6,512,128]{2,1,0:T(8,128)(2,1)}, u32[]{:S(2)}, u32[]{:S(2)}) collective-permute-start(bf16[6,512,128]{2,1,0:T(8,128)(2,1)S(1)} %collective-permute-done.5.refs_2_.refs_8_), channel_id=1, source_target_pairs={{0,14},{2,0},{4,2},{6,4},{8,6},{10,8},{12,10},{14,12},{1,15},{3,1}... | collective-permute-start | bytes 2359304 | tf_op jit(solution)/shard_map/ppermute | solution.py:205
  42.4 1.9 %collective-permute-start.8 = (bf16[6,512,128]{2,1,0:T(8,128)(2,1)}, bf16[6,512,128]{2,1,0:T(8,128)(2,1)}, u32[]{:S(2)}, u32[]{:S(2)}) collective-permute-start(bf16[6,512,128]{2,1,0:T(8,128)(2,1)} %collective-permute-done.4.refs_1_.refs_7_), channel_id=1, source_target_pairs={{0,2},{2,4},{4,6},{6,8},{8,10},{10,12},{12,14},{14,0},{1,3},{3,5},... | collective-permute-start | bytes 2359304 | tf_op jit(solution)/shard_map/ppermute | solution.py:205
  44.4 3.1 %collective-permute-start.7 = (bf16[4,512,128]{2,1,0:T(8,128)(2,1)}, bf16[4,512,128]{2,1,0:T(8,128)(2,1)}, u32[]{:S(2)}, u32[]{:S(2)}) collective-permute-start(bf16[4,512,128]{2,1,0:T(8,128)(2,1)} %shard_map.64), channel_id=1, source_target_pairs={{0,64},{16,80},{32,96},{48,112},{64,128},{80,144},{96,160},{112,17... | collective-permute-start | bytes 1572872 | tf_op jit(solution)/shard_map/ppermute | solution.py:205
  47.5 3.8 %collective-permute-start.10 = (bf16[4,512,128]{2,1,0:T(8,128)(2,1)S(1)}, bf16[4,512,128]{2,1,0:T(8,128)(2,1)}, u32[]{:S(2)}, u32[]{:S(2)}) collective-permute-start(bf16[4,512,128]{2,1,0:T(8,128)(2,1)S(1)} %collective-permute-done.6), channel_id=1, source_target_pairs={{0,448},{16,464},{32,480},{48,496},{64,0},{80,16},{96,32},{112,48}... | collective-permute-start | bytes 1572872 | tf_op jit(solution)/shard_map/ppermute | solution.py:205
  51.3 1.2 pad_maximum_fusion.1.refs_0_
  52.5 4.9 %collective-permute-start.15 = (bf16[3,4,512,128]{3,2,1,0:T(8,128)(2,1)S(1)}, bf16[3,4,512,128]{3,2,1,0:T(8,128)(2,1)}, u32[]{:S(2)}, u32[]{:S(2)}) collective-permute-start(bf16[3,4,512,128]{3,2,1,0:T(8,128)(2,1)S(1)} %pad_maximum_fusion.1.refs_0_), channel_id=1, source_target_pairs={{0,1},{1,0},{2,3},{3,2},{4,5},{5,4},{6,7},{7,6},{8,9},{9,8},{10,11... | collective-permute-start | bytes 4718600 | tf_op jit(solution)/shard_map/ppermute | solution.py:244
  57.5 4.9 %collective-permute-start.14 = (bf16[6,512,128]{2,1,0:T(8,128)(2,1)}, bf16[6,512,128]{2,1,0:T(8,128)(2,1)S(1)}, u32[]{:S(2)}, u32[]{:S(2)}) collective-permute-start(bf16[6,512,128]{2,1,0:T(8,128)(2,1)} %collective-permute-done.9.refs_2_.refs_10_), channel_id=1, source_target_pairs={{0,14},{2,0},{4,2},{6,4},{8,6},{10,8},{12,10},{14,12},{1,15},{3,1}... | collective-permute-start | bytes 2359304 | tf_op jit(solution)/shard_map/ppermute | solution.py:205
  62.3 1.9 %collective-permute-start.13 = (bf16[6,512,128]{2,1,0:T(8,128)(2,1)}, bf16[6,512,128]{2,1,0:T(8,128)(2,1)}, u32[]{:S(2)}, u32[]{:S(2)}) collective-permute-start(bf16[6,512,128]{2,1,0:T(8,128)(2,1)} %collective-permute-done.8.refs_1_.refs_9_), channel_id=1, source_target_pairs={{0,2},{2,4},{4,6},{6,8},{8,10},{10,12},{12,14},{14,0},{1,3},{3,5},... | collective-permute-start | bytes 2359304 | tf_op jit(solution)/shard_map/ppermute | solution.py:205
  64.3 3.0 %collective-permute-start.11 = (bf16[4,512,128]{2,1,0:T(8,128)(2,1)}, bf16[4,512,128]{2,1,0:T(8,128)(2,1)}, u32[]{:S(2)}, u32[]{:S(2)}) collective-permute-start(bf16[4,512,128]{2,1,0:T(8,128)(2,1)} %shard_map.65), channel_id=1, source_target_pairs={{0,64},{16,80},{32,96},{48,112},{64,128},{80,144},{96,160},{112,17... | collective-permute-start | bytes 1572872 | tf_op jit(solution)/shard_map/ppermute | solution.py:205
  67.3 3.8 %collective-permute-start.12 = (bf16[4,512,128]{2,1,0:T(8,128)(2,1)}, bf16[4,512,128]{2,1,0:T(8,128)(2,1)}, u32[]{:S(2)}, u32[]{:S(2)}) collective-permute-start(bf16[4,512,128]{2,1,0:T(8,128)(2,1)} %collective-permute-done.10), channel_id=1, source_target_pairs={{0,448},{16,464},{32,480},{48,496},{64,0},{80,16},{96,32},{112,48}... | collective-permute-start | bytes 1572872 | tf_op jit(solution)/shard_map/ppermute | solution.py:205
  71.1 7.0 %collective-permute-done.11 = bf16[4,512,128]{2,1,0:T(8,128)(2,1)} collective-permute-done((bf16[4,512,128]{2,1,0:T(8,128)(2,1)}, bf16[4,512,128]{2,1,0:T(8,128)(2,1)}, u32[]{:S(2)}, u32[]{:S(2)}) %collective-permute-start.11) | collective-permute-done | bytes 524320 | tf_op jit(solution)/shard_map/ppermute | solution.py:205
  78.0 1.9 %collective-permute-start.16 = (bf16[4,512,128]{2,1,0:T(8,128)(2,1)}, bf16[4,512,128]{2,1,0:T(8,128)(2,1)S(1)}, u32[]{:S(2)}, u32[]{:S(2)}) collective-permute-start(bf16[4,512,128]{2,1,0:T(8,128)(2,1)} %collective-permute-done.11), channel_id=1, source_target_pairs={{0,64},{16,80},{32,96},{48,112},{64,128},{80,144},{96,160},{112,17... | collective-permute-start | bytes 1572872 | tf_op jit(solution)/shard_map/ppermute | solution.py:246
  81.7 4.3 %collective-permute-start.18 = (bf16[3,512,128]{2,1,0:T(8,128)(2,1)}, bf16[3,512,128]{2,1,0:T(8,128)(2,1)S(1)}, u32[]{:S(2)}, u32[]{:S(2)}) collective-permute-start(bf16[3,512,128]{2,1,0:T(8,128)(2,1)} %slice.9), channel_id=1, source_target_pairs={{0,14},{2,0},{4,2},{6,4},{8,6},{10,8},{12,10},{14,12},{1,15},{3,1}... | collective-permute-start | bytes 1179656 | tf_op jit(solution)/shard_map/ppermute | solution.py:205
  86.0 1.8 %slice.8 = bf16[3,512,128]{2,1,0:T(8,128)(2,1)} slice(bf16[6,512,128]{2,1,0:T(8,128)(2,1)} %collective-permute-done.13.refs_1_.refs_11_), slice={[0:3], [0:512], [0:128]} | slice | bytes 786432 | tf_op jit(solution)/shard_map/slice | solution.py:226
  87.7 1.9 %collective-permute-start.17 = (bf16[3,512,128]{2,1,0:T(8,128)(2,1)}, bf16[3,512,128]{2,1,0:T(8,128)(2,1)S(1)}, u32[]{:S(2)}, u32[]{:S(2)}) collective-permute-start(bf16[3,512,128]{2,1,0:T(8,128)(2,1)} %slice.8), channel_id=1, source_target_pairs={{0,2},{2,4},{4,6},{6,8},{8,10},{10,12},{12,14},{14,0},{1,3},{3,5},... | collective-permute-start | bytes 1179656 | tf_op jit(solution)/shard_map/ppermute | solution.py:205
  89.7 1.8 %pad_maximum_fusion.refs_1_ = bf16[4,4,512,128]{3,2,1,0:T(8,128)(2,1)S(1)} fusion(bf16[1,4,512,128]{3,2,1,0:T(8,128)(2,1)} %bitcast.17, bf16[1,4,512,128]{3,2,1,0:T(8,128)(2,1)} %bitcast.16, bf16[1,4,512,128]{3,2,1,0:T(8,128)(2,1)} %bitcast.15, bf16[1,4,512,128]{3,2,1,0:T(8,128)(2,1)} %bitcast.14), kind=kLoop, calls=%fused_computation | loop fusion | flops 3145728 | bytes 4194304 | tf_op jit(solution)/shard_map/stack | solution.py:243
  91.5 6.9 %collective-permute-start.19 = (bf16[4,4,512,128]{3,2,1,0:T(8,128)(2,1)S(1)}, bf16[4,4,512,128]{3,2,1,0:T(8,128)(2,1)}, u32[]{:S(2)}, u32[]{:S(2)}) collective-permute-start(bf16[4,4,512,128]{3,2,1,0:T(8,128)(2,1)S(1)} %pad_maximum_fusion.refs_1_), channel_id=1, source_target_pairs={{0,1},{1,0},{2,3},{3,2},{4,5},{5,4},{6,7},{7,6},{8,9},{9,8},{10,11... | collective-permute-start | bytes 6291464 | tf_op jit(solution)/shard_map/ppermute | solution.py:244
  100.1 6.2 %collective-permute-start.20 = (bf16[1,4,512,128]{3,2,1,0:T(8,128)(2,1)}, bf16[1,4,512,128]{3,2,1,0:T(8,128)(2,1)S(1)}, u32[]{:S(2)}, u32[]{:S(2)}) collective-permute-start(bf16[1,4,512,128]{3,2,1,0:T(8,128)(2,1)} %bitcast.25), channel_id=1, source_target_pairs={{0,1},{1,0},{2,3},{3,2},{4,5},{5,4},{6,7},{7,6},{8,9},{9,8},{10,11... | collective-permute-start | bytes 1572872 | tf_op jit(solution)/shard_map/ppermute | solution.py:249
  106.7 1.4 %collective-permute-done.20.refs_5_ = bf16[1,4,512,128]{3,2,1,0:T(8,128)(2,1)S(1)} collective-permute-done((bf16[1,4,512,128]{3,2,1,0:T(8,128)(2,1)}, bf16[1,4,512,128]{3,2,1,0:T(8,128)(2,1)S(1)}, u32[]{:S(2)}, u32[]{:S(2)}) %collective-permute-start.20) | collective-permute-done | bytes 524320 | tf_op jit(solution)/shard_map/ppermute | solution.py:249
  108.9 1.0 copy-done.1
  111.9 7.6 %shard_map.68 = (bf16[512,384]{1,0:T(8,128)(2,1)S(1)}, bf16[144,384]{1,0:T(8,128)(2,1)S(1)}) custom-call(s32[6]{0:T(128)S(1)} %pad_add_fusion.place, bf16[3,4,512,128]{3,2,1,0:T(8,128)(2,1)} %copy-done.10, bf16[4,4,512,128]{3,2,1,0:T(8,128)(2,1)} %copy-done.9, bf16[1,4,512,128]{3,2,1,0:T(8,128)(2,1)S(1)} %bitcast.26, ...), custom_call_target="tpu_custom_call" | custom-call | flops 3221225472 | bytes 16777216 | tf_op jit(solution)/shard_map/pallas_call | solution.py:259
  119.5 1.3 %collective-permute-start.21 = (bf16[144,384]{1,0:T(8,128)(2,1)S(1)}, bf16[144,384]{1,0:T(8,128)(2,1)S(1)}, u32[]{:S(2)}, u32[]{:S(2)}) collective-permute-start(bf16[144,384]{1,0:T(8,128)(2,1)S(1)} %get-tuple-element.7), channel_id=1, source_target_pairs={{0,2},{2,4},{4,6},{6,8},{8,10},{10,12},{12,14},{1,3},{3,5},{5,7},{... | collective-permute-start | bytes 331784 | tf_op jit(solution)/shard_map/ppermute | solution.py:277
  120.9 3.6 %shard_map.69.given = bf16[512,128]{1,0:T(8,128)(2,1)S(1)} custom-call(s32[6]{0:T(128)S(1)} %pad_add_fusion.place, bf16[512,384]{1,0:T(8,128)(2,1)S(1)} %get-tuple-element.8.raw, f32[7,384]{1,0:T(8,128)S(1)} %bitcast.27, f32[128,128]{1,0:T(8,128)S(1)} %copy-done.6, f32[1,128]{1,0:T(1,128)S(1)} %bitcast.29), custom_call_target="tpu_custom_call" | custom-call | flops 1610612736 | bytes 2097152 | tf_op jit(solution)/shard_map/pallas_call | solution.py:286
  124.5 3.1 %shard_map.70 = bf16[512,128]{1,0:T(8,128)(2,1)} custom-call(s32[6]{0:T(128)S(1)} %pad_add_fusion.place, bf16[144,384]{1,0:T(8,128)(2,1)S(1)} %collective-permute-done.21.before, bf16[512,384]{1,0:T(8,128)(2,1)S(1)} %get-tuple-element.8.raw, f32[7,384]{1,0:T(8,128)S(1)} %bitcast.28, f32[128,128]{1,0:T(8,128)S(1)} %copy-done.6, f32[1,128]{1,0:T(1,128)S(1)} %bitcast.30, ...), custom_call_target="tpu_custom_call" | custom-call | flops 805306368 | bytes 1048576 | tf_op jit(solution)/shard_map/pallas_call | solution.py:295
  (61 shorter events, 7.6 us)
Async XLA Ops:
  0.0 24.5 %collective-permute-start = (bf16[512,128]{1,0:T(8,128)(2,1)}, bf16[512,128]{1,0:T(8,128)(2,1)S(1)}, u32[]{:S(2)}, u32[]{:S(2)}) collective-permute-start(bf16[512,128]{1,0:T(8,128)(2,1)} %bitcast.36), channel_id=1, source_target_pairs={{0,16},{16,32},{32,48},{48,0},{64,80},{80,96},{96,112},{112,64},{1... | collective-permute-start | bytes 393224 | tf_op jit(solution)/shard_map/ppermute | solution.py:233
  3.9 20.6 %collective-permute-start.2 = (bf16[512,128]{1,0:T(8,128)(2,1)}, bf16[512,128]{1,0:T(8,128)(2,1)S(1)}, u32[]{:S(2)}, u32[]{:S(2)}) collective-permute-start(bf16[512,128]{1,0:T(8,128)(2,1)} %bitcast.37), channel_id=1, source_target_pairs={{0,48},{16,0},{32,16},{48,32},{64,112},{80,64},{96,80},{112,96},{1... | collective-permute-start | bytes 393224 | tf_op jit(solution)/shard_map/ppermute | solution.py:233
  7.1 17.4 %collective-permute-start.1 = (bf16[512,128]{1,0:T(8,128)(2,1)}, bf16[512,128]{1,0:T(8,128)(2,1)S(1)}, u32[]{:S(2)}, u32[]{:S(2)}) collective-permute-start(bf16[512,128]{1,0:T(8,128)(2,1)} %bitcast.38), channel_id=1, source_target_pairs={{0,32},{16,48},{32,0},{48,16},{64,96},{80,112},{96,64},{112,80},{1... | collective-permute-start | bytes 393224 | tf_op jit(solution)/shard_map/ppermute | solution.py:233
  10.8 26.3 %collective-permute-start.5 = (bf16[6,512,128]{2,1,0:T(8,128)(2,1)}, bf16[6,512,128]{2,1,0:T(8,128)(2,1)S(1)}, u32[]{:S(2)}, u32[]{:S(2)}) collective-permute-start(bf16[6,512,128]{2,1,0:T(8,128)(2,1)} %bitcast.32), channel_id=1, source_target_pairs={{0,14},{2,0},{4,2},{6,4},{8,6},{10,8},{12,10},{14,12},{1,15},{3,1}... | collective-permute-start | bytes 2359304 | tf_op jit(solution)/shard_map/ppermute | solution.py:205
  21.5 20.9 %collective-permute-start.4 = (bf16[6,512,128]{2,1,0:T(8,128)(2,1)}, bf16[6,512,128]{2,1,0:T(8,128)(2,1)}, u32[]{:S(2)}, u32[]{:S(2)}) collective-permute-start(bf16[6,512,128]{2,1,0:T(8,128)(2,1)} %bitcast.33), channel_id=1, source_target_pairs={{0,2},{2,4},{4,6},{6,8},{8,10},{10,12},{12,14},{14,0},{1,3},{3,5},... | collective-permute-start | bytes 2359304 | tf_op jit(solution)/shard_map/ppermute | solution.py:205
  24.6 19.7 %collective-permute-start.3 = (bf16[4,512,128]{2,1,0:T(8,128)(2,1)S(1)}, bf16[4,512,128]{2,1,0:T(8,128)(2,1)}, u32[]{:S(2)}, u32[]{:S(2)}) collective-permute-start(bf16[4,512,128]{2,1,0:T(8,128)(2,1)S(1)} %bitcast_dynamic-update-slice_fusion), channel_id=1, source_target_pairs={{0,64},{16,80},{32,96},{48,112},{64,128},{80,144},{96,160},{112,17... | collective-permute-start | bytes 1572872 | tf_op jit(solution)/shard_map/ppermute | solution.py:205
  27.8 19.6 %collective-permute-start.6 = (bf16[4,512,128]{2,1,0:T(8,128)(2,1)S(1)}, bf16[4,512,128]{2,1,0:T(8,128)(2,1)S(1)}, u32[]{:S(2)}, u32[]{:S(2)}) collective-permute-start(bf16[4,512,128]{2,1,0:T(8,128)(2,1)S(1)} %bitcast_dynamic-update-slice_fusion), channel_id=1, source_target_pairs={{0,448},{16,464},{32,480},{48,496},{64,0},{80,16},{96,32},{112,48}... | collective-permute-start | bytes 1572872 | tf_op jit(solution)/shard_map/ppermute | solution.py:205
  37.1 7.3 %copy-start.12 = (bf16[6,512,128]{2,1,0:T(8,128)(2,1)}, bf16[6,512,128]{2,1,0:T(8,128)(2,1)S(1)}, u32[]{:S(2)}) copy-start(bf16[6,512,128]{2,1,0:T(8,128)(2,1)S(1)} %collective-permute-done.5.refs_2_.refs_8_) | copy-start | bytes 2359300
  37.1 20.4 %collective-permute-start.9 = (bf16[6,512,128]{2,1,0:T(8,128)(2,1)S(1)}, bf16[6,512,128]{2,1,0:T(8,128)(2,1)}, u32[]{:S(2)}, u32[]{:S(2)}) collective-permute-start(bf16[6,512,128]{2,1,0:T(8,128)(2,1)S(1)} %collective-permute-done.5.refs_2_.refs_8_), channel_id=1, source_target_pairs={{0,14},{2,0},{4,2},{6,4},{8,6},{10,8},{12,10},{14,12},{1,15},{3,1}... | collective-permute-start | bytes 2359304 | tf_op jit(solution)/shard_map/ppermute | solution.py:205
  42.4 19.9 %collective-permute-start.8 = (bf16[6,512,128]{2,1,0:T(8,128)(2,1)}, bf16[6,512,128]{2,1,0:T(8,128)(2,1)}, u32[]{:S(2)}, u32[]{:S(2)}) collective-permute-start(bf16[6,512,128]{2,1,0:T(8,128)(2,1)} %collective-permute-done.4.refs_1_.refs_7_), channel_id=1, source_target_pairs={{0,2},{2,4},{4,6},{6,8},{8,10},{10,12},{12,14},{14,0},{1,3},{3,5},... | collective-permute-start | bytes 2359304 | tf_op jit(solution)/shard_map/ppermute | solution.py:205
  44.4 19.9 %collective-permute-start.7 = (bf16[4,512,128]{2,1,0:T(8,128)(2,1)}, bf16[4,512,128]{2,1,0:T(8,128)(2,1)}, u32[]{:S(2)}, u32[]{:S(2)}) collective-permute-start(bf16[4,512,128]{2,1,0:T(8,128)(2,1)} %shard_map.64), channel_id=1, source_target_pairs={{0,64},{16,80},{32,96},{48,112},{64,128},{80,144},{96,160},{112,17... | collective-permute-start | bytes 1572872 | tf_op jit(solution)/shard_map/ppermute | solution.py:205
  47.5 19.8 %collective-permute-start.10 = (bf16[4,512,128]{2,1,0:T(8,128)(2,1)S(1)}, bf16[4,512,128]{2,1,0:T(8,128)(2,1)}, u32[]{:S(2)}, u32[]{:S(2)}) collective-permute-start(bf16[4,512,128]{2,1,0:T(8,128)(2,1)S(1)} %collective-permute-done.6), channel_id=1, source_target_pairs={{0,448},{16,464},{32,480},{48,496},{64,0},{80,16},{96,32},{112,48}... | collective-permute-start | bytes 1572872 | tf_op jit(solution)/shard_map/ppermute | solution.py:205
  52.5 11.8 %copy-start.10 = (bf16[3,4,512,128]{3,2,1,0:T(8,128)(2,1)}, bf16[3,4,512,128]{3,2,1,0:T(8,128)(2,1)S(1)}, u32[]{:S(2)}) copy-start(bf16[3,4,512,128]{3,2,1,0:T(8,128)(2,1)S(1)} %pad_maximum_fusion.1.refs_0_) | copy-start | bytes 4718596
  52.5 37.1 %collective-permute-start.15 = (bf16[3,4,512,128]{3,2,1,0:T(8,128)(2,1)S(1)}, bf16[3,4,512,128]{3,2,1,0:T(8,128)(2,1)}, u32[]{:S(2)}, u32[]{:S(2)}) collective-permute-start(bf16[3,4,512,128]{3,2,1,0:T(8,128)(2,1)S(1)} %pad_maximum_fusion.1.refs_0_), channel_id=1, source_target_pairs={{0,1},{1,0},{2,3},{3,2},{4,5},{5,4},{6,7},{7,6},{8,9},{9,8},{10,11... | collective-permute-start | bytes 4718600 | tf_op jit(solution)/shard_map/ppermute | solution.py:244
  57.5 22.5 %collective-permute-start.14 = (bf16[6,512,128]{2,1,0:T(8,128)(2,1)}, bf16[6,512,128]{2,1,0:T(8,128)(2,1)S(1)}, u32[]{:S(2)}, u32[]{:S(2)}) collective-permute-start(bf16[6,512,128]{2,1,0:T(8,128)(2,1)} %collective-permute-done.9.refs_2_.refs_10_), channel_id=1, source_target_pairs={{0,14},{2,0},{4,2},{6,4},{8,6},{10,8},{12,10},{14,12},{1,15},{3,1}... | collective-permute-start | bytes 2359304 | tf_op jit(solution)/shard_map/ppermute | solution.py:205
  62.3 23.6 %collective-permute-start.13 = (bf16[6,512,128]{2,1,0:T(8,128)(2,1)}, bf16[6,512,128]{2,1,0:T(8,128)(2,1)}, u32[]{:S(2)}, u32[]{:S(2)}) collective-permute-start(bf16[6,512,128]{2,1,0:T(8,128)(2,1)} %collective-permute-done.8.refs_1_.refs_9_), channel_id=1, source_target_pairs={{0,2},{2,4},{4,6},{6,8},{8,10},{10,12},{12,14},{14,0},{1,3},{3,5},... | collective-permute-start | bytes 2359304 | tf_op jit(solution)/shard_map/ppermute | solution.py:205
  64.3 13.8 %collective-permute-start.11 = (bf16[4,512,128]{2,1,0:T(8,128)(2,1)}, bf16[4,512,128]{2,1,0:T(8,128)(2,1)}, u32[]{:S(2)}, u32[]{:S(2)}) collective-permute-start(bf16[4,512,128]{2,1,0:T(8,128)(2,1)} %shard_map.65), channel_id=1, source_target_pairs={{0,64},{16,80},{32,96},{48,112},{64,128},{80,144},{96,160},{112,17... | collective-permute-start | bytes 1572872 | tf_op jit(solution)/shard_map/ppermute | solution.py:205
  67.3 22.4 %collective-permute-start.12 = (bf16[4,512,128]{2,1,0:T(8,128)(2,1)}, bf16[4,512,128]{2,1,0:T(8,128)(2,1)}, u32[]{:S(2)}, u32[]{:S(2)}) collective-permute-start(bf16[4,512,128]{2,1,0:T(8,128)(2,1)} %collective-permute-done.10), channel_id=1, source_target_pairs={{0,448},{16,464},{32,480},{48,496},{64,0},{80,16},{96,32},{112,48}... | collective-permute-start | bytes 1572872 | tf_op jit(solution)/shard_map/ppermute | solution.py:205
  78.0 20.3 %collective-permute-start.16 = (bf16[4,512,128]{2,1,0:T(8,128)(2,1)}, bf16[4,512,128]{2,1,0:T(8,128)(2,1)S(1)}, u32[]{:S(2)}, u32[]{:S(2)}) collective-permute-start(bf16[4,512,128]{2,1,0:T(8,128)(2,1)} %collective-permute-done.11), channel_id=1, source_target_pairs={{0,64},{16,80},{32,96},{48,112},{64,128},{80,144},{96,160},{112,17... | collective-permute-start | bytes 1572872 | tf_op jit(solution)/shard_map/ppermute | solution.py:246
  81.7 16.7 %collective-permute-start.18 = (bf16[3,512,128]{2,1,0:T(8,128)(2,1)}, bf16[3,512,128]{2,1,0:T(8,128)(2,1)S(1)}, u32[]{:S(2)}, u32[]{:S(2)}) collective-permute-start(bf16[3,512,128]{2,1,0:T(8,128)(2,1)} %slice.9), channel_id=1, source_target_pairs={{0,14},{2,0},{4,2},{6,4},{8,6},{10,8},{12,10},{14,12},{1,15},{3,1}... | collective-permute-start | bytes 1179656 | tf_op jit(solution)/shard_map/ppermute | solution.py:205
  87.7 10.7 %collective-permute-start.17 = (bf16[3,512,128]{2,1,0:T(8,128)(2,1)}, bf16[3,512,128]{2,1,0:T(8,128)(2,1)S(1)}, u32[]{:S(2)}, u32[]{:S(2)}) collective-permute-start(bf16[3,512,128]{2,1,0:T(8,128)(2,1)} %slice.8), channel_id=1, source_target_pairs={{0,2},{2,4},{4,6},{6,8},{8,10},{10,12},{12,14},{14,0},{1,3},{3,5},... | collective-permute-start | bytes 1179656 | tf_op jit(solution)/shard_map/ppermute | solution.py:205
  91.5 8.6 %copy-start.9 = (bf16[4,4,512,128]{3,2,1,0:T(8,128)(2,1)}, bf16[4,4,512,128]{3,2,1,0:T(8,128)(2,1)S(1)}, u32[]{:S(2)}) copy-start(bf16[4,4,512,128]{3,2,1,0:T(8,128)(2,1)S(1)} %pad_maximum_fusion.refs_1_) | copy-start | bytes 6291460
  91.5 14.9 %copy-start.14 = (s32[1,4096]{1,0:T(1,128)S(1)}, s32[1,4096]{1,0:T(1,128)}, u32[]{:S(2)}) copy-start(s32[1,4096]{1,0:T(1,128)} %param.11) | copy-start | bytes 49156
  91.5 16.6 %collective-permute-start.19 = (bf16[4,4,512,128]{3,2,1,0:T(8,128)(2,1)S(1)}, bf16[4,4,512,128]{3,2,1,0:T(8,128)(2,1)}, u32[]{:S(2)}, u32[]{:S(2)}) collective-permute-start(bf16[4,4,512,128]{3,2,1,0:T(8,128)(2,1)S(1)} %pad_maximum_fusion.refs_1_), channel_id=1, source_target_pairs={{0,1},{1,0},{2,3},{3,2},{4,5},{5,4},{6,7},{7,6},{8,9},{9,8},{10,11... | collective-permute-start | bytes 6291464 | tf_op jit(solution)/shard_map/ppermute | solution.py:244
  100.1 8.0 %collective-permute-start.20 = (bf16[1,4,512,128]{3,2,1,0:T(8,128)(2,1)}, bf16[1,4,512,128]{3,2,1,0:T(8,128)(2,1)S(1)}, u32[]{:S(2)}, u32[]{:S(2)}) collective-permute-start(bf16[1,4,512,128]{3,2,1,0:T(8,128)(2,1)} %bitcast.25), channel_id=1, source_target_pairs={{0,1},{1,0},{2,3},{3,2},{4,5},{5,4},{6,7},{7,6},{8,9},{9,8},{10,11... | collective-permute-start | bytes 1572872 | tf_op jit(solution)/shard_map/ppermute | solution.py:249
  106.6 14.3 %copy-start.8 = (f32[128]{0:T(128)S(1)}, f32[128]{0:T(128)}, u32[]{:S(2)}) copy-start(f32[128]{0:T(128)} %param.10) | copy-start | bytes 1540
  108.9 1.0 copy-start.1
  109.9 1.0 copy-start.3
  110.9 1.0 copy-start.5
  111.9 8.9 %copy-start.6 = (f32[128,128]{1,0:T(8,128)S(1)}, f32[128,128]{1,0:T(8,128)}, u32[]{:S(2)}) copy-start(f32[128,128]{1,0:T(8,128)} %taps.3) | copy-start | bytes 196612
  111.9 9.0 %copy-start.7 = (f32[7,3,128]{2,0,1:T(8,128)S(1)}, f32[7,3,128]{2,0,1:T(8,128)}, u32[]{:S(2)}) copy-start(f32[7,3,128]{2,0,1:T(8,128)} %param.8) | copy-start | bytes 32260
  119.5 4.9 %collective-permute-start.21 = (bf16[144,384]{1,0:T(8,128)(2,1)S(1)}, bf16[144,384]{1,0:T(8,128)(2,1)S(1)}, u32[]{:S(2)}, u32[]{:S(2)}) collective-permute-start(bf16[144,384]{1,0:T(8,128)(2,1)S(1)} %get-tuple-element.7), channel_id=1, source_target_pairs={{0,2},{2,4},{4,6},{6,8},{8,10},{10,12},{12,14},{1,3},{3,5},{5,7},{... | collective-permute-start | bytes 331784 | tf_op jit(solution)/shard_map/ppermute | solution.py:277
  (5 other events, 4.2 us)

commit v6 on v5

--- a/solution.py
+++ b/solution.py
@@ -21,7 +21,6 @@
 HBM = pl.BlockSpec(memory_space=pltpu.HBM)
 MIB = 1 << 20
 COST = 20 << 30
-PACE = 2
 
 
 def call(kernel, out_shape, in_specs, out_specs, scratch=(), flops=0, nbytes=0, vmem=8):
@@ -42,53 +41,42 @@
 
 def project(count, offsets, sets, place, *refs):
     mine, other, refs = refs[: len(sets)], refs[len(sets) : 2 * len(sets)], refs[2 * len(sets) :]
-    whole, halves, refs = refs[: count - 1], refs[count - 1 : count + 1], refs[count + 1 :]
+    parts, refs = refs[:count], refs[count:]
     raw, rim, total, held, weights, sem = refs
     core = place[1]
     where = [(a, i) for a, size in enumerate(sets) for i in range(size)]
-    half = halves[0].shape[0]
+    sign = 1 - 2 * core
 
     def landing(k):
         a, i = where[k]
+        b, j = where[offsets.index(-offsets[k])] if 0 < k < count - 1 else where[k]
         return [
             pltpu.make_async_copy(mine[a].at[i], held.at[k, :, core], sem.at[4 * k]),
-            pltpu.make_async_copy(other[a].at[i], held.at[k, :, 1 - core], sem.at[4 * k + 1]),
+            pltpu.make_async_copy(other[b].at[j], held.at[k, :, 1 - core], sem.at[4 * k + 1]),
         ]
 
-    def weight_halves(k, j):
-        first, second = weights.at[k, :half], weights.at[k, half:]
-        sources = halves if j == count - 1 else (whole[j].at[:half], whole[j].at[half:])
-        return [
-            pltpu.make_async_copy(sources[0], first, sem.at[4 * k + 2]),
-            pltpu.make_async_copy(sources[1], second, sem.at[4 * k + 3]),
-        ]
+    def panel(k, j):
+        return pltpu.make_async_copy(parts[j], weights.at[k], sem.at[4 * k + 2])
 
     def start(k):
         for copy in landing(k):
             copy.start()
         for j in range(count):
-            gap = place[0] + offsets[k] - place[2] - offsets[j]
+            gap = place[0] - place[2] + sign * (offsets[k] - offsets[j])
 
             @pl.when(lax.rem(gap + 2 * count, count) == 0)
             def _():
-                for copy in weight_halves(k, j):
-                    copy.start()
+                panel(k, j).start()
 
     for k in range(min(AHEAD, count)):
         start(k)
     for k in range(count):
         if k + AHEAD < count:
             start(k + AHEAD)
-        for copy in landing(k) + weight_halves(k, count - 1):
+        for copy in landing(k) + [panel(k, 0)]:
             copy.wait()
         left = [held[k, j, c] for j in range(held.shape[1]) for c in range(held.shape[2])]
-        per = weights.shape[1] // 3
-        columns = [
-            jnp.concatenate([weights[k, g * per + h] for h in range(per)], 0) for g in range(3)
-        ]
-        term = jnp.dot(
-            jnp.concatenate(left, 1), jnp.concatenate(columns, 1), preferred_element_type=F32
-        )
+        term = jnp.dot(jnp.concatenate(left, 1), wide(weights[k]), preferred_element_type=F32)
         if k == 0:
             total[...] = term
         elif k < count - 1:
@@ -201,8 +189,8 @@
     )(value, *others)
 
 
-def both_ways(pair, axis, hop):
-    return [lax.ppermute(pair[0], axis, hop(1)), lax.ppermute(pair[1], axis, hop(-1))]
+def both_ways(pair, axis, first, second):
+    return [lax.ppermute(pair[0], axis, first), lax.ppermute(pair[1], axis, second)]
 
 
 def body(tokens, w_in, short_taps, mr_taps, skip, genome_ids):
@@ -214,16 +202,22 @@
     x, y = f % xs, f // xs
 
     along_x = lambda d: [(j * xs + i, j * xs + (i + d) % xs) for j in range(ys) for i in range(xs)]
-    along_y = lambda d: [(j * xs + i, (j + d) % ys * xs + i) for j in range(ys) for i in range(xs)]
+    along_y = lambda d: [
+        ((j * xs + i) * tp + t, ((j + d - 2 * d * t) % ys * xs + i) * tp + t)
+        for j in range(ys) for i in range(xs) for t in range(tp)
+    ]
+    along_z = lambda d: [
+        (k * tp + t, (k + d - 2 * d * t) % ctx * tp + t) for k in range(ctx) for t in range(tp)
+    ]
+    on_y, on_z = ("fsdp", "tp"), ("ctx", "tp")
     swap = [(0, 1), (1, 0)]
 
-    along_z = lambda d: [(k, (k + d) % ctx) for k in range(ctx)]
-    columns = jnp.transpose(w_in, (1, 0, 2)).reshape(6, -1, width)
-    weights, pair, half = [], [columns, columns], columns.shape[0] // 2
+    columns = jnp.transpose(w_in, (1, 0, 2))
+    weights, pair = [], [columns, columns]
     for _ in range(1, ctx // 2):
-        pair = both_ways(pair, "ctx", along_z)
+        pair = both_ways(pair, on_z, along_z(1), along_z(-1))
         weights.append(pair)
-    weights.append(both_ways([pair[0][:half], pair[1][half:]], "ctx", along_z))
+    weights.append([lax.ppermute(pair[0], on_z, along_z(1))])
 
     own = tokens[0]
     block = jnp.zeros((xs,) + own.shape, BF16)
@@ -234,19 +228,23 @@
         block = lax.dynamic_update_index_in_dim(block, piece, (x - hop) % xs, 0)
     offsets, pair, fresh, mine, other = [0], [block, block], [block], [], []
     for r in range(1, ys // 2):
-        pair = both_ways(pair, "fsdp", along_y)
+        pair = both_ways(pair, on_y, along_y(1), along_y(-1))
         early = weights[r - 1] + other[:1] if r == 3 else weights[r - 1]
-        k = 0 if r <= PACE else 1
+        k = 0 if r <= 2 else 1
         pair[k] = after(pair[k], early, COST)
         fresh, offsets = fresh + pair, offsets + [-r, r]
         if r in (1, ys // 2 - 1):
             mine.append(jnp.stack(fresh))
             other.append(lax.ppermute(mine[-1], "tp", swap))
             fresh = []
-    final = lax.ppermute(pair[0], "fsdp", along_y(1))
+    final = lax.ppermute(pair[0], on_y, along_y(1))
+    crossed = lax.ppermute(pair[0], on_y, [(i, j // tp * tp + 1 - j % tp) for i, j in along_y(1)])
     final = after(final, weights[-1], COST)
-    mine.append(jnp.stack(fresh + [final]))
-    other.append(lax.ppermute(mine[-1], "tp", swap))
+    if fresh:
+        mine.append(jnp.stack(fresh))
+        other.append(lax.ppermute(mine[-1], "tp", swap))
+    mine.append(final[None])
+    other.append(crossed[None])
     offsets = tuple(offsets + [-(ys // 2)])
     sets = tuple(m.shape[0] for m in mine)
 
@@ -262,7 +260,7 @@
             jax.ShapeDtypeStruct((length, 3 * width), BF16),
             jax.ShapeDtypeStruct((LEAD, 3 * width), BF16),
         ),
-        [SMEM] + [HBM] * (2 * len(sets) + ys + 1),
+        [SMEM] + [HBM] * (2 * len(sets) + ys),
         (VMEM, VMEM),
         [
             pltpu.VMEM((length, 3 * width), F32),

time: 130 us -> 128 us (0.985); the launches traced: 128 us -> 128 us
  waiting for transfers between devices: 13.8 us -> 21.2 us
  local copies, waits for them, and re-layouts: 10 us -> 4 us
    ppermute x15, waiting for transfers between devices: 12.4 us -> 21.2 us  [the longest x6 12.4 us: both_ways(): lax.ppermute(pair[0], axis, first)]
    ppermute x3 -> x2, starting transfers between devices: 18 us -> 10.7 us  [body(): other.append(lax.ppermute(mine[-1], 'tp', swap))]
    ppermute x15, starting transfers between devices: 55.4 us -> 61.5 us  [the longest x6 34.2 us: both_ways(): lax.ppermute(pair[0], axis, first)]
    unnamed x30 -> x22, local copies, waits for them, and re-layouts: 6.42 us -> 2.94 us
    slice x2 -> x0, local copies, waits for them, and re-layouts: 2.56 us -> none  [body(): weights.append(both_ways([pair[0][:half], pair[1][half:]], 'ctx', along_z))]
    ppermute x3 -> x2, waiting for transfers between devices: 1.39 us -> 0.01 us  [body(): other.append(lax.ppermute(mine[-1], 'tp', swap))]
  transfers between devices with their start and end apart: 22 -> 21, of which waited for: 3 -> 5; matrix products, arithmetic and copies ran while one was open for 5% -> 3% of each run, Pallas kernels for 3% -> 3%
where the time goes in v6:
time: 128 us
  starting transfers between devices  84.3 us (66%)
  waiting for transfers between devices  21.2 us (17%)
  Pallas kernels  14.2 us (11%)
  local copies, waits for them, and re-layouts  4 us (3%)
  other arithmetic  3.29 us (3%)
    ppermute x6, starting transfers between devices, both_ways(): lax.ppermute(pair[0], axis, first)  34.2 us
    ppermute x6, starting transfers between devices, both_ways(): lax.ppermute(pair[1], axis, second)  13.6 us
    ppermute x6, waiting for transfers between devices, both_ways(): lax.ppermute(pair[0], axis, first)  12.4 us
    ppermute x3, starting transfers between devices, body(): piece = lax.ppermute(own, 'fsdp', along_x(hop))  10.8 us
    ppermute x2, starting transfers between devices, body(): other.append(lax.ppermute(mine[-1], 'tp', swap))  10.7 us
    ppermute x1, waiting for transfers between devices, body(): lax.ppermute(pair[0], on_y, [(i, j // tp * tp + 1 - j % tp) for i, j in a...  7.5 us
    pallas_call x1, Pallas kernels, body(): call(functools.partial(project, ys, offsets, sets), (jax.ShapeDtypeStruct...  7.26 us
    ppermute x1, starting transfers between devices, body(): final = lax.ppermute(pair[0], on_y, along_y(1))  5.31 us
  transfers between devices with their start and end apart: 21, of which 5 were waited for; matrix products, arithmetic and copies ran while one was open for 3% of the time, Pallas kernels for 3%

profile of v6, /device:TPU:1, one launch (start us, length us, event | category | flops | bytes accessed | tf_op | source)
XLA Modules:
  0.0 127.6 jit_solution(9607024801462750219)
XLA Ops:
  0.0 3.9 %collective-permute-start = (bf16[512,128]{1,0:T(8,128)(2,1)}, bf16[512,128]{1,0:T(8,128)(2,1)S(1)}, u32[]{:S(2)}, u32[]{:S(2)}) collective-permute-start(bf16[512,128]{1,0:T(8,128)(2,1)} %bitcast.36), channel_id=1, source_target_pairs={{0,16},{16,32},{32,48},{48,0},{64,80},{80,96},{96,112},{112,64},{1... | collective-permute-start | bytes 393224 | tf_op jit(solution)/shard_map/ppermute | solution.py:227
  3.9 3.2 %collective-permute-start.2 = (bf16[512,128]{1,0:T(8,128)(2,1)}, bf16[512,128]{1,0:T(8,128)(2,1)S(1)}, u32[]{:S(2)}, u32[]{:S(2)}) collective-permute-start(bf16[512,128]{1,0:T(8,128)(2,1)} %bitcast.37), channel_id=1, source_target_pairs={{0,48},{16,0},{32,16},{48,32},{64,112},{80,64},{96,80},{112,96},{1... | collective-permute-start | bytes 393224 | tf_op jit(solution)/shard_map/ppermute | solution.py:227
  7.1 3.6 %collective-permute-start.1 = (bf16[512,128]{1,0:T(8,128)(2,1)}, bf16[512,128]{1,0:T(8,128)(2,1)S(1)}, u32[]{:S(2)}, u32[]{:S(2)}) collective-permute-start(bf16[512,128]{1,0:T(8,128)(2,1)} %bitcast.38), channel_id=1, source_target_pairs={{0,32},{16,48},{32,0},{48,16},{64,96},{80,112},{96,64},{112,80},{1... | collective-permute-start | bytes 393224 | tf_op jit(solution)/shard_map/ppermute | solution.py:227
  10.8 4.0 %collective-permute-start.5 = (bf16[3,1024,128]{2,1,0:T(8,128)(2,1)}, bf16[3,1024,128]{2,1,0:T(8,128)(2,1)S(1)}, u32[]{:S(2)}, u32[]{:S(2)}) collective-permute-start(bf16[3,1024,128]{2,1,0:T(8,128)(2,1)} %bitcast.31), channel_id=1, source_target_pairs={{0,14},{1,3},{2,0},{3,5},{4,2},{5,7},{6,4},{7,9},{8,6},{9,11},{10,... | collective-permute-start | bytes 2359304 | tf_op jit(solution)/shard_map/ppermute | solution.py:193
  14.8 8.6 %collective-permute-start.4 = (bf16[3,1024,128]{2,1,0:T(8,128)(2,1)}, bf16[3,1024,128]{2,1,0:T(8,128)(2,1)}, u32[]{:S(2)}, u32[]{:S(2)}) collective-permute-start(bf16[3,1024,128]{2,1,0:T(8,128)(2,1)} %bitcast.32), channel_id=1, source_target_pairs={{0,2},{1,15},{2,4},{3,1},{4,6},{5,3},{6,8},{7,5},{8,10},{9,7},{10,... | collective-permute-start | bytes 2359304 | tf_op jit(solution)/shard_map/ppermute | solution.py:193
  24.6 5.1 %collective-permute-start.3 = (bf16[4,512,128]{2,1,0:T(8,128)(2,1)S(1)}, bf16[4,512,128]{2,1,0:T(8,128)(2,1)}, u32[]{:S(2)}, u32[]{:S(2)}) collective-permute-start(bf16[4,512,128]{2,1,0:T(8,128)(2,1)S(1)} %bitcast_dynamic-update-slice_fusion), channel_id=1, source_target_pairs={{0,64},{1,449},{16,80},{17,465},{32,96},{33,481},{48,112},{49,497}... | collective-permute-start | bytes 1572872 | tf_op jit(solution)/shard_map/ppermute | solution.py:193
  29.7 1.9 %collective-permute-start.6 = (bf16[4,512,128]{2,1,0:T(8,128)(2,1)S(1)}, bf16[4,512,128]{2,1,0:T(8,128)(2,1)S(1)}, u32[]{:S(2)}, u32[]{:S(2)}) collective-permute-start(bf16[4,512,128]{2,1,0:T(8,128)(2,1)S(1)} %bitcast_dynamic-update-slice_fusion), channel_id=1, source_target_pairs={{0,448},{1,65},{16,464},{17,81},{32,480},{33,97},{48,496},{49,113}... | collective-permute-start | bytes 1572872 | tf_op jit(solution)/shard_map/ppermute | solution.py:193
  31.6 1.3 %collective-permute-done.5.refs_2_.refs_8_ = bf16[3,1024,128]{2,1,0:T(8,128)(2,1)S(1)} collective-permute-done((bf16[3,1024,128]{2,1,0:T(8,128)(2,1)}, bf16[3,1024,128]{2,1,0:T(8,128)(2,1)S(1)}, u32[]{:S(2)}, u32[]{:S(2)}) %collective-permute-start.5) | collective-permute-done | bytes 786464 | tf_op jit(solution)/shard_map/ppermute | solution.py:193
  33.0 1.9 %collective-permute-start.9 = (bf16[3,1024,128]{2,1,0:T(8,128)(2,1)S(1)}, bf16[3,1024,128]{2,1,0:T(8,128)(2,1)}, u32[]{:S(2)}, u32[]{:S(2)}) collective-permute-start(bf16[3,1024,128]{2,1,0:T(8,128)(2,1)S(1)} %collective-permute-done.5.refs_2_.refs_8_), channel_id=1, source_target_pairs={{0,14},{1,3},{2,0},{3,5},{4,2},{5,7},{6,4},{7,9},{8,6},{9,11},{10,... | collective-permute-start | bytes 2359304 | tf_op jit(solution)/shard_map/ppermute | solution.py:193
  34.9 6.1 %collective-permute-done.4.refs_1_.refs_7_ = bf16[3,1024,128]{2,1,0:T(8,128)(2,1)} collective-permute-done((bf16[3,1024,128]{2,1,0:T(8,128)(2,1)}, bf16[3,1024,128]{2,1,0:T(8,128)(2,1)}, u32[]{:S(2)}, u32[]{:S(2)}) %collective-permute-start.4) | collective-permute-done | bytes 786464 | tf_op jit(solution)/shard_map/ppermute | solution.py:193
  41.0 5.3 %collective-permute-start.8 = (bf16[3,1024,128]{2,1,0:T(8,128)(2,1)}, bf16[3,1024,128]{2,1,0:T(8,128)(2,1)}, u32[]{:S(2)}, u32[]{:S(2)}) collective-permute-start(bf16[3,1024,128]{2,1,0:T(8,128)(2,1)} %collective-permute-done.4.refs_1_.refs_7_), channel_id=1, source_target_pairs={{0,2},{1,15},{2,4},{3,1},{4,6},{5,3},{6,8},{7,5},{8,10},{9,7},{10,... | collective-permute-start | bytes 2359304 | tf_op jit(solution)/shard_map/ppermute | solution.py:193
  46.4 5.0 %collective-permute-start.7 = (bf16[4,512,128]{2,1,0:T(8,128)(2,1)}, bf16[4,512,128]{2,1,0:T(8,128)(2,1)}, u32[]{:S(2)}, u32[]{:S(2)}) collective-permute-start(bf16[4,512,128]{2,1,0:T(8,128)(2,1)} %shard_map.64), channel_id=1, source_target_pairs={{0,64},{1,449},{16,80},{17,465},{32,96},{33,481},{48,112},{49,497}... | collective-permute-start | bytes 1572872 | tf_op jit(solution)/shard_map/ppermute | solution.py:193
  51.4 1.9 %collective-permute-start.10 = (bf16[4,512,128]{2,1,0:T(8,128)(2,1)S(1)}, bf16[4,512,128]{2,1,0:T(8,128)(2,1)}, u32[]{:S(2)}, u32[]{:S(2)}) collective-permute-start(bf16[4,512,128]{2,1,0:T(8,128)(2,1)S(1)} %collective-permute-done.6), channel_id=1, source_target_pairs={{0,448},{1,65},{16,464},{17,81},{32,480},{33,97},{48,496},{49,113}... | collective-permute-start | bytes 1572872 | tf_op jit(solution)/shard_map/ppermute | solution.py:193
  53.3 1.2 pad_maximum_fusion.1.refs_0_
  54.5 5.0 %collective-permute-start.15 = (bf16[3,4,512,128]{3,2,1,0:T(8,128)(2,1)S(1)}, bf16[3,4,512,128]{3,2,1,0:T(8,128)(2,1)}, u32[]{:S(2)}, u32[]{:S(2)}) collective-permute-start(bf16[3,4,512,128]{3,2,1,0:T(8,128)(2,1)S(1)} %pad_maximum_fusion.1.refs_0_), channel_id=1, source_target_pairs={{0,1},{1,0},{2,3},{3,2},{4,5},{5,4},{6,7},{7,6},{8,9},{9,8},{10,11... | collective-permute-start | bytes 4718600 | tf_op jit(solution)/shard_map/ppermute | solution.py:238
  59.5 1.9 %collective-permute-start.14 = (bf16[3,1024,128]{2,1,0:T(8,128)(2,1)}, bf16[3,1024,128]{2,1,0:T(8,128)(2,1)S(1)}, u32[]{:S(2)}, u32[]{:S(2)}) collective-permute-start(bf16[3,1024,128]{2,1,0:T(8,128)(2,1)} %collective-permute-done.9.refs_2_.refs_10_), channel_id=1, source_target_pairs={{0,14},{1,3},{2,0},{3,5},{4,2},{5,7},{6,4},{7,9},{8,6},{9,11},{10,... | collective-permute-start | bytes 2359304 | tf_op jit(solution)/shard_map/ppermute | solution.py:193
  61.5 2.0 %collective-permute-done.8.refs_1_.refs_9_ = bf16[3,1024,128]{2,1,0:T(8,128)(2,1)} collective-permute-done((bf16[3,1024,128]{2,1,0:T(8,128)(2,1)}, bf16[3,1024,128]{2,1,0:T(8,128)(2,1)}, u32[]{:S(2)}, u32[]{:S(2)}) %collective-permute-start.8) | collective-permute-done | bytes 786464 | tf_op jit(solution)/shard_map/ppermute | solution.py:193
  63.4 5.3 %collective-permute-start.13 = (bf16[3,1024,128]{2,1,0:T(8,128)(2,1)}, bf16[3,1024,128]{2,1,0:T(8,128)(2,1)}, u32[]{:S(2)}, u32[]{:S(2)}) collective-permute-start(bf16[3,1024,128]{2,1,0:T(8,128)(2,1)} %collective-permute-done.8.refs_1_.refs_9_), channel_id=1, source_target_pairs={{0,2},{1,15},{2,4},{3,1},{4,6},{5,3},{6,8},{7,5},{8,10},{9,7},{10,... | collective-permute-start | bytes 2359304 | tf_op jit(solution)/shard_map/ppermute | solution.py:193
  68.8 4.9 %collective-permute-start.11 = (bf16[4,512,128]{2,1,0:T(8,128)(2,1)}, bf16[4,512,128]{2,1,0:T(8,128)(2,1)}, u32[]{:S(2)}, u32[]{:S(2)}) collective-permute-start(bf16[4,512,128]{2,1,0:T(8,128)(2,1)} %shard_map.65), channel_id=1, source_target_pairs={{0,64},{1,449},{16,80},{17,465},{32,96},{33,481},{48,112},{49,497}... | collective-permute-start | bytes 1572872 | tf_op jit(solution)/shard_map/ppermute | solution.py:193
  73.7 1.9 %collective-permute-start.12 = (bf16[4,512,128]{2,1,0:T(8,128)(2,1)}, bf16[4,512,128]{2,1,0:T(8,128)(2,1)S(1)}, u32[]{:S(2)}, u32[]{:S(2)}) collective-permute-start(bf16[4,512,128]{2,1,0:T(8,128)(2,1)} %collective-permute-done.10), channel_id=1, source_target_pairs={{0,448},{1,65},{16,464},{17,81},{32,480},{33,97},{48,496},{49,113}... | collective-permute-start | bytes 1572872 | tf_op jit(solution)/shard_map/ppermute | solution.py:193
  75.9 4.2 %collective-permute-done.11 = bf16[4,512,128]{2,1,0:T(8,128)(2,1)} collective-permute-done((bf16[4,512,128]{2,1,0:T(8,128)(2,1)}, bf16[4,512,128]{2,1,0:T(8,128)(2,1)}, u32[]{:S(2)}, u32[]{:S(2)}) %collective-permute-start.11) | collective-permute-done | bytes 524320 | tf_op jit(solution)/shard_map/ppermute | solution.py:193
  80.1 5.3 %collective-permute-start.16 = (bf16[4,512,128]{2,1,0:T(8,128)(2,1)}, bf16[4,512,128]{2,1,0:T(8,128)(2,1)S(1)}, u32[]{:S(2)}, u32[]{:S(2)}) collective-permute-start(bf16[4,512,128]{2,1,0:T(8,128)(2,1)} %collective-permute-done.11), channel_id=1, source_target_pairs={{0,64},{1,449},{16,80},{17,465},{32,96},{33,481},{48,112},{49,497}... | collective-permute-start | bytes 1572872 | tf_op jit(solution)/shard_map/ppermute | solution.py:240
  85.4 4.9 %collective-permute-start.17 = (bf16[3,1024,128]{2,1,0:T(8,128)(2,1)}, bf16[3,1024,128]{2,1,0:T(8,128)(2,1)}, u32[]{:S(2)}, u32[]{:S(2)}) collective-permute-start(bf16[3,1024,128]{2,1,0:T(8,128)(2,1)} %collective-permute-done.13.refs_1_.refs_11_), channel_id=1, source_target_pairs={{0,2},{1,15},{2,4},{3,1},{4,6},{5,3},{6,8},{7,5},{8,10},{9,7},{10,... | collective-permute-start | bytes 2359304 | tf_op jit(solution)/shard_map/ppermute | solution.py:220
  91.4 1.8 %pad_maximum_fusion.refs_1_ = bf16[4,4,512,128]{3,2,1,0:T(8,128)(2,1)S(1)} fusion(bf16[1,4,512,128]{3,2,1,0:T(8,128)(2,1)} %bitcast.35, bf16[1,4,512,128]{3,2,1,0:T(8,128)(2,1)} %bitcast.14, bf16[1,4,512,128]{3,2,1,0:T(8,128)(2,1)} %bitcast.13, bf16[1,4,512,128]{3,2,1,0:T(8,128)(2,1)} %bitcast.12), kind=kLoop, calls=%fused_computation | loop fusion | flops 3145728 | bytes 4194304 | tf_op jit(solution)/shard_map/stack | solution.py:237
  93.2 5.7 %collective-permute-start.18 = (bf16[4,4,512,128]{3,2,1,0:T(8,128)(2,1)S(1)}, bf16[4,4,512,128]{3,2,1,0:T(8,128)(2,1)}, u32[]{:S(2)}, u32[]{:S(2)}) collective-permute-start(bf16[4,4,512,128]{3,2,1,0:T(8,128)(2,1)S(1)} %pad_maximum_fusion.refs_1_), channel_id=1, source_target_pairs={{0,1},{1,0},{2,3},{3,2},{4,5},{5,4},{6,7},{7,6},{8,9},{9,8},{10,11... | collective-permute-start | bytes 6291464 | tf_op jit(solution)/shard_map/ppermute | solution.py:238
  99.1 3.6 %collective-permute-start.19 = (bf16[4,512,128]{2,1,0:T(8,128)(2,1)}, bf16[4,512,128]{2,1,0:T(8,128)(2,1)S(1)}, u32[]{:S(2)}, u32[]{:S(2)}) collective-permute-start(bf16[4,512,128]{2,1,0:T(8,128)(2,1)} %collective-permute-done.11), channel_id=1, source_target_pairs={{0,65},{1,448},{16,81},{17,464},{32,97},{33,480},{48,113},{49,496}... | collective-permute-start | bytes 1572872 | tf_op jit(solution)/shard_map/ppermute | solution.py:241
  103.5 7.5 %collective-permute-done.19 = bf16[4,512,128]{2,1,0:T(8,128)(2,1)S(1)} collective-permute-done((bf16[4,512,128]{2,1,0:T(8,128)(2,1)}, bf16[4,512,128]{2,1,0:T(8,128)(2,1)S(1)}, u32[]{:S(2)}, u32[]{:S(2)}) %collective-permute-start.19) | collective-permute-done | bytes 524320 | tf_op jit(solution)/shard_map/ppermute | solution.py:241
  111.0 1.0 copy-done.1
  112.0 7.3 %shard_map.68 = (bf16[512,384]{1,0:T(8,128)(2,1)S(1)}, bf16[144,384]{1,0:T(8,128)(2,1)S(1)}) custom-call(s32[6]{0:T(128)S(1)} %pad_add_fusion.place, bf16[3,4,512,128]{3,2,1,0:T(8,128)(2,1)} %copy-done.6, bf16[4,4,512,128]{3,2,1,0:T(8,128)(2,1)} %copy-done.5, bf16[1,4,512,128]{3,2,1,0:T(8,128)(2,1)S(1)} %bitcast.24, ...), custom_call_target="tpu_custom_call" | custom-call | flops 3221225472 | bytes 16777216 | tf_op jit(solution)/shard_map/pallas_call | solution.py:257
  119.3 1.3 %collective-permute-start.20 = (bf16[144,384]{1,0:T(8,128)(2,1)S(1)}, bf16[144,384]{1,0:T(8,128)(2,1)S(1)}, u32[]{:S(2)}, u32[]{:S(2)}) collective-permute-start(bf16[144,384]{1,0:T(8,128)(2,1)S(1)} %get-tuple-element.7), channel_id=1, source_target_pairs={{0,2},{2,4},{4,6},{6,8},{8,10},{10,12},{12,14},{1,3},{3,5},{5,7},{... | collective-permute-start | bytes 331784 | tf_op jit(solution)/shard_map/ppermute | solution.py:275
  120.6 3.9 %shard_map.69.given = bf16[512,128]{1,0:T(8,128)(2,1)S(1)} custom-call(s32[6]{0:T(128)S(1)} %pad_add_fusion.place, bf16[512,384]{1,0:T(8,128)(2,1)S(1)} %get-tuple-element.8.raw, f32[7,384]{1,0:T(8,128)S(1)} %bitcast.26, f32[128,128]{1,0:T(8,128)S(1)} %copy-done.2, f32[1,128]{1,0:T(1,128)S(1)} %bitcast.28), custom_call_target="tpu_custom_call" | custom-call | flops 1610612736 | bytes 2097152 | tf_op jit(solution)/shard_map/pallas_call | solution.py:284
  124.5 3.1 %shard_map.70 = bf16[512,128]{1,0:T(8,128)(2,1)} custom-call(s32[6]{0:T(128)S(1)} %pad_add_fusion.place, bf16[144,384]{1,0:T(8,128)(2,1)S(1)} %collective-permute-done.20.before, bf16[512,384]{1,0:T(8,128)(2,1)S(1)} %get-tuple-element.8.raw, f32[7,384]{1,0:T(8,128)S(1)} %bitcast.27, f32[128,128]{1,0:T(8,128)S(1)} %copy-done.2, f32[1,128]{1,0:T(1,128)S(1)} %bitcast.29, ...), custom_call_target="tpu_custom_call" | custom-call | flops 805306368 | bytes 1048576 | tf_op jit(solution)/shard_map/pallas_call | solution.py:293
  (49 shorter events, 3.3 us)
Async XLA Ops:
  0.0 24.5 %collective-permute-start = (bf16[512,128]{1,0:T(8,128)(2,1)}, bf16[512,128]{1,0:T(8,128)(2,1)S(1)}, u32[]{:S(2)}, u32[]{:S(2)}) collective-permute-start(bf16[512,128]{1,0:T(8,128)(2,1)} %bitcast.36), channel_id=1, source_target_pairs={{0,16},{16,32},{32,48},{48,0},{64,80},{80,96},{96,112},{112,64},{1... | collective-permute-start | bytes 393224 | tf_op jit(solution)/shard_map/ppermute | solution.py:227
  3.9 20.6 %collective-permute-start.2 = (bf16[512,128]{1,0:T(8,128)(2,1)}, bf16[512,128]{1,0:T(8,128)(2,1)S(1)}, u32[]{:S(2)}, u32[]{:S(2)}) collective-permute-start(bf16[512,128]{1,0:T(8,128)(2,1)} %bitcast.37), channel_id=1, source_target_pairs={{0,48},{16,0},{32,16},{48,32},{64,112},{80,64},{96,80},{112,96},{1... | collective-permute-start | bytes 393224 | tf_op jit(solution)/shard_map/ppermute | solution.py:227
  7.1 17.4 %collective-permute-start.1 = (bf16[512,128]{1,0:T(8,128)(2,1)}, bf16[512,128]{1,0:T(8,128)(2,1)S(1)}, u32[]{:S(2)}, u32[]{:S(2)}) collective-permute-start(bf16[512,128]{1,0:T(8,128)(2,1)} %bitcast.38), channel_id=1, source_target_pairs={{0,32},{16,48},{32,0},{48,16},{64,96},{80,112},{96,64},{112,80},{1... | collective-permute-start | bytes 393224 | tf_op jit(solution)/shard_map/ppermute | solution.py:227
  10.8 22.2 %collective-permute-start.5 = (bf16[3,1024,128]{2,1,0:T(8,128)(2,1)}, bf16[3,1024,128]{2,1,0:T(8,128)(2,1)S(1)}, u32[]{:S(2)}, u32[]{:S(2)}) collective-permute-start(bf16[3,1024,128]{2,1,0:T(8,128)(2,1)} %bitcast.31), channel_id=1, source_target_pairs={{0,14},{1,3},{2,0},{3,5},{4,2},{5,7},{6,4},{7,9},{8,6},{9,11},{10,... | collective-permute-start | bytes 2359304 | tf_op jit(solution)/shard_map/ppermute | solution.py:193
  14.8 26.2 %collective-permute-start.4 = (bf16[3,1024,128]{2,1,0:T(8,128)(2,1)}, bf16[3,1024,128]{2,1,0:T(8,128)(2,1)}, u32[]{:S(2)}, u32[]{:S(2)}) collective-permute-start(bf16[3,1024,128]{2,1,0:T(8,128)(2,1)} %bitcast.32), channel_id=1, source_target_pairs={{0,2},{1,15},{2,4},{3,1},{4,6},{5,3},{6,8},{7,5},{8,10},{9,7},{10,... | collective-permute-start | bytes 2359304 | tf_op jit(solution)/shard_map/ppermute | solution.py:193
  24.6 21.7 %collective-permute-start.3 = (bf16[4,512,128]{2,1,0:T(8,128)(2,1)S(1)}, bf16[4,512,128]{2,1,0:T(8,128)(2,1)}, u32[]{:S(2)}, u32[]{:S(2)}) collective-permute-start(bf16[4,512,128]{2,1,0:T(8,128)(2,1)S(1)} %bitcast_dynamic-update-slice_fusion), channel_id=1, source_target_pairs={{0,64},{1,449},{16,80},{17,465},{32,96},{33,481},{48,112},{49,497}... | collective-permute-start | bytes 1572872 | tf_op jit(solution)/shard_map/ppermute | solution.py:193
  29.7 21.6 %collective-permute-start.6 = (bf16[4,512,128]{2,1,0:T(8,128)(2,1)S(1)}, bf16[4,512,128]{2,1,0:T(8,128)(2,1)S(1)}, u32[]{:S(2)}, u32[]{:S(2)}) collective-permute-start(bf16[4,512,128]{2,1,0:T(8,128)(2,1)S(1)} %bitcast_dynamic-update-slice_fusion), channel_id=1, source_target_pairs={{0,448},{1,65},{16,464},{17,81},{32,480},{33,97},{48,496},{49,113}... | collective-permute-start | bytes 1572872 | tf_op jit(solution)/shard_map/ppermute | solution.py:193
  33.0 13.4 %copy-start.7 = (bf16[3,1024,128]{2,1,0:T(8,128)(2,1)}, bf16[3,1024,128]{2,1,0:T(8,128)(2,1)S(1)}, u32[]{:S(2)}) copy-start(bf16[3,1024,128]{2,1,0:T(8,128)(2,1)S(1)} %collective-permute-done.5.refs_2_.refs_8_) | copy-start | bytes 2359300
  33.0 26.6 %collective-permute-start.9 = (bf16[3,1024,128]{2,1,0:T(8,128)(2,1)S(1)}, bf16[3,1024,128]{2,1,0:T(8,128)(2,1)}, u32[]{:S(2)}, u32[]{:S(2)}) collective-permute-start(bf16[3,1024,128]{2,1,0:T(8,128)(2,1)S(1)} %collective-permute-done.5.refs_2_.refs_8_), channel_id=1, source_target_pairs={{0,14},{1,3},{2,0},{3,5},{4,2},{5,7},{6,4},{7,9},{8,6},{9,11},{10,... | collective-permute-start | bytes 2359304 | tf_op jit(solution)/shard_map/ppermute | solution.py:193
  41.0 22.4 %collective-permute-start.8 = (bf16[3,1024,128]{2,1,0:T(8,128)(2,1)}, bf16[3,1024,128]{2,1,0:T(8,128)(2,1)}, u32[]{:S(2)}, u32[]{:S(2)}) collective-permute-start(bf16[3,1024,128]{2,1,0:T(8,128)(2,1)} %collective-permute-done.4.refs_1_.refs_7_), channel_id=1, source_target_pairs={{0,2},{1,15},{2,4},{3,1},{4,6},{5,3},{6,8},{7,5},{8,10},{9,7},{10,... | collective-permute-start | bytes 2359304 | tf_op jit(solution)/shard_map/ppermute | solution.py:193
  46.4 22.4 %collective-permute-start.7 = (bf16[4,512,128]{2,1,0:T(8,128)(2,1)}, bf16[4,512,128]{2,1,0:T(8,128)(2,1)}, u32[]{:S(2)}, u32[]{:S(2)}) collective-permute-start(bf16[4,512,128]{2,1,0:T(8,128)(2,1)} %shard_map.64), channel_id=1, source_target_pairs={{0,64},{1,449},{16,80},{17,465},{32,96},{33,481},{48,112},{49,497}... | collective-permute-start | bytes 1572872 | tf_op jit(solution)/shard_map/ppermute | solution.py:193
  51.4 22.3 %collective-permute-start.10 = (bf16[4,512,128]{2,1,0:T(8,128)(2,1)S(1)}, bf16[4,512,128]{2,1,0:T(8,128)(2,1)}, u32[]{:S(2)}, u32[]{:S(2)}) collective-permute-start(bf16[4,512,128]{2,1,0:T(8,128)(2,1)S(1)} %collective-permute-done.6), channel_id=1, source_target_pairs={{0,448},{1,65},{16,464},{17,81},{32,480},{33,97},{48,496},{49,113}... | collective-permute-start | bytes 1572872 | tf_op jit(solution)/shard_map/ppermute | solution.py:193
  54.5 14.3 %copy-start.6 = (bf16[3,4,512,128]{3,2,1,0:T(8,128)(2,1)}, bf16[3,4,512,128]{3,2,1,0:T(8,128)(2,1)S(1)}, u32[]{:S(2)}) copy-start(bf16[3,4,512,128]{3,2,1,0:T(8,128)(2,1)S(1)} %pad_maximum_fusion.1.refs_0_) | copy-start | bytes 4718596
  54.5 21.1 %copy-start.10 = (s32[1,4096]{1,0:T(1,128)S(1)}, s32[1,4096]{1,0:T(1,128)}, u32[]{:S(2)}) copy-start(s32[1,4096]{1,0:T(1,128)} %param.11) | copy-start | bytes 49156
  54.5 35.8 %collective-permute-start.15 = (bf16[3,4,512,128]{3,2,1,0:T(8,128)(2,1)S(1)}, bf16[3,4,512,128]{3,2,1,0:T(8,128)(2,1)}, u32[]{:S(2)}, u32[]{:S(2)}) collective-permute-start(bf16[3,4,512,128]{3,2,1,0:T(8,128)(2,1)S(1)} %pad_maximum_fusion.1.refs_0_), channel_id=1, source_target_pairs={{0,1},{1,0},{2,3},{3,2},{4,5},{5,4},{6,7},{7,6},{8,9},{9,8},{10,11... | collective-permute-start | bytes 4718600 | tf_op jit(solution)/shard_map/ppermute | solution.py:238
  59.5 30.8 %collective-permute-start.14 = (bf16[3,1024,128]{2,1,0:T(8,128)(2,1)}, bf16[3,1024,128]{2,1,0:T(8,128)(2,1)S(1)}, u32[]{:S(2)}, u32[]{:S(2)}) collective-permute-start(bf16[3,1024,128]{2,1,0:T(8,128)(2,1)} %collective-permute-done.9.refs_2_.refs_10_), channel_id=1, source_target_pairs={{0,14},{1,3},{2,0},{3,5},{4,2},{5,7},{6,4},{7,9},{8,6},{9,11},{10,... | collective-permute-start | bytes 2359304 | tf_op jit(solution)/shard_map/ppermute | solution.py:193
  63.4 22.0 %collective-permute-start.13 = (bf16[3,1024,128]{2,1,0:T(8,128)(2,1)}, bf16[3,1024,128]{2,1,0:T(8,128)(2,1)}, u32[]{:S(2)}, u32[]{:S(2)}) collective-permute-start(bf16[3,1024,128]{2,1,0:T(8,128)(2,1)} %collective-permute-done.8.refs_1_.refs_9_), channel_id=1, source_target_pairs={{0,2},{1,15},{2,4},{3,1},{4,6},{5,3},{6,8},{7,5},{8,10},{9,7},{10,... | collective-permute-start | bytes 2359304 | tf_op jit(solution)/shard_map/ppermute | solution.py:193
  68.8 11.3 %collective-permute-start.11 = (bf16[4,512,128]{2,1,0:T(8,128)(2,1)}, bf16[4,512,128]{2,1,0:T(8,128)(2,1)}, u32[]{:S(2)}, u32[]{:S(2)}) collective-permute-start(bf16[4,512,128]{2,1,0:T(8,128)(2,1)} %shard_map.65), channel_id=1, source_target_pairs={{0,64},{1,449},{16,80},{17,465},{32,96},{33,481},{48,112},{49,497}... | collective-permute-start | bytes 1572872 | tf_op jit(solution)/shard_map/ppermute | solution.py:193
  73.7 16.6 %collective-permute-start.12 = (bf16[4,512,128]{2,1,0:T(8,128)(2,1)}, bf16[4,512,128]{2,1,0:T(8,128)(2,1)S(1)}, u32[]{:S(2)}, u32[]{:S(2)}) collective-permute-start(bf16[4,512,128]{2,1,0:T(8,128)(2,1)} %collective-permute-done.10), channel_id=1, source_target_pairs={{0,448},{1,65},{16,464},{17,81},{32,480},{33,97},{48,496},{49,113}... | collective-permute-start | bytes 1572872 | tf_op jit(solution)/shard_map/ppermute | solution.py:193
  80.1 22.5 %collective-permute-start.16 = (bf16[4,512,128]{2,1,0:T(8,128)(2,1)}, bf16[4,512,128]{2,1,0:T(8,128)(2,1)S(1)}, u32[]{:S(2)}, u32[]{:S(2)}) collective-permute-start(bf16[4,512,128]{2,1,0:T(8,128)(2,1)} %collective-permute-done.11), channel_id=1, source_target_pairs={{0,64},{1,449},{16,80},{17,465},{32,96},{33,481},{48,112},{49,497}... | collective-permute-start | bytes 1572872 | tf_op jit(solution)/shard_map/ppermute | solution.py:240
  85.4 17.2 %collective-permute-start.17 = (bf16[3,1024,128]{2,1,0:T(8,128)(2,1)}, bf16[3,1024,128]{2,1,0:T(8,128)(2,1)}, u32[]{:S(2)}, u32[]{:S(2)}) collective-permute-start(bf16[3,1024,128]{2,1,0:T(8,128)(2,1)} %collective-permute-done.13.refs_1_.refs_11_), channel_id=1, source_target_pairs={{0,2},{1,15},{2,4},{3,1},{4,6},{5,3},{6,8},{7,5},{8,10},{9,7},{10,... | collective-permute-start | bytes 2359304 | tf_op jit(solution)/shard_map/ppermute | solution.py:220
  90.3 0.8 copy-start.9
  90.3 1.1 copy-start.8
  93.2 10.3 %copy-start.5 = (bf16[4,4,512,128]{3,2,1,0:T(8,128)(2,1)}, bf16[4,4,512,128]{3,2,1,0:T(8,128)(2,1)S(1)}, u32[]{:S(2)}) copy-start(bf16[4,4,512,128]{3,2,1,0:T(8,128)(2,1)S(1)} %pad_maximum_fusion.refs_1_) | copy-start | bytes 6291460
  93.2 17.8 %collective-permute-start.18 = (bf16[4,4,512,128]{3,2,1,0:T(8,128)(2,1)S(1)}, bf16[4,4,512,128]{3,2,1,0:T(8,128)(2,1)}, u32[]{:S(2)}, u32[]{:S(2)}) collective-permute-start(bf16[4,4,512,128]{3,2,1,0:T(8,128)(2,1)S(1)} %pad_maximum_fusion.refs_1_), channel_id=1, source_target_pairs={{0,1},{1,0},{2,3},{3,2},{4,5},{5,4},{6,7},{7,6},{8,9},{9,8},{10,11... | collective-permute-start | bytes 6291464 | tf_op jit(solution)/shard_map/ppermute | solution.py:238
  99.1 11.9 %collective-permute-start.19 = (bf16[4,512,128]{2,1,0:T(8,128)(2,1)}, bf16[4,512,128]{2,1,0:T(8,128)(2,1)S(1)}, u32[]{:S(2)}, u32[]{:S(2)}) collective-permute-start(bf16[4,512,128]{2,1,0:T(8,128)(2,1)} %collective-permute-done.11), channel_id=1, source_target_pairs={{0,65},{1,448},{16,81},{17,464},{32,97},{33,480},{48,113},{49,496}... | collective-permute-start | bytes 1572872 | tf_op jit(solution)/shard_map/ppermute | solution.py:241
  102.6 0.8 copy-start
  111.0 1.0 copy-start.1
  112.0 8.6 %copy-start.2 = (f32[128,128]{1,0:T(8,128)S(1)}, f32[128,128]{1,0:T(8,128)}, u32[]{:S(2)}) copy-start(f32[128,128]{1,0:T(8,128)} %taps.3) | copy-start | bytes 196612
  112.0 8.6 %copy-start.3 = (f32[7,3,128]{2,0,1:T(8,128)S(1)}, f32[7,3,128]{2,0,1:T(8,128)}, u32[]{:S(2)}) copy-start(f32[7,3,128]{2,0,1:T(8,128)} %param.8) | copy-start | bytes 32260
  112.0 8.6 %copy-start.4 = (f32[128]{0:T(128)S(1)}, f32[128]{0:T(128)}, u32[]{:S(2)}) copy-start(f32[128]{0:T(128)} %param.10) | copy-start | bytes 1540
  119.3 5.2 %collective-permute-start.20 = (bf16[144,384]{1,0:T(8,128)(2,1)S(1)}, bf16[144,384]{1,0:T(8,128)(2,1)S(1)}, u32[]{:S(2)}, u32[]{:S(2)}) collective-permute-start(bf16[144,384]{1,0:T(8,128)(2,1)S(1)} %get-tuple-element.7), channel_id=1, source_target_pairs={{0,2},{2,4},{4,6},{6,8},{8,10},{10,12},{12,14},{1,3},{3,5},{5,7},{... | collective-permute-start | bytes 331784 | tf_op jit(solution)/shard_map/ppermute | solution.py:275

commit v7 on v6

--- a/solution.py
+++ b/solution.py
@@ -20,7 +20,7 @@
 ANY = pl.BlockSpec(memory_space=pl.ANY)
 HBM = pl.BlockSpec(memory_space=pltpu.HBM)
 MIB = 1 << 20
-COST = 20 << 30
+COST = 5 << 30
 
 
 def call(kernel, out_shape, in_specs, out_specs, scratch=(), flops=0, nbytes=0, vmem=8):
@@ -42,7 +42,7 @@
 def project(count, offsets, sets, place, *refs):
     mine, other, refs = refs[: len(sets)], refs[len(sets) : 2 * len(sets)], refs[2 * len(sets) :]
     parts, refs = refs[:count], refs[count:]
-    raw, rim, total, held, weights, sem = refs
+    gathered, raw, rim, total, held, weights, sem = refs
     core = place[1]
     where = [(a, i) for a, size in enumerate(sets) for i in range(size)]
     sign = 1 - 2 * core
@@ -56,10 +56,14 @@
         ]
 
     def panel(k, j):
-        return pltpu.make_async_copy(parts[j], weights.at[k], sem.at[4 * k + 2])
+        return pltpu.make_async_copy(parts[j], weights.at[k, 0], sem.at[4 * k + 2])
+
+    def others(k):
+        slot = lax.rem(place[0] + sign * offsets[k] + count, count)
+        return pltpu.make_async_copy(gathered.at[slot], weights.at[k, 1:], sem.at[4 * k + 3])
 
     def start(k):
-        for copy in landing(k):
+        for copy in landing(k) + [others(k)]:
             copy.start()
         for j in range(count):
             gap = place[0] - place[2] + sign * (offsets[k] - offsets[j])
@@ -73,7 +77,7 @@
     for k in range(count):
         if k + AHEAD < count:
             start(k + AHEAD)
-        for copy in landing(k) + [panel(k, 0)]:
+        for copy in landing(k) + [others(k), panel(k, 0)]:
             copy.wait()
         left = [held[k, j, c] for j in range(held.shape[1]) for c in range(held.shape[2])]
         term = jnp.dot(jnp.concatenate(left, 1), wide(weights[k]), preferred_element_type=F32)
@@ -212,7 +216,9 @@
     on_y, on_z = ("fsdp", "tp"), ("ctx", "tp")
     swap = [(0, 1), (1, 0)]
 
-    columns = jnp.transpose(w_in, (1, 0, 2))
+    planes = jnp.transpose(w_in, (1, 0, 2))
+    gathered = lax.all_gather(planes[1:], "ctx", axis=0)
+    columns = planes[0]
     weights, pair = [], [columns, columns]
     for _ in range(1, ctx // 2):
         pair = both_ways(pair, on_z, along_z(1), along_z(-1))
@@ -260,18 +266,18 @@
             jax.ShapeDtypeStruct((length, 3 * width), BF16),
             jax.ShapeDtypeStruct((LEAD, 3 * width), BF16),
         ),
-        [SMEM] + [HBM] * (2 * len(sets) + ys),
+        [SMEM] + [HBM] * (2 * len(sets) + ys + 1),
         (VMEM, VMEM),
         [
             pltpu.VMEM((length, 3 * width), F32),
             pltpu.VMEM((ys, xs, tp, length, width), BF16),
-            pltpu.VMEM((ctx,) + columns.shape, BF16),
+            pltpu.VMEM((ctx,) + planes.shape, BF16),
             pltpu.SemaphoreType.DMA((4 * ctx,)),
         ],
         flops=every,
         nbytes=16 * MIB,
         vmem=VMEM_DOT,
-    )(place, *mine, *other, columns, *[w for pair in weights for w in pair])
+    )(place, *mine, *other, columns, *[w for pair in weights for w in pair], gathered)
     before = lax.ppermute(rim, "ctx", [(k, k + 1) for k in range(ctx - 1)])
     work = lambda rows: [
         pltpu.VMEM((rows, 3 * width), F32),

time: 128 us -> 158 us (1.23)
  waiting for transfers between devices: 21.2 us -> 38.3 us
  between operations: 0.57 us -> 14 us
  starting transfers between devices: 84.3 us -> 77.1 us
  local copies, waits for them, and re-layouts: 4 us -> 7.99 us
  other arithmetic: 3.29 us -> 4.95 us
    ppermute x6, waiting for transfers between devices: 1.32 us -> 22.2 us  [both_ways(): lax.ppermute(pair[1], axis, second)]
    ppermute x6, waiting for transfers between devices: 12.4 us -> 4.02 us  [both_ways(): lax.ppermute(pair[0], axis, first)]
    ppermute x3, waiting for transfers between devices: 0.01 us -> 3.66 us  [body(): piece = lax.ppermute(own, 'fsdp', along_x(hop))]
    ppermute x6, starting transfers between devices: 34.2 us -> 31 us  [both_ways(): lax.ppermute(pair[0], axis, first)]
    ppermute x1, starting transfers between devices: 5.31 us -> 2.46 us  [body(): final = lax.ppermute(pair[0], on_y, along_y(1))]
    unnamed x22 -> x48, local copies, waits for them, and re-layouts: 2.94 us -> 4.93 us
    slice x0 -> x1, local copies, waits for them, and re-layouts: none -> 1.9 us  [body(): gathered = lax.all_gather(planes[1:], 'ctx', axis=0)]
    ppermute x1, starting transfers between devices: 3.58 us -> 1.91 us  [body(): lax.ppermute(pair[0], on_y, [(i, j // tp * tp + 1 - j % tp) for i, j in a...]
  transfers between devices with their start and end apart: 21 -> 22, of which waited for: 5 -> 8; matrix products, arithmetic and copies ran while one was open for 3% -> 4% of each run, Pallas kernels for 3% -> 2%
where the time goes in v7:
time: 158 us; the launch traced here: 157 us
  starting transfers between devices  77.1 us (49%)
  waiting for transfers between devices  38.3 us (24%)
  Pallas kernels  14.8 us (9%)
  between operations  14 us (9%)
  local copies, waits for them, and re-layouts  7.99 us (5%)
  other arithmetic  4.95 us (3%)
    ppermute x6, starting transfers between devices, both_ways(): lax.ppermute(pair[0], axis, first)  31 us
    ppermute x6, waiting for transfers between devices, both_ways(): lax.ppermute(pair[1], axis, second)  22.2 us
    ppermute x6, starting transfers between devices, both_ways(): lax.ppermute(pair[1], axis, second)  14.6 us
    ppermute x3, starting transfers between devices, body(): piece = lax.ppermute(own, 'fsdp', along_x(hop))  10.8 us
    ppermute x2, starting transfers between devices, body(): other.append(lax.ppermute(mine[-1], 'tp', swap))  10.1 us
    pallas_call x1, Pallas kernels, body(): call(functools.partial(project, ys, offsets, sets), (jax.ShapeDtypeStruct...  8.19 us
    ppermute x1, waiting for transfers between devices, body(): lax.ppermute(pair[0], on_y, [(i, j // tp * tp + 1 - j % tp) for i, j in a...  7.35 us
    ppermute x1, starting transfers between devices, body(): weights.append([lax.ppermute(pair[0], on_z, along_z(1))])  4.95 us
  transfers between devices with their start and end apart: 22, of which 8 were waited for; matrix products, arithmetic and copies ran while one was open for 4% of the time, Pallas kernels for 2%

profile of v7, /device:TPU:1, one launch (start us, length us, event | category | flops | bytes accessed | tf_op | source)
XLA Modules:
  0.0 157.2 jit_solution(538764259152059298)
XLA Ops:
  6.5 1.9 %slice.9 = bf16[2,1024,128]{2,1,0:T(8,128)(2,1)} slice(bf16[3,1024,128]{2,1,0:T(8,128)(2,1)} %bitcast.33), slice={[1:3], [0:1024], [0:128]} | slice | bytes 1048576 | tf_op jit(solution)/shard_map/slice | solution.py:220
  8.5 4.0 %collective-permute-start = (bf16[512,128]{1,0:T(8,128)(2,1)}, bf16[512,128]{1,0:T(8,128)(2,1)S(1)}, u32[]{:S(2)}, u32[]{:S(2)}) collective-permute-start(bf16[512,128]{1,0:T(8,128)(2,1)} %bitcast.38), channel_id=1, source_target_pairs={{0,16},{16,32},{32,48},{48,0},{64,80},{80,96},{96,112},{112,64},{1... | collective-permute-start | bytes 393224 | tf_op jit(solution)/shard_map/ppermute | solution.py:233
  12.4 3.2 %collective-permute-start.2 = (bf16[512,128]{1,0:T(8,128)(2,1)}, bf16[512,128]{1,0:T(8,128)(2,1)S(1)}, u32[]{:S(2)}, u32[]{:S(2)}) collective-permute-start(bf16[512,128]{1,0:T(8,128)(2,1)} %bitcast.39), channel_id=1, source_target_pairs={{0,48},{16,0},{32,16},{48,32},{64,112},{80,64},{96,80},{112,96},{1... | collective-permute-start | bytes 393224 | tf_op jit(solution)/shard_map/ppermute | solution.py:233
  15.6 3.6 %collective-permute-start.1 = (bf16[512,128]{1,0:T(8,128)(2,1)}, bf16[512,128]{1,0:T(8,128)(2,1)S(1)}, u32[]{:S(2)}, u32[]{:S(2)}) collective-permute-start(bf16[512,128]{1,0:T(8,128)(2,1)} %bitcast.40), channel_id=1, source_target_pairs={{0,32},{16,48},{32,0},{48,16},{64,96},{80,112},{96,64},{112,80},{1... | collective-permute-start | bytes 393224 | tf_op jit(solution)/shard_map/ppermute | solution.py:233
  19.5 3.7 %collective-permute-done.1 = bf16[512,128]{1,0:T(8,128)(2,1)S(1)} collective-permute-done((bf16[512,128]{1,0:T(8,128)(2,1)}, bf16[512,128]{1,0:T(8,128)(2,1)S(1)}, u32[]{:S(2)}, u32[]{:S(2)}) %collective-permute-start.1) | collective-permute-done | bytes 131104 | tf_op jit(solution)/shard_map/ppermute | solution.py:233
  23.2 5.2 %collective-permute-start.3 = (bf16[4,512,128]{2,1,0:T(8,128)(2,1)S(1)}, bf16[4,512,128]{2,1,0:T(8,128)(2,1)S(1)}, u32[]{:S(2)}, u32[]{:S(2)}) collective-permute-start(bf16[4,512,128]{2,1,0:T(8,128)(2,1)S(1)} %bitcast_dynamic-update-slice_fusion), channel_id=1, source_target_pairs={{0,64},{1,449},{16,80},{17,465},{32,96},{33,481},{48,112},{49,497}... | collective-permute-start | bytes 1572872 | tf_op jit(solution)/shard_map/ppermute | solution.py:197
  29.4 4.0 %collective-permute-start.5 = (bf16[1024,128]{1,0:T(8,128)(2,1)S(1)}, bf16[1024,128]{1,0:T(8,128)(2,1)S(1)}, u32[]{:S(2)}, u32[]{:S(2)}) collective-permute-start(bf16[1024,128]{1,0:T(8,128)(2,1)S(1)} %slice_bitcast_fusion.refs_6_), channel_id=1, source_target_pairs={{0,14},{1,3},{2,0},{3,5},{4,2},{5,7},{6,4},{7,9},{8,6},{9,11},{10,... | collective-permute-start | bytes 786440 | tf_op jit(solution)/shard_map/ppermute | solution.py:197
  33.4 8.6 %collective-permute-start.4 = (bf16[1024,128]{1,0:T(8,128)(2,1)S(1)}, bf16[1024,128]{1,0:T(8,128)(2,1)S(1)}, u32[]{:S(2)}, u32[]{:S(2)}) collective-permute-start(bf16[1024,128]{1,0:T(8,128)(2,1)S(1)} %slice_bitcast_fusion.refs_6_), channel_id=1, source_target_pairs={{0,2},{1,15},{2,4},{3,1},{4,6},{5,3},{6,8},{7,5},{8,10},{9,7},{10,... | collective-permute-start | bytes 786440 | tf_op jit(solution)/shard_map/ppermute | solution.py:197
  42.0 1.9 %collective-permute-start.6 = (bf16[4,512,128]{2,1,0:T(8,128)(2,1)S(1)}, bf16[4,512,128]{2,1,0:T(8,128)(2,1)}, u32[]{:S(2)}, u32[]{:S(2)}) collective-permute-start(bf16[4,512,128]{2,1,0:T(8,128)(2,1)S(1)} %bitcast_dynamic-update-slice_fusion), channel_id=1, source_target_pairs={{0,448},{1,65},{16,464},{17,81},{32,480},{33,97},{48,496},{49,113}... | collective-permute-start | bytes 1572872 | tf_op jit(solution)/shard_map/ppermute | solution.py:197
  43.9 6.7 %collective-permute-done.5.refs_2_.refs_8_ = bf16[1024,128]{1,0:T(8,128)(2,1)S(1)} collective-permute-done((bf16[1024,128]{1,0:T(8,128)(2,1)S(1)}, bf16[1024,128]{1,0:T(8,128)(2,1)S(1)}, u32[]{:S(2)}, u32[]{:S(2)}) %collective-permute-start.5) | collective-permute-done | bytes 262176 | tf_op jit(solution)/shard_map/ppermute | solution.py:197
  50.6 2.7 %collective-permute-done.4.refs_1_.refs_7_ = bf16[1024,128]{1,0:T(8,128)(2,1)S(1)} collective-permute-done((bf16[1024,128]{1,0:T(8,128)(2,1)S(1)}, bf16[1024,128]{1,0:T(8,128)(2,1)S(1)}, u32[]{:S(2)}, u32[]{:S(2)}) %collective-permute-start.4) | collective-permute-done | bytes 262176 | tf_op jit(solution)/shard_map/ppermute | solution.py:197
  54.8 1.5 pad_maximum_fusion.1.refs_0_
  56.3 5.6 %collective-permute-start.15 = (bf16[3,4,512,128]{3,2,1,0:T(8,128)(2,1)S(1)}, bf16[3,4,512,128]{3,2,1,0:T(8,128)(2,1)}, u32[]{:S(2)}, u32[]{:S(2)}) collective-permute-start(bf16[3,4,512,128]{3,2,1,0:T(8,128)(2,1)S(1)} %pad_maximum_fusion.1.refs_0_), channel_id=1, source_target_pairs={{0,1},{1,0},{2,3},{3,2},{4,5},{5,4},{6,7},{7,6},{8,9},{9,8},{10,11... | collective-permute-start | bytes 4718600 | tf_op jit(solution)/shard_map/ppermute | solution.py:244
  61.9 2.4 %collective-permute-start.10 = (bf16[4,512,128]{2,1,0:T(8,128)(2,1)}, bf16[4,512,128]{2,1,0:T(8,128)(2,1)}, u32[]{:S(2)}, u32[]{:S(2)}) collective-permute-start(bf16[4,512,128]{2,1,0:T(8,128)(2,1)} %collective-permute-done.6), channel_id=1, source_target_pairs={{0,448},{1,65},{16,464},{17,81},{32,480},{33,97},{48,496},{49,113}... | collective-permute-start | bytes 1572872 | tf_op jit(solution)/shard_map/ppermute | solution.py:197
  64.4 4.1 %collective-permute-start.7 = (bf16[4,512,128]{2,1,0:T(8,128)(2,1)S(1)}, bf16[4,512,128]{2,1,0:T(8,128)(2,1)}, u32[]{:S(2)}, u32[]{:S(2)}) collective-permute-start(bf16[4,512,128]{2,1,0:T(8,128)(2,1)S(1)} %copy-done.20), channel_id=1, source_target_pairs={{0,64},{1,449},{16,80},{17,465},{32,96},{33,481},{48,112},{49,497}... | collective-permute-start | bytes 1572872 | tf_op jit(solution)/shard_map/ppermute | solution.py:197
  68.4 1.9 %collective-permute-start.9 = (bf16[1024,128]{1,0:T(8,128)(2,1)S(1)}, bf16[1024,128]{1,0:T(8,128)(2,1)S(1)}, u32[]{:S(2)}, u32[]{:S(2)}) collective-permute-start(bf16[1024,128]{1,0:T(8,128)(2,1)S(1)} %copy-done.1), channel_id=1, source_target_pairs={{0,14},{1,3},{2,0},{3,5},{4,2},{5,7},{6,4},{7,9},{8,6},{9,11},{10,... | collective-permute-start | bytes 786440 | tf_op jit(solution)/shard_map/ppermute | solution.py:197
  70.4 4.6 %collective-permute-start.8 = (bf16[1024,128]{1,0:T(8,128)(2,1)S(1)}, bf16[1024,128]{1,0:T(8,128)(2,1)S(1)}, u32[]{:S(2)}, u32[]{:S(2)}) collective-permute-start(bf16[1024,128]{1,0:T(8,128)(2,1)S(1)} %copy-done.3), channel_id=1, source_target_pairs={{0,2},{1,15},{2,4},{3,1},{4,6},{5,3},{6,8},{7,5},{8,10},{9,7},{10,... | collective-permute-start | bytes 786440 | tf_op jit(solution)/shard_map/ppermute | solution.py:197
  75.0 8.4 %collective-permute-done.9.refs_2_.refs_10_ = bf16[1024,128]{1,0:T(8,128)(2,1)S(1)} collective-permute-done((bf16[1024,128]{1,0:T(8,128)(2,1)S(1)}, bf16[1024,128]{1,0:T(8,128)(2,1)S(1)}, u32[]{:S(2)}, u32[]{:S(2)}) %collective-permute-start.9) | collective-permute-done | bytes 262176 | tf_op jit(solution)/shard_map/ppermute | solution.py:197
  83.3 1.9 %collective-permute-start.14 = (bf16[1024,128]{1,0:T(8,128)(2,1)S(1)}, bf16[1024,128]{1,0:T(8,128)(2,1)S(1)}, u32[]{:S(2)}, u32[]{:S(2)}) collective-permute-start(bf16[1024,128]{1,0:T(8,128)(2,1)S(1)} %collective-permute-done.9.refs_2_.refs_10_), channel_id=1, source_target_pairs={{0,14},{1,3},{2,0},{3,5},{4,2},{5,7},{6,4},{7,9},{8,6},{9,11},{10,... | collective-permute-start | bytes 786440 | tf_op jit(solution)/shard_map/ppermute | solution.py:197
  85.3 4.6 %collective-permute-start.13 = (bf16[1024,128]{1,0:T(8,128)(2,1)S(1)}, bf16[1024,128]{1,0:T(8,128)(2,1)S(1)}, u32[]{:S(2)}, u32[]{:S(2)}) collective-permute-start(bf16[1024,128]{1,0:T(8,128)(2,1)S(1)} %collective-permute-done.8.refs_1_.refs_9_), channel_id=1, source_target_pairs={{0,2},{1,15},{2,4},{3,1},{4,6},{5,3},{6,8},{7,5},{8,10},{9,7},{10,... | collective-permute-start | bytes 786440 | tf_op jit(solution)/shard_map/ppermute | solution.py:197
  89.9 2.5 %collective-permute-start.12 = (bf16[4,512,128]{2,1,0:T(8,128)(2,1)}, bf16[4,512,128]{2,1,0:T(8,128)(2,1)}, u32[]{:S(2)}, u32[]{:S(2)}) collective-permute-start(bf16[4,512,128]{2,1,0:T(8,128)(2,1)} %collective-permute-done.10), channel_id=1, source_target_pairs={{0,448},{1,65},{16,464},{17,81},{32,480},{33,97},{48,496},{49,113}... | collective-permute-start | bytes 1572872 | tf_op jit(solution)/shard_map/ppermute | solution.py:197
  92.4 4.0 %collective-permute-start.11 = (bf16[4,512,128]{2,1,0:T(8,128)(2,1)}, bf16[4,512,128]{2,1,0:T(8,128)(2,1)}, u32[]{:S(2)}, u32[]{:S(2)}) collective-permute-start(bf16[4,512,128]{2,1,0:T(8,128)(2,1)} %shard_map.65), channel_id=1, source_target_pairs={{0,64},{1,449},{16,80},{17,465},{32,96},{33,481},{48,112},{49,497}... | collective-permute-start | bytes 1572872 | tf_op jit(solution)/shard_map/ppermute | solution.py:197
  96.5 7.2 %collective-permute-done.12.refs_0_ = bf16[4,512,128]{2,1,0:T(8,128)(2,1)} collective-permute-done((bf16[4,512,128]{2,1,0:T(8,128)(2,1)}, bf16[4,512,128]{2,1,0:T(8,128)(2,1)}, u32[]{:S(2)}, u32[]{:S(2)}) %collective-permute-start.12) | collective-permute-done | bytes 524320 | tf_op jit(solution)/shard_map/ppermute | solution.py:197
  105.0 3.2 %pad_maximum_fusion.refs_1_ = bf16[4,4,512,128]{3,2,1,0:T(8,128)(2,1)} fusion(bf16[1,4,512,128]{3,2,1,0:T(8,128)(2,1)} %bitcast.16, bf16[1,4,512,128]{3,2,1,0:T(8,128)(2,1)} %bitcast.15, bf16[1,4,512,128]{3,2,1,0:T(8,128)(2,1)} %bitcast.14, bf16[1,4,512,128]{3,2,1,0:T(8,128)(2,1)} %bitcast.13), kind=kLoop, calls=%fused_computation | loop fusion | flops 3145728 | bytes 4194304 | tf_op jit(solution)/shard_map/stack | solution.py:243
  108.2 4.5 %collective-permute-start.18 = (bf16[4,4,512,128]{3,2,1,0:T(8,128)(2,1)}, bf16[4,4,512,128]{3,2,1,0:T(8,128)(2,1)}, u32[]{:S(2)}, u32[]{:S(2)}) collective-permute-start(bf16[4,4,512,128]{3,2,1,0:T(8,128)(2,1)} %pad_maximum_fusion.refs_1_), channel_id=1, source_target_pairs={{0,1},{1,0},{2,3},{3,2},{4,5},{5,4},{6,7},{7,6},{8,9},{9,8},{10,11... | collective-permute-start | bytes 6291464 | tf_op jit(solution)/shard_map/ppermute | solution.py:244
  112.7 2.5 %collective-permute-start.16 = (bf16[4,512,128]{2,1,0:T(8,128)(2,1)}, bf16[4,512,128]{2,1,0:T(8,128)(2,1)S(1)}, u32[]{:S(2)}, u32[]{:S(2)}) collective-permute-start(bf16[4,512,128]{2,1,0:T(8,128)(2,1)} %collective-permute-done.11), channel_id=1, source_target_pairs={{0,64},{1,449},{16,80},{17,465},{32,96},{33,481},{48,112},{49,497}... | collective-permute-start | bytes 1572872 | tf_op jit(solution)/shard_map/ppermute | solution.py:246
  115.2 4.9 %collective-permute-start.17 = (bf16[1024,128]{1,0:T(8,128)(2,1)S(1)}, bf16[1024,128]{1,0:T(8,128)(2,1)S(1)}, u32[]{:S(2)}, u32[]{:S(2)}) collective-permute-start(bf16[1024,128]{1,0:T(8,128)(2,1)S(1)} %copy-done.11), channel_id=1, source_target_pairs={{0,2},{1,15},{2,4},{3,1},{4,6},{5,3},{6,8},{7,5},{8,10},{9,7},{10,... | collective-permute-start | bytes 786440 | tf_op jit(solution)/shard_map/ppermute | solution.py:226
  120.4 1.9 %collective-permute-start.19 = (bf16[4,512,128]{2,1,0:T(8,128)(2,1)}, bf16[4,512,128]{2,1,0:T(8,128)(2,1)S(1)}, u32[]{:S(2)}, u32[]{:S(2)}) collective-permute-start(bf16[4,512,128]{2,1,0:T(8,128)(2,1)} %collective-permute-done.11), channel_id=1, source_target_pairs={{0,65},{1,448},{16,81},{17,464},{32,97},{33,480},{48,113},{49,496}... | collective-permute-start | bytes 1572872 | tf_op jit(solution)/shard_map/ppermute | solution.py:247
  125.0 7.4 %collective-permute-done.19 = bf16[4,512,128]{2,1,0:T(8,128)(2,1)S(1)} collective-permute-done((bf16[4,512,128]{2,1,0:T(8,128)(2,1)}, bf16[4,512,128]{2,1,0:T(8,128)(2,1)S(1)}, u32[]{:S(2)}, u32[]{:S(2)}) %collective-permute-start.19) | collective-permute-done | bytes 524320 | tf_op jit(solution)/shard_map/ppermute | solution.py:247
  133.2 8.2 %shard_map.68 = (bf16[512,384]{1,0:T(8,128)(2,1)}, bf16[144,384]{1,0:T(8,128)(2,1)S(1)}) custom-call(s32[6]{0:T(128)S(1)} %pad_add_fusion.place, bf16[3,4,512,128]{3,2,1,0:T(8,128)(2,1)} %copy-done.16, bf16[4,4,512,128]{3,2,1,0:T(8,128)(2,1)} %pad_maximum_fusion.refs_1_, bf16[1,4,512,128]{3,2,1,0:T(8,128)(2,1)} %bitcast.35, ...), custom_call_target="tpu_custom_call" | custom-call | flops 3221225472 | bytes 16777216 | tf_op jit(solution)/shard_map/pallas_call | solution.py:263
  143.7 3.6 %shard_map.69.given = bf16[512,128]{1,0:T(8,128)(2,1)S(1)} custom-call(s32[6]{0:T(128)S(1)} %pad_add_fusion.place, bf16[512,384]{1,0:T(8,128)(2,1)S(1)} %copy-done.12, f32[7,384]{1,0:T(8,128)S(1)} %bitcast.27, f32[128,128]{1,0:T(8,128)S(1)} %copy-done.13, f32[1,128]{1,0:T(1,128)S(1)} %bitcast.29), custom_call_target="tpu_custom_call" | custom-call | flops 1610612736 | bytes 2097152 | tf_op jit(solution)/shard_map/pallas_call | solution.py:290
  147.3 3.1 %shard_map.70 = bf16[512,128]{1,0:T(8,128)(2,1)} custom-call(s32[6]{0:T(128)S(1)} %pad_add_fusion.place, bf16[144,384]{1,0:T(8,128)(2,1)S(1)} %collective-permute-done.20.before, bf16[512,384]{1,0:T(8,128)(2,1)S(1)} %copy-done.12, f32[7,384]{1,0:T(8,128)S(1)} %bitcast.28, f32[128,128]{1,0:T(8,128)S(1)} %copy-done.13, f32[1,128]{1,0:T(1,128)S(1)} %bitcast.30, ...), custom_call_target="tpu_custom_call" | custom-call | flops 805306368 | bytes 1048576 | tf_op jit(solution)/shard_map/pallas_call | solution.py:299
  (80 shorter events, 10.1 us)
Async XLA Ops:
  6.5 12.9 %copy-start.22 = (bf16[1,512,128]{2,1,0:T(8,128)(2,1)S(1)}, bf16[1,512,128]{2,1,0:T(8,128)(2,1)}, u32[]{:S(2)}) copy-start(bf16[1,512,128]{2,1,0:T(8,128)(2,1)} %param.6) | copy-start | bytes 393220
  6.5 125.8 %all-gather.3.cloned.1.call-start = ((), (), s32[]{:S(2)}) async-start(), calls=%async_computation | async-start | bytes 4718592 | tf_op jit(solution)/shard_map/all_gather | solution.py:220
  8.5 11.0 %collective-permute-start = (bf16[512,128]{1,0:T(8,128)(2,1)}, bf16[512,128]{1,0:T(8,128)(2,1)S(1)}, u32[]{:S(2)}, u32[]{:S(2)}) collective-permute-start(bf16[512,128]{1,0:T(8,128)(2,1)} %bitcast.38), channel_id=1, source_target_pairs={{0,16},{16,32},{32,48},{48,0},{64,80},{80,96},{96,112},{112,64},{1... | collective-permute-start | bytes 393224 | tf_op jit(solution)/shard_map/ppermute | solution.py:233
  12.4 10.8 %collective-permute-start.2 = (bf16[512,128]{1,0:T(8,128)(2,1)}, bf16[512,128]{1,0:T(8,128)(2,1)S(1)}, u32[]{:S(2)}, u32[]{:S(2)}) collective-permute-start(bf16[512,128]{1,0:T(8,128)(2,1)} %bitcast.39), channel_id=1, source_target_pairs={{0,48},{16,0},{32,16},{48,32},{64,112},{80,64},{96,80},{112,96},{1... | collective-permute-start | bytes 393224 | tf_op jit(solution)/shard_map/ppermute | solution.py:233
  15.6 7.5 %collective-permute-start.1 = (bf16[512,128]{1,0:T(8,128)(2,1)}, bf16[512,128]{1,0:T(8,128)(2,1)S(1)}, u32[]{:S(2)}, u32[]{:S(2)}) collective-permute-start(bf16[512,128]{1,0:T(8,128)(2,1)} %bitcast.40), channel_id=1, source_target_pairs={{0,32},{16,48},{32,0},{48,16},{64,96},{80,112},{96,64},{112,80},{1... | collective-permute-start | bytes 393224 | tf_op jit(solution)/shard_map/ppermute | solution.py:233
  23.2 30.0 %collective-permute-start.3 = (bf16[4,512,128]{2,1,0:T(8,128)(2,1)S(1)}, bf16[4,512,128]{2,1,0:T(8,128)(2,1)S(1)}, u32[]{:S(2)}, u32[]{:S(2)}) collective-permute-start(bf16[4,512,128]{2,1,0:T(8,128)(2,1)S(1)} %bitcast_dynamic-update-slice_fusion), channel_id=1, source_target_pairs={{0,64},{1,449},{16,80},{17,465},{32,96},{33,481},{48,112},{49,497}... | collective-permute-start | bytes 1572872 | tf_op jit(solution)/shard_map/ppermute | solution.py:197
  29.4 21.2 %collective-permute-start.5 = (bf16[1024,128]{1,0:T(8,128)(2,1)S(1)}, bf16[1024,128]{1,0:T(8,128)(2,1)S(1)}, u32[]{:S(2)}, u32[]{:S(2)}) collective-permute-start(bf16[1024,128]{1,0:T(8,128)(2,1)S(1)} %slice_bitcast_fusion.refs_6_), channel_id=1, source_target_pairs={{0,14},{1,3},{2,0},{3,5},{4,2},{5,7},{6,4},{7,9},{8,6},{9,11},{10,... | collective-permute-start | bytes 786440 | tf_op jit(solution)/shard_map/ppermute | solution.py:197
  33.4 19.8 %collective-permute-start.4 = (bf16[1024,128]{1,0:T(8,128)(2,1)S(1)}, bf16[1024,128]{1,0:T(8,128)(2,1)S(1)}, u32[]{:S(2)}, u32[]{:S(2)}) collective-permute-start(bf16[1024,128]{1,0:T(8,128)(2,1)S(1)} %slice_bitcast_fusion.refs_6_), channel_id=1, source_target_pairs={{0,2},{1,15},{2,4},{3,1},{4,6},{5,3},{6,8},{7,5},{8,10},{9,7},{10,... | collective-permute-start | bytes 786440 | tf_op jit(solution)/shard_map/ppermute | solution.py:197
  42.0 12.8 %collective-permute-start.6 = (bf16[4,512,128]{2,1,0:T(8,128)(2,1)S(1)}, bf16[4,512,128]{2,1,0:T(8,128)(2,1)}, u32[]{:S(2)}, u32[]{:S(2)}) collective-permute-start(bf16[4,512,128]{2,1,0:T(8,128)(2,1)S(1)} %bitcast_dynamic-update-slice_fusion), channel_id=1, source_target_pairs={{0,448},{1,65},{16,464},{17,81},{32,480},{33,97},{48,496},{49,113}... | collective-permute-start | bytes 1572872 | tf_op jit(solution)/shard_map/ppermute | solution.py:197
  54.8 9.6 %copy-start.20 = (bf16[4,512,128]{2,1,0:T(8,128)(2,1)S(1)}, bf16[4,512,128]{2,1,0:T(8,128)(2,1)}, u32[]{:S(2)}) copy-start(bf16[4,512,128]{2,1,0:T(8,128)(2,1)} %shard_map.64) | copy-start | bytes 1572868
  54.8 13.7 %copy-start.1 = (bf16[1024,128]{1,0:T(8,128)(2,1)S(1)}, bf16[1024,128]{1,0:T(8,128)(2,1)}, u32[]{:S(2)}) copy-start(bf16[1024,128]{1,0:T(8,128)(2,1)} %copy-done) | copy-start | bytes 786436
  54.8 15.6 %copy-start.3 = (bf16[1024,128]{1,0:T(8,128)(2,1)S(1)}, bf16[1024,128]{1,0:T(8,128)(2,1)}, u32[]{:S(2)}) copy-start(bf16[1024,128]{1,0:T(8,128)(2,1)} %copy-done.2) | copy-start | bytes 786436
  56.3 36.1 %copy-start.16 = (bf16[3,4,512,128]{3,2,1,0:T(8,128)(2,1)}, bf16[3,4,512,128]{3,2,1,0:T(8,128)(2,1)S(1)}, u32[]{:S(2)}) copy-start(bf16[3,4,512,128]{3,2,1,0:T(8,128)(2,1)S(1)} %pad_maximum_fusion.1.refs_0_) | copy-start | bytes 4718596
  56.3 47.4 %collective-permute-start.15 = (bf16[3,4,512,128]{3,2,1,0:T(8,128)(2,1)S(1)}, bf16[3,4,512,128]{3,2,1,0:T(8,128)(2,1)}, u32[]{:S(2)}, u32[]{:S(2)}) collective-permute-start(bf16[3,4,512,128]{3,2,1,0:T(8,128)(2,1)S(1)} %pad_maximum_fusion.1.refs_0_), channel_id=1, source_target_pairs={{0,1},{1,0},{2,3},{3,2},{4,5},{5,4},{6,7},{7,6},{8,9},{9,8},{10,11... | collective-permute-start | bytes 4718600 | tf_op jit(solution)/shard_map/ppermute | solution.py:244
  61.9 27.9 %collective-permute-start.10 = (bf16[4,512,128]{2,1,0:T(8,128)(2,1)}, bf16[4,512,128]{2,1,0:T(8,128)(2,1)}, u32[]{:S(2)}, u32[]{:S(2)}) collective-permute-start(bf16[4,512,128]{2,1,0:T(8,128)(2,1)} %collective-permute-done.6), channel_id=1, source_target_pairs={{0,448},{1,65},{16,464},{17,81},{32,480},{33,97},{48,496},{49,113}... | collective-permute-start | bytes 1572872 | tf_op jit(solution)/shard_map/ppermute | solution.py:197
  64.4 28.0 %collective-permute-start.7 = (bf16[4,512,128]{2,1,0:T(8,128)(2,1)S(1)}, bf16[4,512,128]{2,1,0:T(8,128)(2,1)}, u32[]{:S(2)}, u32[]{:S(2)}) collective-permute-start(bf16[4,512,128]{2,1,0:T(8,128)(2,1)S(1)} %copy-done.20), channel_id=1, source_target_pairs={{0,64},{1,449},{16,80},{17,465},{32,96},{33,481},{48,112},{49,497}... | collective-permute-start | bytes 1572872 | tf_op jit(solution)/shard_map/ppermute | solution.py:197
  68.4 14.9 %collective-permute-start.9 = (bf16[1024,128]{1,0:T(8,128)(2,1)S(1)}, bf16[1024,128]{1,0:T(8,128)(2,1)S(1)}, u32[]{:S(2)}, u32[]{:S(2)}) collective-permute-start(bf16[1024,128]{1,0:T(8,128)(2,1)S(1)} %copy-done.1), channel_id=1, source_target_pairs={{0,14},{1,3},{2,0},{3,5},{4,2},{5,7},{6,4},{7,9},{8,6},{9,11},{10,... | collective-permute-start | bytes 786440 | tf_op jit(solution)/shard_map/ppermute | solution.py:197
  70.4 14.9 %collective-permute-start.8 = (bf16[1024,128]{1,0:T(8,128)(2,1)S(1)}, bf16[1024,128]{1,0:T(8,128)(2,1)S(1)}, u32[]{:S(2)}, u32[]{:S(2)}) collective-permute-start(bf16[1024,128]{1,0:T(8,128)(2,1)S(1)} %copy-done.3), channel_id=1, source_target_pairs={{0,2},{1,15},{2,4},{3,1},{4,6},{5,3},{6,8},{7,5},{8,10},{9,7},{10,... | collective-permute-start | bytes 786440 | tf_op jit(solution)/shard_map/ppermute | solution.py:197
  83.3 13.1 %collective-permute-start.14 = (bf16[1024,128]{1,0:T(8,128)(2,1)S(1)}, bf16[1024,128]{1,0:T(8,128)(2,1)S(1)}, u32[]{:S(2)}, u32[]{:S(2)}) collective-permute-start(bf16[1024,128]{1,0:T(8,128)(2,1)S(1)} %collective-permute-done.9.refs_2_.refs_10_), channel_id=1, source_target_pairs={{0,14},{1,3},{2,0},{3,5},{4,2},{5,7},{6,4},{7,9},{8,6},{9,11},{10,... | collective-permute-start | bytes 786440 | tf_op jit(solution)/shard_map/ppermute | solution.py:197
  85.3 11.2 %collective-permute-start.13 = (bf16[1024,128]{1,0:T(8,128)(2,1)S(1)}, bf16[1024,128]{1,0:T(8,128)(2,1)S(1)}, u32[]{:S(2)}, u32[]{:S(2)}) collective-permute-start(bf16[1024,128]{1,0:T(8,128)(2,1)S(1)} %collective-permute-done.8.refs_1_.refs_9_), channel_id=1, source_target_pairs={{0,2},{1,15},{2,4},{3,1},{4,6},{5,3},{6,8},{7,5},{8,10},{9,7},{10,... | collective-permute-start | bytes 786440 | tf_op jit(solution)/shard_map/ppermute | solution.py:197
  89.9 13.8 %collective-permute-start.12 = (bf16[4,512,128]{2,1,0:T(8,128)(2,1)}, bf16[4,512,128]{2,1,0:T(8,128)(2,1)}, u32[]{:S(2)}, u32[]{:S(2)}) collective-permute-start(bf16[4,512,128]{2,1,0:T(8,128)(2,1)} %collective-permute-done.10), channel_id=1, source_target_pairs={{0,448},{1,65},{16,464},{17,81},{32,480},{33,97},{48,496},{49,113}... | collective-permute-start | bytes 1572872 | tf_op jit(solution)/shard_map/ppermute | solution.py:197
  92.4 12.7 %collective-permute-start.11 = (bf16[4,512,128]{2,1,0:T(8,128)(2,1)}, bf16[4,512,128]{2,1,0:T(8,128)(2,1)}, u32[]{:S(2)}, u32[]{:S(2)}) collective-permute-start(bf16[4,512,128]{2,1,0:T(8,128)(2,1)} %shard_map.65), channel_id=1, source_target_pairs={{0,64},{1,449},{16,80},{17,465},{32,96},{33,481},{48,112},{49,497}... | collective-permute-start | bytes 1572872 | tf_op jit(solution)/shard_map/ppermute | solution.py:197
  105.0 10.1 %copy-start.11 = (bf16[1024,128]{1,0:T(8,128)(2,1)S(1)}, bf16[1024,128]{1,0:T(8,128)(2,1)}, u32[]{:S(2)}) copy-start(bf16[1024,128]{1,0:T(8,128)(2,1)} %copy-done.10) | copy-start | bytes 786436
  105.0 15.1 %copy-start.23 = (s32[1,4096]{1,0:T(1,128)S(1)}, s32[1,4096]{1,0:T(1,128)}, u32[]{:S(2)}) copy-start(s32[1,4096]{1,0:T(1,128)} %param.11) | copy-start | bytes 49156
  108.2 24.1 %collective-permute-start.18 = (bf16[4,4,512,128]{3,2,1,0:T(8,128)(2,1)}, bf16[4,4,512,128]{3,2,1,0:T(8,128)(2,1)}, u32[]{:S(2)}, u32[]{:S(2)}) collective-permute-start(bf16[4,4,512,128]{3,2,1,0:T(8,128)(2,1)} %pad_maximum_fusion.refs_1_), channel_id=1, source_target_pairs={{0,1},{1,0},{2,3},{3,2},{4,5},{5,4},{6,7},{7,6},{8,9},{9,8},{10,11... | collective-permute-start | bytes 6291464 | tf_op jit(solution)/shard_map/ppermute | solution.py:244
  112.7 10.7 %collective-permute-start.16 = (bf16[4,512,128]{2,1,0:T(8,128)(2,1)}, bf16[4,512,128]{2,1,0:T(8,128)(2,1)S(1)}, u32[]{:S(2)}, u32[]{:S(2)}) collective-permute-start(bf16[4,512,128]{2,1,0:T(8,128)(2,1)} %collective-permute-done.11), channel_id=1, source_target_pairs={{0,64},{1,449},{16,80},{17,465},{32,96},{33,481},{48,112},{49,497}... | collective-permute-start | bytes 1572872 | tf_op jit(solution)/shard_map/ppermute | solution.py:246
  115.2 8.3 %collective-permute-start.17 = (bf16[1024,128]{1,0:T(8,128)(2,1)S(1)}, bf16[1024,128]{1,0:T(8,128)(2,1)S(1)}, u32[]{:S(2)}, u32[]{:S(2)}) collective-permute-start(bf16[1024,128]{1,0:T(8,128)(2,1)S(1)} %copy-done.11), channel_id=1, source_target_pairs={{0,2},{1,15},{2,4},{3,1},{4,6},{5,3},{6,8},{7,5},{8,10},{9,7},{10,... | collective-permute-start | bytes 786440 | tf_op jit(solution)/shard_map/ppermute | solution.py:226
  120.4 11.9 %collective-permute-start.19 = (bf16[4,512,128]{2,1,0:T(8,128)(2,1)}, bf16[4,512,128]{2,1,0:T(8,128)(2,1)S(1)}, u32[]{:S(2)}, u32[]{:S(2)}) collective-permute-start(bf16[4,512,128]{2,1,0:T(8,128)(2,1)} %collective-permute-done.11), channel_id=1, source_target_pairs={{0,65},{1,448},{16,81},{17,464},{32,97},{33,480},{48,113},{49,496}... | collective-permute-start | bytes 1572872 | tf_op jit(solution)/shard_map/ppermute | solution.py:247
  122.4 10.7 %copy-start.5 = (bf16[1024,128]{1,0:T(8,128)(2,1)S(1)}, bf16[1024,128]{1,0:T(8,128)(2,1)}, u32[]{:S(2)}) copy-start(bf16[1024,128]{1,0:T(8,128)(2,1)} %copy-done.4) | copy-start | bytes 786436
  122.4 10.7 %copy-start.7 = (bf16[1024,128]{1,0:T(8,128)(2,1)S(1)}, bf16[1024,128]{1,0:T(8,128)(2,1)}, u32[]{:S(2)}) copy-start(bf16[1024,128]{1,0:T(8,128)(2,1)} %copy-done.6) | copy-start | bytes 786436
  122.4 10.7 %copy-start.9 = (bf16[1024,128]{1,0:T(8,128)(2,1)S(1)}, bf16[1024,128]{1,0:T(8,128)(2,1)}, u32[]{:S(2)}) copy-start(bf16[1024,128]{1,0:T(8,128)(2,1)} %copy-done.8) | copy-start | bytes 786436
  141.4 5.9 %collective-permute-start.20 = (bf16[144,384]{1,0:T(8,128)(2,1)S(1)}, bf16[144,384]{1,0:T(8,128)(2,1)S(1)}, u32[]{:S(2)}, u32[]{:S(2)}) collective-permute-start(bf16[144,384]{1,0:T(8,128)(2,1)S(1)} %get-tuple-element.7), channel_id=1, source_target_pairs={{0,2},{2,4},{4,6},{6,8},{8,10},{10,12},{12,14},{1,3},{3,5},{5,7},{... | collective-permute-start | bytes 331784 | tf_op jit(solution)/shard_map/ppermute | solution.py:281
  (14 other events, 66.8 us)
Sparse Core Ops, SparseCore 0:
  9.4 72.5 all-gather.2

commit v8 on v4

--- a/solution.py
+++ b/solution.py
@@ -139,23 +139,30 @@
     lax.fori_loop(0, (last - first) // GROUP, group, 0)
 
 
-def main_part(place, raw, short, taps, skip, out, wider, mixed, queries, window, ids):
+def main_part(
+    place, raw, short, taps, skip, out, top_mixed, top_queries, wider, mixed, queries, window, ids
+):
     rows = raw.shape[0]
     fill(place, rows, ids)
     wider[...] = raw[...].astype(F32)
     features(PAD, rows, 0, wider, ids, short, mixed, queries)
+    top_mixed[...] = mixed[PAD:HEAD, :]
+    top_queries[...] = queries[PAD:HEAD, :]
     long_filter(HEAD, rows, 0, place, ids, mixed, queries, taps, skip, out, window)
 
 
 def head_part(
-    place, before, raw, short, taps, skip, given, out, wider, mixed, queries, window, ids
+    place, before, raw, short, taps, skip, given, top_mixed, top_queries,
+    out, wider, mixed, queries, window, ids,
 ):
     rim = before.shape[0]
     fill(place, out.shape[0], ids)
     wider[:rim, :] = before[...].astype(F32)
-    wider[rim:, :] = raw[:HEAD, :].astype(F32)
+    wider[rim:, :] = raw[:PAD, :].astype(F32)
     features(PAD - rim, 0, rim, wider, ids, short, mixed, queries)
-    features(0, HEAD, rim, wider, ids, short, mixed, queries)
+    features(0, PAD, rim, wider, ids, short, mixed, queries)
+    mixed[rim + PAD :, :] = top_mixed[...]
+    queries[PAD:HEAD, :] = top_queries[...]
     out[HEAD:, :] = given[HEAD:, :]
     long_filter(0, HEAD, rim, place, ids, mixed, queries, taps, skip, out, window)
 
@@ -222,32 +229,33 @@
         vmem=VMEM_DOT,
     )(place, *blocks, *others, weights)
     before = lax.ppermute(rim, "ctx", [(k, k + 1) for k in range(ctx - 1)])
-    work = lambda rows: [
-        pltpu.VMEM((rows, 3 * width), F32),
+    work = lambda rows, wide_rows: [
+        pltpu.VMEM((wide_rows, 3 * width), F32),
         pltpu.VMEM((rows, width), F32),
         pltpu.VMEM((length, width), F32),
         pltpu.VMEM((reach + GROUP, width), F32),
         pltpu.VMEM((LEAD + length, width), jnp.int32),
     ]
     outline = jax.ShapeDtypeStruct((length, width), BF16)
-    part = call(
+    top = jax.ShapeDtypeStruct((HEAD - PAD, width), F32)
+    part, *tops = call(
         main_part,
-        outline,
+        (outline, top, top),
         [SMEM] + [VMEM] * 4,
-        VMEM,
-        work(length),
+        (VMEM, VMEM, VMEM),
+        work(length, length),
         flops=every // 2,
         nbytes=2 * MIB,
     )(place, raw, short, mr_taps, bias)
     gated = call(
         head_part,
         outline,
-        [SMEM] + [VMEM] * 6,
+        [SMEM] + [VMEM] * 8,
         VMEM,
-        work(LEAD + HEAD),
+        work(LEAD + HEAD, LEAD + PAD),
         flops=every // 4,
         nbytes=1 * MIB,
-    )(place, before, raw, short, mr_taps, bias, part)
+    )(place, before, raw, short, mr_taps, bias, part, *tops)
     return gated[None]
 
 

time: 116 us -> 115 us (level)
  no operation moved by 1% of the time
where the time goes in v8:
time: 115 us
  starting transfers between devices  62.1 us (54%)
  waiting for transfers between devices  23 us (20%)
  between operations  13.9 us (12%)
  Pallas kernels  13.4 us (12%)
    ppermute x8, starting transfers between devices, body(): others = [lax.ppermute(b, 'tp', swap) for b in blocks]  26.1 us
    ppermute x3, starting transfers between devices, two_way(): down = lax.ppermute(down, axis, hop(-1))  13.5 us
    ppermute x4, waiting for transfers between devices, two_way(): up = lax.ppermute(up, axis, hop(1))  12.8 us
    ppermute x3, starting transfers between devices, body(): piece = lax.ppermute(own, 'fsdp', along_x(hop))  10.8 us
    ppermute x4, starting transfers between devices, two_way(): up = lax.ppermute(up, axis, hop(1))  10.4 us
    pallas_call x1, Pallas kernels, body(): call(functools.partial(project, ys, offsets), (jax.ShapeDtypeStruct((leng...  6.99 us
    pallas_call x1, Pallas kernels, body(): call(main_part, (outline, top, top), [SMEM] + [VMEM] * 4, (VMEM, VMEM, VM...  3.58 us
    all_gather x1, waiting for transfers between devices, body(): weights = lax.all_gather(jnp.transpose(w_in, (1, 0, 2)), 'ctx', axis=0)  3.19 us
  transfers between devices with their start and end apart: 20, of which 7 were waited for; matrix products, arithmetic and copies ran while one was open for 2% of the time, Pallas kernels for 3%

profile of v8, /device:TPU:1, one launch (start us, length us, event | category | flops | bytes accessed | tf_op | source)
XLA Modules:
  0.0 114.6 jit_solution(7669234498429251435)
XLA Ops:
  6.5 0.7 all-gather.3.cloned.1.call-update
  7.3 4.0 %collective-permute-start = (bf16[512,128]{1,0:T(8,128)(2,1)}, bf16[512,128]{1,0:T(8,128)(2,1)S(1)}, u32[]{:S(2)}, u32[]{:S(2)}) collective-permute-start(bf16[512,128]{1,0:T(8,128)(2,1)} %bitcast.22), channel_id=1, source_target_pairs={{0,16},{16,32},{32,48},{48,0},{64,80},{80,96},{96,112},{112,64},{1... | collective-permute-start | bytes 393224 | tf_op jit(solution)/shard_map/ppermute | solution.py:202
  11.2 3.2 %collective-permute-start.2 = (bf16[512,128]{1,0:T(8,128)(2,1)}, bf16[512,128]{1,0:T(8,128)(2,1)S(1)}, u32[]{:S(2)}, u32[]{:S(2)}) collective-permute-start(bf16[512,128]{1,0:T(8,128)(2,1)} %bitcast.23), channel_id=1, source_target_pairs={{0,48},{16,0},{32,16},{48,32},{64,112},{80,64},{96,80},{112,96},{1... | collective-permute-start | bytes 393224 | tf_op jit(solution)/shard_map/ppermute | solution.py:202
  14.4 3.6 %collective-permute-start.1 = (bf16[512,128]{1,0:T(8,128)(2,1)}, bf16[512,128]{1,0:T(8,128)(2,1)S(1)}, u32[]{:S(2)}, u32[]{:S(2)}) collective-permute-start(bf16[512,128]{1,0:T(8,128)(2,1)} %bitcast.24), channel_id=1, source_target_pairs={{0,32},{16,48},{32,0},{48,16},{64,96},{80,112},{96,64},{112,80},{1... | collective-permute-start | bytes 393224 | tf_op jit(solution)/shard_map/ppermute | solution.py:202
  18.2 0.9 constant_dynamic-update-slice_fusion
  19.2 2.8 %collective-permute-done.1 = bf16[512,128]{1,0:T(8,128)(2,1)S(1)} collective-permute-done((bf16[512,128]{1,0:T(8,128)(2,1)}, bf16[512,128]{1,0:T(8,128)(2,1)S(1)}, u32[]{:S(2)}, u32[]{:S(2)}) %collective-permute-start.1) | collective-permute-done | bytes 131104 | tf_op jit(solution)/shard_map/ppermute | solution.py:202
  22.0 3.3 %collective-permute-start.3 = (bf16[4,512,128]{2,1,0:T(8,128)(2,1)S(1)}, bf16[4,512,128]{2,1,0:T(8,128)(2,1)S(1)}, u32[]{:S(2)}, u32[]{:S(2)}) collective-permute-start(bf16[4,512,128]{2,1,0:T(8,128)(2,1)S(1)} %bitcast_dynamic-update-slice_fusion.refs_0_), channel_id=1, source_target_pairs={{0,64},{16,80},{32,96},{48,112},{64,128},{80,144},{96,160},{112,17... | collective-permute-start | bytes 1572872 | tf_op jit(solution)/shard_map/ppermute | solution.py:173
  25.3 3.8 %collective-permute-start.4 = (bf16[4,512,128]{2,1,0:T(8,128)(2,1)S(1)}, bf16[4,512,128]{2,1,0:T(8,128)(2,1)S(1)}, u32[]{:S(2)}, u32[]{:S(2)}) collective-permute-start(bf16[4,512,128]{2,1,0:T(8,128)(2,1)S(1)} %bitcast_dynamic-update-slice_fusion.refs_0_), channel_id=1, source_target_pairs={{0,448},{16,464},{32,480},{48,496},{64,0},{80,16},{96,32},{112,48}... | collective-permute-start | bytes 1572872 | tf_op jit(solution)/shard_map/ppermute | solution.py:177
  29.1 5.0 %collective-permute-done.3.refs_1_ = bf16[4,512,128]{2,1,0:T(8,128)(2,1)S(1)} collective-permute-done((bf16[4,512,128]{2,1,0:T(8,128)(2,1)S(1)}, bf16[4,512,128]{2,1,0:T(8,128)(2,1)S(1)}, u32[]{:S(2)}, u32[]{:S(2)}) %collective-permute-start.3) | collective-permute-done | bytes 524320 | tf_op jit(solution)/shard_map/ppermute | solution.py:173
  34.2 3.2 %collective-permute-start.5 = (bf16[4,512,128]{2,1,0:T(8,128)(2,1)S(1)}, bf16[4,512,128]{2,1,0:T(8,128)(2,1)S(1)}, u32[]{:S(2)}, u32[]{:S(2)}) collective-permute-start(bf16[4,512,128]{2,1,0:T(8,128)(2,1)S(1)} %collective-permute-done.3.refs_1_), channel_id=1, source_target_pairs={{0,64},{16,80},{32,96},{48,112},{64,128},{80,144},{96,160},{112,17... | collective-permute-start | bytes 1572872 | tf_op jit(solution)/shard_map/ppermute | solution.py:173
  37.3 4.8 %collective-permute-start.6 = (bf16[4,512,128]{2,1,0:T(8,128)(2,1)S(1)}, bf16[4,512,128]{2,1,0:T(8,128)(2,1)S(1)}, u32[]{:S(2)}, u32[]{:S(2)}) collective-permute-start(bf16[4,512,128]{2,1,0:T(8,128)(2,1)S(1)} %collective-permute-done.4.refs_2_), channel_id=1, source_target_pairs={{0,448},{16,464},{32,480},{48,496},{64,0},{80,16},{96,32},{112,48}... | collective-permute-start | bytes 1572872 | tf_op jit(solution)/shard_map/ppermute | solution.py:177
  42.2 5.3 %collective-permute-done.5.refs_3_ = bf16[4,512,128]{2,1,0:T(8,128)(2,1)S(1)} collective-permute-done((bf16[4,512,128]{2,1,0:T(8,128)(2,1)S(1)}, bf16[4,512,128]{2,1,0:T(8,128)(2,1)S(1)}, u32[]{:S(2)}, u32[]{:S(2)}) %collective-permute-start.5) | collective-permute-done | bytes 524320 | tf_op jit(solution)/shard_map/ppermute | solution.py:173
  47.5 2.0 %collective-permute-start.7 = (bf16[4,512,128]{2,1,0:T(8,128)(2,1)S(1)}, bf16[4,512,128]{2,1,0:T(8,128)(2,1)S(1)}, u32[]{:S(2)}, u32[]{:S(2)}) collective-permute-start(bf16[4,512,128]{2,1,0:T(8,128)(2,1)S(1)} %collective-permute-done.5.refs_3_), channel_id=1, source_target_pairs={{0,64},{16,80},{32,96},{48,112},{64,128},{80,144},{96,160},{112,17... | collective-permute-start | bytes 1572872 | tf_op jit(solution)/shard_map/ppermute | solution.py:173
  49.5 9.6 %collective-permute-start.10 = (bf16[4,512,128]{2,1,0:T(8,128)(2,1)S(1)}, bf16[4,512,128]{2,1,0:T(8,128)(2,1)S(1)}, u32[]{:S(2)}, u32[]{:S(2)}) collective-permute-start(bf16[4,512,128]{2,1,0:T(8,128)(2,1)S(1)} %bitcast_dynamic-update-slice_fusion.refs_0_), channel_id=1, source_target_pairs={{0,1},{1,0},{2,3},{3,2},{4,5},{5,4},{6,7},{7,6},{8,9},{9,8},{10,11... | collective-permute-start | bytes 1572872 | tf_op jit(solution)/shard_map/ppermute | solution.py:205
  59.1 1.9 %collective-permute-start.12 = (bf16[4,512,128]{2,1,0:T(8,128)(2,1)S(1)}, bf16[4,512,128]{2,1,0:T(8,128)(2,1)S(1)}, u32[]{:S(2)}, u32[]{:S(2)}) collective-permute-start(bf16[4,512,128]{2,1,0:T(8,128)(2,1)S(1)} %collective-permute-done.4.refs_2_), channel_id=1, source_target_pairs={{0,1},{1,0},{2,3},{3,2},{4,5},{5,4},{6,7},{7,6},{8,9},{9,8},{10,11... | collective-permute-start | bytes 1572872 | tf_op jit(solution)/shard_map/ppermute | solution.py:205
  61.0 2.4 %collective-permute-start.11 = (bf16[4,512,128]{2,1,0:T(8,128)(2,1)S(1)}, bf16[4,512,128]{2,1,0:T(8,128)(2,1)S(1)}, u32[]{:S(2)}, u32[]{:S(2)}) collective-permute-start(bf16[4,512,128]{2,1,0:T(8,128)(2,1)S(1)} %collective-permute-done.3.refs_1_), channel_id=1, source_target_pairs={{0,1},{1,0},{2,3},{3,2},{4,5},{5,4},{6,7},{7,6},{8,9},{9,8},{10,11... | collective-permute-start | bytes 1572872 | tf_op jit(solution)/shard_map/ppermute | solution.py:205
  63.5 4.9 %collective-permute-start.8 = (bf16[4,512,128]{2,1,0:T(8,128)(2,1)S(1)}, bf16[4,512,128]{2,1,0:T(8,128)(2,1)}, u32[]{:S(2)}, u32[]{:S(2)}) collective-permute-start(bf16[4,512,128]{2,1,0:T(8,128)(2,1)S(1)} %collective-permute-done.6.refs_4_), channel_id=1, source_target_pairs={{0,448},{16,464},{32,480},{48,496},{64,0},{80,16},{96,32},{112,48}... | collective-permute-start | bytes 1572872 | tf_op jit(solution)/shard_map/ppermute | solution.py:177
  68.3 1.9 %collective-permute-start.9 = (bf16[4,512,128]{2,1,0:T(8,128)(2,1)S(1)}, bf16[4,512,128]{2,1,0:T(8,128)(2,1)}, u32[]{:S(2)}, u32[]{:S(2)}) collective-permute-start(bf16[4,512,128]{2,1,0:T(8,128)(2,1)S(1)} %collective-permute-done.7.refs_5_), channel_id=1, source_target_pairs={{0,64},{16,80},{32,96},{48,112},{64,128},{80,144},{96,160},{112,17... | collective-permute-start | bytes 1572872 | tf_op jit(solution)/shard_map/ppermute | solution.py:173
  70.3 2.2 %collective-permute-start.14 = (bf16[4,512,128]{2,1,0:T(8,128)(2,1)S(1)}, bf16[4,512,128]{2,1,0:T(8,128)(2,1)}, u32[]{:S(2)}, u32[]{:S(2)}) collective-permute-start(bf16[4,512,128]{2,1,0:T(8,128)(2,1)S(1)} %collective-permute-done.6.refs_4_), channel_id=1, source_target_pairs={{0,1},{1,0},{2,3},{3,2},{4,5},{5,4},{6,7},{7,6},{8,9},{9,8},{10,11... | collective-permute-start | bytes 1572872 | tf_op jit(solution)/shard_map/ppermute | solution.py:205
  72.5 2.1 %collective-permute-start.13 = (bf16[4,512,128]{2,1,0:T(8,128)(2,1)S(1)}, bf16[4,512,128]{2,1,0:T(8,128)(2,1)}, u32[]{:S(2)}, u32[]{:S(2)}) collective-permute-start(bf16[4,512,128]{2,1,0:T(8,128)(2,1)S(1)} %collective-permute-done.5.refs_3_), channel_id=1, source_target_pairs={{0,1},{1,0},{2,3},{3,2},{4,5},{5,4},{6,7},{7,6},{8,9},{9,8},{10,11... | collective-permute-start | bytes 1572872 | tf_op jit(solution)/shard_map/ppermute | solution.py:205
  74.7 2.2 %collective-permute-start.15 = (bf16[4,512,128]{2,1,0:T(8,128)(2,1)S(1)}, bf16[4,512,128]{2,1,0:T(8,128)(2,1)}, u32[]{:S(2)}, u32[]{:S(2)}) collective-permute-start(bf16[4,512,128]{2,1,0:T(8,128)(2,1)S(1)} %collective-permute-done.7.refs_5_), channel_id=1, source_target_pairs={{0,1},{1,0},{2,3},{3,2},{4,5},{5,4},{6,7},{7,6},{8,9},{9,8},{10,11... | collective-permute-start | bytes 1572872 | tf_op jit(solution)/shard_map/ppermute | solution.py:205
  76.9 2.8 %collective-permute-done.8.refs_6_ = bf16[4,512,128]{2,1,0:T(8,128)(2,1)} collective-permute-done((bf16[4,512,128]{2,1,0:T(8,128)(2,1)S(1)}, bf16[4,512,128]{2,1,0:T(8,128)(2,1)}, u32[]{:S(2)}, u32[]{:S(2)}) %collective-permute-start.8) | collective-permute-done | bytes 524320 | tf_op jit(solution)/shard_map/ppermute | solution.py:177
  79.6 2.7 %collective-permute-start.16 = (bf16[4,512,128]{2,1,0:T(8,128)(2,1)}, bf16[4,512,128]{2,1,0:T(8,128)(2,1)}, u32[]{:S(2)}, u32[]{:S(2)}) collective-permute-start(bf16[4,512,128]{2,1,0:T(8,128)(2,1)} %collective-permute-done.8.refs_6_), channel_id=1, source_target_pairs={{0,1},{1,0},{2,3},{3,2},{4,5},{5,4},{6,7},{7,6},{8,9},{9,8},{10,11... | collective-permute-start | bytes 1572872 | tf_op jit(solution)/shard_map/ppermute | solution.py:205
  82.3 2.4 %collective-permute-done.9.refs_7_ = bf16[4,512,128]{2,1,0:T(8,128)(2,1)} collective-permute-done((bf16[4,512,128]{2,1,0:T(8,128)(2,1)S(1)}, bf16[4,512,128]{2,1,0:T(8,128)(2,1)}, u32[]{:S(2)}, u32[]{:S(2)}) %collective-permute-start.9) | collective-permute-done | bytes 524320 | tf_op jit(solution)/shard_map/ppermute | solution.py:173
  84.8 3.0 %collective-permute-start.17 = (bf16[4,512,128]{2,1,0:T(8,128)(2,1)}, bf16[4,512,128]{2,1,0:T(8,128)(2,1)}, u32[]{:S(2)}, u32[]{:S(2)}) collective-permute-start(bf16[4,512,128]{2,1,0:T(8,128)(2,1)} %collective-permute-done.9.refs_7_), channel_id=1, source_target_pairs={{0,1},{1,0},{2,3},{3,2},{4,5},{5,4},{6,7},{7,6},{8,9},{9,8},{10,11... | collective-permute-start | bytes 1572872 | tf_op jit(solution)/shard_map/ppermute | solution.py:205
  87.9 0.9 convert_reduce_fusion
  88.9 0.8 collective-permute-done.17.refs_15_
  89.7 3.2 %all-gather.3.cloned.1.call-done = bf16[24,1024,128]{2,1,0:T(8,128)(2,1)} async-done(((bf16[3,1024,128]{2,1,0:T(8,128)(2,1)}), bf16[24,1024,128]{2,1,0:T(8,128)(2,1)}) %all-gather.3.cloned.1.call-update) | async-done | bytes 6291472 | tf_op jit(solution)/shard_map/all_gather | solution.py:195
  92.9 7.0 %shard_map.64 = (bf16[512,384]{1,0:T(8,128)(2,1)S(1)}, bf16[144,384]{1,0:T(8,128)(2,1)S(1)}) custom-call(s32[6]{0:T(128)S(1)} %pad_add_fusion.place, bf16[4,512,128]{2,1,0:T(8,128)(2,1)S(1)} %bitcast_dynamic-update-slice_fusion.refs_0_, bf16[4,512,128]{2,1,0:T(8,128)(2,1)S(1)} %collective-permute-done.3.refs_1_, bf16[4,512,128]{2,1,0:T(8,128)(2,1)} %copy-done.3, ...), custom_call_target="tpu_custom_call" | custom-call | flops 3221225472 | bytes 16777216 | tf_op jit(solution)/shard_map/pallas_call | solution.py:213
  99.9 1.3 %collective-permute-start.18 = (bf16[144,384]{1,0:T(8,128)(2,1)S(1)}, bf16[144,384]{1,0:T(8,128)(2,1)S(1)}, u32[]{:S(2)}, u32[]{:S(2)}) collective-permute-start(bf16[144,384]{1,0:T(8,128)(2,1)S(1)} %get-tuple-element.10), channel_id=1, source_target_pairs={{0,2},{2,4},{4,6},{6,8},{8,10},{10,12},{12,14},{1,3},{3,5},{5,7},{... | collective-permute-start | bytes 331784 | tf_op jit(solution)/shard_map/ppermute | solution.py:231
  101.3 3.6 %shard_map.65 = (bf16[512,128]{1,0:T(8,128)(2,1)S(1)}, f32[176,128]{1,0:T(8,128)S(1)}, f32[176,128]{1,0:T(8,128)S(1)}) custom-call(s32[6]{0:T(128)S(1)} %pad_add_fusion.place, bf16[512,384]{1,0:T(8,128)(2,1)S(1)} %get-tuple-element.11.raw, f32[7,384]{1,0:T(8,128)S(1)} %bitcast.16, f32[128,128]{1,0:T(8,128)S(1)} %copy-done, f32[1,128]{1,0:T(1,128)S(1)} %bitcast.18), custom_call_target="tpu_custom_call" | custom-call | flops 1610612736 | bytes 2097152 | tf_op jit(solution)/shard_map/pallas_call | solution.py:241
  104.8 2.9 %shard_map.66 = bf16[512,128]{1,0:T(8,128)(2,1)} custom-call(s32[6]{0:T(128)S(1)} %pad_add_fusion.place, bf16[144,384]{1,0:T(8,128)(2,1)S(1)} %collective-permute-done.18.before, bf16[512,384]{1,0:T(8,128)(2,1)S(1)} %get-tuple-element.11.raw, f32[7,384]{1,0:T(8,128)S(1)} %bitcast.17, f32[128,128]{1,0:T(8,128)S(1)} %copy-done, f32[1,128]{1,0:T(1,128)S(1)} %bitcast.19, ...), custom_call_target="tpu_custom_call" | custom-call | flops 805306368 | bytes 1048576 | tf_op jit(solution)/shard_map/pallas_call | solution.py:250
  (40 shorter events, 0.3 us)
Async XLA Ops:
  6.5 86.3 %all-gather.3.cloned.1.call-start = ((), (), s32[]{:S(2)}) async-start(), calls=%async_computation | async-start | bytes 7077888 | tf_op jit(solution)/shard_map/all_gather | solution.py:195
  7.3 11.9 %collective-permute-start = (bf16[512,128]{1,0:T(8,128)(2,1)}, bf16[512,128]{1,0:T(8,128)(2,1)S(1)}, u32[]{:S(2)}, u32[]{:S(2)}) collective-permute-start(bf16[512,128]{1,0:T(8,128)(2,1)} %bitcast.22), channel_id=1, source_target_pairs={{0,16},{16,32},{32,48},{48,0},{64,80},{80,96},{96,112},{112,64},{1... | collective-permute-start | bytes 393224 | tf_op jit(solution)/shard_map/ppermute | solution.py:202
  11.2 10.8 %collective-permute-start.2 = (bf16[512,128]{1,0:T(8,128)(2,1)}, bf16[512,128]{1,0:T(8,128)(2,1)S(1)}, u32[]{:S(2)}, u32[]{:S(2)}) collective-permute-start(bf16[512,128]{1,0:T(8,128)(2,1)} %bitcast.23), channel_id=1, source_target_pairs={{0,48},{16,0},{32,16},{48,32},{64,112},{80,64},{96,80},{112,96},{1... | collective-permute-start | bytes 393224 | tf_op jit(solution)/shard_map/ppermute | solution.py:202
  14.4 7.5 %collective-permute-start.1 = (bf16[512,128]{1,0:T(8,128)(2,1)}, bf16[512,128]{1,0:T(8,128)(2,1)S(1)}, u32[]{:S(2)}, u32[]{:S(2)}) collective-permute-start(bf16[512,128]{1,0:T(8,128)(2,1)} %bitcast.24), channel_id=1, source_target_pairs={{0,32},{16,48},{32,0},{48,16},{64,96},{80,112},{96,64},{112,80},{1... | collective-permute-start | bytes 393224 | tf_op jit(solution)/shard_map/ppermute | solution.py:202
  22.0 12.1 %collective-permute-start.3 = (bf16[4,512,128]{2,1,0:T(8,128)(2,1)S(1)}, bf16[4,512,128]{2,1,0:T(8,128)(2,1)S(1)}, u32[]{:S(2)}, u32[]{:S(2)}) collective-permute-start(bf16[4,512,128]{2,1,0:T(8,128)(2,1)S(1)} %bitcast_dynamic-update-slice_fusion.refs_0_), channel_id=1, source_target_pairs={{0,64},{16,80},{32,96},{48,112},{64,128},{80,144},{96,160},{112,17... | collective-permute-start | bytes 1572872 | tf_op jit(solution)/shard_map/ppermute | solution.py:173
  25.3 12.0 %collective-permute-start.4 = (bf16[4,512,128]{2,1,0:T(8,128)(2,1)S(1)}, bf16[4,512,128]{2,1,0:T(8,128)(2,1)S(1)}, u32[]{:S(2)}, u32[]{:S(2)}) collective-permute-start(bf16[4,512,128]{2,1,0:T(8,128)(2,1)S(1)} %bitcast_dynamic-update-slice_fusion.refs_0_), channel_id=1, source_target_pairs={{0,448},{16,464},{32,480},{48,496},{64,0},{80,16},{96,32},{112,48}... | collective-permute-start | bytes 1572872 | tf_op jit(solution)/shard_map/ppermute | solution.py:177
  34.2 13.3 %collective-permute-start.5 = (bf16[4,512,128]{2,1,0:T(8,128)(2,1)S(1)}, bf16[4,512,128]{2,1,0:T(8,128)(2,1)S(1)}, u32[]{:S(2)}, u32[]{:S(2)}) collective-permute-start(bf16[4,512,128]{2,1,0:T(8,128)(2,1)S(1)} %collective-permute-done.3.refs_1_), channel_id=1, source_target_pairs={{0,64},{16,80},{32,96},{48,112},{64,128},{80,144},{96,160},{112,17... | collective-permute-start | bytes 1572872 | tf_op jit(solution)/shard_map/ppermute | solution.py:173
  37.3 55.6 %copy-start.3 = (bf16[4,512,128]{2,1,0:T(8,128)(2,1)}, bf16[4,512,128]{2,1,0:T(8,128)(2,1)S(1)}, u32[]{:S(2)}) copy-start(bf16[4,512,128]{2,1,0:T(8,128)(2,1)S(1)} %collective-permute-done.4.refs_2_) | copy-start | bytes 1572868
  37.3 26.1 %collective-permute-start.6 = (bf16[4,512,128]{2,1,0:T(8,128)(2,1)S(1)}, bf16[4,512,128]{2,1,0:T(8,128)(2,1)S(1)}, u32[]{:S(2)}, u32[]{:S(2)}) collective-permute-start(bf16[4,512,128]{2,1,0:T(8,128)(2,1)S(1)} %collective-permute-done.4.refs_2_), channel_id=1, source_target_pairs={{0,448},{16,464},{32,480},{48,496},{64,0},{80,16},{96,32},{112,48}... | collective-permute-start | bytes 1572872 | tf_op jit(solution)/shard_map/ppermute | solution.py:177
  47.5 45.4 %copy-start.4 = (bf16[4,512,128]{2,1,0:T(8,128)(2,1)}, bf16[4,512,128]{2,1,0:T(8,128)(2,1)S(1)}, u32[]{:S(2)}) copy-start(bf16[4,512,128]{2,1,0:T(8,128)(2,1)S(1)} %collective-permute-done.5.refs_3_) | copy-start | bytes 1572868
  47.5 20.9 %collective-permute-start.7 = (bf16[4,512,128]{2,1,0:T(8,128)(2,1)S(1)}, bf16[4,512,128]{2,1,0:T(8,128)(2,1)S(1)}, u32[]{:S(2)}, u32[]{:S(2)}) collective-permute-start(bf16[4,512,128]{2,1,0:T(8,128)(2,1)S(1)} %collective-permute-done.5.refs_3_), channel_id=1, source_target_pairs={{0,64},{16,80},{32,96},{48,112},{64,128},{80,144},{96,160},{112,17... | collective-permute-start | bytes 1572872 | tf_op jit(solution)/shard_map/ppermute | solution.py:173
  49.5 20.8 %collective-permute-start.10 = (bf16[4,512,128]{2,1,0:T(8,128)(2,1)S(1)}, bf16[4,512,128]{2,1,0:T(8,128)(2,1)S(1)}, u32[]{:S(2)}, u32[]{:S(2)}) collective-permute-start(bf16[4,512,128]{2,1,0:T(8,128)(2,1)S(1)} %bitcast_dynamic-update-slice_fusion.refs_0_), channel_id=1, source_target_pairs={{0,1},{1,0},{2,3},{3,2},{4,5},{5,4},{6,7},{7,6},{8,9},{9,8},{10,11... | collective-permute-start | bytes 1572872 | tf_op jit(solution)/shard_map/ppermute | solution.py:205
  59.1 13.4 %collective-permute-start.12 = (bf16[4,512,128]{2,1,0:T(8,128)(2,1)S(1)}, bf16[4,512,128]{2,1,0:T(8,128)(2,1)S(1)}, u32[]{:S(2)}, u32[]{:S(2)}) collective-permute-start(bf16[4,512,128]{2,1,0:T(8,128)(2,1)S(1)} %collective-permute-done.4.refs_2_), channel_id=1, source_target_pairs={{0,1},{1,0},{2,3},{3,2},{4,5},{5,4},{6,7},{7,6},{8,9},{9,8},{10,11... | collective-permute-start | bytes 1572872 | tf_op jit(solution)/shard_map/ppermute | solution.py:205
  61.0 13.6 %collective-permute-start.11 = (bf16[4,512,128]{2,1,0:T(8,128)(2,1)S(1)}, bf16[4,512,128]{2,1,0:T(8,128)(2,1)S(1)}, u32[]{:S(2)}, u32[]{:S(2)}) collective-permute-start(bf16[4,512,128]{2,1,0:T(8,128)(2,1)S(1)} %collective-permute-done.3.refs_1_), channel_id=1, source_target_pairs={{0,1},{1,0},{2,3},{3,2},{4,5},{5,4},{6,7},{7,6},{8,9},{9,8},{10,11... | collective-permute-start | bytes 1572872 | tf_op jit(solution)/shard_map/ppermute | solution.py:205
  63.5 29.4 %copy-start.5 = (bf16[4,512,128]{2,1,0:T(8,128)(2,1)}, bf16[4,512,128]{2,1,0:T(8,128)(2,1)S(1)}, u32[]{:S(2)}) copy-start(bf16[4,512,128]{2,1,0:T(8,128)(2,1)S(1)} %collective-permute-done.6.refs_4_) | copy-start | bytes 1572868
  63.5 16.2 %collective-permute-start.8 = (bf16[4,512,128]{2,1,0:T(8,128)(2,1)S(1)}, bf16[4,512,128]{2,1,0:T(8,128)(2,1)}, u32[]{:S(2)}, u32[]{:S(2)}) collective-permute-start(bf16[4,512,128]{2,1,0:T(8,128)(2,1)S(1)} %collective-permute-done.6.refs_4_), channel_id=1, source_target_pairs={{0,448},{16,464},{32,480},{48,496},{64,0},{80,16},{96,32},{112,48}... | collective-permute-start | bytes 1572872 | tf_op jit(solution)/shard_map/ppermute | solution.py:177
  68.3 24.5 %copy-start.6 = (bf16[4,512,128]{2,1,0:T(8,128)(2,1)}, bf16[4,512,128]{2,1,0:T(8,128)(2,1)S(1)}, u32[]{:S(2)}) copy-start(bf16[4,512,128]{2,1,0:T(8,128)(2,1)S(1)} %collective-permute-done.7.refs_5_) | copy-start | bytes 1572868
  68.3 16.4 %collective-permute-start.9 = (bf16[4,512,128]{2,1,0:T(8,128)(2,1)S(1)}, bf16[4,512,128]{2,1,0:T(8,128)(2,1)}, u32[]{:S(2)}, u32[]{:S(2)}) collective-permute-start(bf16[4,512,128]{2,1,0:T(8,128)(2,1)S(1)} %collective-permute-done.7.refs_5_), channel_id=1, source_target_pairs={{0,64},{16,80},{32,96},{48,112},{64,128},{80,144},{96,160},{112,17... | collective-permute-start | bytes 1572872 | tf_op jit(solution)/shard_map/ppermute | solution.py:173
  70.3 14.5 %copy-start.7 = (bf16[4,512,128]{2,1,0:T(8,128)(2,1)}, bf16[4,512,128]{2,1,0:T(8,128)(2,1)S(1)}, u32[]{:S(2)}) copy-start(bf16[4,512,128]{2,1,0:T(8,128)(2,1)S(1)} %collective-permute-done.10.refs_8_) | copy-start | bytes 1572868
  70.3 18.6 %collective-permute-start.14 = (bf16[4,512,128]{2,1,0:T(8,128)(2,1)S(1)}, bf16[4,512,128]{2,1,0:T(8,128)(2,1)}, u32[]{:S(2)}, u32[]{:S(2)}) collective-permute-start(bf16[4,512,128]{2,1,0:T(8,128)(2,1)S(1)} %collective-permute-done.6.refs_4_), channel_id=1, source_target_pairs={{0,1},{1,0},{2,3},{3,2},{4,5},{5,4},{6,7},{7,6},{8,9},{9,8},{10,11... | collective-permute-start | bytes 1572872 | tf_op jit(solution)/shard_map/ppermute | solution.py:205
  72.5 12.3 %copy-start.8 = (bf16[4,512,128]{2,1,0:T(8,128)(2,1)}, bf16[4,512,128]{2,1,0:T(8,128)(2,1)S(1)}, u32[]{:S(2)}) copy-start(bf16[4,512,128]{2,1,0:T(8,128)(2,1)S(1)} %collective-permute-done.12.refs_10_) | copy-start | bytes 1572868
  72.5 16.3 %collective-permute-start.13 = (bf16[4,512,128]{2,1,0:T(8,128)(2,1)S(1)}, bf16[4,512,128]{2,1,0:T(8,128)(2,1)}, u32[]{:S(2)}, u32[]{:S(2)}) collective-permute-start(bf16[4,512,128]{2,1,0:T(8,128)(2,1)S(1)} %collective-permute-done.5.refs_3_), channel_id=1, source_target_pairs={{0,1},{1,0},{2,3},{3,2},{4,5},{5,4},{6,7},{7,6},{8,9},{9,8},{10,11... | collective-permute-start | bytes 1572872 | tf_op jit(solution)/shard_map/ppermute | solution.py:205
  74.7 10.1 %copy-start.9 = (bf16[4,512,128]{2,1,0:T(8,128)(2,1)}, bf16[4,512,128]{2,1,0:T(8,128)(2,1)S(1)}, u32[]{:S(2)}) copy-start(bf16[4,512,128]{2,1,0:T(8,128)(2,1)S(1)} %collective-permute-done.11.refs_9_) | copy-start | bytes 1572868
  74.7 14.2 %collective-permute-start.15 = (bf16[4,512,128]{2,1,0:T(8,128)(2,1)S(1)}, bf16[4,512,128]{2,1,0:T(8,128)(2,1)}, u32[]{:S(2)}, u32[]{:S(2)}) collective-permute-start(bf16[4,512,128]{2,1,0:T(8,128)(2,1)S(1)} %collective-permute-done.7.refs_5_), channel_id=1, source_target_pairs={{0,1},{1,0},{2,3},{3,2},{4,5},{5,4},{6,7},{7,6},{8,9},{9,8},{10,11... | collective-permute-start | bytes 1572872 | tf_op jit(solution)/shard_map/ppermute | solution.py:205
  79.6 9.2 %collective-permute-start.16 = (bf16[4,512,128]{2,1,0:T(8,128)(2,1)}, bf16[4,512,128]{2,1,0:T(8,128)(2,1)}, u32[]{:S(2)}, u32[]{:S(2)}) collective-permute-start(bf16[4,512,128]{2,1,0:T(8,128)(2,1)} %collective-permute-done.8.refs_6_), channel_id=1, source_target_pairs={{0,1},{1,0},{2,3},{3,2},{4,5},{5,4},{6,7},{7,6},{8,9},{9,8},{10,11... | collective-permute-start | bytes 1572872 | tf_op jit(solution)/shard_map/ppermute | solution.py:205
  84.8 4.9 %collective-permute-start.17 = (bf16[4,512,128]{2,1,0:T(8,128)(2,1)}, bf16[4,512,128]{2,1,0:T(8,128)(2,1)}, u32[]{:S(2)}, u32[]{:S(2)}) collective-permute-start(bf16[4,512,128]{2,1,0:T(8,128)(2,1)} %collective-permute-done.9.refs_7_), channel_id=1, source_target_pairs={{0,1},{1,0},{2,3},{3,2},{4,5},{5,4},{6,7},{7,6},{8,9},{9,8},{10,11... | collective-permute-start | bytes 1572872 | tf_op jit(solution)/shard_map/ppermute | solution.py:205
  92.9 8.3 %copy-start = (f32[128,128]{1,0:T(8,128)S(1)}, f32[128,128]{1,0:T(8,128)}, u32[]{:S(2)}) copy-start(f32[128,128]{1,0:T(8,128)} %taps.3) | copy-start | bytes 196612
  92.9 8.3 %copy-start.1 = (f32[7,3,128]{2,0,1:T(8,128)S(1)}, f32[7,3,128]{2,0,1:T(8,128)}, u32[]{:S(2)}) copy-start(f32[7,3,128]{2,0,1:T(8,128)} %param.8) | copy-start | bytes 32260
  92.9 8.3 %copy-start.2 = (f32[128]{0:T(128)S(1)}, f32[128]{0:T(128)}, u32[]{:S(2)}) copy-start(f32[128]{0:T(128)} %param.10) | copy-start | bytes 1540
  99.9 4.9 %collective-permute-start.18 = (bf16[144,384]{1,0:T(8,128)(2,1)S(1)}, bf16[144,384]{1,0:T(8,128)(2,1)S(1)}, u32[]{:S(2)}, u32[]{:S(2)}) collective-permute-start(bf16[144,384]{1,0:T(8,128)(2,1)S(1)} %get-tuple-element.10), channel_id=1, source_target_pairs={{0,2},{2,4},{4,6},{6,8},{8,10},{10,12},{12,14},{1,3},{3,5},{5,7},{... | collective-permute-start | bytes 331784 | tf_op jit(solution)/shard_map/ppermute | solution.py:231
Sparse Core Ops, SparseCore 0:
  9.4 83.3 all-gather.2

commit v9 on v8

--- a/solution.py
+++ b/solution.py
@@ -10,8 +10,8 @@
 PAD = 16
 LEAD = 128 + PAD
 HEAD = 192
-STEP = 64
-AHEAD = 3
+STEP = 128
+AHEAD = 8
 VMEM_DOT = 52
 GROUP = 64
 BF16, F32 = jnp.bfloat16, jnp.float32

time: 115 us -> 115 us (level)
  no operation moved by 1% of the time
where the time goes in v9:
time: 115 us
  starting transfers between devices  62.1 us (54%)
  waiting for transfers between devices  23 us (20%)
  between operations  13.9 us (12%)
  Pallas kernels  13.4 us (12%)
    ppermute x8, starting transfers between devices, body(): others = [lax.ppermute(b, 'tp', swap) for b in blocks]  26.1 us
    ppermute x3, starting transfers between devices, two_way(): down = lax.ppermute(down, axis, hop(-1))  13.5 us
    ppermute x4, waiting for transfers between devices, two_way(): up = lax.ppermute(up, axis, hop(1))  12.8 us
    ppermute x3, starting transfers between devices, body(): piece = lax.ppermute(own, 'fsdp', along_x(hop))  10.8 us
    ppermute x4, starting transfers between devices, two_way(): up = lax.ppermute(up, axis, hop(1))  10.4 us
    pallas_call x1, Pallas kernels, body(): call(functools.partial(project, ys, offsets), (jax.ShapeDtypeStruct((leng...  6.99 us
    pallas_call x1, Pallas kernels, body(): call(main_part, (outline, top, top), [SMEM] + [VMEM] * 4, (VMEM, VMEM, VM...  3.83 us
    all_gather x1, waiting for transfers between devices, body(): weights = lax.all_gather(jnp.transpose(w_in, (1, 0, 2)), 'ctx', axis=0)  3.19 us
  transfers between devices with their start and end apart: 20, of which 7 were waited for; matrix products, arithmetic and copies ran while one was open for 2% of the time, Pallas kernels for 3%

profile of v9, /device:TPU:1, one launch (start us, length us, event | category | flops | bytes accessed | tf_op | source)
XLA Modules:
  0.0 114.5 jit_solution(6358199406024325877)
XLA Ops:
  6.5 0.7 all-gather.3.cloned.1.call-update
  7.3 4.0 %collective-permute-start = (bf16[512,128]{1,0:T(8,128)(2,1)}, bf16[512,128]{1,0:T(8,128)(2,1)S(1)}, u32[]{:S(2)}, u32[]{:S(2)}) collective-permute-start(bf16[512,128]{1,0:T(8,128)(2,1)} %bitcast.22), channel_id=1, source_target_pairs={{0,16},{16,32},{32,48},{48,0},{64,80},{80,96},{96,112},{112,64},{1... | collective-permute-start | bytes 393224 | tf_op jit(solution)/shard_map/ppermute | solution.py:202
  11.2 3.2 %collective-permute-start.2 = (bf16[512,128]{1,0:T(8,128)(2,1)}, bf16[512,128]{1,0:T(8,128)(2,1)S(1)}, u32[]{:S(2)}, u32[]{:S(2)}) collective-permute-start(bf16[512,128]{1,0:T(8,128)(2,1)} %bitcast.23), channel_id=1, source_target_pairs={{0,48},{16,0},{32,16},{48,32},{64,112},{80,64},{96,80},{112,96},{1... | collective-permute-start | bytes 393224 | tf_op jit(solution)/shard_map/ppermute | solution.py:202
  14.4 3.6 %collective-permute-start.1 = (bf16[512,128]{1,0:T(8,128)(2,1)}, bf16[512,128]{1,0:T(8,128)(2,1)S(1)}, u32[]{:S(2)}, u32[]{:S(2)}) collective-permute-start(bf16[512,128]{1,0:T(8,128)(2,1)} %bitcast.24), channel_id=1, source_target_pairs={{0,32},{16,48},{32,0},{48,16},{64,96},{80,112},{96,64},{112,80},{1... | collective-permute-start | bytes 393224 | tf_op jit(solution)/shard_map/ppermute | solution.py:202
  18.2 0.9 constant_dynamic-update-slice_fusion
  19.2 2.8 %collective-permute-done.1 = bf16[512,128]{1,0:T(8,128)(2,1)S(1)} collective-permute-done((bf16[512,128]{1,0:T(8,128)(2,1)}, bf16[512,128]{1,0:T(8,128)(2,1)S(1)}, u32[]{:S(2)}, u32[]{:S(2)}) %collective-permute-start.1) | collective-permute-done | bytes 131104 | tf_op jit(solution)/shard_map/ppermute | solution.py:202
  22.0 3.3 %collective-permute-start.3 = (bf16[4,512,128]{2,1,0:T(8,128)(2,1)S(1)}, bf16[4,512,128]{2,1,0:T(8,128)(2,1)S(1)}, u32[]{:S(2)}, u32[]{:S(2)}) collective-permute-start(bf16[4,512,128]{2,1,0:T(8,128)(2,1)S(1)} %bitcast_dynamic-update-slice_fusion.refs_0_), channel_id=1, source_target_pairs={{0,64},{16,80},{32,96},{48,112},{64,128},{80,144},{96,160},{112,17... | collective-permute-start | bytes 1572872 | tf_op jit(solution)/shard_map/ppermute | solution.py:173
  25.3 3.8 %collective-permute-start.4 = (bf16[4,512,128]{2,1,0:T(8,128)(2,1)S(1)}, bf16[4,512,128]{2,1,0:T(8,128)(2,1)S(1)}, u32[]{:S(2)}, u32[]{:S(2)}) collective-permute-start(bf16[4,512,128]{2,1,0:T(8,128)(2,1)S(1)} %bitcast_dynamic-update-slice_fusion.refs_0_), channel_id=1, source_target_pairs={{0,448},{16,464},{32,480},{48,496},{64,0},{80,16},{96,32},{112,48}... | collective-permute-start | bytes 1572872 | tf_op jit(solution)/shard_map/ppermute | solution.py:177
  29.1 5.0 %collective-permute-done.3.refs_1_ = bf16[4,512,128]{2,1,0:T(8,128)(2,1)S(1)} collective-permute-done((bf16[4,512,128]{2,1,0:T(8,128)(2,1)S(1)}, bf16[4,512,128]{2,1,0:T(8,128)(2,1)S(1)}, u32[]{:S(2)}, u32[]{:S(2)}) %collective-permute-start.3) | collective-permute-done | bytes 524320 | tf_op jit(solution)/shard_map/ppermute | solution.py:173
  34.2 3.2 %collective-permute-start.5 = (bf16[4,512,128]{2,1,0:T(8,128)(2,1)S(1)}, bf16[4,512,128]{2,1,0:T(8,128)(2,1)S(1)}, u32[]{:S(2)}, u32[]{:S(2)}) collective-permute-start(bf16[4,512,128]{2,1,0:T(8,128)(2,1)S(1)} %collective-permute-done.3.refs_1_), channel_id=1, source_target_pairs={{0,64},{16,80},{32,96},{48,112},{64,128},{80,144},{96,160},{112,17... | collective-permute-start | bytes 1572872 | tf_op jit(solution)/shard_map/ppermute | solution.py:173
  37.3 4.8 %collective-permute-start.6 = (bf16[4,512,128]{2,1,0:T(8,128)(2,1)S(1)}, bf16[4,512,128]{2,1,0:T(8,128)(2,1)S(1)}, u32[]{:S(2)}, u32[]{:S(2)}) collective-permute-start(bf16[4,512,128]{2,1,0:T(8,128)(2,1)S(1)} %collective-permute-done.4.refs_2_), channel_id=1, source_target_pairs={{0,448},{16,464},{32,480},{48,496},{64,0},{80,16},{96,32},{112,48}... | collective-permute-start | bytes 1572872 | tf_op jit(solution)/shard_map/ppermute | solution.py:177
  42.2 5.3 %collective-permute-done.5.refs_3_ = bf16[4,512,128]{2,1,0:T(8,128)(2,1)S(1)} collective-permute-done((bf16[4,512,128]{2,1,0:T(8,128)(2,1)S(1)}, bf16[4,512,128]{2,1,0:T(8,128)(2,1)S(1)}, u32[]{:S(2)}, u32[]{:S(2)}) %collective-permute-start.5) | collective-permute-done | bytes 524320 | tf_op jit(solution)/shard_map/ppermute | solution.py:173
  47.5 2.0 %collective-permute-start.7 = (bf16[4,512,128]{2,1,0:T(8,128)(2,1)S(1)}, bf16[4,512,128]{2,1,0:T(8,128)(2,1)S(1)}, u32[]{:S(2)}, u32[]{:S(2)}) collective-permute-start(bf16[4,512,128]{2,1,0:T(8,128)(2,1)S(1)} %collective-permute-done.5.refs_3_), channel_id=1, source_target_pairs={{0,64},{16,80},{32,96},{48,112},{64,128},{80,144},{96,160},{112,17... | collective-permute-start | bytes 1572872 | tf_op jit(solution)/shard_map/ppermute | solution.py:173
  49.5 9.6 %collective-permute-start.10 = (bf16[4,512,128]{2,1,0:T(8,128)(2,1)S(1)}, bf16[4,512,128]{2,1,0:T(8,128)(2,1)S(1)}, u32[]{:S(2)}, u32[]{:S(2)}) collective-permute-start(bf16[4,512,128]{2,1,0:T(8,128)(2,1)S(1)} %bitcast_dynamic-update-slice_fusion.refs_0_), channel_id=1, source_target_pairs={{0,1},{1,0},{2,3},{3,2},{4,5},{5,4},{6,7},{7,6},{8,9},{9,8},{10,11... | collective-permute-start | bytes 1572872 | tf_op jit(solution)/shard_map/ppermute | solution.py:205
  59.1 1.9 %collective-permute-start.12 = (bf16[4,512,128]{2,1,0:T(8,128)(2,1)S(1)}, bf16[4,512,128]{2,1,0:T(8,128)(2,1)S(1)}, u32[]{:S(2)}, u32[]{:S(2)}) collective-permute-start(bf16[4,512,128]{2,1,0:T(8,128)(2,1)S(1)} %collective-permute-done.4.refs_2_), channel_id=1, source_target_pairs={{0,1},{1,0},{2,3},{3,2},{4,5},{5,4},{6,7},{7,6},{8,9},{9,8},{10,11... | collective-permute-start | bytes 1572872 | tf_op jit(solution)/shard_map/ppermute | solution.py:205
  61.0 2.4 %collective-permute-start.11 = (bf16[4,512,128]{2,1,0:T(8,128)(2,1)S(1)}, bf16[4,512,128]{2,1,0:T(8,128)(2,1)S(1)}, u32[]{:S(2)}, u32[]{:S(2)}) collective-permute-start(bf16[4,512,128]{2,1,0:T(8,128)(2,1)S(1)} %collective-permute-done.3.refs_1_), channel_id=1, source_target_pairs={{0,1},{1,0},{2,3},{3,2},{4,5},{5,4},{6,7},{7,6},{8,9},{9,8},{10,11... | collective-permute-start | bytes 1572872 | tf_op jit(solution)/shard_map/ppermute | solution.py:205
  63.5 4.9 %collective-permute-start.8 = (bf16[4,512,128]{2,1,0:T(8,128)(2,1)S(1)}, bf16[4,512,128]{2,1,0:T(8,128)(2,1)}, u32[]{:S(2)}, u32[]{:S(2)}) collective-permute-start(bf16[4,512,128]{2,1,0:T(8,128)(2,1)S(1)} %collective-permute-done.6.refs_4_), channel_id=1, source_target_pairs={{0,448},{16,464},{32,480},{48,496},{64,0},{80,16},{96,32},{112,48}... | collective-permute-start | bytes 1572872 | tf_op jit(solution)/shard_map/ppermute | solution.py:177
  68.3 1.9 %collective-permute-start.9 = (bf16[4,512,128]{2,1,0:T(8,128)(2,1)S(1)}, bf16[4,512,128]{2,1,0:T(8,128)(2,1)}, u32[]{:S(2)}, u32[]{:S(2)}) collective-permute-start(bf16[4,512,128]{2,1,0:T(8,128)(2,1)S(1)} %collective-permute-done.7.refs_5_), channel_id=1, source_target_pairs={{0,64},{16,80},{32,96},{48,112},{64,128},{80,144},{96,160},{112,17... | collective-permute-start | bytes 1572872 | tf_op jit(solution)/shard_map/ppermute | solution.py:173
  70.3 2.2 %collective-permute-start.14 = (bf16[4,512,128]{2,1,0:T(8,128)(2,1)S(1)}, bf16[4,512,128]{2,1,0:T(8,128)(2,1)}, u32[]{:S(2)}, u32[]{:S(2)}) collective-permute-start(bf16[4,512,128]{2,1,0:T(8,128)(2,1)S(1)} %collective-permute-done.6.refs_4_), channel_id=1, source_target_pairs={{0,1},{1,0},{2,3},{3,2},{4,5},{5,4},{6,7},{7,6},{8,9},{9,8},{10,11... | collective-permute-start | bytes 1572872 | tf_op jit(solution)/shard_map/ppermute | solution.py:205
  72.5 2.1 %collective-permute-start.13 = (bf16[4,512,128]{2,1,0:T(8,128)(2,1)S(1)}, bf16[4,512,128]{2,1,0:T(8,128)(2,1)}, u32[]{:S(2)}, u32[]{:S(2)}) collective-permute-start(bf16[4,512,128]{2,1,0:T(8,128)(2,1)S(1)} %collective-permute-done.5.refs_3_), channel_id=1, source_target_pairs={{0,1},{1,0},{2,3},{3,2},{4,5},{5,4},{6,7},{7,6},{8,9},{9,8},{10,11... | collective-permute-start | bytes 1572872 | tf_op jit(solution)/shard_map/ppermute | solution.py:205
  74.7 2.2 %collective-permute-start.15 = (bf16[4,512,128]{2,1,0:T(8,128)(2,1)S(1)}, bf16[4,512,128]{2,1,0:T(8,128)(2,1)}, u32[]{:S(2)}, u32[]{:S(2)}) collective-permute-start(bf16[4,512,128]{2,1,0:T(8,128)(2,1)S(1)} %collective-permute-done.7.refs_5_), channel_id=1, source_target_pairs={{0,1},{1,0},{2,3},{3,2},{4,5},{5,4},{6,7},{7,6},{8,9},{9,8},{10,11... | collective-permute-start | bytes 1572872 | tf_op jit(solution)/shard_map/ppermute | solution.py:205
  76.9 2.8 %collective-permute-done.8.refs_6_ = bf16[4,512,128]{2,1,0:T(8,128)(2,1)} collective-permute-done((bf16[4,512,128]{2,1,0:T(8,128)(2,1)S(1)}, bf16[4,512,128]{2,1,0:T(8,128)(2,1)}, u32[]{:S(2)}, u32[]{:S(2)}) %collective-permute-start.8) | collective-permute-done | bytes 524320 | tf_op jit(solution)/shard_map/ppermute | solution.py:177
  79.6 2.7 %collective-permute-start.16 = (bf16[4,512,128]{2,1,0:T(8,128)(2,1)}, bf16[4,512,128]{2,1,0:T(8,128)(2,1)}, u32[]{:S(2)}, u32[]{:S(2)}) collective-permute-start(bf16[4,512,128]{2,1,0:T(8,128)(2,1)} %collective-permute-done.8.refs_6_), channel_id=1, source_target_pairs={{0,1},{1,0},{2,3},{3,2},{4,5},{5,4},{6,7},{7,6},{8,9},{9,8},{10,11... | collective-permute-start | bytes 1572872 | tf_op jit(solution)/shard_map/ppermute | solution.py:205
  82.3 2.4 %collective-permute-done.9.refs_7_ = bf16[4,512,128]{2,1,0:T(8,128)(2,1)} collective-permute-done((bf16[4,512,128]{2,1,0:T(8,128)(2,1)S(1)}, bf16[4,512,128]{2,1,0:T(8,128)(2,1)}, u32[]{:S(2)}, u32[]{:S(2)}) %collective-permute-start.9) | collective-permute-done | bytes 524320 | tf_op jit(solution)/shard_map/ppermute | solution.py:173
  84.8 3.0 %collective-permute-start.17 = (bf16[4,512,128]{2,1,0:T(8,128)(2,1)}, bf16[4,512,128]{2,1,0:T(8,128)(2,1)}, u32[]{:S(2)}, u32[]{:S(2)}) collective-permute-start(bf16[4,512,128]{2,1,0:T(8,128)(2,1)} %collective-permute-done.9.refs_7_), channel_id=1, source_target_pairs={{0,1},{1,0},{2,3},{3,2},{4,5},{5,4},{6,7},{7,6},{8,9},{9,8},{10,11... | collective-permute-start | bytes 1572872 | tf_op jit(solution)/shard_map/ppermute | solution.py:205
  87.9 0.9 convert_reduce_fusion
  88.9 0.8 collective-permute-done.17.refs_15_
  89.7 3.2 %all-gather.3.cloned.1.call-done = bf16[24,1024,128]{2,1,0:T(8,128)(2,1)} async-done(((bf16[3,1024,128]{2,1,0:T(8,128)(2,1)}), bf16[24,1024,128]{2,1,0:T(8,128)(2,1)}) %all-gather.3.cloned.1.call-update) | async-done | bytes 6291472 | tf_op jit(solution)/shard_map/all_gather | solution.py:195
  92.9 7.0 %shard_map.64 = (bf16[512,384]{1,0:T(8,128)(2,1)S(1)}, bf16[144,384]{1,0:T(8,128)(2,1)S(1)}) custom-call(s32[6]{0:T(128)S(1)} %pad_add_fusion.place, bf16[4,512,128]{2,1,0:T(8,128)(2,1)S(1)} %bitcast_dynamic-update-slice_fusion.refs_0_, bf16[4,512,128]{2,1,0:T(8,128)(2,1)S(1)} %collective-permute-done.3.refs_1_, bf16[4,512,128]{2,1,0:T(8,128)(2,1)} %copy-done.3, ...), custom_call_target="tpu_custom_call" | custom-call | flops 3221225472 | bytes 16777216 | tf_op jit(solution)/shard_map/pallas_call | solution.py:213
  99.9 1.3 %collective-permute-start.18 = (bf16[144,384]{1,0:T(8,128)(2,1)S(1)}, bf16[144,384]{1,0:T(8,128)(2,1)S(1)}, u32[]{:S(2)}, u32[]{:S(2)}) collective-permute-start(bf16[144,384]{1,0:T(8,128)(2,1)S(1)} %get-tuple-element.10), channel_id=1, source_target_pairs={{0,2},{2,4},{4,6},{6,8},{8,10},{10,12},{12,14},{1,3},{3,5},{5,7},{... | collective-permute-start | bytes 331784 | tf_op jit(solution)/shard_map/ppermute | solution.py:231
  101.3 3.8 %shard_map.65 = (bf16[512,128]{1,0:T(8,128)(2,1)S(1)}, f32[176,128]{1,0:T(8,128)S(1)}, f32[176,128]{1,0:T(8,128)S(1)}) custom-call(s32[6]{0:T(128)S(1)} %pad_add_fusion.place, bf16[512,384]{1,0:T(8,128)(2,1)S(1)} %get-tuple-element.11.raw, f32[7,384]{1,0:T(8,128)S(1)} %bitcast.16, f32[128,128]{1,0:T(8,128)S(1)} %copy-done, f32[1,128]{1,0:T(1,128)S(1)} %bitcast.18), custom_call_target="tpu_custom_call" | custom-call | flops 1610612736 | bytes 2097152 | tf_op jit(solution)/shard_map/pallas_call | solution.py:241
  105.1 2.6 %shard_map.66 = bf16[512,128]{1,0:T(8,128)(2,1)} custom-call(s32[6]{0:T(128)S(1)} %pad_add_fusion.place, bf16[144,384]{1,0:T(8,128)(2,1)S(1)} %collective-permute-done.18.before, bf16[512,384]{1,0:T(8,128)(2,1)S(1)} %get-tuple-element.11.raw, f32[7,384]{1,0:T(8,128)S(1)} %bitcast.17, f32[128,128]{1,0:T(8,128)S(1)} %copy-done, f32[1,128]{1,0:T(1,128)S(1)} %bitcast.19, ...), custom_call_target="tpu_custom_call" | custom-call | flops 805306368 | bytes 1048576 | tf_op jit(solution)/shard_map/pallas_call | solution.py:250
  (40 shorter events, 0.3 us)
Async XLA Ops:
  6.5 86.3 %all-gather.3.cloned.1.call-start = ((), (), s32[]{:S(2)}) async-start(), calls=%async_computation | async-start | bytes 7077888 | tf_op jit(solution)/shard_map/all_gather | solution.py:195
  7.3 11.9 %collective-permute-start = (bf16[512,128]{1,0:T(8,128)(2,1)}, bf16[512,128]{1,0:T(8,128)(2,1)S(1)}, u32[]{:S(2)}, u32[]{:S(2)}) collective-permute-start(bf16[512,128]{1,0:T(8,128)(2,1)} %bitcast.22), channel_id=1, source_target_pairs={{0,16},{16,32},{32,48},{48,0},{64,80},{80,96},{96,112},{112,64},{1... | collective-permute-start | bytes 393224 | tf_op jit(solution)/shard_map/ppermute | solution.py:202
  11.2 10.8 %collective-permute-start.2 = (bf16[512,128]{1,0:T(8,128)(2,1)}, bf16[512,128]{1,0:T(8,128)(2,1)S(1)}, u32[]{:S(2)}, u32[]{:S(2)}) collective-permute-start(bf16[512,128]{1,0:T(8,128)(2,1)} %bitcast.23), channel_id=1, source_target_pairs={{0,48},{16,0},{32,16},{48,32},{64,112},{80,64},{96,80},{112,96},{1... | collective-permute-start | bytes 393224 | tf_op jit(solution)/shard_map/ppermute | solution.py:202
  14.4 7.5 %collective-permute-start.1 = (bf16[512,128]{1,0:T(8,128)(2,1)}, bf16[512,128]{1,0:T(8,128)(2,1)S(1)}, u32[]{:S(2)}, u32[]{:S(2)}) collective-permute-start(bf16[512,128]{1,0:T(8,128)(2,1)} %bitcast.24), channel_id=1, source_target_pairs={{0,32},{16,48},{32,0},{48,16},{64,96},{80,112},{96,64},{112,80},{1... | collective-permute-start | bytes 393224 | tf_op jit(solution)/shard_map/ppermute | solution.py:202
  22.0 12.1 %collective-permute-start.3 = (bf16[4,512,128]{2,1,0:T(8,128)(2,1)S(1)}, bf16[4,512,128]{2,1,0:T(8,128)(2,1)S(1)}, u32[]{:S(2)}, u32[]{:S(2)}) collective-permute-start(bf16[4,512,128]{2,1,0:T(8,128)(2,1)S(1)} %bitcast_dynamic-update-slice_fusion.refs_0_), channel_id=1, source_target_pairs={{0,64},{16,80},{32,96},{48,112},{64,128},{80,144},{96,160},{112,17... | collective-permute-start | bytes 1572872 | tf_op jit(solution)/shard_map/ppermute | solution.py:173
  25.3 12.0 %collective-permute-start.4 = (bf16[4,512,128]{2,1,0:T(8,128)(2,1)S(1)}, bf16[4,512,128]{2,1,0:T(8,128)(2,1)S(1)}, u32[]{:S(2)}, u32[]{:S(2)}) collective-permute-start(bf16[4,512,128]{2,1,0:T(8,128)(2,1)S(1)} %bitcast_dynamic-update-slice_fusion.refs_0_), channel_id=1, source_target_pairs={{0,448},{16,464},{32,480},{48,496},{64,0},{80,16},{96,32},{112,48}... | collective-permute-start | bytes 1572872 | tf_op jit(solution)/shard_map/ppermute | solution.py:177
  34.2 13.3 %collective-permute-start.5 = (bf16[4,512,128]{2,1,0:T(8,128)(2,1)S(1)}, bf16[4,512,128]{2,1,0:T(8,128)(2,1)S(1)}, u32[]{:S(2)}, u32[]{:S(2)}) collective-permute-start(bf16[4,512,128]{2,1,0:T(8,128)(2,1)S(1)} %collective-permute-done.3.refs_1_), channel_id=1, source_target_pairs={{0,64},{16,80},{32,96},{48,112},{64,128},{80,144},{96,160},{112,17... | collective-permute-start | bytes 1572872 | tf_op jit(solution)/shard_map/ppermute | solution.py:173
  37.3 55.6 %copy-start.3 = (bf16[4,512,128]{2,1,0:T(8,128)(2,1)}, bf16[4,512,128]{2,1,0:T(8,128)(2,1)S(1)}, u32[]{:S(2)}) copy-start(bf16[4,512,128]{2,1,0:T(8,128)(2,1)S(1)} %collective-permute-done.4.refs_2_) | copy-start | bytes 1572868
  37.3 26.1 %collective-permute-start.6 = (bf16[4,512,128]{2,1,0:T(8,128)(2,1)S(1)}, bf16[4,512,128]{2,1,0:T(8,128)(2,1)S(1)}, u32[]{:S(2)}, u32[]{:S(2)}) collective-permute-start(bf16[4,512,128]{2,1,0:T(8,128)(2,1)S(1)} %collective-permute-done.4.refs_2_), channel_id=1, source_target_pairs={{0,448},{16,464},{32,480},{48,496},{64,0},{80,16},{96,32},{112,48}... | collective-permute-start | bytes 1572872 | tf_op jit(solution)/shard_map/ppermute | solution.py:177
  47.5 45.4 %copy-start.4 = (bf16[4,512,128]{2,1,0:T(8,128)(2,1)}, bf16[4,512,128]{2,1,0:T(8,128)(2,1)S(1)}, u32[]{:S(2)}) copy-start(bf16[4,512,128]{2,1,0:T(8,128)(2,1)S(1)} %collective-permute-done.5.refs_3_) | copy-start | bytes 1572868
  47.5 20.9 %collective-permute-start.7 = (bf16[4,512,128]{2,1,0:T(8,128)(2,1)S(1)}, bf16[4,512,128]{2,1,0:T(8,128)(2,1)S(1)}, u32[]{:S(2)}, u32[]{:S(2)}) collective-permute-start(bf16[4,512,128]{2,1,0:T(8,128)(2,1)S(1)} %collective-permute-done.5.refs_3_), channel_id=1, source_target_pairs={{0,64},{16,80},{32,96},{48,112},{64,128},{80,144},{96,160},{112,17... | collective-permute-start | bytes 1572872 | tf_op jit(solution)/shard_map/ppermute | solution.py:173
  49.5 20.8 %collective-permute-start.10 = (bf16[4,512,128]{2,1,0:T(8,128)(2,1)S(1)}, bf16[4,512,128]{2,1,0:T(8,128)(2,1)S(1)}, u32[]{:S(2)}, u32[]{:S(2)}) collective-permute-start(bf16[4,512,128]{2,1,0:T(8,128)(2,1)S(1)} %bitcast_dynamic-update-slice_fusion.refs_0_), channel_id=1, source_target_pairs={{0,1},{1,0},{2,3},{3,2},{4,5},{5,4},{6,7},{7,6},{8,9},{9,8},{10,11... | collective-permute-start | bytes 1572872 | tf_op jit(solution)/shard_map/ppermute | solution.py:205
  59.1 13.4 %collective-permute-start.12 = (bf16[4,512,128]{2,1,0:T(8,128)(2,1)S(1)}, bf16[4,512,128]{2,1,0:T(8,128)(2,1)S(1)}, u32[]{:S(2)}, u32[]{:S(2)}) collective-permute-start(bf16[4,512,128]{2,1,0:T(8,128)(2,1)S(1)} %collective-permute-done.4.refs_2_), channel_id=1, source_target_pairs={{0,1},{1,0},{2,3},{3,2},{4,5},{5,4},{6,7},{7,6},{8,9},{9,8},{10,11... | collective-permute-start | bytes 1572872 | tf_op jit(solution)/shard_map/ppermute | solution.py:205
  61.0 13.6 %collective-permute-start.11 = (bf16[4,512,128]{2,1,0:T(8,128)(2,1)S(1)}, bf16[4,512,128]{2,1,0:T(8,128)(2,1)S(1)}, u32[]{:S(2)}, u32[]{:S(2)}) collective-permute-start(bf16[4,512,128]{2,1,0:T(8,128)(2,1)S(1)} %collective-permute-done.3.refs_1_), channel_id=1, source_target_pairs={{0,1},{1,0},{2,3},{3,2},{4,5},{5,4},{6,7},{7,6},{8,9},{9,8},{10,11... | collective-permute-start | bytes 1572872 | tf_op jit(solution)/shard_map/ppermute | solution.py:205
  63.5 29.4 %copy-start.5 = (bf16[4,512,128]{2,1,0:T(8,128)(2,1)}, bf16[4,512,128]{2,1,0:T(8,128)(2,1)S(1)}, u32[]{:S(2)}) copy-start(bf16[4,512,128]{2,1,0:T(8,128)(2,1)S(1)} %collective-permute-done.6.refs_4_) | copy-start | bytes 1572868
  63.5 16.2 %collective-permute-start.8 = (bf16[4,512,128]{2,1,0:T(8,128)(2,1)S(1)}, bf16[4,512,128]{2,1,0:T(8,128)(2,1)}, u32[]{:S(2)}, u32[]{:S(2)}) collective-permute-start(bf16[4,512,128]{2,1,0:T(8,128)(2,1)S(1)} %collective-permute-done.6.refs_4_), channel_id=1, source_target_pairs={{0,448},{16,464},{32,480},{48,496},{64,0},{80,16},{96,32},{112,48}... | collective-permute-start | bytes 1572872 | tf_op jit(solution)/shard_map/ppermute | solution.py:177
  68.3 24.5 %copy-start.6 = (bf16[4,512,128]{2,1,0:T(8,128)(2,1)}, bf16[4,512,128]{2,1,0:T(8,128)(2,1)S(1)}, u32[]{:S(2)}) copy-start(bf16[4,512,128]{2,1,0:T(8,128)(2,1)S(1)} %collective-permute-done.7.refs_5_) | copy-start | bytes 1572868
  68.3 16.4 %collective-permute-start.9 = (bf16[4,512,128]{2,1,0:T(8,128)(2,1)S(1)}, bf16[4,512,128]{2,1,0:T(8,128)(2,1)}, u32[]{:S(2)}, u32[]{:S(2)}) collective-permute-start(bf16[4,512,128]{2,1,0:T(8,128)(2,1)S(1)} %collective-permute-done.7.refs_5_), channel_id=1, source_target_pairs={{0,64},{16,80},{32,96},{48,112},{64,128},{80,144},{96,160},{112,17... | collective-permute-start | bytes 1572872 | tf_op jit(solution)/shard_map/ppermute | solution.py:173
  70.3 14.5 %copy-start.7 = (bf16[4,512,128]{2,1,0:T(8,128)(2,1)}, bf16[4,512,128]{2,1,0:T(8,128)(2,1)S(1)}, u32[]{:S(2)}) copy-start(bf16[4,512,128]{2,1,0:T(8,128)(2,1)S(1)} %collective-permute-done.10.refs_8_) | copy-start | bytes 1572868
  70.3 18.6 %collective-permute-start.14 = (bf16[4,512,128]{2,1,0:T(8,128)(2,1)S(1)}, bf16[4,512,128]{2,1,0:T(8,128)(2,1)}, u32[]{:S(2)}, u32[]{:S(2)}) collective-permute-start(bf16[4,512,128]{2,1,0:T(8,128)(2,1)S(1)} %collective-permute-done.6.refs_4_), channel_id=1, source_target_pairs={{0,1},{1,0},{2,3},{3,2},{4,5},{5,4},{6,7},{7,6},{8,9},{9,8},{10,11... | collective-permute-start | bytes 1572872 | tf_op jit(solution)/shard_map/ppermute | solution.py:205
  72.5 12.3 %copy-start.8 = (bf16[4,512,128]{2,1,0:T(8,128)(2,1)}, bf16[4,512,128]{2,1,0:T(8,128)(2,1)S(1)}, u32[]{:S(2)}) copy-start(bf16[4,512,128]{2,1,0:T(8,128)(2,1)S(1)} %collective-permute-done.12.refs_10_) | copy-start | bytes 1572868
  72.5 16.3 %collective-permute-start.13 = (bf16[4,512,128]{2,1,0:T(8,128)(2,1)S(1)}, bf16[4,512,128]{2,1,0:T(8,128)(2,1)}, u32[]{:S(2)}, u32[]{:S(2)}) collective-permute-start(bf16[4,512,128]{2,1,0:T(8,128)(2,1)S(1)} %collective-permute-done.5.refs_3_), channel_id=1, source_target_pairs={{0,1},{1,0},{2,3},{3,2},{4,5},{5,4},{6,7},{7,6},{8,9},{9,8},{10,11... | collective-permute-start | bytes 1572872 | tf_op jit(solution)/shard_map/ppermute | solution.py:205
  74.7 10.1 %copy-start.9 = (bf16[4,512,128]{2,1,0:T(8,128)(2,1)}, bf16[4,512,128]{2,1,0:T(8,128)(2,1)S(1)}, u32[]{:S(2)}) copy-start(bf16[4,512,128]{2,1,0:T(8,128)(2,1)S(1)} %collective-permute-done.11.refs_9_) | copy-start | bytes 1572868
  74.7 14.2 %collective-permute-start.15 = (bf16[4,512,128]{2,1,0:T(8,128)(2,1)S(1)}, bf16[4,512,128]{2,1,0:T(8,128)(2,1)}, u32[]{:S(2)}, u32[]{:S(2)}) collective-permute-start(bf16[4,512,128]{2,1,0:T(8,128)(2,1)S(1)} %collective-permute-done.7.refs_5_), channel_id=1, source_target_pairs={{0,1},{1,0},{2,3},{3,2},{4,5},{5,4},{6,7},{7,6},{8,9},{9,8},{10,11... | collective-permute-start | bytes 1572872 | tf_op jit(solution)/shard_map/ppermute | solution.py:205
  79.6 9.2 %collective-permute-start.16 = (bf16[4,512,128]{2,1,0:T(8,128)(2,1)}, bf16[4,512,128]{2,1,0:T(8,128)(2,1)}, u32[]{:S(2)}, u32[]{:S(2)}) collective-permute-start(bf16[4,512,128]{2,1,0:T(8,128)(2,1)} %collective-permute-done.8.refs_6_), channel_id=1, source_target_pairs={{0,1},{1,0},{2,3},{3,2},{4,5},{5,4},{6,7},{7,6},{8,9},{9,8},{10,11... | collective-permute-start | bytes 1572872 | tf_op jit(solution)/shard_map/ppermute | solution.py:205
  84.8 4.9 %collective-permute-start.17 = (bf16[4,512,128]{2,1,0:T(8,128)(2,1)}, bf16[4,512,128]{2,1,0:T(8,128)(2,1)}, u32[]{:S(2)}, u32[]{:S(2)}) collective-permute-start(bf16[4,512,128]{2,1,0:T(8,128)(2,1)} %collective-permute-done.9.refs_7_), channel_id=1, source_target_pairs={{0,1},{1,0},{2,3},{3,2},{4,5},{5,4},{6,7},{7,6},{8,9},{9,8},{10,11... | collective-permute-start | bytes 1572872 | tf_op jit(solution)/shard_map/ppermute | solution.py:205
  92.9 8.3 %copy-start = (f32[128,128]{1,0:T(8,128)S(1)}, f32[128,128]{1,0:T(8,128)}, u32[]{:S(2)}) copy-start(f32[128,128]{1,0:T(8,128)} %taps.3) | copy-start | bytes 196612
  92.9 8.3 %copy-start.1 = (f32[7,3,128]{2,0,1:T(8,128)S(1)}, f32[7,3,128]{2,0,1:T(8,128)}, u32[]{:S(2)}) copy-start(f32[7,3,128]{2,0,1:T(8,128)} %param.8) | copy-start | bytes 32260
  92.9 8.3 %copy-start.2 = (f32[128]{0:T(128)S(1)}, f32[128]{0:T(128)}, u32[]{:S(2)}) copy-start(f32[128]{0:T(128)} %param.10) | copy-start | bytes 1540
  99.9 5.2 %collective-permute-start.18 = (bf16[144,384]{1,0:T(8,128)(2,1)S(1)}, bf16[144,384]{1,0:T(8,128)(2,1)S(1)}, u32[]{:S(2)}, u32[]{:S(2)}) collective-permute-start(bf16[144,384]{1,0:T(8,128)(2,1)S(1)} %get-tuple-element.10), channel_id=1, source_target_pairs={{0,2},{2,4},{4,6},{6,8},{8,10},{10,12},{12,14},{1,3},{3,5},{5,7},{... | collective-permute-start | bytes 331784 | tf_op jit(solution)/shard_map/ppermute | solution.py:231
Sparse Core Ops, SparseCore 0:
  9.4 83.3 all-gather.2
